TPU v7x, 32 devices: a whole 2x2x4 slice. The times are simulated.
32 devices in a mesh: groups: 2 (over y), video: 4 (over x, core), frame: 4 (over z).
Axes of the slice: x: 2, y: 2, z: 4, core: 2. Of those that a mesh axis runs over, the one named last changes fastest.
Arguments:
- latents: bfloat16 [8, 4, 256, 320], P(('groups', 'video'), 'frame'), parts along dimension 0, may hold values from -6 to 6
- timesteps: int32 [8], P(('groups', 'video')), parts along dimension 0, may hold values from 0 to 999
- matchings: int32 [2, 8], P(None, 'groups'), parts along dimension 1, may hold values from 0 to 3, each once within a row
- tile_mask: int32 [2, 8, 2, 2], P(None, 'groups'), parts along dimension 1, may hold values from 0 to 1, as said below
- conv_first: bfloat16 [3, 3, 320, 320], replicated, may hold values from -0.109375 to 0.109375
- conv_second: bfloat16 [3, 3, 320, 320], replicated, may hold values from -0.109375 to 0.109375
- time_proj: bfloat16 [1280, 320], P('frame'), may hold values from -0.15625 to 0.15625
- epi_in: bfloat16 [3, 320, 320], P(None, 'frame'), may hold values from -48 to 48
- epi_out: bfloat16 [320, 320], P('frame'), may hold values from -0.3125 to 0.3125
- temp_in: bfloat16 [3, 320, 320], P(None, 'frame'), may hold values from -48 to 48
- temp_out: bfloat16 [320, 320], P('frame'), may hold values from -0.3125 to 0.3125
Outputs:
- denoised: bfloat16 [8, 4, 256, 320], P(('groups', 'video'), 'frame'), parts along dimension 0
There are 2 independent parts, one for each index of `groups`. A program takes and returns all parts, laid end to end along the dimension named above; an argument that names none is the same for every part. Nothing has to cross between parts.
Inputs may be any that keep to these rules, and one draw needn't show every extreme that they name: Every row tile_mask[m, u, i, :] holds at least one 1.
All inputs are finite; a program needn't handle non-finite values.
Results may differ from a plain program's by a relative error of at most 0.035.
Values may be sent and summed in bfloat16 or wider, within the bound.
No kernel may reach another device: no remote copies, remote signals or barrier semaphores. Data moves between devices by JAX's collectives and lax.ppermute only.
A program may use at most 64 MiB of HBM per device.

v0:
```python
import math

import jax
import jax.numpy as jnp
from jax import lax
from jax.sharding import PartitionSpec as P

HEADS = 8
NORM_GROUPS = 32
TEMB = 1280
H = 8
W = 32


epsilon = 1e-05
masked_fill = -1e30


def group_norm(values):
    row_count, channels = values.shape
    grouped = values.reshape(row_count, NORM_GROUPS, channels // NORM_GROUPS)
    average = jnp.mean(grouped, axis=(0, 2), keepdims=True)
    spread = jnp.mean(jnp.square(grouped - average), axis=(0, 2), keepdims=True)
    return ((grouped - average) / jnp.sqrt(spread + epsilon)).reshape(row_count, channels)


def layer_norm(values):
    average = jnp.mean(values, axis=-1, keepdims=True)
    spread = jnp.mean(jnp.square(values - average), axis=-1, keepdims=True)
    return (values - average) / jnp.sqrt(spread + epsilon)


def convolve(activations, weight):
    channels = activations.shape[-1]
    planar = activations.reshape(H, W, channels)
    padded = jnp.pad(planar, ((1, 1), (1, 1), (0, 0)))
    totals = jnp.zeros((H * W, weight.shape[-1]), jnp.float32)
    for row_shift in range(3):
        for col_shift in range(3):
            window = padded[row_shift : row_shift + H, col_shift : col_shift + W].reshape(
                H * W, channels
            )
            totals = totals + jnp.dot(
                window, weight[row_shift, col_shift], preferred_element_type=jnp.float32
            )
    return totals


def sinusoid(timestep):
    half_width = TEMB // 2
    frequency = jnp.exp(-math.log(10000.0) * jnp.arange(half_width, dtype=jnp.float32) / half_width)
    angles = timestep.astype(jnp.float32)[:, None] * frequency[None, :]
    return jnp.concatenate([jnp.cos(angles), jnp.sin(angles)], axis=-1)


def softmax_last(scores):
    maxima = jnp.max(scores, axis=-1, keepdims=True)
    powers = jnp.exp(scores - maxima)
    return powers / jnp.sum(powers, axis=-1, keepdims=True)


def epipolar(queries, key_rows, value_rows, pair_mask):
    row_count, channels = queries.shape
    tiles = pair_mask.shape[0]
    width = row_count // tiles
    split = (row_count, HEADS, channels // HEADS)
    scaling = 1.0 / math.sqrt(channels // HEADS)
    scores = (
        jnp.einsum(
            "qhd,khd->hqk",
            queries.reshape(split),
            key_rows.reshape(split),
            preferred_element_type=jnp.float32,
        )
        * scaling
    )
    scores = scores.reshape(HEADS, tiles, width, tiles, width)
    scores = jnp.where(pair_mask[None, :, None, :, None] > 0, scores, masked_fill)
    weights = softmax_last(scores.reshape(HEADS, row_count, row_count)).astype(jnp.bfloat16)
    result = jnp.einsum(
        "hqk,khd->qhd", weights, value_rows.reshape(split), preferred_element_type=jnp.float32
    )
    return result.reshape(row_count, channels)


def frame_attention(queries, key_rows, value_rows):
    frames, pixels, channels = queries.shape
    split = (frames, pixels, HEADS, channels // HEADS)
    scaling = 1.0 / math.sqrt(channels // HEADS)
    scores = (
        jnp.einsum(
            "fphd,gphd->phfg",
            queries.reshape(split),
            key_rows.reshape(split),
            preferred_element_type=jnp.float32,
        )
        * scaling
    )
    weights = softmax_last(scores).astype(jnp.bfloat16)
    result = jnp.einsum(
        "phfg,gphd->fphd", weights, value_rows.reshape(split), preferred_element_type=jnp.float32
    )
    return result.astype(jnp.bfloat16).reshape(frames, pixels, channels)


def project_block(blocks, weight):
    return jnp.einsum("fpc,cd->fpd", blocks, weight, preferred_element_type=jnp.float32).astype(
        jnp.bfloat16
    )


def per_device(
    latents,
    timesteps,
    matchings,
    tile_mask,
    conv_first,
    conv_second,
    time_proj,
    epi_in,
    epi_out,
    temp_in,
    temp_out,
):
    time_act = jax.nn.silu(sinusoid(timesteps)).astype(jnp.bfloat16)
    time_full, epi_whole, epi_final, temp_whole, temp_final = (
        lax.all_gather(time_proj, "frame", axis=0, tiled=True),
        lax.all_gather(epi_in, "frame", axis=1, tiled=True),
        lax.all_gather(epi_out, "frame", axis=0, tiled=True),
        lax.all_gather(temp_in, "frame", axis=1, tiled=True),
        lax.all_gather(temp_out, "frame", axis=0, tiled=True),
    )
    time_bias = jnp.dot(time_act, time_full, preferred_element_type=jnp.float32)
    tokens = latents.shape[2]
    channels = latents.shape[3]
    source = latents.reshape(tokens, channels)
    first_act = jax.nn.silu(group_norm(source.astype(jnp.float32))).astype(jnp.bfloat16)
    inner_sum = convolve(first_act, conv_first) + time_bias
    second_act = jax.nn.silu(group_norm(inner_sum)).astype(jnp.bfloat16)
    hidden = (source.astype(jnp.float32) + convolve(second_act, conv_second)).astype(jnp.bfloat16)
    normed = layer_norm(hidden.astype(jnp.float32)).astype(jnp.bfloat16)
    own_video = lax.axis_index("video")
    targets = matchings[:, own_video]
    shard_rows = lax.all_gather(normed.reshape(1, 1, tokens, channels), "video", axis=0, tiled=True)
    shard_count = shard_rows.shape[0]
    owners = jnp.arange(shard_count, dtype=jnp.int32)
    one_hot = (owners[None, :] == targets[:, None]).astype(jnp.bfloat16)
    selected = jnp.einsum(
        "mk,ktc->mtc", one_hot, shard_rows[:, 0], preferred_element_type=jnp.float32
    )
    matched = selected.astype(jnp.bfloat16)
    pair_masks = tile_mask[:, own_video]
    queries = jnp.dot(normed, epi_whole[0], preferred_element_type=jnp.float32).astype(jnp.bfloat16)
    key_all = jnp.einsum(
        "mtc,cd->mtd", matched, epi_whole[1], preferred_element_type=jnp.float32
    ).astype(jnp.bfloat16)
    value_all = jnp.einsum(
        "mtc,cd->mtd", matched, epi_whole[2], preferred_element_type=jnp.float32
    ).astype(jnp.bfloat16)
    summed = jnp.zeros((tokens, channels), jnp.float32)
    for matching in range(2):
        summed = summed + epipolar(
            queries, key_all[matching], value_all[matching], pair_masks[matching]
        )
    mixture = summed.astype(jnp.bfloat16)
    second_hidden = (
        hidden.astype(jnp.float32) + jnp.dot(mixture, epi_final, preferred_element_type=jnp.float32)
    ).astype(jnp.bfloat16)
    temp_normed = layer_norm(second_hidden.astype(jnp.float32)).astype(jnp.bfloat16)
    frames = lax.axis_size("frame")
    blocks = temp_normed.reshape(frames, tokens // frames, channels)
    regrouped = lax.all_to_all(blocks, "frame", split_axis=0, concat_axis=0, tiled=True)
    attended = frame_attention(
        project_block(regrouped, temp_whole[0]),
        project_block(regrouped, temp_whole[1]),
        project_block(regrouped, temp_whole[2]),
    )
    restored = lax.all_to_all(attended, "frame", split_axis=0, concat_axis=0, tiled=True)
    outcome = restored.reshape(tokens, channels)
    denoised = (
        second_hidden.astype(jnp.float32)
        + jnp.dot(outcome, temp_final, preferred_element_type=jnp.float32)
    ).astype(jnp.bfloat16)
    return denoised.reshape(1, 1, tokens, channels)


def solution(mesh):
    placed = (
        P(("groups", "video"), "frame", None, None),
        P(("groups", "video")),
        P(None, "groups"),
        P(None, "groups", None, None),
        P(),
        P(),
        P("frame", None),
        P(None, "frame", None),
        P("frame", None),
        P(None, "frame", None),
        P("frame", None),
    )
    return jax.shard_map(
        per_device,
        mesh=mesh,
        in_specs=placed,
        out_specs=P(("groups", "video"), "frame", None, None),
        check_vma=False,
    )
```

profile of v0, /device:TPU:0, one launch (start us, length us, event | category | flops | bytes accessed | tf_op | source)
XLA Modules:
  0.0 144.0 jit_solution(8931145181968467575)
XLA Ops:
  0.0 1.9 %copy.61 = f32[1,1,256,320]{3,2,1,0:T(8,128)} copy(bf16[1,1,256,320]{2,3,1,0:T(8,128)(2,1)} %param.11) | data formatting | bytes 491520 | tf_op jit(solution)/shard_map/convert_element_type | solution.py:140
  1.9 1.1 convert_reduce_fusion
  3.8 23.7 %all_gather.18 = bf16[1280,320]{1,0:T(8,128)(2,1)S(1)} all-gather(bf16[320,320]{1,0:T(8,128)(2,1)} %param.17), channel_id=1, replica_groups=mesh['groups'=2,'video'=4,'frame'=4] {'frame'}, dimensions={0}, use_global_device_ids=true | all-gather | bytes 1024000 | tf_op jit(solution)/shard_map/all_gather | solution.py:127
  27.9 1.1 fusion.27
  29.5 1.1 multiply_convert_fusion
  33.7 1.5 %fusion.92 = (f32[320]{0:T(512)S(1)}, f32[256,320]{0,1:T(8,128)S(1)}) fusion(f32[320]{0:T(512)S(1)} %convolution_reduce_fusion, f32[256,320]{0,1:T(8,128)S(1)} %convolution_add_fusion.11, bf16[256,320]{1,0:T(8,128)(2,1)S(1)} %bitcast.195, bf16[3,3,320,320]{3,2,1,0:T(8,128)(2,1)} %param.15), kind=kOutput, calls=%fused_computation.174 | convolution fusion | flops 52674240 | bytes 1067520 | tf_op jit(solution)/shard_map/dot_general | solution.py:43
  39.7 7.9 %all-gather = bf16[1024,320]{0,1:T(8,128)(2,1)S(1)} all-gather(bf16[256,320]{0,1:T(8,128)(2,1)S(1)} %divide_convert_fusion.7), channel_id=2, replica_groups=mesh['groups'=2,'video'=4,'frame'=4] {'video'}, dimensions={0}, use_global_device_ids=true | all-gather | bytes 819200 | tf_op jit(solution)/shard_map/all_gather | solution.py:144
  48.1 17.8 %all_gather.20 = bf16[3,320,320]{2,1,0:T(8,128)(2,1)S(1)} all-gather(bf16[3,80,320]{2,1,0:T(8,128)(2,1)S(1)} %copy-done.4), channel_id=1, replica_groups=mesh['groups'=2,'video'=4,'frame'=4] {'frame'}, dimensions={1}, use_global_device_ids=true | all-gather | bytes 768000 | tf_op jit(solution)/shard_map/all_gather | solution.py:128
  68.8 14.6 %all_gather.21 = bf16[320,320]{1,0:T(8,128)(2,1)S(1)} all-gather(bf16[80,320]{1,0:T(8,128)(2,1)S(1)} %copy-done.6), channel_id=1, replica_groups=mesh['groups'=2,'video'=4,'frame'=4] {'frame'}, dimensions={0}, use_global_device_ids=true | all-gather | bytes 256000 | tf_op jit(solution)/shard_map/all_gather | solution.py:129
  83.4 2.2 %fusion.94 = (f32[8,256]{1,0:T(8,128)S(1)}, f32[8,256,256]{1,2,0:T(8,128)}) fusion(pred[256,256]{0,1:T(8,128)(4,1)S(1)} %copy.65, bf16[256,8,40]{0,2,1:T(8,128)(2,1)S(1)} %bitcast.218, bf16[256,8,40]{0,2,1:T(8,128)(2,1)S(1)} %bitcast.216), kind=kOutput, calls=%fused_computation.176 | convolution fusion | flops 44040448 | bytes 2498560 | tf_op jit(solution)/shard_map/sub | solution.py:58
  85.6 2.1 %fusion.95 = (f32[8,256]{1,0:T(8,128)S(1)}, f32[8,256,256]{1,2,0:T(8,128)}) fusion(pred[256,256]{0,1:T(8,128)(4,1)S(1)} %copy.69, bf16[256,8,40]{0,2,1:T(8,128)(2,1)S(1)} %bitcast.219, bf16[256,8,40]{0,2,1:T(8,128)(2,1)S(1)} %bitcast.215), kind=kOutput, calls=%fused_computation.177 | convolution fusion | flops 44040448 | bytes 2498560 | tf_op jit(solution)/shard_map/sub | solution.py:58
  87.7 2.0 %fusion.23 = f32[8,40,256]{2,1,0:T(8,128)S(1)} fusion(bf16[256,8,40]{0,2,1:T(8,128)(2,1)S(1)} %bitcast.214, f32[8,256,256]{1,2,0:T(8,128)} %get-tuple-element.32, f32[8,256]{1,0:T(8,128)S(1)} %get-tuple-element.31), kind=kOutput, calls=%fused_computation.59 | convolution fusion | flops 42991616 | bytes 2596864 | tf_op jit(solution)/shard_map/hqk,khd->qhd/dot_general | solution.py:80
  90.7 0.8 copy.71
  91.5 3.4 %all-to-all-start = ((bf16[4,64,320]{2,1,0:T(8,128)(2,1)}), bf16[4,64,320]{2,1,0:T(8,128)(2,1)S(1)}, u32[]{:S(2)}, u32[]{:S(2)}) async-start(bf16[4,64,320]{2,1,0:T(8,128)(2,1)} %bitcast.53), calls=%async_computation | async-start | bytes 393216 | tf_op jit(solution)/shard_map/all_to_all | solution.py:172
  94.9 19.6 %all_gather.22 = bf16[3,320,320]{2,1,0:T(8,128)(2,1)S(1)} all-gather(bf16[3,80,320]{2,1,0:T(8,128)(2,1)S(1)} %copy-done.5), channel_id=1, replica_groups=mesh['groups'=2,'video'=4,'frame'=4] {'frame'}, dimensions={1}, use_global_device_ids=true | all-gather | bytes 768000 | tf_op jit(solution)/shard_map/all_gather | solution.py:130
  115.0 0.8 copy.77
  116.3 0.8 copy.75
  117.6 0.8 copy.76
  118.4 2.7 %fusion.97 = (f32[64,8,4]{2,1,0:T(8,128)S(1)}, f32[64,8,4,4]{2,3,1,0:T(4,128)}) fusion(bf16[4,64,8,40]{3,0,2,1:T(4,128)(2,1)S(1)} %copy.75, bf16[4,64,8,40]{3,0,2,1:T(4,128)(2,1)S(1)} %copy.76), kind=kOutput, calls=%fused_computation.179 | convolution fusion | flops 679939 | bytes 368640 | tf_op jit(solution)/shard_map/sub | solution.py:58
  121.1 2.1 %fusion.7 = bf16[4,64,8,40]{3,0,2,1:T(4,128)(2,1)S(1)} fusion(bf16[4,64,8,40]{3,0,2,1:T(4,128)(2,1)S(1)} %copy.77, f32[64,8,4,4]{2,3,1,0:T(4,128)} %get-tuple-element.38, f32[64,8,4]{2,1,0:T(8,128)S(1)} %get-tuple-element.37), kind=kOutput, calls=%fused_computation.15 | convolution fusion | flops 753664 | bytes 368640 | tf_op jit(solution)/shard_map/phfg,gphd->fphd/dot_general | solution.py:100
  123.8 0.8 copy.80
  124.6 3.4 %all-to-all-start.1 = ((bf16[4,64,320]{2,1,0:T(8,128)(2,1)}), bf16[4,64,320]{2,1,0:T(8,128)(2,1)S(1)}, u32[]{:S(2)}, u32[]{:S(2)}) async-start(bf16[4,64,320]{2,1,0:T(8,128)(2,1)} %copy.80), calls=%async_computation.1 | async-start | bytes 393216 | tf_op jit(solution)/shard_map/all_to_all | solution.py:178
  128.0 15.1 %all_gather.23 = bf16[320,320]{1,0:T(8,128)(2,1)S(1)} all-gather(bf16[80,320]{1,0:T(8,128)(2,1)S(1)} %copy-done.7), channel_id=1, replica_groups=mesh['groups'=2,'video'=4,'frame'=4] {'frame'}, dimensions={0}, use_global_device_ids=true | all-gather | bytes 256000 | tf_op jit(solution)/shard_map/all_gather | solution.py:131
  143.0 1.0 fusion.16
  (100 shorter events, 14.5 us)
Async XLA Ops:
  0.0 66.3 %copy-start = (s32[2,4]{1,0:T(2,128)S(1)}, s32[2,4]{1,0:T(2,128)}, u32[]{:S(2)}) copy-start(s32[2,4]{1,0:T(2,128)} %param.13) | copy-start | bytes 100
  0.0 30.8 %copy-start.3 = (bf16[3,3,320,320]{3,2,1,0:T(8,128)(2,1)S(1)}, bf16[3,3,320,320]{3,2,1,0:T(8,128)(2,1)}, u32[]{:S(2)}) copy-start(bf16[3,3,320,320]{3,2,1,0:T(8,128)(2,1)} %param.15) | copy-start | bytes 5529604
  30.8 1.3 copy-start.1
  33.7 3.1 %copy-start.2 = (bf16[3,3,320,320]{3,2,1,0:T(8,128)(2,1)S(1)}, bf16[3,3,320,320]{3,2,1,0:T(8,128)(2,1)}, u32[]{:S(2)}) copy-start(bf16[3,3,320,320]{3,2,1,0:T(8,128)(2,1)} %param.16) | copy-start | bytes 5529604
  39.3 8.8 %copy-start.4 = (bf16[3,80,320]{2,1,0:T(8,128)(2,1)S(1)}, bf16[3,80,320]{2,1,0:T(8,128)(2,1)}, u32[]{:S(2)}) copy-start(bf16[3,80,320]{2,1,0:T(8,128)(2,1)} %param.18) | copy-start | bytes 460804
  66.3 1.6 %copy-start.8 = (s32[2,4,2,2]{1,3,2,0:T(2,128)S(1)}, s32[2,4,2,2]{1,3,2,0:T(2,128)}, u32[]{:S(2)}) copy-start(s32[2,4,2,2]{1,3,2,0:T(2,128)} %param.14) | copy-start | bytes 388
  67.0 1.8 %copy-start.6 = (bf16[80,320]{1,0:T(8,128)(2,1)S(1)}, bf16[80,320]{1,0:T(8,128)(2,1)}, u32[]{:S(2)}) copy-start(bf16[80,320]{1,0:T(8,128)(2,1)} %param.19) | copy-start | bytes 153604
  87.7 2.2 %copy-start.9 = (f32[8,256,256]{1,2,0:T(8,128)S(1)}, f32[8,256,256]{1,2,0:T(8,128)}, u32[]{:S(2)}) copy-start(f32[8,256,256]{1,2,0:T(8,128)} %get-tuple-element.34) | copy-start | bytes 6291460
  90.3 4.6 %copy-start.5 = (bf16[3,80,320]{2,1,0:T(8,128)(2,1)S(1)}, bf16[3,80,320]{2,1,0:T(8,128)(2,1)}, u32[]{:S(2)}) copy-start(bf16[3,80,320]{2,1,0:T(8,128)(2,1)} %param.20) | copy-start | bytes 460804
  91.5 23.0 %all-to-all-start = ((bf16[4,64,320]{2,1,0:T(8,128)(2,1)}), bf16[4,64,320]{2,1,0:T(8,128)(2,1)S(1)}, u32[]{:S(2)}, u32[]{:S(2)}) async-start(bf16[4,64,320]{2,1,0:T(8,128)(2,1)} %bitcast.53), calls=%async_computation | async-start | bytes 393216 | tf_op jit(solution)/shard_map/all_to_all | solution.py:172
  121.1 6.9 %copy-start.7 = (bf16[80,320]{1,0:T(8,128)(2,1)S(1)}, bf16[80,320]{1,0:T(8,128)(2,1)}, u32[]{:S(2)}) copy-start(bf16[80,320]{1,0:T(8,128)(2,1)} %param.21) | copy-start | bytes 153604
  124.6 18.5 %all-to-all-start.1 = ((bf16[4,64,320]{2,1,0:T(8,128)(2,1)}), bf16[4,64,320]{2,1,0:T(8,128)(2,1)S(1)}, u32[]{:S(2)}, u32[]{:S(2)}) async-start(bf16[4,64,320]{2,1,0:T(8,128)(2,1)} %copy.80), calls=%async_computation.1 | async-start | bytes 393216 | tf_op jit(solution)/shard_map/all_to_all | solution.py:178
where the time goes:
time: 145 us; the launch traced here: 144 us
  blocking collectives  98.7 us (68%)
  matrix products  22.1 us (15%)
  local copies, waits for them, and re-layouts  10.5 us (7%)
  starting transfers between devices  6.73 us (5%)
  other arithmetic  4.76 us (3%)
    all_gather x1, blocking collectives, per_device(): lax.all_gather(time_proj, 'frame', axis=0, tiled=True)  23.7 us
    all_gather x1, blocking collectives, per_device(): lax.all_gather(temp_in, 'frame', axis=1, tiled=True)  19.6 us
    all_gather x1, blocking collectives, per_device(): lax.all_gather(epi_in, 'frame', axis=1, tiled=True)  17.8 us
    all_gather x1, blocking collectives, per_device(): lax.all_gather(temp_out, 'frame', axis=0, tiled=True)  15.1 us
    all_gather x1, blocking collectives, per_device(): lax.all_gather(epi_out, 'frame', axis=0, tiled=True)  14.6 us
    all_gather x1, blocking collectives, per_device(): lax.all_gather(normed.reshape(1, 1, tokens, channels), 'video', axis=0, t...  7.89 us
    sub x3, matrix products, softmax_last(): powers = jnp.exp(scores - maxima)  7.05 us
    dot_general x18, matrix products, convolve(): jnp.dot(window, weight[row_shift, col_shift], preferred_element_type=jnp....  6.74 us
  transfers between devices with their start and end apart: 2, of which 0 were waited for; matrix products, arithmetic and copies ran while one was open for 0% of the time, Pallas kernels for 0%

commit v1 on v0

v1 whole, which is shorter than its diff:
```python
import functools
import math

import jax
import jax.numpy as jnp
from jax import lax
from jax.experimental import pallas as pl
from jax.experimental.pallas import tpu as pltpu
from jax.sharding import PartitionSpec as P

HEADS = 8
NORM_GROUPS = 32
TEMB = 1280
H = 8
W = 32

EPSILON = 1e-05
MASKED = -1e30
LOG2E = 1.4426950408889634

VMEM = pl.BlockSpec(memory_space=pltpu.VMEM)
SMEM = pl.BlockSpec(memory_space=pltpu.SMEM)
ANY = pl.BlockSpec(memory_space=pl.ANY)
f32 = jnp.float32
bf16 = jnp.bfloat16


def params():
    return pltpu.CompilerParams(vmem_limit_bytes=48 * 1024 * 1024)


def dot(a, b):
    return jnp.dot(a, b, preferred_element_type=f32)


def block_diagonal(size, width):
    rows = lax.broadcasted_iota(jnp.int32, (size, 1), 0).astype(f32)
    cols = lax.broadcasted_iota(jnp.int32, (1, size), 1).astype(f32)
    rows = jnp.floor((rows + 0.5) * (1.0 / width))
    cols = jnp.floor((cols + 0.5) * (1.0 / width))
    return (rows == cols).astype(f32).astype(bf16)


def group_sum(row, ones):
    first = row.astype(bf16).astype(f32)
    second = (row - first).astype(bf16).astype(f32)
    third = row - first - second
    index = lax.broadcasted_iota(jnp.int32, (16, row.shape[1]), 0)
    stacked = jnp.where(
        index == 0, first, jnp.where(index == 1, second, jnp.where(index == 2, third, 0.0))
    )
    return jnp.sum(dot(stacked.astype(bf16), ones), axis=0, keepdims=True)


def group_norm_silu(x):
    tokens, channels = x.shape
    width = channels // NORM_GROUPS
    ones = block_diagonal(channels, width)
    inverse = 1.0 / (tokens * width)
    average = group_sum(jnp.sum(x, axis=0, keepdims=True), ones) * inverse
    centred = x - average
    spread = group_sum(jnp.sum(centred * centred, axis=0, keepdims=True), ones) * inverse
    y = centred * lax.rsqrt(spread + EPSILON)
    return y / (1.0 + jnp.exp(-y))


def layer_norm(x):
    inverse = 1.0 / x.shape[1]
    average = jnp.sum(x, axis=1, keepdims=True) * inverse
    centred = x - average
    spread = jnp.sum(centred * centred, axis=1, keepdims=True) * inverse
    return centred * lax.rsqrt(spread + EPSILON)


def convolve(y, weight, padded):
    tokens, channels = y.shape
    column = lax.broadcasted_iota(jnp.int32, (tokens, 1), 0) & (W - 1)
    before = jnp.where(column == 0, 0.0, pltpu.roll(y, 1, 0))
    after = jnp.where(column == W - 1, 0.0, pltpu.roll(y, tokens - 1, 0))
    padded[pl.ds(0, W), :] = jnp.zeros((W, 3 * channels), bf16)
    padded[pl.ds(tokens + W, W), :] = jnp.zeros((W, 3 * channels), bf16)
    padded[pl.ds(W, tokens), :] = jnp.concatenate(
        [before.astype(bf16), y.astype(bf16), after.astype(bf16)], axis=1
    )
    total = dot(padded[pl.ds(0, tokens), :], weight[0])
    total += dot(padded[pl.ds(W, tokens), :], weight[1])
    total += dot(padded[pl.ds(2 * W, tokens), :], weight[2])
    return total


def first_kernel(source, weight_hbm, inner, weight, padded, sem):
    copy = pltpu.make_async_copy(weight_hbm, weight, sem)
    copy.start()
    y = group_norm_silu(source[...].astype(f32))
    copy.wait()
    inner[...] = convolve(y, weight, padded)


def second_kernel(source, inner, bias, weight_hbm, hidden, normed, weight, padded, sem):
    copy = pltpu.make_async_copy(weight_hbm, weight, sem)
    copy.start()
    y = group_norm_silu(inner[...] + bias[...])
    copy.wait()
    total = source[...].astype(f32) + convolve(y, weight, padded)
    rounded = total.astype(bf16)
    hidden[...] = rounded
    normed[...] = layer_norm(rounded.astype(f32)).astype(bf16)


def assemble(pieces, whole):
    parts, kinds, rows, _ = pieces.shape
    for part in range(parts):
        for kind in range(kinds):
            whole[kind, pl.ds(part * rows, rows), :] = pieces[part, kind]


def view_kernel(count, tiles, *refs):
    select, mask, me, hidden = refs[:4]
    maps = refs[4 : 4 + count]
    pieces, second, blocks, weights, chosen, totals = refs[4 + count :]
    tokens, channels = hidden.shape
    head = channels // HEADS
    width = tokens // tiles
    assemble(pieces, weights)
    scale = LOG2E / math.sqrt(head)
    queries = dot(maps[0][...], weights[0]).astype(bf16).astype(f32).T
    lane_tile = lax.broadcasted_iota(jnp.int32, (1, tokens), 1) // width
    windows = []
    for h in range(HEADS):
        low = h * head // 128 * 128
        high = min(channels, -(-(h + 1) * head // 128) * 128)
        row = lax.broadcasted_iota(jnp.int32, (high - low, 1), 0) + low
        inside = (row >= h * head) & (row < (h + 1) * head)
        windows.append((low, high, jnp.where(inside, queries[low:high], 0.0).astype(bf16)))
    for matching in range(2):
        for j in range(count):

            @pl.when(select[matching] == j)
            def _():
                chosen[...] = maps[j][...]

        other = chosen[...]
        keys = dot(other, weights[1]).astype(bf16)
        values = dot(other, weights[2]).T
        shifts = []
        for j in range(tiles):
            row = jnp.zeros((1, tokens), f32)
            for i in range(tiles):
                bit = mask[(matching * tiles + i) * tiles + j]
                row = jnp.where(lane_tile == i, jnp.where(bit > 0, 0.0, MASKED), row)
            shifts.append(row)
        for h in range(HEADS):
            low, high, wanted = windows[h]
            scores = dot(keys[:, low:high], wanted) * scale
            scores = jnp.concatenate(
                [scores[j * width : (j + 1) * width] + shifts[j] for j in range(tiles)], axis=0
            )
            powers = jnp.exp2(scores - jnp.max(scores, axis=0, keepdims=True))
            norm = 1.0 / jnp.sum(powers, axis=0, keepdims=True)
            part = dot(values[h * head : (h + 1) * head].astype(bf16), powers.astype(bf16)) * norm
            if matching == 0:
                totals[pl.ds(h * head, head), :] = part
            else:
                totals[pl.ds(h * head, head), :] += part
    mixture = totals[...].T.astype(bf16)
    result = (hidden[...].astype(f32) + dot(mixture, weights[3])).astype(bf16)
    second[...] = result
    blocks[...] = layer_norm(result.astype(f32)).astype(bf16)


def time_kernel(frames, *refs):
    blocks = refs[:frames]
    pieces = refs[frames]
    outs = refs[frames + 1 : 2 * frames + 1]
    weights, rows_in, attended = refs[2 * frames + 1 :]
    pixels, channels = blocks[0].shape
    head = channels // HEADS
    assemble(pieces, weights)
    for f in range(frames):
        rows_in[pl.ds(f * pixels, pixels), :] = blocks[f][...]
    rows = rows_in[...]
    ones = block_diagonal(channels, head)
    queries = dot(rows, weights[0]).astype(bf16).astype(f32)
    keys = dot(rows, weights[1]).astype(bf16).astype(f32).reshape(frames, pixels, channels)
    values = dot(rows, weights[2]).astype(bf16).astype(f32).reshape(frames, pixels, channels)
    scale = LOG2E / math.sqrt(head)
    for f in range(frames):
        one = queries[f * pixels : (f + 1) * pixels]
        products = (one[None] * keys).reshape(frames * pixels, channels)
        high = products.astype(bf16)
        low = (products - high.astype(f32)).astype(bf16)
        scores = (dot(high, ones) + dot(low, ones)) * scale
        scores = scores.reshape(frames, pixels, channels)
        powers = jnp.exp2(scores - jnp.max(scores, axis=0, keepdims=True))
        norm = 1.0 / jnp.sum(powers, axis=0, keepdims=True)
        probs = (powers * norm).astype(bf16).astype(f32)
        attended[pl.ds(f * pixels, pixels), :] = jnp.sum(probs * values, axis=0).astype(bf16)
    result = dot(attended[...], weights[3]).astype(bf16)
    for f in range(frames):
        outs[f][...] = result[f * pixels : (f + 1) * pixels]


def last_kernel(frames, *refs):
    where = refs[0]
    second = refs[1]
    blocks = refs[2 : 2 + frames]
    out = refs[2 + frames]
    pixels = blocks[0].shape[0]
    for k in range(frames):
        rows = pl.ds(pl.multiple_of(where[k] * pixels, 16), pixels)
        out[rows, :] = (second[rows, :].astype(f32) + blocks[k][...].astype(f32)).astype(bf16)


def is_power(n):
    return n & (n - 1) == 0


def partner_permutation(size, k):
    if is_power(size):
        return [(i, i ^ k) for i in range(size)]
    return [(i, (i + k) % size) for i in range(size)]


def partner(me, size, k, sign=1):
    if is_power(size):
        return me ^ k
    return (me + sign * k) % size


def gather_maps(own, axis, size):
    maps = {0: own}
    if is_power(size):
        bit = size // 2
        while bit:
            for k in list(maps):
                maps[k | bit] = lax.ppermute(maps[k], axis, partner_permutation(size, bit))
            bit //= 2
    else:
        for k in range(1, size):
            maps[k] = lax.ppermute(own, axis, partner_permutation(size, k))
    return [maps[k] for k in range(size)]


def sum_over(value, axis, size):
    if not is_power(size):
        return lax.psum(value, axis)
    bit = 1
    while bit < size:
        value = value + lax.ppermute(value, axis, partner_permutation(size, bit))
        bit *= 2
    return value


def gather_weights(three, one):
    own = jnp.concatenate([three, one[None]], axis=0)
    parts = lax.all_gather(own, "frame", axis=0)
    if own.shape[1] % 16:
        parts = parts.transpose(1, 0, 2, 3).reshape(1, 4, -1, own.shape[2])
    return parts


def per_device(
    latents,
    timesteps,
    matchings,
    tile_mask,
    conv_first,
    conv_second,
    time_proj,
    epi_in,
    epi_out,
    temp_in,
    temp_out,
):
    tokens, channels = latents.shape[2:]
    tiles = tile_mask.shape[2]
    frames = lax.axis_size("frame")
    videos = lax.axis_size("video")
    frame = lax.axis_index("frame")
    video = lax.axis_index("video")
    pixels = tokens // frames
    source = latents.reshape(tokens, channels)
    epi_parts = gather_weights(epi_in, epi_out)
    temp_parts = gather_weights(temp_in, temp_out)

    rows = time_proj.shape[0]
    half = rows * frames // 2
    index = frame * rows + jnp.arange(rows, dtype=jnp.int32)
    exponent = jnp.where(index < half, index, index - half).astype(f32)
    frequency = jnp.exp(-math.log(10000.0) * exponent / half)
    angles = timesteps.astype(f32)[:, None] * frequency[None, :]
    wave = jnp.where(index[None, :] < half, jnp.cos(angles), jnp.sin(angles))
    time_act = jax.nn.silu(wave).astype(bf16)
    bias = sum_over(dot(time_act, time_proj), "frame", frames)

    conv_scratch = [
        pltpu.VMEM((3, 3 * channels, channels), bf16),
        pltpu.VMEM((tokens + 2 * W, 3 * channels), bf16),
        pltpu.SemaphoreType.DMA,
    ]
    conv_cost = pl.CostEstimate(
        flops=2 * 9 * tokens * channels * channels,
        bytes_accessed=2 * 9 * channels * channels + 8 * tokens * channels,
        transcendentals=tokens * channels,
    )
    inner = pl.pallas_call(
        first_kernel,
        out_shape=jax.ShapeDtypeStruct((tokens, channels), f32),
        in_specs=[VMEM, ANY],
        out_specs=VMEM,
        scratch_shapes=conv_scratch,
        compiler_params=params(),
        cost_estimate=conv_cost,
        name="first_conv",
    )(source, conv_first.reshape(3, 3 * channels, channels))
    hidden, normed = pl.pallas_call(
        second_kernel,
        out_shape=[jax.ShapeDtypeStruct((tokens, channels), bf16)] * 2,
        in_specs=[VMEM, VMEM, VMEM, ANY],
        out_specs=[VMEM, VMEM],
        scratch_shapes=conv_scratch,
        compiler_params=params(),
        cost_estimate=conv_cost,
        name="second_conv",
    )(source, inner, bias, conv_second.reshape(3, 3 * channels, channels))

    maps = gather_maps(normed, "video", videos)
    targets = lax.dynamic_index_in_dim(matchings, video, 1, keepdims=False)
    if is_power(videos):
        select = video ^ targets
    else:
        select = (video - targets) % videos
    mask = lax.dynamic_index_in_dim(tile_mask, video, 1, keepdims=False).reshape(-1)
    second, blocks = pl.pallas_call(
        functools.partial(view_kernel, videos, tiles),
        out_shape=[jax.ShapeDtypeStruct((tokens, channels), bf16)] * 2,
        in_specs=[SMEM, SMEM, SMEM, VMEM] + [VMEM] * videos + [VMEM],
        out_specs=[VMEM, VMEM],
        scratch_shapes=[
            pltpu.VMEM((4, channels, channels), bf16),
            pltpu.VMEM((tokens, channels), bf16),
            pltpu.VMEM((channels, tokens), f32),
        ],
        compiler_params=params(),
        name="cross_view",
    )(select, mask, frame.reshape(1), hidden, *maps, epi_parts)

    split = blocks.reshape(frames, pixels, channels)
    received = []
    for k in range(frames):
        block = lax.dynamic_index_in_dim(split, partner(frame, frames, k), 0, keepdims=False)
        if k:
            block = lax.ppermute(block, "frame", partner_permutation(frames, k))
        received.append(block)
    outs = pl.pallas_call(
        functools.partial(time_kernel, frames),
        out_shape=[jax.ShapeDtypeStruct((pixels, channels), bf16)] * frames,
        in_specs=[VMEM] * (frames + 1),
        out_specs=[VMEM] * frames,
        scratch_shapes=[
            pltpu.VMEM((4, channels, channels), bf16),
            pltpu.VMEM((tokens, channels), bf16),
            pltpu.VMEM((tokens, channels), bf16),
        ],
        compiler_params=params(),
        name="temporal",
    )(*received, temp_parts)
    returned = [outs[0]]
    for k in range(1, frames):
        back = [(j, i) for i, j in partner_permutation(frames, k)]
        returned.append(lax.ppermute(outs[k], "frame", back))
    where = jnp.stack([partner(frame, frames, k) for k in range(frames)]).astype(jnp.int32)
    denoised = pl.pallas_call(
        functools.partial(last_kernel, frames),
        out_shape=jax.ShapeDtypeStruct((tokens, channels), bf16),
        in_specs=[SMEM] + [VMEM] * (frames + 1),
        out_specs=VMEM,
        compiler_params=params(),
        name="last",
    )(where, second, *returned)
    return denoised.reshape(1, 1, tokens, channels)


def solution(mesh):
    placed = (
        P(("groups", "video"), "frame", None, None),
        P(("groups", "video")),
        P(None, "groups"),
        P(None, "groups", None, None),
        P(),
        P(),
        P("frame", None),
        P(None, "frame", None),
        P("frame", None),
        P(None, "frame", None),
        P("frame", None),
    )
    return jax.shard_map(
        per_device,
        mesh=mesh,
        in_specs=placed,
        out_specs=P(("groups", "video"), "frame", None, None),
        check_vma=False,
    )
```

time: 145 us -> 83.5 us (0.58)
  blocking collectives: 98.7 us -> 41.8 us
  matrix products: 22.1 us -> 0.12 us
  Pallas kernels: 0 us -> 12.9 us
  starting transfers between devices: 6.73 us -> 16.6 us
  waiting for transfers between devices: 0.01 us -> 6.52 us
  local copies, waits for them, and re-layouts: 10.5 us -> 4.06 us
  other arithmetic: 4.76 us -> 0.43 us
    all_gather x6 -> x2, blocking collectives: 98.7 us -> 41.8 us  [gather_weights(): parts = lax.all_gather(own, 'frame', axis=0)]
    ppermute x0 -> x11, starting transfers between devices: none -> 16.6 us  [the longest x2 6.09 us: sum_over(): value = value + lax.ppermute(value, axis, partner_permutation(size, bit))]
    dot_general x31 -> x1, matrix products: 15 us -> 0.12 us  [dot(): return jnp.dot(a, b, preferred_element_type=f32)]
    pallas_call x0 -> x5, Pallas kernels: none -> 12.9 us  [the longest x1 6.43 us: per_device(): pl.pallas_call(functools.partial(view_kernel, videos, tiles), out_shape=[...]
    sub x3 -> x0, matrix products: 7.05 us -> none  [softmax_last(): powers = jnp.exp(scores - maxima)]
    all_to_all x2 -> x0, starting transfers between devices: 6.73 us -> none  [the longest x1 3.36 us: per_device(): lax.all_to_all(blocks, 'frame', split_axis=0, concat_axis=0, tiled=True)]
    ppermute x0 -> x11, waiting for transfers between devices: none -> 6.52 us  [the longest x3 4.05 us: gather_maps(): maps[k | bit] = lax.ppermute(maps[k], axis, partner_permutation(size, bit))]
    convert_element_type x8 -> x1, local copies, waits for them, and re-layouts: 4.19 us -> 0.01 us  [per_device(): time_act = jax.nn.silu(wave).astype(bf16)]
  transfers between devices with their start and end apart: 2 -> 11, of which waited for: 0 -> 4; matrix products, arithmetic and copies ran while one was open for 0% -> 2% of each run, Pallas kernels for 0% -> 2%
where the time goes in v1:
time: 83.5 us; the launch traced here: 83.3 us
  blocking collectives  41.8 us (50%)
  starting transfers between devices  16.6 us (20%)
  Pallas kernels  12.9 us (15%)
  waiting for transfers between devices  6.52 us (8%)
  local copies, waits for them, and re-layouts  4.06 us (5%)
  between operations  0.89 us (1%)
    all_gather x2, blocking collectives, gather_weights(): parts = lax.all_gather(own, 'frame', axis=0)  41.8 us
    pallas_call x1, Pallas kernels, per_device(): pl.pallas_call(functools.partial(view_kernel, videos, tiles), out_shape=[...  6.43 us
    ppermute x2, starting transfers between devices, sum_over(): value = value + lax.ppermute(value, axis, partner_permutation(size, bit))  6.09 us
    ppermute x3, starting transfers between devices, per_device(): returned.append(lax.ppermute(outs[k], 'frame', back))  4.45 us
    ppermute x3, starting transfers between devices, per_device(): block = lax.ppermute(block, 'frame', partner_permutation(frames, k))  4.45 us
    ppermute x3, waiting for transfers between devices, gather_maps(): maps[k | bit] = lax.ppermute(maps[k], axis, partner_permutation(size, bit))  4.05 us
    unnamed x19, local copies, waits for them, and re-layouts  2.93 us
    pallas_call x1, Pallas kernels, per_device(): pl.pallas_call(functools.partial(time_kernel, frames), out_shape=[jax.Sha...  2.04 us
  transfers between devices with their start and end apart: 11, of which 4 were waited for; matrix products, arithmetic and copies ran while one was open for 2% of the time, Pallas kernels for 2%

profile of v1, /device:TPU:0, one launch (start us, length us, event | category | flops | bytes accessed | tf_op | source)
XLA Modules:
  0.0 83.3 jit_solution(14046769337582658694)
XLA Ops:
  1.1 3.1 %collective-permute-start = (f32[1,320]{1,0:T(1,128)S(1)}, f32[1,320]{1,0:T(1,128)S(1)}, u32[]{:S(2)}, u32[]{:S(2)}) collective-permute-start(f32[1,320]{1,0:T(1,128)S(1)} %fusion.7), channel_id=1, source_target_pairs={{0,1},{1,0},{2,3},{3,2},{4,5},{5,4},{6,7},{7,6},{8,9},{9,8},{10,11... | collective-permute-start | bytes 3848 | tf_op jit(solution)/shard_map/ppermute | solution.py:249
  4.1 1.1 %copy.16 = bf16[1,1,256,320]{3,2,1,0:T(8,128)(2,1)S(1)} copy(bf16[1,1,256,320]{2,3,1,0:T(8,128)(2,1)} %param.11) | data formatting | bytes 327680 | tf_op args[0]
  5.2 0.5 collective-permute-done
  5.7 3.0 %collective-permute-start.1 = (f32[1,320]{1,0:T(1,128)S(1)}, f32[1,320]{1,0:T(1,128)S(1)}, u32[]{:S(2)}, u32[]{:S(2)}) collective-permute-start(f32[1,320]{1,0:T(1,128)S(1)} %add.47), channel_id=1, source_target_pairs={{0,2},{1,3},{2,0},{3,1},{4,6},{5,7},{6,4},{7,5},{8,10},{9,11},{10,... | collective-permute-start | bytes 3848 | tf_op jit(solution)/shard_map/ppermute | solution.py:249
  8.7 1.6 %copy-done.1 = bf16[3,3,320,320]{3,2,1,0:T(8,128)(2,1)S(1)} copy-done((bf16[3,3,320,320]{3,2,1,0:T(8,128)(2,1)S(1)}, bf16[3,3,320,320]{3,2,1,0:T(8,128)(2,1)}, u32[]{:S(2)}) %copy-start.1) | copy-done | bytes 1843224
  10.4 1.9 %first_conv.1.inner = f32[256,320]{1,0:T(8,128)S(1)} custom-call(bf16[256,320]{1,0:T(8,128)(2,1)S(1)} %bitcast.28, bf16[3,960,320]{2,1,0:T(8,128)(2,1)S(1)} %bitcast.26), custom_call_target="tpu_custom_call" | custom-call | flops 471859200 | bytes 2498560 | tf_op jit(solution)/shard_map/first_conv/pallas_call | solution.py:306
  12.3 2.0 %second_conv.1 = (bf16[256,320]{1,0:T(8,128)(2,1)S(1)}, bf16[256,320]{1,0:T(8,128)(2,1)S(1)}) custom-call(bf16[256,320]{1,0:T(8,128)(2,1)S(1)} %bitcast.29, f32[256,320]{1,0:T(8,128)S(1)} %first_conv.1.inner, f32[1,320]{1,0:T(1,128)S(1)} %add.48.bias, bf16[3,960,320]{2,1,0:T(8,128)(2,1)S(1)} %bitcast.27), custom_call_target="tpu_custom_call" | custom-call | flops 471859200 | bytes 2498560 | tf_op jit(solution)/shard_map/second_conv/pallas_call | solution.py:316
  14.3 1.6 %collective-permute-start.3 = (bf16[256,320]{1,0:T(8,128)(2,1)S(1)}, bf16[256,320]{1,0:T(8,128)(2,1)S(1)}, u32[]{:S(2)}, u32[]{:S(2)}) collective-permute-start(bf16[256,320]{1,0:T(8,128)(2,1)S(1)} %get-tuple-element.14.refs_4_), channel_id=1, source_target_pairs={{0,8},{4,12},{8,0},{12,4},{1,9},{5,13},{9,1},{13,5},{2,10},{6,14},... | collective-permute-start | bytes 491528 | tf_op jit(solution)/shard_map/ppermute | solution.py:236
  16.0 4.0 %collective-permute-done.3.refs_6_ = bf16[256,320]{1,0:T(8,128)(2,1)S(1)} collective-permute-done((bf16[256,320]{1,0:T(8,128)(2,1)S(1)}, bf16[256,320]{1,0:T(8,128)(2,1)S(1)}, u32[]{:S(2)}, u32[]{:S(2)}) %collective-permute-start.3) | collective-permute-done | bytes 163872 | tf_op jit(solution)/shard_map/ppermute | solution.py:236
  20.1 21.0 %all-gather = bf16[16,80,320]{2,1,0:T(8,128)(2,1)S(1)} all-gather(bf16[4,80,320]{2,1,0:T(8,128)(2,1)S(1)} %pad_maximum_fusion), channel_id=2, replica_groups=mesh['groups'=2,'video'=4,'frame'=4] {'frame'}, dimensions={0}, use_global_device_ids=true | all-gather | bytes 1024000 | tf_op jit(solution)/shard_map/all_gather | solution.py:256
  41.1 0.2 dynamic-slice_reduce_fusion
  41.7 6.4 %cross_view.1 = (bf16[256,320]{1,0:T(8,128)(2,1)S(1)}, bf16[256,320]{1,0:T(8,128)(2,1)S(1)}) custom-call(s32[2]{0:T(128)S(1)} %fusion.6.refs_0_, s32[8]{0:T(128)S(1)} %reshape.39.refs_1_, s32[1]{0:T(128)} %bitcast.refs_2_, bf16[256,320]{1,0:T(8,128)(2,1)S(1)} %get-tuple-element.13.refs_3_, bf16[256,320]{1,0:T(8,128)(2,1)S(1)} %get-tuple-element.14.refs_4_, ...), custom_call_target="tpu_custom_call" | custom-call | tf_op jit(solution)/shard_map/cross_view/pallas_call | solution.py:334
  48.2 0.2 collective-permute-start.5
  48.4 2.7 %collective-permute-start.6 = (bf16[64,320]{1,0:T(8,128)(2,1)S(1)}, bf16[64,320]{1,0:T(8,128)(2,1)S(1)}, u32[]{:S(2)}, u32[]{:S(2)}) collective-permute-start(bf16[64,320]{1,0:T(8,128)(2,1)S(1)} %get-tuple-element.22), channel_id=1, source_target_pairs={{0,2},{1,3},{2,0},{3,1},{4,6},{5,7},{6,4},{7,5},{8,10},{9,11},{10,... | collective-permute-start | bytes 122888 | tf_op jit(solution)/shard_map/ppermute | solution.py:353
  51.1 1.5 %collective-permute-start.7 = (bf16[64,320]{1,0:T(8,128)(2,1)S(1)}, bf16[64,320]{1,0:T(8,128)(2,1)S(1)}, u32[]{:S(2)}, u32[]{:S(2)}) collective-permute-start(bf16[64,320]{1,0:T(8,128)(2,1)S(1)} %get-tuple-element.21), channel_id=1, source_target_pairs={{0,3},{1,2},{2,1},{3,0},{4,7},{5,6},{6,5},{7,4},{8,11},{9,10},{10,... | collective-permute-start | bytes 122888 | tf_op jit(solution)/shard_map/ppermute | solution.py:353
  52.6 20.8 %all-gather.1 = bf16[16,80,320]{2,1,0:T(8,128)(2,1)S(1)} all-gather(bf16[4,80,320]{2,1,0:T(8,128)(2,1)S(1)} %pad_maximum_fusion.1), channel_id=3, replica_groups=mesh['groups'=2,'video'=4,'frame'=4] {'frame'}, dimensions={0}, use_global_device_ids=true | all-gather | bytes 1024000 | tf_op jit(solution)/shard_map/all_gather | solution.py:256
  73.4 2.0 %temporal.1 = (bf16[64,320]{1,0:T(8,128)(2,1)S(1)}, bf16[64,320]{1,0:T(8,128)(2,1)S(1)}, bf16[64,320]{1,0:T(8,128)(2,1)S(1)}, bf16[64,320]{1,0:T(8,128)(2,1)S(1)}) custom-call(bf16[64,320]{1,0:T(8,128)(2,1)S(1)} %get-tuple-element.24.refs_0_, bf16[64,320]{1,0:T(8,128)(2,1)S(1)} %collective-permute-done.5.refs_1_, ...), custom_call_target="tpu_custom_call" | custom-call | tf_op jit(solution)/shard_map/temporal/pallas_call | solution.py:355
  75.4 1.2 %collective-permute-start.10 = (bf16[64,320]{1,0:T(8,128)(2,1)S(1)}, bf16[64,320]{1,0:T(8,128)(2,1)S(1)}, u32[]{:S(2)}, u32[]{:S(2)}) collective-permute-start(bf16[64,320]{1,0:T(8,128)(2,1)S(1)} %get-tuple-element.20), channel_id=1, source_target_pairs={{3,0},{2,1},{1,2},{0,3},{7,4},{6,5},{5,6},{4,7},{11,8},{10,9},{9,1... | collective-permute-start | bytes 122888 | tf_op jit(solution)/shard_map/ppermute | solution.py:371
  76.7 0.3 collective-permute-start.8
  76.9 2.9 %collective-permute-start.9 = (bf16[64,320]{1,0:T(8,128)(2,1)S(1)}, bf16[64,320]{1,0:T(8,128)(2,1)S(1)}, u32[]{:S(2)}, u32[]{:S(2)}) collective-permute-start(bf16[64,320]{1,0:T(8,128)(2,1)S(1)} %get-tuple-element.19), channel_id=1, source_target_pairs={{2,0},{3,1},{0,2},{1,3},{6,4},{7,5},{4,6},{5,7},{10,8},{11,9},{8,1... | collective-permute-start | bytes 122888 | tf_op jit(solution)/shard_map/ppermute | solution.py:371
  80.0 1.4 %collective-permute-done.10.refs_5_ = bf16[64,320]{1,0:T(8,128)(2,1)S(1)} collective-permute-done((bf16[64,320]{1,0:T(8,128)(2,1)S(1)}, bf16[64,320]{1,0:T(8,128)(2,1)S(1)}, u32[]{:S(2)}, u32[]{:S(2)}) %collective-permute-start.10) | collective-permute-done | bytes 40992 | tf_op jit(solution)/shard_map/ppermute | solution.py:371
  81.4 0.6 collective-permute-done.9.refs_4_
  81.9 0.6 last.1
  82.5 0.8 copy.17
  (37 shorter events, 1.0 us)
Async XLA Ops:
  0.0 1.0 %copy-start = (bf16[320,320]{1,0:T(8,128)(2,1)S(1)}, bf16[320,320]{1,0:T(8,128)(2,1)}, u32[]{:S(2)}) copy-start(bf16[320,320]{1,0:T(8,128)(2,1)} %param.17) | copy-start | bytes 614404
  1.1 4.6 %collective-permute-start = (f32[1,320]{1,0:T(1,128)S(1)}, f32[1,320]{1,0:T(1,128)S(1)}, u32[]{:S(2)}, u32[]{:S(2)}) collective-permute-start(f32[1,320]{1,0:T(1,128)S(1)} %fusion.7), channel_id=1, source_target_pairs={{0,1},{1,0},{2,3},{3,2},{4,5},{5,4},{6,7},{7,6},{8,9},{9,8},{10,11... | collective-permute-start | bytes 3848 | tf_op jit(solution)/shard_map/ppermute | solution.py:249
  5.7 6.5 %collective-permute-start.1 = (f32[1,320]{1,0:T(1,128)S(1)}, f32[1,320]{1,0:T(1,128)S(1)}, u32[]{:S(2)}, u32[]{:S(2)}) collective-permute-start(f32[1,320]{1,0:T(1,128)S(1)} %add.47), channel_id=1, source_target_pairs={{0,2},{1,3},{2,0},{3,1},{4,6},{5,7},{6,4},{7,5},{8,10},{9,11},{10,... | collective-permute-start | bytes 3848 | tf_op jit(solution)/shard_map/ppermute | solution.py:249
  8.7 1.6 %copy-start.1 = (bf16[3,3,320,320]{3,2,1,0:T(8,128)(2,1)S(1)}, bf16[3,3,320,320]{3,2,1,0:T(8,128)(2,1)}, u32[]{:S(2)}) copy-start(bf16[3,3,320,320]{3,2,1,0:T(8,128)(2,1)} %param.15) | copy-start | bytes 5529604
  10.4 1.9 %copy-start.2 = (bf16[3,3,320,320]{3,2,1,0:T(8,128)(2,1)S(1)}, bf16[3,3,320,320]{3,2,1,0:T(8,128)(2,1)}, u32[]{:S(2)}) copy-start(bf16[3,3,320,320]{3,2,1,0:T(8,128)(2,1)} %param.16) | copy-start | bytes 5529604
  10.4 5.5 %copy-start.3 = (bf16[3,80,320]{2,1,0:T(8,128)(2,1)S(1)}, bf16[3,80,320]{2,1,0:T(8,128)(2,1)}, u32[]{:S(2)}) copy-start(bf16[3,80,320]{2,1,0:T(8,128)(2,1)} %param.18) | copy-start | bytes 460804
  10.4 5.5 %copy-start.5 = (bf16[80,320]{1,0:T(8,128)(2,1)S(1)}, bf16[80,320]{1,0:T(8,128)(2,1)}, u32[]{:S(2)}) copy-start(bf16[80,320]{1,0:T(8,128)(2,1)} %param.19) | copy-start | bytes 153604
  12.3 28.8 %copy-start.7 = (s32[2,4,2,2]{1,3,2,0:T(2,128)S(1)}, s32[2,4,2,2]{1,3,2,0:T(2,128)}, u32[]{:S(2)}) copy-start(s32[2,4,2,2]{1,3,2,0:T(2,128)} %param.14) | copy-start | bytes 388
  12.3 29.1 %copy-start.8 = (s32[2,4]{1,0:T(2,128)S(1)}, s32[2,4]{1,0:T(2,128)}, u32[]{:S(2)}) copy-start(s32[2,4]{1,0:T(2,128)} %param.13) | copy-start | bytes 100
  12.3 29.3 %copy-start.4 = (bf16[3,80,320]{2,1,0:T(8,128)(2,1)S(1)}, bf16[3,80,320]{2,1,0:T(8,128)(2,1)}, u32[]{:S(2)}) copy-start(bf16[3,80,320]{2,1,0:T(8,128)(2,1)} %param.20) | copy-start | bytes 460804
  12.3 29.3 %copy-start.6 = (bf16[80,320]{1,0:T(8,128)(2,1)S(1)}, bf16[80,320]{1,0:T(8,128)(2,1)}, u32[]{:S(2)}) copy-start(bf16[80,320]{1,0:T(8,128)(2,1)} %param.21) | copy-start | bytes 153604
  14.3 5.7 %collective-permute-start.3 = (bf16[256,320]{1,0:T(8,128)(2,1)S(1)}, bf16[256,320]{1,0:T(8,128)(2,1)S(1)}, u32[]{:S(2)}, u32[]{:S(2)}) collective-permute-start(bf16[256,320]{1,0:T(8,128)(2,1)S(1)} %get-tuple-element.14.refs_4_), channel_id=1, source_target_pairs={{0,8},{4,12},{8,0},{12,4},{1,9},{5,13},{9,1},{13,5},{2,10},{6,14},... | collective-permute-start | bytes 491528 | tf_op jit(solution)/shard_map/ppermute | solution.py:236
  16.0 25.7 %collective-permute-start.2 = (bf16[256,320]{1,0:T(8,128)(2,1)S(1)}, bf16[256,320]{1,0:T(8,128)(2,1)S(1)}, u32[]{:S(2)}, u32[]{:S(2)}) collective-permute-start(bf16[256,320]{1,0:T(8,128)(2,1)S(1)} %get-tuple-element.14.refs_4_), channel_id=1, source_target_pairs={{0,4},{4,0},{8,12},{12,8},{1,5},{5,1},{9,13},{13,9},{2,6},{6,2},{1... | collective-permute-start | bytes 491528 | tf_op jit(solution)/shard_map/ppermute | solution.py:236
  20.1 21.6 %collective-permute-start.4 = (bf16[256,320]{1,0:T(8,128)(2,1)S(1)}, bf16[256,320]{1,0:T(8,128)(2,1)S(1)}, u32[]{:S(2)}, u32[]{:S(2)}) collective-permute-start(bf16[256,320]{1,0:T(8,128)(2,1)S(1)} %collective-permute-done.3.refs_6_), channel_id=1, source_target_pairs={{0,4},{4,0},{8,12},{12,8},{1,5},{5,1},{9,13},{13,9},{2,6},{6,2},{1... | collective-permute-start | bytes 491528 | tf_op jit(solution)/shard_map/ppermute | solution.py:236
  48.2 25.2 %collective-permute-start.5 = (bf16[64,320]{1,0:T(8,128)(2,1)S(1)}, bf16[64,320]{1,0:T(8,128)(2,1)S(1)}, u32[]{:S(2)}, u32[]{:S(2)}) collective-permute-start(bf16[64,320]{1,0:T(8,128)(2,1)S(1)} %get-tuple-element.23), channel_id=1, source_target_pairs={{0,1},{1,0},{2,3},{3,2},{4,5},{5,4},{6,7},{7,6},{8,9},{9,8},{10,11... | collective-permute-start | bytes 122888 | tf_op jit(solution)/shard_map/ppermute | solution.py:353
  48.4 25.0 %collective-permute-start.6 = (bf16[64,320]{1,0:T(8,128)(2,1)S(1)}, bf16[64,320]{1,0:T(8,128)(2,1)S(1)}, u32[]{:S(2)}, u32[]{:S(2)}) collective-permute-start(bf16[64,320]{1,0:T(8,128)(2,1)S(1)} %get-tuple-element.22), channel_id=1, source_target_pairs={{0,2},{1,3},{2,0},{3,1},{4,6},{5,7},{6,4},{7,5},{8,10},{9,11},{10,... | collective-permute-start | bytes 122888 | tf_op jit(solution)/shard_map/ppermute | solution.py:353
  51.1 22.3 %collective-permute-start.7 = (bf16[64,320]{1,0:T(8,128)(2,1)S(1)}, bf16[64,320]{1,0:T(8,128)(2,1)S(1)}, u32[]{:S(2)}, u32[]{:S(2)}) collective-permute-start(bf16[64,320]{1,0:T(8,128)(2,1)S(1)} %get-tuple-element.21), channel_id=1, source_target_pairs={{0,3},{1,2},{2,1},{3,0},{4,7},{5,6},{6,5},{7,4},{8,11},{9,10},{10,... | collective-permute-start | bytes 122888 | tf_op jit(solution)/shard_map/ppermute | solution.py:353
  75.4 6.0 %collective-permute-start.10 = (bf16[64,320]{1,0:T(8,128)(2,1)S(1)}, bf16[64,320]{1,0:T(8,128)(2,1)S(1)}, u32[]{:S(2)}, u32[]{:S(2)}) collective-permute-start(bf16[64,320]{1,0:T(8,128)(2,1)S(1)} %get-tuple-element.20), channel_id=1, source_target_pairs={{3,0},{2,1},{1,2},{0,3},{7,4},{6,5},{5,6},{4,7},{11,8},{10,9},{9,1... | collective-permute-start | bytes 122888 | tf_op jit(solution)/shard_map/ppermute | solution.py:371
  76.7 4.7 %collective-permute-start.8 = (bf16[64,320]{1,0:T(8,128)(2,1)S(1)}, bf16[64,320]{1,0:T(8,128)(2,1)S(1)}, u32[]{:S(2)}, u32[]{:S(2)}) collective-permute-start(bf16[64,320]{1,0:T(8,128)(2,1)S(1)} %get-tuple-element.18), channel_id=1, source_target_pairs={{1,0},{0,1},{3,2},{2,3},{5,4},{4,5},{7,6},{6,7},{9,8},{8,9},{11,10... | collective-permute-start | bytes 122888 | tf_op jit(solution)/shard_map/ppermute | solution.py:371
  76.9 5.0 %collective-permute-start.9 = (bf16[64,320]{1,0:T(8,128)(2,1)S(1)}, bf16[64,320]{1,0:T(8,128)(2,1)S(1)}, u32[]{:S(2)}, u32[]{:S(2)}) collective-permute-start(bf16[64,320]{1,0:T(8,128)(2,1)S(1)} %get-tuple-element.19), channel_id=1, source_target_pairs={{2,0},{3,1},{0,2},{1,3},{6,4},{7,5},{4,6},{5,7},{10,8},{11,9},{8,1... | collective-permute-start | bytes 122888 | tf_op jit(solution)/shard_map/ppermute | solution.py:371

commit v2 on v1

--- a/solution.py
+++ b/solution.py
@@ -91,7 +91,7 @@
 def first_kernel(source, weight_hbm, inner, weight, padded, sem):
     copy = pltpu.make_async_copy(weight_hbm, weight, sem)
     copy.start()
-    y = group_norm_silu(source[...].astype(f32))
+    y = group_norm_silu(source[...].astype(f32).T)
     copy.wait()
     inner[...] = convolve(y, weight, padded)
 
@@ -101,29 +101,42 @@
     copy.start()
     y = group_norm_silu(inner[...] + bias[...])
     copy.wait()
-    total = source[...].astype(f32) + convolve(y, weight, padded)
+    total = source[...].astype(f32).T + convolve(y, weight, padded)
     rounded = total.astype(bf16)
     hidden[...] = rounded
     normed[...] = layer_norm(rounded.astype(f32)).astype(bf16)
 
 
-def assemble(pieces, whole):
-    parts, kinds, rows, _ = pieces.shape
-    for part in range(parts):
-        for kind in range(kinds):
-            whole[kind, pl.ds(part * rows, rows), :] = pieces[part, kind]
+def assemble(where, own, received, swapped, whole, first, kinds):
+    rows = own.shape[1]
+    start = 0 if first == 0 else 2
+    for kind in range(kinds):
+        whole[kind, pl.ds(pl.multiple_of(where[0] * rows, 16), rows), :] = own[first + kind]
+    for k in range(1, len(received) + 1):
+        place = pl.ds(pl.multiple_of(where[k] * rows, 16), rows)
+        for j in range(2):
+            mine = where[len(received) + 1] * 2 + j
+            whole[mine, place, :] = received[k - 1][start + j]
+            whole[2 - mine + 2 * j, place, :] = swapped[k - 1][start + j]
+
+
+def query_kernel(count, where, normed, own, *refs):
+    received, swapped = refs[:count], refs[count : 2 * count]
+    queries, epi, temp = refs[2 * count :]
+    assemble(where, own, received, swapped, epi, 0, 4)
+    assemble(where, own, received, swapped, temp, 4, 4)
+    queries[...] = dot(normed[...], epi[0]).astype(bf16).astype(f32).T
 
 
 def view_kernel(count, tiles, *refs):
-    select, mask, me, hidden = refs[:4]
-    maps = refs[4 : 4 + count]
-    pieces, second, blocks, weights, chosen, totals = refs[4 + count :]
+    select, mask, hidden, query_ref, weights = refs[:5]
+    maps = refs[5 : 5 + count]
+    second, blocks, chosen, totals = refs[5 + count :]
     tokens, channels = hidden.shape
     head = channels // HEADS
     width = tokens // tiles
-    assemble(pieces, weights)
     scale = LOG2E / math.sqrt(head)
-    queries = dot(maps[0][...], weights[0]).astype(bf16).astype(f32).T
+    queries = query_ref[...]
     lane_tile = lax.broadcasted_iota(jnp.int32, (1, tokens), 1) // width
     windows = []
     for h in range(HEADS):
@@ -170,12 +183,11 @@
 
 def time_kernel(frames, *refs):
     blocks = refs[:frames]
-    pieces = refs[frames]
+    weights = refs[frames]
     outs = refs[frames + 1 : 2 * frames + 1]
-    weights, rows_in, attended = refs[2 * frames + 1 :]
+    rows_in, attended = refs[2 * frames + 1 :]
     pixels, channels = blocks[0].shape
     head = channels // HEADS
-    assemble(pieces, weights)
     for f in range(frames):
         rows_in[pl.ds(f * pixels, pixels), :] = blocks[f][...]
     rows = rows_in[...]
@@ -204,11 +216,12 @@
     where = refs[0]
     second = refs[1]
     blocks = refs[2 : 2 + frames]
-    out = refs[2 + frames]
+    out, total = refs[2 + frames :]
     pixels = blocks[0].shape[0]
     for k in range(frames):
         rows = pl.ds(pl.multiple_of(where[k] * pixels, 16), pixels)
-        out[rows, :] = (second[rows, :].astype(f32) + blocks[k][...].astype(f32)).astype(bf16)
+        total[rows, :] = second[rows, :].astype(f32) + blocks[k][...].astype(f32)
+    out[...] = total[...].T.astype(bf16)
 
 
 def is_power(n):
@@ -251,12 +264,16 @@
     return value
 
 
-def gather_weights(three, one):
-    own = jnp.concatenate([three, one[None]], axis=0)
-    parts = lax.all_gather(own, "frame", axis=0)
-    if own.shape[1] % 16:
-        parts = parts.transpose(1, 0, 2, 3).reshape(1, 4, -1, own.shape[2])
-    return parts
+def gather_weights(parts, frames, videos, video):
+    kinds, rows, channels = parts.shape
+    halves = parts.reshape(2, 2, 2, rows, channels)
+    mine = lax.dynamic_index_in_dim(halves, video % 2, 1, keepdims=False)
+    mine = mine.reshape(4, rows, channels)
+    received = [
+        lax.ppermute(mine, "frame", partner_permutation(frames, k)) for k in range(1, frames)
+    ]
+    swapped = [lax.ppermute(part, "video", partner_permutation(videos, 1)) for part in received]
+    return received, swapped
 
 
 def per_device(
@@ -279,9 +296,16 @@
     frame = lax.axis_index("frame")
     video = lax.axis_index("video")
     pixels = tokens // frames
-    source = latents.reshape(tokens, channels)
-    epi_parts = gather_weights(epi_in, epi_out)
-    temp_parts = gather_weights(temp_in, temp_out)
+    source = latents.reshape(tokens, channels).T
+    where = jnp.stack([partner(frame, frames, k) for k in range(frames)]).astype(jnp.int32)
+    parts = jnp.concatenate([epi_in, epi_out[None], temp_in, temp_out[None]], axis=0)
+    if is_power(frames) and videos % 2 == 0 and is_power(videos) and parts.shape[1] % 16 == 0:
+        received, swapped = gather_weights(parts, frames, videos, video)
+        places = jnp.concatenate([where, (video % 2).astype(jnp.int32)[None]])
+    else:
+        parts = lax.all_gather(parts, "frame", axis=1, tiled=True)
+        received, swapped = [], []
+        places = jnp.zeros((2,), jnp.int32)
 
     rows = time_proj.shape[0]
     half = rows * frames // 2
@@ -331,54 +355,65 @@
     else:
         select = (video - targets) % videos
     mask = lax.dynamic_index_in_dim(tile_mask, video, 1, keepdims=False).reshape(-1)
+    square = (4, channels, channels)
+    queries, epi, temp = pl.pallas_call(
+        functools.partial(query_kernel, len(received)),
+        out_shape=[
+            jax.ShapeDtypeStruct((channels, tokens), f32),
+            jax.ShapeDtypeStruct(square, bf16),
+            jax.ShapeDtypeStruct(square, bf16),
+        ],
+        in_specs=[SMEM, VMEM, VMEM] + [VMEM] * (2 * len(received)),
+        out_specs=[VMEM] * 3,
+        compiler_params=params(),
+        name="query",
+    )(places, normed, parts, *received, *swapped)
     second, blocks = pl.pallas_call(
         functools.partial(view_kernel, videos, tiles),
         out_shape=[jax.ShapeDtypeStruct((tokens, channels), bf16)] * 2,
-        in_specs=[SMEM, SMEM, SMEM, VMEM] + [VMEM] * videos + [VMEM],
+        in_specs=[SMEM, SMEM, VMEM, VMEM, VMEM] + [VMEM] * videos,
         out_specs=[VMEM, VMEM],
         scratch_shapes=[
-            pltpu.VMEM((4, channels, channels), bf16),
             pltpu.VMEM((tokens, channels), bf16),
             pltpu.VMEM((channels, tokens), f32),
         ],
         compiler_params=params(),
         name="cross_view",
-    )(select, mask, frame.reshape(1), hidden, *maps, epi_parts)
+    )(select, mask, hidden, queries, epi, *maps)
 
     split = blocks.reshape(frames, pixels, channels)
-    received = []
+    regrouped = []
     for k in range(frames):
         block = lax.dynamic_index_in_dim(split, partner(frame, frames, k), 0, keepdims=False)
         if k:
             block = lax.ppermute(block, "frame", partner_permutation(frames, k))
-        received.append(block)
+        regrouped.append(block)
     outs = pl.pallas_call(
         functools.partial(time_kernel, frames),
         out_shape=[jax.ShapeDtypeStruct((pixels, channels), bf16)] * frames,
         in_specs=[VMEM] * (frames + 1),
         out_specs=[VMEM] * frames,
         scratch_shapes=[
-            pltpu.VMEM((4, channels, channels), bf16),
             pltpu.VMEM((tokens, channels), bf16),
             pltpu.VMEM((tokens, channels), bf16),
         ],
         compiler_params=params(),
         name="temporal",
-    )(*received, temp_parts)
+    )(*regrouped, temp)
     returned = [outs[0]]
     for k in range(1, frames):
         back = [(j, i) for i, j in partner_permutation(frames, k)]
         returned.append(lax.ppermute(outs[k], "frame", back))
-    where = jnp.stack([partner(frame, frames, k) for k in range(frames)]).astype(jnp.int32)
     denoised = pl.pallas_call(
         functools.partial(last_kernel, frames),
-        out_shape=jax.ShapeDtypeStruct((tokens, channels), bf16),
+        out_shape=jax.ShapeDtypeStruct((channels, tokens), bf16),
         in_specs=[SMEM] + [VMEM] * (frames + 1),
         out_specs=VMEM,
+        scratch_shapes=[pltpu.VMEM((tokens, channels), f32)],
         compiler_params=params(),
         name="last",
     )(where, second, *returned)
-    return denoised.reshape(1, 1, tokens, channels)
+    return denoised.T.reshape(1, 1, tokens, channels)
 
 
 def solution(mesh):

time: 83.5 us -> 66.9 us (0.80)
  blocking collectives: 41.8 us -> 0 us
  waiting for transfers between devices: 6.52 us -> 25.8 us
  starting transfers between devices: 16.6 us -> 20.7 us
  Pallas kernels: 12.9 us -> 14.4 us
  other arithmetic: 0.43 us -> 1.51 us
  local copies, waits for them, and re-layouts: 4.06 us -> 3.2 us
    all_gather x2 -> x0, blocking collectives: 41.8 us -> none  [gather_weights(): parts = lax.all_gather(own, 'frame', axis=0)]
    ppermute x2, waiting for transfers between devices: 0.48 us -> 13.8 us  [sum_over(): value = value + lax.ppermute(value, axis, partner_permutation(size, bit))]
    ppermute x3, waiting for transfers between devices: 0.01 us -> 5.72 us  [per_device(): block = lax.ppermute(block, 'frame', partner_permutation(frames, k))]
    ppermute x0 -> x6, starting transfers between devices: none -> 5.02 us  [the longest x3 4.44 us: gather_weights(): lax.ppermute(mine, 'frame', partner_permutation(frames, k))]
    ppermute x2, starting transfers between devices: 6.09 us -> 4.74 us  [sum_over(): value = value + lax.ppermute(value, axis, partner_permutation(size, bit))]
    ppermute x3, waiting for transfers between devices: 1.99 us -> 3.16 us  [per_device(): returned.append(lax.ppermute(outs[k], 'frame', back))]
    concatenate x2 -> x1, other arithmetic: 0.1 us -> 1.19 us  [per_device(): jnp.concatenate([epi_in, epi_out[None], temp_in, temp_out[None]], axis=0)]
    pallas_call x0 -> x1, Pallas kernels: none -> 1.07 us  [per_device(): pl.pallas_call(functools.partial(query_kernel, len(received)), out_shape=...]
  transfers between devices with their start and end apart: 11 -> 17, of which waited for: 4 -> 6; matrix products, arithmetic and copies ran while one was open for 2% -> 3% of each run, Pallas kernels for 2% -> 7%
where the time goes in v2:
time: 66.9 us; the launch traced here: 66.6 us
  waiting for transfers between devices  25.8 us (39%)
  starting transfers between devices  20.7 us (31%)
  Pallas kernels  14.4 us (22%)
  local copies, waits for them, and re-layouts  3.2 us (5%)
  other arithmetic  1.51 us (2%)
  between operations  0.85 us (1%)
    ppermute x2, waiting for transfers between devices, sum_over(): value = value + lax.ppermute(value, axis, partner_permutation(size, bit))  13.8 us
    pallas_call x1, Pallas kernels, per_device(): pl.pallas_call(functools.partial(view_kernel, videos, tiles), out_shape=[...  6.07 us
    ppermute x3, waiting for transfers between devices, per_device(): block = lax.ppermute(block, 'frame', partner_permutation(frames, k))  5.72 us
    ppermute x2, starting transfers between devices, sum_over(): value = value + lax.ppermute(value, axis, partner_permutation(size, bit))  4.74 us
    ppermute x3, starting transfers between devices, per_device(): block = lax.ppermute(block, 'frame', partner_permutation(frames, k))  4.45 us
    ppermute x3, starting transfers between devices, per_device(): returned.append(lax.ppermute(outs[k], 'frame', back))  4.44 us
    ppermute x3, starting transfers between devices, gather_weights(): lax.ppermute(mine, 'frame', partner_permutation(frames, k))  4.44 us
    ppermute x3, waiting for transfers between devices, per_device(): returned.append(lax.ppermute(outs[k], 'frame', back))  3.16 us
  transfers between devices with their start and end apart: 17, of which 6 were waited for; matrix products, arithmetic and copies ran while one was open for 3% of the time, Pallas kernels for 7%

profile of v2, /device:TPU:0, one launch (start us, length us, event | category | flops | bytes accessed | tf_op | source)
XLA Modules:
  0.0 66.6 jit_solution(12734744257376962765)
XLA Ops:
  1.1 3.1 %collective-permute-start = (f32[1,320]{1,0:T(1,128)S(1)}, f32[1,320]{1,0:T(1,128)S(1)}, u32[]{:S(2)}, u32[]{:S(2)}) collective-permute-start(f32[1,320]{1,0:T(1,128)S(1)} %fusion.7), channel_id=1, source_target_pairs={{0,1},{1,0},{2,3},{3,2},{4,5},{5,4},{6,7},{7,6},{8,9},{9,8},{10,11... | collective-permute-start | bytes 3848 | tf_op jit(solution)/shard_map/ppermute | solution.py:262
  4.1 1.2 %pad_maximum_fusion.own = bf16[8,80,320]{2,1,0:T(8,128)(2,1)S(1)} fusion(bf16[1,80,320]{2,1,0:T(8,128)(2,1)} %bitcast.40, bf16[3,80,320]{2,1,0:T(8,128)(2,1)} %param.20, bf16[1,80,320]{2,1,0:T(8,128)(2,1)} %bitcast.41, bf16[3,80,320]{2,1,0:T(8,128)(2,1)} %param.18), kind=kLoop, calls=%fused_computation | loop fusion | flops 614400 | bytes 819200 | tf_op jit(solution)/shard_map/concatenate | solution.py:301
  5.4 3.0 %collective-permute-start.3 = (bf16[4,80,320]{2,1,0:T(8,128)(2,1)S(1)}, bf16[4,80,320]{2,1,0:T(8,128)(2,1)S(1)}, u32[]{:S(2)}, u32[]{:S(2)}) collective-permute-start(bf16[4,80,320]{2,1,0:T(8,128)(2,1)S(1)} %bitcast.38), channel_id=1, source_target_pairs={{0,2},{1,3},{2,0},{3,1},{4,6},{5,7},{6,4},{7,5},{8,10},{9,11},{10,... | collective-permute-start | bytes 614408 | tf_op jit(solution)/shard_map/ppermute | solution.py:273
  8.5 1.3 %collective-permute-start.4 = (bf16[4,80,320]{2,1,0:T(8,128)(2,1)S(1)}, bf16[4,80,320]{2,1,0:T(8,128)(2,1)S(1)}, u32[]{:S(2)}, u32[]{:S(2)}) collective-permute-start(bf16[4,80,320]{2,1,0:T(8,128)(2,1)S(1)} %bitcast.39), channel_id=1, source_target_pairs={{0,3},{1,2},{2,1},{3,0},{4,7},{5,6},{6,5},{7,4},{8,11},{9,10},{10,... | collective-permute-start | bytes 614408 | tf_op jit(solution)/shard_map/ppermute | solution.py:273
  9.8 1.7 %collective-permute-start.1 = (f32[1,320]{1,0:T(1,128)S(1)}, f32[1,320]{1,0:T(1,128)S(1)}, u32[]{:S(2)}, u32[]{:S(2)}) collective-permute-start(f32[1,320]{1,0:T(1,128)S(1)} %add.56), channel_id=1, source_target_pairs={{0,2},{1,3},{2,0},{3,1},{4,6},{5,7},{6,4},{7,5},{8,10},{9,11},{10,... | collective-permute-start | bytes 3848 | tf_op jit(solution)/shard_map/ppermute | solution.py:262
  11.5 1.6 %copy-done.1 = bf16[3,3,320,320]{3,2,1,0:T(8,128)(2,1)S(1)} copy-done((bf16[3,3,320,320]{3,2,1,0:T(8,128)(2,1)S(1)}, bf16[3,3,320,320]{3,2,1,0:T(8,128)(2,1)}, u32[]{:S(2)}) %copy-start.1) | copy-done | bytes 1843224
  13.1 0.9 %copy-done.3 = bf16[1,1,256,320]{2,3,1,0:T(8,128)(2,1)S(1)} copy-done((bf16[1,1,256,320]{2,3,1,0:T(8,128)(2,1)S(1)}, bf16[1,1,256,320]{2,3,1,0:T(8,128)(2,1)}, u32[]{:S(2)}) %copy-start.3) | copy-done | bytes 163864
  14.1 1.9 %first_conv.1.inner = f32[256,320]{1,0:T(8,128)S(1)} custom-call(bf16[320,256]{1,0:T(8,128)(2,1)S(1)} %bitcast.34, bf16[3,960,320]{2,1,0:T(8,128)(2,1)S(1)} %bitcast.32), custom_call_target="tpu_custom_call" | custom-call | flops 471859200 | bytes 2498560 | tf_op jit(solution)/shard_map/first_conv/pallas_call | solution.py:330
  16.0 13.8 %collective-permute-done.1 = f32[1,320]{1,0:T(1,128)S(1)} collective-permute-done((f32[1,320]{1,0:T(1,128)S(1)}, f32[1,320]{1,0:T(1,128)S(1)}, u32[]{:S(2)}, u32[]{:S(2)}) %collective-permute-start.1) | collective-permute-done | bytes 1312 | tf_op jit(solution)/shard_map/ppermute | solution.py:262
  29.8 2.0 %second_conv.1 = (bf16[256,320]{1,0:T(8,128)(2,1)S(1)}, bf16[256,320]{1,0:T(8,128)(2,1)S(1)}) custom-call(bf16[320,256]{1,0:T(8,128)(2,1)S(1)} %bitcast.35, f32[256,320]{1,0:T(8,128)S(1)} %first_conv.1.inner, f32[1,320]{1,0:T(1,128)S(1)} %add.57.bias, bf16[3,960,320]{2,1,0:T(8,128)(2,1)S(1)} %bitcast.33), custom_call_target="tpu_custom_call" | custom-call | flops 471859200 | bytes 2498560 | tf_op jit(solution)/shard_map/second_conv/pallas_call | solution.py:340
  31.8 1.6 %collective-permute-start.9 = (bf16[256,320]{1,0:T(8,128)(2,1)S(1)}, bf16[256,320]{1,0:T(8,128)(2,1)S(1)}, u32[]{:S(2)}, u32[]{:S(2)}) collective-permute-start(bf16[256,320]{1,0:T(8,128)(2,1)S(1)} %get-tuple-element.17.normed.refs_5_), channel_id=1, source_target_pairs={{0,8},{4,12},{8,0},{12,4},{1,9},{5,13},{9,1},{13,5},{2,10},{6,14},... | collective-permute-start | bytes 491528 | tf_op jit(solution)/shard_map/ppermute | solution.py:249
  34.5 3.1 %collective-permute-done.9.refs_7_ = bf16[256,320]{1,0:T(8,128)(2,1)S(1)} collective-permute-done((bf16[256,320]{1,0:T(8,128)(2,1)S(1)}, bf16[256,320]{1,0:T(8,128)(2,1)S(1)}, u32[]{:S(2)}, u32[]{:S(2)}) %collective-permute-start.9) | collective-permute-done | bytes 163872 | tf_op jit(solution)/shard_map/ppermute | solution.py:249
  38.2 1.1 %query.1 = (f32[320,256]{1,0:T(8,128)S(1)}, bf16[4,320,320]{2,1,0:T(8,128)(2,1)S(1)}, bf16[4,320,320]{2,1,0:T(8,128)(2,1)S(1)}) custom-call(s32[5]{0:T(128)S(1)} %concatenate.7.where, bf16[256,320]{1,0:T(8,128)(2,1)S(1)} %get-tuple-element.17.normed.refs_5_, bf16[8,80,320]{2,1,0:T(8,128)(2,1)S(1)} %pad_maximum_fusion.own, ...), custom_call_target="tpu_custom_call" | custom-call | tf_op jit(solution)/shard_map/query/pallas_call | solution.py:359
  39.3 6.1 %cross_view.1 = (bf16[256,320]{1,0:T(8,128)(2,1)S(1)}, bf16[256,320]{1,0:T(8,128)(2,1)S(1)}) custom-call(s32[2]{0:T(128)S(1)} %fusion.6.refs_0_, s32[8]{0:T(128)S(1)} %reshape.45.refs_1_, bf16[256,320]{1,0:T(8,128)(2,1)S(1)} %get-tuple-element.16.refs_2_, f32[320,256]{1,0:T(8,128)S(1)} %get-tuple-element.18.refs_3_, ...), custom_call_target="tpu_custom_call" | custom-call | tf_op jit(solution)/shard_map/cross_view/pallas_call | solution.py:371
  45.4 0.9 %collective-permute-start.11 = (bf16[64,320]{1,0:T(8,128)(2,1)S(1)}, bf16[64,320]{1,0:T(8,128)(2,1)S(1)}, u32[]{:S(2)}, u32[]{:S(2)}) collective-permute-start(bf16[64,320]{1,0:T(8,128)(2,1)S(1)} %get-tuple-element.29), channel_id=1, source_target_pairs={{0,1},{1,0},{2,3},{3,2},{4,5},{5,4},{6,7},{7,6},{8,9},{9,8},{10,11... | collective-permute-start | bytes 122888 | tf_op jit(solution)/shard_map/ppermute | solution.py:389
  46.3 3.4 %collective-permute-start.12 = (bf16[64,320]{1,0:T(8,128)(2,1)S(1)}, bf16[64,320]{1,0:T(8,128)(2,1)S(1)}, u32[]{:S(2)}, u32[]{:S(2)}) collective-permute-start(bf16[64,320]{1,0:T(8,128)(2,1)S(1)} %get-tuple-element.28), channel_id=1, source_target_pairs={{0,2},{1,3},{2,0},{3,1},{4,6},{5,7},{6,4},{7,5},{8,10},{9,11},{10,... | collective-permute-start | bytes 122888 | tf_op jit(solution)/shard_map/ppermute | solution.py:389
  49.8 3.2 %collective-permute-done.12.refs_2_ = bf16[64,320]{1,0:T(8,128)(2,1)S(1)} collective-permute-done((bf16[64,320]{1,0:T(8,128)(2,1)S(1)}, bf16[64,320]{1,0:T(8,128)(2,1)S(1)}, u32[]{:S(2)}, u32[]{:S(2)}) %collective-permute-start.12) | collective-permute-done | bytes 40992 | tf_op jit(solution)/shard_map/ppermute | solution.py:389
  53.0 2.5 %collective-permute-done.13.refs_3_ = bf16[64,320]{1,0:T(8,128)(2,1)S(1)} collective-permute-done((bf16[64,320]{1,0:T(8,128)(2,1)S(1)}, bf16[64,320]{1,0:T(8,128)(2,1)S(1)}, u32[]{:S(2)}, u32[]{:S(2)}) %collective-permute-start.13) | collective-permute-done | bytes 40992 | tf_op jit(solution)/shard_map/ppermute | solution.py:389
  55.5 2.0 %temporal.1 = (bf16[64,320]{1,0:T(8,128)(2,1)S(1)}, bf16[64,320]{1,0:T(8,128)(2,1)S(1)}, bf16[64,320]{1,0:T(8,128)(2,1)S(1)}, bf16[64,320]{1,0:T(8,128)(2,1)S(1)}) custom-call(bf16[64,320]{1,0:T(8,128)(2,1)S(1)} %get-tuple-element.30.refs_0_, bf16[64,320]{1,0:T(8,128)(2,1)S(1)} %collective-permute-done.11.refs_1_, ...), custom_call_target="tpu_custom_call" | custom-call | tf_op jit(solution)/shard_map/temporal/pallas_call | solution.py:391
  57.6 1.7 %collective-permute-start.15 = (bf16[64,320]{1,0:T(8,128)(2,1)S(1)}, bf16[64,320]{1,0:T(8,128)(2,1)S(1)}, u32[]{:S(2)}, u32[]{:S(2)}) collective-permute-start(bf16[64,320]{1,0:T(8,128)(2,1)S(1)} %get-tuple-element.25), channel_id=1, source_target_pairs={{2,0},{3,1},{0,2},{1,3},{6,4},{7,5},{4,6},{5,7},{10,8},{11,9},{8,1... | collective-permute-start | bytes 122888 | tf_op jit(solution)/shard_map/ppermute | solution.py:406
  59.4 2.7 %collective-permute-start.16 = (bf16[64,320]{1,0:T(8,128)(2,1)S(1)}, bf16[64,320]{1,0:T(8,128)(2,1)S(1)}, u32[]{:S(2)}, u32[]{:S(2)}) collective-permute-start(bf16[64,320]{1,0:T(8,128)(2,1)S(1)} %get-tuple-element.26), channel_id=1, source_target_pairs={{3,0},{2,1},{1,2},{0,3},{7,4},{6,5},{5,6},{4,7},{11,8},{10,9},{9,1... | collective-permute-start | bytes 122888 | tf_op jit(solution)/shard_map/ppermute | solution.py:406
  62.1 1.3 %collective-permute-done.15.refs_4_ = bf16[64,320]{1,0:T(8,128)(2,1)S(1)} collective-permute-done((bf16[64,320]{1,0:T(8,128)(2,1)S(1)}, bf16[64,320]{1,0:T(8,128)(2,1)S(1)}, u32[]{:S(2)}, u32[]{:S(2)}) %collective-permute-start.15) | collective-permute-done | bytes 40992 | tf_op jit(solution)/shard_map/ppermute | solution.py:406
  63.4 1.9 %collective-permute-done.16.refs_5_ = bf16[64,320]{1,0:T(8,128)(2,1)S(1)} collective-permute-done((bf16[64,320]{1,0:T(8,128)(2,1)S(1)}, bf16[64,320]{1,0:T(8,128)(2,1)S(1)}, u32[]{:S(2)}, u32[]{:S(2)}) %collective-permute-start.16) | collective-permute-done | bytes 40992 | tf_op jit(solution)/shard_map/ppermute | solution.py:406
  65.3 1.4 %last.1 = bf16[320,256]{1,0:T(8,128)(2,1)} custom-call(s32[4]{0:T(128)S(1)} %pad_add_fusion.refs_0_, bf16[256,320]{1,0:T(8,128)(2,1)S(1)} %get-tuple-element.20.refs_1_, bf16[64,320]{1,0:T(8,128)(2,1)S(1)} %get-tuple-element.23.refs_2_, bf16[64,320]{1,0:T(8,128)(2,1)S(1)} %collective-permute-done.14.refs_3_, ...), custom_call_target="tpu_custom_call" | custom-call | tf_op jit(solution)/shard_map/last/pallas_call | solution.py:407
  (41 shorter events, 2.5 us)
Async XLA Ops:
  0.0 1.0 %copy-start = (bf16[320,320]{1,0:T(8,128)(2,1)S(1)}, bf16[320,320]{1,0:T(8,128)(2,1)}, u32[]{:S(2)}) copy-start(bf16[320,320]{1,0:T(8,128)(2,1)} %param.17) | copy-start | bytes 614404
  1.1 8.7 %collective-permute-start = (f32[1,320]{1,0:T(1,128)S(1)}, f32[1,320]{1,0:T(1,128)S(1)}, u32[]{:S(2)}, u32[]{:S(2)}) collective-permute-start(f32[1,320]{1,0:T(1,128)S(1)} %fusion.7), channel_id=1, source_target_pairs={{0,1},{1,0},{2,3},{3,2},{4,5},{5,4},{6,7},{7,6},{8,9},{9,8},{10,11... | collective-permute-start | bytes 3848 | tf_op jit(solution)/shard_map/ppermute | solution.py:262
  5.4 28.1 %collective-permute-start.2 = (bf16[4,80,320]{2,1,0:T(8,128)(2,1)S(1)}, bf16[4,80,320]{2,1,0:T(8,128)(2,1)S(1)}, u32[]{:S(2)}, u32[]{:S(2)}) collective-permute-start(bf16[4,80,320]{2,1,0:T(8,128)(2,1)S(1)} %bitcast.37), channel_id=1, source_target_pairs={{0,1},{1,0},{2,3},{3,2},{4,5},{5,4},{6,7},{7,6},{8,9},{9,8},{10,11... | collective-permute-start | bytes 614408 | tf_op jit(solution)/shard_map/ppermute | solution.py:273
  5.4 28.0 %collective-permute-start.3 = (bf16[4,80,320]{2,1,0:T(8,128)(2,1)S(1)}, bf16[4,80,320]{2,1,0:T(8,128)(2,1)S(1)}, u32[]{:S(2)}, u32[]{:S(2)}) collective-permute-start(bf16[4,80,320]{2,1,0:T(8,128)(2,1)S(1)} %bitcast.38), channel_id=1, source_target_pairs={{0,2},{1,3},{2,0},{3,1},{4,6},{5,7},{6,4},{7,5},{8,10},{9,11},{10,... | collective-permute-start | bytes 614408 | tf_op jit(solution)/shard_map/ppermute | solution.py:273
  8.5 25.5 %collective-permute-start.4 = (bf16[4,80,320]{2,1,0:T(8,128)(2,1)S(1)}, bf16[4,80,320]{2,1,0:T(8,128)(2,1)S(1)}, u32[]{:S(2)}, u32[]{:S(2)}) collective-permute-start(bf16[4,80,320]{2,1,0:T(8,128)(2,1)S(1)} %bitcast.39), channel_id=1, source_target_pairs={{0,3},{1,2},{2,1},{3,0},{4,7},{5,6},{6,5},{7,4},{8,11},{9,10},{10,... | collective-permute-start | bytes 614408 | tf_op jit(solution)/shard_map/ppermute | solution.py:273
  9.8 19.9 %collective-permute-start.1 = (f32[1,320]{1,0:T(1,128)S(1)}, f32[1,320]{1,0:T(1,128)S(1)}, u32[]{:S(2)}, u32[]{:S(2)}) collective-permute-start(f32[1,320]{1,0:T(1,128)S(1)} %add.56), channel_id=1, source_target_pairs={{0,2},{1,3},{2,0},{3,1},{4,6},{5,7},{6,4},{7,5},{8,10},{9,11},{10,... | collective-permute-start | bytes 3848 | tf_op jit(solution)/shard_map/ppermute | solution.py:262
  11.5 1.6 %copy-start.1 = (bf16[3,3,320,320]{3,2,1,0:T(8,128)(2,1)S(1)}, bf16[3,3,320,320]{3,2,1,0:T(8,128)(2,1)}, u32[]{:S(2)}) copy-start(bf16[3,3,320,320]{3,2,1,0:T(8,128)(2,1)} %param.15) | copy-start | bytes 5529604
  13.1 0.9 %copy-start.3 = (bf16[1,1,256,320]{2,3,1,0:T(8,128)(2,1)S(1)}, bf16[1,1,256,320]{2,3,1,0:T(8,128)(2,1)}, u32[]{:S(2)}) copy-start(bf16[1,1,256,320]{2,3,1,0:T(8,128)(2,1)} %param.11) | copy-start | bytes 491524
  14.1 15.7 %copy-start.2 = (bf16[3,3,320,320]{3,2,1,0:T(8,128)(2,1)S(1)}, bf16[3,3,320,320]{3,2,1,0:T(8,128)(2,1)}, u32[]{:S(2)}) copy-start(bf16[3,3,320,320]{3,2,1,0:T(8,128)(2,1)} %param.16) | copy-start | bytes 5529604
  14.1 23.5 %copy-start.4 = (s32[2,4,2,2]{1,3,2,0:T(2,128)S(1)}, s32[2,4,2,2]{1,3,2,0:T(2,128)}, u32[]{:S(2)}) copy-start(s32[2,4,2,2]{1,3,2,0:T(2,128)} %param.14) | copy-start | bytes 388
  14.1 23.9 %copy-start.5 = (s32[2,4]{1,0:T(2,128)S(1)}, s32[2,4]{1,0:T(2,128)}, u32[]{:S(2)}) copy-start(s32[2,4]{1,0:T(2,128)} %param.13) | copy-start | bytes 100
  31.8 5.7 %collective-permute-start.9 = (bf16[256,320]{1,0:T(8,128)(2,1)S(1)}, bf16[256,320]{1,0:T(8,128)(2,1)S(1)}, u32[]{:S(2)}, u32[]{:S(2)}) collective-permute-start(bf16[256,320]{1,0:T(8,128)(2,1)S(1)} %get-tuple-element.17.normed.refs_5_), channel_id=1, source_target_pairs={{0,8},{4,12},{8,0},{12,4},{1,9},{5,13},{9,1},{13,5},{2,10},{6,14},... | collective-permute-start | bytes 491528 | tf_op jit(solution)/shard_map/ppermute | solution.py:249
  33.4 4.7 %collective-permute-start.5 = (bf16[4,80,320]{2,1,0:T(8,128)(2,1)S(1)}, bf16[4,80,320]{2,1,0:T(8,128)(2,1)S(1)}, u32[]{:S(2)}, u32[]{:S(2)}) collective-permute-start(bf16[4,80,320]{2,1,0:T(8,128)(2,1)S(1)} %collective-permute-done.2.refs_0_), channel_id=1, source_target_pairs={{0,4},{4,0},{8,12},{12,8},{1,5},{5,1},{9,13},{13,9},{2,6},{6,2},{1... | collective-permute-start | bytes 614408 | tf_op jit(solution)/shard_map/ppermute | solution.py:275
  33.4 4.7 %collective-permute-start.6 = (bf16[4,80,320]{2,1,0:T(8,128)(2,1)S(1)}, bf16[4,80,320]{2,1,0:T(8,128)(2,1)S(1)}, u32[]{:S(2)}, u32[]{:S(2)}) collective-permute-start(bf16[4,80,320]{2,1,0:T(8,128)(2,1)S(1)} %collective-permute-done.3.refs_1_), channel_id=1, source_target_pairs={{0,4},{4,0},{8,12},{12,8},{1,5},{5,1},{9,13},{13,9},{2,6},{6,2},{1... | collective-permute-start | bytes 614408 | tf_op jit(solution)/shard_map/ppermute | solution.py:275
  33.9 4.2 %collective-permute-start.7 = (bf16[4,80,320]{2,1,0:T(8,128)(2,1)S(1)}, bf16[4,80,320]{2,1,0:T(8,128)(2,1)S(1)}, u32[]{:S(2)}, u32[]{:S(2)}) collective-permute-start(bf16[4,80,320]{2,1,0:T(8,128)(2,1)S(1)} %collective-permute-done.4.refs_2_), channel_id=1, source_target_pairs={{0,4},{4,0},{8,12},{12,8},{1,5},{5,1},{9,13},{13,9},{2,6},{6,2},{1... | collective-permute-start | bytes 614408 | tf_op jit(solution)/shard_map/ppermute | solution.py:275
  34.0 5.2 %collective-permute-start.8 = (bf16[256,320]{1,0:T(8,128)(2,1)S(1)}, bf16[256,320]{1,0:T(8,128)(2,1)S(1)}, u32[]{:S(2)}, u32[]{:S(2)}) collective-permute-start(bf16[256,320]{1,0:T(8,128)(2,1)S(1)} %get-tuple-element.17.normed.refs_5_), channel_id=1, source_target_pairs={{0,4},{4,0},{8,12},{12,8},{1,5},{5,1},{9,13},{13,9},{2,6},{6,2},{1... | collective-permute-start | bytes 491528 | tf_op jit(solution)/shard_map/ppermute | solution.py:249
  37.5 1.7 %collective-permute-start.10 = (bf16[256,320]{1,0:T(8,128)(2,1)S(1)}, bf16[256,320]{1,0:T(8,128)(2,1)S(1)}, u32[]{:S(2)}, u32[]{:S(2)}) collective-permute-start(bf16[256,320]{1,0:T(8,128)(2,1)S(1)} %collective-permute-done.9.refs_7_), channel_id=1, source_target_pairs={{0,4},{4,0},{8,12},{12,8},{1,5},{5,1},{9,13},{13,9},{2,6},{6,2},{1... | collective-permute-start | bytes 491528 | tf_op jit(solution)/shard_map/ppermute | solution.py:249
  45.4 4.5 %collective-permute-start.11 = (bf16[64,320]{1,0:T(8,128)(2,1)S(1)}, bf16[64,320]{1,0:T(8,128)(2,1)S(1)}, u32[]{:S(2)}, u32[]{:S(2)}) collective-permute-start(bf16[64,320]{1,0:T(8,128)(2,1)S(1)} %get-tuple-element.29), channel_id=1, source_target_pairs={{0,1},{1,0},{2,3},{3,2},{4,5},{5,4},{6,7},{7,6},{8,9},{9,8},{10,11... | collective-permute-start | bytes 122888 | tf_op jit(solution)/shard_map/ppermute | solution.py:389
  46.3 6.8 %collective-permute-start.12 = (bf16[64,320]{1,0:T(8,128)(2,1)S(1)}, bf16[64,320]{1,0:T(8,128)(2,1)S(1)}, u32[]{:S(2)}, u32[]{:S(2)}) collective-permute-start(bf16[64,320]{1,0:T(8,128)(2,1)S(1)} %get-tuple-element.28), channel_id=1, source_target_pairs={{0,2},{1,3},{2,0},{3,1},{4,6},{5,7},{6,4},{7,5},{8,10},{9,11},{10,... | collective-permute-start | bytes 122888 | tf_op jit(solution)/shard_map/ppermute | solution.py:389
  49.7 5.9 %collective-permute-start.13 = (bf16[64,320]{1,0:T(8,128)(2,1)S(1)}, bf16[64,320]{1,0:T(8,128)(2,1)S(1)}, u32[]{:S(2)}, u32[]{:S(2)}) collective-permute-start(bf16[64,320]{1,0:T(8,128)(2,1)S(1)} %get-tuple-element.27), channel_id=1, source_target_pairs={{0,3},{1,2},{2,1},{3,0},{4,7},{5,6},{6,5},{7,4},{8,11},{9,10},{10,... | collective-permute-start | bytes 122888 | tf_op jit(solution)/shard_map/ppermute | solution.py:389
  57.6 4.5 %collective-permute-start.14 = (bf16[64,320]{1,0:T(8,128)(2,1)S(1)}, bf16[64,320]{1,0:T(8,128)(2,1)S(1)}, u32[]{:S(2)}, u32[]{:S(2)}) collective-permute-start(bf16[64,320]{1,0:T(8,128)(2,1)S(1)} %get-tuple-element.24), channel_id=1, source_target_pairs={{1,0},{0,1},{3,2},{2,3},{5,4},{4,5},{7,6},{6,7},{9,8},{8,9},{11,10... | collective-permute-start | bytes 122888 | tf_op jit(solution)/shard_map/ppermute | solution.py:406
  57.6 5.7 %collective-permute-start.15 = (bf16[64,320]{1,0:T(8,128)(2,1)S(1)}, bf16[64,320]{1,0:T(8,128)(2,1)S(1)}, u32[]{:S(2)}, u32[]{:S(2)}) collective-permute-start(bf16[64,320]{1,0:T(8,128)(2,1)S(1)} %get-tuple-element.25), channel_id=1, source_target_pairs={{2,0},{3,1},{0,2},{1,3},{6,4},{7,5},{4,6},{5,7},{10,8},{11,9},{8,1... | collective-permute-start | bytes 122888 | tf_op jit(solution)/shard_map/ppermute | solution.py:406
  59.4 5.9 %collective-permute-start.16 = (bf16[64,320]{1,0:T(8,128)(2,1)S(1)}, bf16[64,320]{1,0:T(8,128)(2,1)S(1)}, u32[]{:S(2)}, u32[]{:S(2)}) collective-permute-start(bf16[64,320]{1,0:T(8,128)(2,1)S(1)} %get-tuple-element.26), channel_id=1, source_target_pairs={{3,0},{2,1},{1,2},{0,3},{7,4},{6,5},{5,6},{4,7},{11,8},{10,9},{9,1... | collective-permute-start | bytes 122888 | tf_op jit(solution)/shard_map/ppermute | solution.py:406

commit v3 on v2

--- a/solution.py
+++ b/solution.py
@@ -20,13 +20,12 @@
 
 VMEM = pl.BlockSpec(memory_space=pltpu.VMEM)
 SMEM = pl.BlockSpec(memory_space=pltpu.SMEM)
-ANY = pl.BlockSpec(memory_space=pl.ANY)
 f32 = jnp.float32
 bf16 = jnp.bfloat16
 
 
 def params():
-    return pltpu.CompilerParams(vmem_limit_bytes=48 * 1024 * 1024)
+    return pltpu.CompilerParams(vmem_limit_bytes=16 * 1024 * 1024)
 
 
 def dot(a, b):
@@ -82,25 +81,23 @@
     padded[pl.ds(W, tokens), :] = jnp.concatenate(
         [before.astype(bf16), y.astype(bf16), after.astype(bf16)], axis=1
     )
-    total = dot(padded[pl.ds(0, tokens), :], weight[0])
-    total += dot(padded[pl.ds(W, tokens), :], weight[1])
-    total += dot(padded[pl.ds(2 * W, tokens), :], weight[2])
+    total = None
+    for k in range(3):
+        part = dot(padded[pl.ds(k * W, tokens), :], weight[k])
+        total = part if total is None else total + part
     return total
 
 
-def first_kernel(source, weight_hbm, inner, weight, padded, sem):
-    copy = pltpu.make_async_copy(weight_hbm, weight, sem)
-    copy.start()
-    y = group_norm_silu(source[...].astype(f32).T)
-    copy.wait()
-    inner[...] = convolve(y, weight, padded)
-
-
-def second_kernel(source, inner, bias, weight_hbm, hidden, normed, weight, padded, sem):
-    copy = pltpu.make_async_copy(weight_hbm, weight, sem)
-    copy.start()
+def share_kernel(act, proj, share):
+    share[...] = dot(act[...], proj[...])
+
+
+def first_kernel(source, weight, inner, padded):
+    inner[...] = convolve(group_norm_silu(source[...].astype(f32).T), weight, padded)
+
+
+def second_kernel(source, inner, bias, weight, hidden, normed, padded):
     y = group_norm_silu(inner[...] + bias[...])
-    copy.wait()
     total = source[...].astype(f32).T + convolve(y, weight, padded)
     rounded = total.astype(bf16)
     hidden[...] = rounded
@@ -181,47 +178,42 @@
     blocks[...] = layer_norm(result.astype(f32)).astype(bf16)
 
 
-def time_kernel(frames, *refs):
-    blocks = refs[:frames]
-    weights = refs[frames]
-    outs = refs[frames + 1 : 2 * frames + 1]
-    rows_in, attended = refs[2 * frames + 1 :]
-    pixels, channels = blocks[0].shape
+def frame_part(queries, rows, weights):
+    channels = rows.shape[1]
     head = channels // HEADS
-    for f in range(frames):
-        rows_in[pl.ds(f * pixels, pixels), :] = blocks[f][...]
-    rows = rows_in[...]
     ones = block_diagonal(channels, head)
-    queries = dot(rows, weights[0]).astype(bf16).astype(f32)
-    keys = dot(rows, weights[1]).astype(bf16).astype(f32).reshape(frames, pixels, channels)
-    values = dot(rows, weights[2]).astype(bf16).astype(f32).reshape(frames, pixels, channels)
-    scale = LOG2E / math.sqrt(head)
-    for f in range(frames):
-        one = queries[f * pixels : (f + 1) * pixels]
-        products = (one[None] * keys).reshape(frames * pixels, channels)
-        high = products.astype(bf16)
-        low = (products - high.astype(f32)).astype(bf16)
-        scores = (dot(high, ones) + dot(low, ones)) * scale
-        scores = scores.reshape(frames, pixels, channels)
-        powers = jnp.exp2(scores - jnp.max(scores, axis=0, keepdims=True))
-        norm = 1.0 / jnp.sum(powers, axis=0, keepdims=True)
-        probs = (powers * norm).astype(bf16).astype(f32)
-        attended[pl.ds(f * pixels, pixels), :] = jnp.sum(probs * values, axis=0).astype(bf16)
-    result = dot(attended[...], weights[3]).astype(bf16)
-    for f in range(frames):
-        outs[f][...] = result[f * pixels : (f + 1) * pixels]
+    keys = dot(rows, weights[1]).astype(bf16).astype(f32)
+    values = dot(rows, weights[2]).astype(bf16)
+    products = queries * keys
+    high = products.astype(bf16)
+    low = (products - high.astype(f32)).astype(bf16)
+    return (dot(high, ones) + dot(low, ones)) * (LOG2E / math.sqrt(head)), values
+
+
+def own_frame_kernel(rows, weights, queries, scores, values):
+    queries[...] = dot(rows[...], weights[0]).astype(bf16)
+    scores[...], values[...] = frame_part(queries[...].astype(f32), rows[...], weights)
+
+
+def frame_kernel(queries, rows, weights, scores, values):
+    scores[...], values[...] = frame_part(queries[...].astype(f32), rows[...], weights)
 
 
 def last_kernel(frames, *refs):
-    where = refs[0]
-    second = refs[1]
-    blocks = refs[2 : 2 + frames]
-    out, total = refs[2 + frames :]
-    pixels = blocks[0].shape[0]
-    for k in range(frames):
-        rows = pl.ds(pl.multiple_of(where[k] * pixels, 16), pixels)
-        total[rows, :] = second[rows, :].astype(f32) + blocks[k][...].astype(f32)
-    out[...] = total[...].T.astype(bf16)
+    second, queries, rows, weights = refs[:4]
+    scores = refs[4 : 3 + frames]
+    values = refs[3 + frames : 2 + 2 * frames]
+    out = refs[-1]
+    last_scores, last_values = frame_part(queries[...].astype(f32), rows[...], weights)
+    every = [ref[...] for ref in scores] + [last_scores]
+    most = functools.reduce(jnp.maximum, every)
+    powers = [jnp.exp2(one - most) for one in every]
+    norm = 1.0 / functools.reduce(jnp.add, powers)
+    total = (powers[-1] * norm).astype(bf16).astype(f32) * last_values.astype(f32)
+    for power, value in zip(powers, values):
+        total += (power * norm).astype(bf16).astype(f32) * value[...].astype(f32)
+    result = second[...].astype(f32) + dot(total.astype(bf16), weights[3])
+    out[...] = result.T.astype(bf16)
 
 
 def is_power(n):
@@ -254,14 +246,17 @@
     return [maps[k] for k in range(size)]
 
 
-def sum_over(value, axis, size):
+def sum_over(value, beside, later, axis, size):
     if not is_power(size):
-        return lax.psum(value, axis)
+        return lax.psum(value, axis), beside, later
     bit = 1
     while bit < size:
         value = value + lax.ppermute(value, axis, partner_permutation(size, bit))
+        if bit == 1:
+            value, beside = lax.optimization_barrier((value, beside))
         bit *= 2
-    return value
+    value, later = lax.optimization_barrier((value, later))
+    return value, beside, later
 
 
 def gather_weights(parts, frames, videos, video):
@@ -298,14 +293,6 @@
     pixels = tokens // frames
     source = latents.reshape(tokens, channels).T
     where = jnp.stack([partner(frame, frames, k) for k in range(frames)]).astype(jnp.int32)
-    parts = jnp.concatenate([epi_in, epi_out[None], temp_in, temp_out[None]], axis=0)
-    if is_power(frames) and videos % 2 == 0 and is_power(videos) and parts.shape[1] % 16 == 0:
-        received, swapped = gather_weights(parts, frames, videos, video)
-        places = jnp.concatenate([where, (video % 2).astype(jnp.int32)[None]])
-    else:
-        parts = lax.all_gather(parts, "frame", axis=1, tiled=True)
-        received, swapped = [], []
-        places = jnp.zeros((2,), jnp.int32)
 
     rows = time_proj.shape[0]
     half = rows * frames // 2
@@ -315,12 +302,20 @@
     angles = timesteps.astype(f32)[:, None] * frequency[None, :]
     wave = jnp.where(index[None, :] < half, jnp.cos(angles), jnp.sin(angles))
     time_act = jax.nn.silu(wave).astype(bf16)
-    bias = sum_over(dot(time_act, time_proj), "frame", frames)
+    share = pl.pallas_call(
+        share_kernel,
+        out_shape=jax.ShapeDtypeStruct((1, channels), f32),
+        in_specs=[VMEM, VMEM],
+        out_specs=VMEM,
+        compiler_params=params(),
+        cost_estimate=pl.CostEstimate(flops=10**10, bytes_accessed=1 << 20, transcendentals=0),
+        name="time_share",
+    )(time_act, time_proj)
+    parts = jnp.concatenate([epi_in, epi_out[None], temp_in, temp_out[None]], axis=0)
+    bias, source, parts = sum_over(share, source, parts, "frame", frames)
 
     conv_scratch = [
-        pltpu.VMEM((3, 3 * channels, channels), bf16),
         pltpu.VMEM((tokens + 2 * W, 3 * channels), bf16),
-        pltpu.SemaphoreType.DMA,
     ]
     conv_cost = pl.CostEstimate(
         flops=2 * 9 * tokens * channels * channels,
@@ -330,17 +325,24 @@
     inner = pl.pallas_call(
         first_kernel,
         out_shape=jax.ShapeDtypeStruct((tokens, channels), f32),
-        in_specs=[VMEM, ANY],
+        in_specs=[VMEM, VMEM],
         out_specs=VMEM,
         scratch_shapes=conv_scratch,
         compiler_params=params(),
         cost_estimate=conv_cost,
         name="first_conv",
     )(source, conv_first.reshape(3, 3 * channels, channels))
+    if is_power(frames) and videos % 2 == 0 and is_power(videos) and parts.shape[1] % 16 == 0:
+        received, swapped = gather_weights(parts, frames, videos, video)
+        places = jnp.concatenate([where, (video % 2).astype(jnp.int32)[None]])
+    else:
+        parts = lax.all_gather(parts, "frame", axis=1, tiled=True)
+        received, swapped = [], []
+        places = jnp.zeros((2,), jnp.int32)
     hidden, normed = pl.pallas_call(
         second_kernel,
         out_shape=[jax.ShapeDtypeStruct((tokens, channels), bf16)] * 2,
-        in_specs=[VMEM, VMEM, VMEM, ANY],
+        in_specs=[VMEM, VMEM, VMEM, VMEM],
         out_specs=[VMEM, VMEM],
         scratch_shapes=conv_scratch,
         compiler_params=params(),
@@ -381,38 +383,47 @@
         name="cross_view",
     )(select, mask, hidden, queries, epi, *maps)
 
-    split = blocks.reshape(frames, pixels, channels)
-    regrouped = []
-    for k in range(frames):
-        block = lax.dynamic_index_in_dim(split, partner(frame, frames, k), 0, keepdims=False)
-        if k:
-            block = lax.ppermute(block, "frame", partner_permutation(frames, k))
-        regrouped.append(block)
-    outs = pl.pallas_call(
-        functools.partial(time_kernel, frames),
-        out_shape=[jax.ShapeDtypeStruct((pixels, channels), bf16)] * frames,
-        in_specs=[VMEM] * (frames + 1),
-        out_specs=[VMEM] * frames,
-        scratch_shapes=[
-            pltpu.VMEM((tokens, channels), bf16),
-            pltpu.VMEM((tokens, channels), bf16),
-        ],
-        compiler_params=params(),
-        name="temporal",
-    )(*regrouped, temp)
-    returned = [outs[0]]
-    for k in range(1, frames):
-        back = [(j, i) for i, j in partner_permutation(frames, k)]
-        returned.append(lax.ppermute(outs[k], "frame", back))
+    arrived = {}
+    for k in reversed(range(1, frames)):
+        arrived[k] = lax.ppermute(blocks, "frame", partner_permutation(frames, k))
+    score_shape = jax.ShapeDtypeStruct((tokens, channels), f32)
+    value_shape = jax.ShapeDtypeStruct((tokens, channels), bf16)
+    frame_cost = pl.CostEstimate(
+        flops=8 * tokens * channels * channels,
+        bytes_accessed=8 * channels * channels + 8 * tokens * channels,
+        transcendentals=0,
+    )
+    frame_queries, *first = pl.pallas_call(
+        own_frame_kernel,
+        out_shape=[value_shape, score_shape, value_shape],
+        in_specs=[VMEM] * 2,
+        out_specs=[VMEM] * 3,
+        compiler_params=params(),
+        cost_estimate=frame_cost,
+        name="own_frame",
+    )(blocks, temp)
+    scores, values = [first[0]], [first[1]]
+    order = [1] + list(range(frames - 1, 1, -1)) if frames > 1 else []
+    for k in order[:-1]:
+        one = pl.pallas_call(
+            frame_kernel,
+            out_shape=[score_shape, value_shape],
+            in_specs=[VMEM] * 3,
+            out_specs=[VMEM] * 2,
+            compiler_params=params(),
+            cost_estimate=frame_cost,
+            name="other_frame",
+        )(frame_queries, arrived[k], temp)
+        scores.append(one[0])
+        values.append(one[1])
     denoised = pl.pallas_call(
         functools.partial(last_kernel, frames),
         out_shape=jax.ShapeDtypeStruct((channels, tokens), bf16),
-        in_specs=[SMEM] + [VMEM] * (frames + 1),
+        in_specs=[VMEM] * (2 + 2 * frames),
         out_specs=VMEM,
-        scratch_shapes=[pltpu.VMEM((tokens, channels), f32)],
         compiler_params=params(),
         name="last",
-    )(where, second, *returned)
+    )(second, frame_queries, arrived[order[-1]], temp, *scores, *values)
     return denoised.T.reshape(1, 1, tokens, channels)
 
 

time: 66.9 us -> 66.6 us (level)
  waiting for transfers between devices: 25.8 us -> 29.6 us
  local copies, waits for them, and re-layouts: 3.2 us -> 1.39 us
  starting transfers between devices: 20.7 us -> 19.2 us
  other arithmetic: 1.51 us -> 0.39 us
  Pallas kernels: 14.4 us -> 15.1 us
    ppermute x3, waiting for transfers between devices: 0.01 us -> 11.5 us  [gather_weights(): lax.ppermute(mine, 'frame', partner_permutation(frames, k))]
    ppermute x2, waiting for transfers between devices: 13.8 us -> 2.95 us  [sum_over(): value = value + lax.ppermute(value, axis, partner_permutation(size, bit))]
    ppermute x6 -> x3, waiting for transfers between devices: 8.88 us -> 14.6 us  [per_device(): arrived[k] = lax.ppermute(blocks, 'frame', partner_permutation(frames, k))]
    ppermute x6 -> x3, starting transfers between devices: 8.9 us -> 5.71 us  [per_device(): arrived[k] = lax.ppermute(blocks, 'frame', partner_permutation(frames, k))]
    ppermute x3, waiting for transfers between devices: 3.1 us -> 0.01 us  [gather_maps(): maps[k | bit] = lax.ppermute(maps[k], axis, partner_permutation(size, bit))]
    unnamed x12 -> x20, local copies, waits for them, and re-layouts: 2.74 us -> 0.99 us
    ppermute x2, starting transfers between devices: 4.74 us -> 6.1 us  [sum_over(): value = value + lax.ppermute(value, axis, partner_permutation(size, bit))]
    concatenate x1, other arithmetic: 1.19 us -> 0.12 us  [per_device(): jnp.concatenate([epi_in, epi_out[None], temp_in, temp_out[None]], axis=0)]
  transfers between devices with their start and end apart: 17 -> 14, of which waited for: 6 -> 8; matrix products, arithmetic and copies ran while one was open for 3% -> 1% of each run, Pallas kernels for 7% -> 10%
where the time goes in v3:
time: 66.6 us; the launch traced here: 66.4 us
  waiting for transfers between devices  29.6 us (44%)
  starting transfers between devices  19.2 us (29%)
  Pallas kernels  15.1 us (23%)
  local copies, waits for them, and re-layouts  1.39 us (2%)
  between operations  0.85 us (1%)
    ppermute x3, waiting for transfers between devices, per_device(): arrived[k] = lax.ppermute(blocks, 'frame', partner_permutation(frames, k))  14.6 us
    ppermute x3, waiting for transfers between devices, gather_weights(): lax.ppermute(mine, 'frame', partner_permutation(frames, k))  11.5 us
    ppermute x2, starting transfers between devices, sum_over(): value = value + lax.ppermute(value, axis, partner_permutation(size, bit))  6.1 us
    pallas_call x1, Pallas kernels, per_device(): pl.pallas_call(functools.partial(view_kernel, videos, tiles), out_shape=[...  6.08 us
    ppermute x3, starting transfers between devices, per_device(): arrived[k] = lax.ppermute(blocks, 'frame', partner_permutation(frames, k))  5.71 us
    ppermute x3, starting transfers between devices, gather_weights(): lax.ppermute(mine, 'frame', partner_permutation(frames, k))  4.57 us
    ppermute x2, waiting for transfers between devices, sum_over(): value = value + lax.ppermute(value, axis, partner_permutation(size, bit))  2.95 us
    ppermute x3, starting transfers between devices, gather_maps(): maps[k | bit] = lax.ppermute(maps[k], axis, partner_permutation(size, bit))  2.28 us
  transfers between devices with their start and end apart: 14, of which 8 were waited for; matrix products, arithmetic and copies ran while one was open for 1% of the time, Pallas kernels for 10%

profile of v3, /device:TPU:0, one launch (start us, length us, event | category | flops | bytes accessed | tf_op | source)
XLA Modules:
  0.0 66.4 jit_solution(16449183791350561531)
XLA Ops:
  0.8 0.9 %copy-done.4 = bf16[320,320]{1,0:T(8,128)(2,1)S(1)} copy-done((bf16[320,320]{1,0:T(8,128)(2,1)S(1)}, bf16[320,320]{1,0:T(8,128)(2,1)}, u32[]{:S(2)}) %copy-start.4) | copy-done | bytes 204824
  1.9 3.1 %collective-permute-start = (f32[1,320]{1,0:T(1,128)S(1)}, f32[1,320]{1,0:T(1,128)S(1)}, u32[]{:S(2)}, u32[]{:S(2)}) collective-permute-start(f32[1,320]{1,0:T(1,128)S(1)} %time_share.1), channel_id=1, source_target_pairs={{0,1},{1,0},{2,3},{3,2},{4,5},{5,4},{6,7},{7,6},{8,9},{9,8},{10,11... | collective-permute-start | bytes 3848 | tf_op jit(solution)/shard_map/ppermute | solution.py:254
  4.9 1.6 %collective-permute-done = f32[1,320]{1,0:T(1,128)S(1)} collective-permute-done((f32[1,320]{1,0:T(1,128)S(1)}, f32[1,320]{1,0:T(1,128)S(1)}, u32[]{:S(2)}, u32[]{:S(2)}) %collective-permute-start) | collective-permute-done | bytes 1312 | tf_op jit(solution)/shard_map/ppermute | solution.py:254
  6.5 3.0 %collective-permute-start.1 = (f32[1,320]{1,0:T(1,128)S(1)}, f32[1,320]{1,0:T(1,128)S(1)}, u32[]{:S(2)}, u32[]{:S(2)}) collective-permute-start(f32[1,320]{1,0:T(1,128)S(1)} %add.58), channel_id=1, source_target_pairs={{0,2},{1,3},{2,0},{3,1},{4,6},{5,7},{6,4},{7,5},{8,10},{9,11},{10,... | collective-permute-start | bytes 3848 | tf_op jit(solution)/shard_map/ppermute | solution.py:254
  9.7 1.4 %collective-permute-done.1 = f32[1,320]{1,0:T(1,128)S(1)} collective-permute-done((f32[1,320]{1,0:T(1,128)S(1)}, f32[1,320]{1,0:T(1,128)S(1)}, u32[]{:S(2)}, u32[]{:S(2)}) %collective-permute-start.1) | collective-permute-done | bytes 1312 | tf_op jit(solution)/shard_map/ppermute | solution.py:254
  11.1 2.0 %collective-permute-start.2 = (bf16[4,80,320]{2,1,0:T(8,128)(2,1)S(1)}, bf16[4,80,320]{2,1,0:T(8,128)(2,1)S(1)}, u32[]{:S(2)}, u32[]{:S(2)}) collective-permute-start(bf16[4,80,320]{2,1,0:T(8,128)(2,1)S(1)} %bitcast.25), channel_id=1, source_target_pairs={{0,1},{1,0},{2,3},{3,2},{4,5},{5,4},{6,7},{7,6},{8,9},{9,8},{10,11... | collective-permute-start | bytes 614408 | tf_op jit(solution)/shard_map/ppermute | solution.py:268
  13.1 2.6 %collective-permute-start.3 = (bf16[4,80,320]{2,1,0:T(8,128)(2,1)S(1)}, bf16[4,80,320]{2,1,0:T(8,128)(2,1)S(1)}, u32[]{:S(2)}, u32[]{:S(2)}) collective-permute-start(bf16[4,80,320]{2,1,0:T(8,128)(2,1)S(1)} %bitcast.26), channel_id=1, source_target_pairs={{0,2},{1,3},{2,0},{3,1},{4,6},{5,7},{6,4},{7,5},{8,10},{9,11},{10,... | collective-permute-start | bytes 614408 | tf_op jit(solution)/shard_map/ppermute | solution.py:268
  15.7 1.6 %first_conv.1.inner = f32[256,320]{1,0:T(8,128)S(1)} custom-call(bf16[320,256]{1,0:T(8,128)(2,1)S(1)} %bitcast.23, bf16[3,960,320]{2,1,0:T(8,128)(2,1)S(1)} %bitcast.21), custom_call_target="tpu_custom_call" | custom-call | flops 471859200 | bytes 2498560 | tf_op jit(solution)/shard_map/first_conv/pallas_call | solution.py:325
  17.4 1.7 %second_conv.1 = (bf16[256,320]{1,0:T(8,128)(2,1)S(1)}, bf16[256,320]{1,0:T(8,128)(2,1)S(1)}) custom-call(bf16[320,256]{1,0:T(8,128)(2,1)S(1)} %bitcast.24, f32[256,320]{1,0:T(8,128)S(1)} %first_conv.1.inner, f32[1,320]{1,0:T(1,128)S(1)} %add.59.bias, bf16[3,960,320]{2,1,0:T(8,128)(2,1)S(1)} %bitcast.22), custom_call_target="tpu_custom_call" | custom-call | flops 471859200 | bytes 2498560 | tf_op jit(solution)/shard_map/second_conv/pallas_call | solution.py:342
  19.1 1.8 %collective-permute-start.9 = (bf16[256,320]{1,0:T(8,128)(2,1)S(1)}, bf16[256,320]{1,0:T(8,128)(2,1)S(1)}, u32[]{:S(2)}, u32[]{:S(2)}) collective-permute-start(bf16[256,320]{1,0:T(8,128)(2,1)S(1)} %get-tuple-element.27.normed.refs_5_), channel_id=1, source_target_pairs={{0,8},{4,12},{8,0},{12,4},{1,9},{5,13},{9,1},{13,5},{2,10},{6,14},... | collective-permute-start | bytes 491528 | tf_op jit(solution)/shard_map/ppermute | solution.py:241
  20.9 11.5 %collective-permute-done.3.refs_1_ = bf16[4,80,320]{2,1,0:T(8,128)(2,1)S(1)} collective-permute-done((bf16[4,80,320]{2,1,0:T(8,128)(2,1)S(1)}, bf16[4,80,320]{2,1,0:T(8,128)(2,1)S(1)}, u32[]{:S(2)}, u32[]{:S(2)}) %collective-permute-start.3) | collective-permute-done | bytes 204832 | tf_op jit(solution)/shard_map/ppermute | solution.py:268
  32.3 0.5 collective-permute-start.7
  32.9 0.5 collective-permute-start.10
  34.5 1.5 %query.1 = (f32[320,256]{1,0:T(8,128)S(1)}, bf16[4,320,320]{2,1,0:T(8,128)(2,1)S(1)}, bf16[4,320,320]{2,1,0:T(8,128)(2,1)S(1)}) custom-call(s32[5]{0:T(128)S(1)} %concatenate.7.where, bf16[256,320]{1,0:T(8,128)(2,1)S(1)} %get-tuple-element.27.normed.refs_5_, bf16[8,80,320]{2,1,0:T(8,128)(2,1)S(1)} %pad_maximum_fusion.own, ...), custom_call_target="tpu_custom_call" | custom-call | tf_op jit(solution)/shard_map/query/pallas_call | solution.py:361
  36.0 6.1 %cross_view.1 = (bf16[256,320]{1,0:T(8,128)(2,1)S(1)}, bf16[256,320]{1,0:T(8,128)(2,1)S(1)}) custom-call(s32[2]{0:T(128)S(1)} %xor_reduce_fusion.refs_0_, s32[8]{0:T(128)S(1)} %reshape.94.refs_1_, bf16[256,320]{1,0:T(8,128)(2,1)S(1)} %get-tuple-element.26.refs_2_, f32[320,256]{1,0:T(8,128)S(1)} %get-tuple-element.29.refs_3_, ...), custom_call_target="tpu_custom_call" | custom-call | tf_op jit(solution)/shard_map/cross_view/pallas_call | solution.py:373
  42.1 3.2 %collective-permute-start.12 = (bf16[256,320]{1,0:T(8,128)(2,1)S(1)}, bf16[256,320]{1,0:T(8,128)(2,1)S(1)}, u32[]{:S(2)}, u32[]{:S(2)}) collective-permute-start(bf16[256,320]{1,0:T(8,128)(2,1)S(1)} %get-tuple-element.32.rows), channel_id=1, source_target_pairs={{0,1},{1,0},{2,3},{3,2},{4,5},{5,4},{6,7},{7,6},{8,9},{9,8},{10,11... | collective-permute-start | bytes 491528 | tf_op jit(solution)/shard_map/ppermute | solution.py:388
  45.3 2.5 %collective-permute-start.13 = (bf16[256,320]{1,0:T(8,128)(2,1)S(1)}, bf16[256,320]{1,0:T(8,128)(2,1)S(1)}, u32[]{:S(2)}, u32[]{:S(2)}) collective-permute-start(bf16[256,320]{1,0:T(8,128)(2,1)S(1)} %get-tuple-element.32.rows), channel_id=1, source_target_pairs={{0,3},{1,2},{2,1},{3,0},{4,7},{5,6},{6,5},{7,4},{8,11},{9,10},{10,... | collective-permute-start | bytes 491528 | tf_op jit(solution)/shard_map/ppermute | solution.py:388
  47.8 0.8 %own_frame.1 = (bf16[256,320]{1,0:T(8,128)(2,1)S(1)}, f32[256,320]{1,0:T(8,128)S(1)}, bf16[256,320]{1,0:T(8,128)(2,1)S(1)}) custom-call(bf16[256,320]{1,0:T(8,128)(2,1)S(1)} %get-tuple-element.32.rows, bf16[4,320,320]{2,1,0:T(8,128)(2,1)S(1)} %get-tuple-element.33.weights.refs_3_), custom_call_target="tpu_custom_call" | custom-call | flops 209715200 | bytes 1474560 | tf_op jit(solution)/shard_map/own_frame/pallas_call | solution.py:396
  48.6 2.0 %collective-permute-done.12.rows = bf16[256,320]{1,0:T(8,128)(2,1)S(1)} collective-permute-done((bf16[256,320]{1,0:T(8,128)(2,1)S(1)}, bf16[256,320]{1,0:T(8,128)(2,1)S(1)}, u32[]{:S(2)}, u32[]{:S(2)}) %collective-permute-start.12) | collective-permute-done | bytes 163872 | tf_op jit(solution)/shard_map/ppermute | solution.py:388
  50.6 0.6 other_frame.2
  51.2 6.6 %collective-permute-done.13.rows = bf16[256,320]{1,0:T(8,128)(2,1)S(1)} collective-permute-done((bf16[256,320]{1,0:T(8,128)(2,1)S(1)}, bf16[256,320]{1,0:T(8,128)(2,1)S(1)}, u32[]{:S(2)}, u32[]{:S(2)}) %collective-permute-start.13) | collective-permute-done | bytes 163872 | tf_op jit(solution)/shard_map/ppermute | solution.py:388
  57.8 0.6 other_frame.3
  58.5 5.9 %collective-permute-done.11.refs_2_ = bf16[256,320]{1,0:T(8,128)(2,1)S(1)} collective-permute-done((bf16[256,320]{1,0:T(8,128)(2,1)S(1)}, bf16[256,320]{1,0:T(8,128)(2,1)S(1)}, u32[]{:S(2)}, u32[]{:S(2)}) %collective-permute-start.11) | collective-permute-done | bytes 163872 | tf_op jit(solution)/shard_map/ppermute | solution.py:388
  64.4 2.0 %last.1 = bf16[320,256]{1,0:T(8,128)(2,1)} custom-call(bf16[256,320]{1,0:T(8,128)(2,1)S(1)} %get-tuple-element.31.refs_0_, bf16[256,320]{1,0:T(8,128)(2,1)S(1)} %get-tuple-element.34.queries.refs_1_, bf16[256,320]{1,0:T(8,128)(2,1)S(1)} %collective-permute-done.11.refs_2_, bf16[4,320,320]{2,1,0:T(8,128)(2,1)S(1)} %get-tuple-element.33.weights.refs_3_, ...), custom_call_target="tpu_custom_call" | custom-call | tf_op jit(solution)/shard_map/last/pallas_call | solution.py:419
  (42 shorter events, 1.6 us)
Async XLA Ops:
  0.0 33.4 %copy-start = (s32[2,4,2,2]{1,3,2,0:T(2,128)S(1)}, s32[2,4,2,2]{1,3,2,0:T(2,128)}, u32[]{:S(2)}) copy-start(s32[2,4,2,2]{1,3,2,0:T(2,128)} %param.14) | copy-start | bytes 388
  0.8 1.0 %copy-start.4 = (bf16[320,320]{1,0:T(8,128)(2,1)S(1)}, bf16[320,320]{1,0:T(8,128)(2,1)}, u32[]{:S(2)}) copy-start(bf16[320,320]{1,0:T(8,128)(2,1)} %proj.1) | copy-start | bytes 614404
  1.7 7.8 %copy-start.5 = (bf16[3,80,320]{2,1,0:T(8,128)(2,1)S(1)}, bf16[3,80,320]{2,1,0:T(8,128)(2,1)}, u32[]{:S(2)}) copy-start(bf16[3,80,320]{2,1,0:T(8,128)(2,1)} %param.20) | copy-start | bytes 460804
  1.7 7.8 %copy-start.6 = (bf16[3,80,320]{2,1,0:T(8,128)(2,1)S(1)}, bf16[3,80,320]{2,1,0:T(8,128)(2,1)}, u32[]{:S(2)}) copy-start(bf16[3,80,320]{2,1,0:T(8,128)(2,1)} %param.18) | copy-start | bytes 460804
  1.7 7.8 %copy-start.7 = (bf16[80,320]{1,0:T(8,128)(2,1)S(1)}, bf16[80,320]{1,0:T(8,128)(2,1)}, u32[]{:S(2)}) copy-start(bf16[80,320]{1,0:T(8,128)(2,1)} %param.21) | copy-start | bytes 153604
  1.7 7.8 %copy-start.8 = (bf16[80,320]{1,0:T(8,128)(2,1)S(1)}, bf16[80,320]{1,0:T(8,128)(2,1)}, u32[]{:S(2)}) copy-start(bf16[80,320]{1,0:T(8,128)(2,1)} %param.19) | copy-start | bytes 153604
  1.7 14.0 %copy-start.1 = (bf16[3,3,320,320]{3,2,1,0:T(8,128)(2,1)S(1)}, bf16[3,3,320,320]{3,2,1,0:T(8,128)(2,1)}, u32[]{:S(2)}) copy-start(bf16[3,3,320,320]{3,2,1,0:T(8,128)(2,1)} %param.15) | copy-start | bytes 5529604
  1.7 14.0 %copy-start.3 = (bf16[1,1,256,320]{2,3,1,0:T(8,128)(2,1)S(1)}, bf16[1,1,256,320]{2,3,1,0:T(8,128)(2,1)}, u32[]{:S(2)}) copy-start(bf16[1,1,256,320]{2,3,1,0:T(8,128)(2,1)} %param.11) | copy-start | bytes 491524
  1.9 4.6 %collective-permute-start = (f32[1,320]{1,0:T(1,128)S(1)}, f32[1,320]{1,0:T(1,128)S(1)}, u32[]{:S(2)}, u32[]{:S(2)}) collective-permute-start(f32[1,320]{1,0:T(1,128)S(1)} %time_share.1), channel_id=1, source_target_pairs={{0,1},{1,0},{2,3},{3,2},{4,5},{5,4},{6,7},{7,6},{8,9},{9,8},{10,11... | collective-permute-start | bytes 3848 | tf_op jit(solution)/shard_map/ppermute | solution.py:254
  6.5 4.6 %collective-permute-start.1 = (f32[1,320]{1,0:T(1,128)S(1)}, f32[1,320]{1,0:T(1,128)S(1)}, u32[]{:S(2)}, u32[]{:S(2)}) collective-permute-start(f32[1,320]{1,0:T(1,128)S(1)} %add.58), channel_id=1, source_target_pairs={{0,2},{1,3},{2,0},{3,1},{4,6},{5,7},{6,4},{7,5},{8,10},{9,11},{10,... | collective-permute-start | bytes 3848 | tf_op jit(solution)/shard_map/ppermute | solution.py:254
  9.7 7.7 %copy-start.2 = (bf16[3,3,320,320]{3,2,1,0:T(8,128)(2,1)S(1)}, bf16[3,3,320,320]{3,2,1,0:T(8,128)(2,1)}, u32[]{:S(2)}) copy-start(bf16[3,3,320,320]{3,2,1,0:T(8,128)(2,1)} %param.16) | copy-start | bytes 5529604
  11.1 9.7 %collective-permute-start.2 = (bf16[4,80,320]{2,1,0:T(8,128)(2,1)S(1)}, bf16[4,80,320]{2,1,0:T(8,128)(2,1)S(1)}, u32[]{:S(2)}, u32[]{:S(2)}) collective-permute-start(bf16[4,80,320]{2,1,0:T(8,128)(2,1)S(1)} %bitcast.25), channel_id=1, source_target_pairs={{0,1},{1,0},{2,3},{3,2},{4,5},{5,4},{6,7},{7,6},{8,9},{9,8},{10,11... | collective-permute-start | bytes 614408 | tf_op jit(solution)/shard_map/ppermute | solution.py:268
  13.1 19.2 %collective-permute-start.3 = (bf16[4,80,320]{2,1,0:T(8,128)(2,1)S(1)}, bf16[4,80,320]{2,1,0:T(8,128)(2,1)S(1)}, u32[]{:S(2)}, u32[]{:S(2)}) collective-permute-start(bf16[4,80,320]{2,1,0:T(8,128)(2,1)S(1)} %bitcast.26), channel_id=1, source_target_pairs={{0,2},{1,3},{2,0},{3,1},{4,6},{5,7},{6,4},{7,5},{8,10},{9,11},{10,... | collective-permute-start | bytes 614408 | tf_op jit(solution)/shard_map/ppermute | solution.py:268
  15.7 16.6 %collective-permute-start.4 = (bf16[4,80,320]{2,1,0:T(8,128)(2,1)S(1)}, bf16[4,80,320]{2,1,0:T(8,128)(2,1)}, u32[]{:S(2)}, u32[]{:S(2)}) collective-permute-start(bf16[4,80,320]{2,1,0:T(8,128)(2,1)S(1)} %bitcast.27), channel_id=1, source_target_pairs={{0,3},{1,2},{2,1},{3,0},{4,7},{5,6},{6,5},{7,4},{8,11},{9,10},{10,... | collective-permute-start | bytes 614408 | tf_op jit(solution)/shard_map/ppermute | solution.py:268
  15.7 18.0 %copy-start.9 = (s32[2,4]{1,0:T(2,128)S(1)}, s32[2,4]{1,0:T(2,128)}, u32[]{:S(2)}) copy-start(s32[2,4]{1,0:T(2,128)} %param.13) | copy-start | bytes 100
  19.1 13.8 %collective-permute-start.9 = (bf16[256,320]{1,0:T(8,128)(2,1)S(1)}, bf16[256,320]{1,0:T(8,128)(2,1)S(1)}, u32[]{:S(2)}, u32[]{:S(2)}) collective-permute-start(bf16[256,320]{1,0:T(8,128)(2,1)S(1)} %get-tuple-element.27.normed.refs_5_), channel_id=1, source_target_pairs={{0,8},{4,12},{8,0},{12,4},{1,9},{5,13},{9,1},{13,5},{2,10},{6,14},... | collective-permute-start | bytes 491528 | tf_op jit(solution)/shard_map/ppermute | solution.py:241
  20.9 13.1 %collective-permute-start.5 = (bf16[4,80,320]{2,1,0:T(8,128)(2,1)S(1)}, bf16[4,80,320]{2,1,0:T(8,128)(2,1)S(1)}, u32[]{:S(2)}, u32[]{:S(2)}) collective-permute-start(bf16[4,80,320]{2,1,0:T(8,128)(2,1)S(1)} %collective-permute-done.2.refs_0_), channel_id=1, source_target_pairs={{0,4},{4,0},{8,12},{12,8},{1,5},{5,1},{9,13},{13,9},{2,6},{6,2},{1... | collective-permute-start | bytes 614408 | tf_op jit(solution)/shard_map/ppermute | solution.py:270
  32.3 1.8 %collective-permute-start.6 = (bf16[4,80,320]{2,1,0:T(8,128)(2,1)S(1)}, bf16[4,80,320]{2,1,0:T(8,128)(2,1)S(1)}, u32[]{:S(2)}, u32[]{:S(2)}) collective-permute-start(bf16[4,80,320]{2,1,0:T(8,128)(2,1)S(1)} %collective-permute-done.3.refs_1_), channel_id=1, source_target_pairs={{0,4},{4,0},{8,12},{12,8},{1,5},{5,1},{9,13},{13,9},{2,6},{6,2},{1... | collective-permute-start | bytes 614408 | tf_op jit(solution)/shard_map/ppermute | solution.py:270
  32.3 2.2 %collective-permute-start.7 = (bf16[4,80,320]{2,1,0:T(8,128)(2,1)}, bf16[4,80,320]{2,1,0:T(8,128)(2,1)S(1)}, u32[]{:S(2)}, u32[]{:S(2)}) collective-permute-start(bf16[4,80,320]{2,1,0:T(8,128)(2,1)} %collective-permute-done.4.refs_2_), channel_id=1, source_target_pairs={{0,4},{4,0},{8,12},{12,8},{1,5},{5,1},{9,13},{13,9},{2,6},{6,2},{1... | collective-permute-start | bytes 614408 | tf_op jit(solution)/shard_map/ppermute | solution.py:270
  32.8 3.1 %collective-permute-start.8 = (bf16[256,320]{1,0:T(8,128)(2,1)S(1)}, bf16[256,320]{1,0:T(8,128)(2,1)S(1)}, u32[]{:S(2)}, u32[]{:S(2)}) collective-permute-start(bf16[256,320]{1,0:T(8,128)(2,1)S(1)} %get-tuple-element.27.normed.refs_5_), channel_id=1, source_target_pairs={{0,4},{4,0},{8,12},{12,8},{1,5},{5,1},{9,13},{13,9},{2,6},{6,2},{1... | collective-permute-start | bytes 491528 | tf_op jit(solution)/shard_map/ppermute | solution.py:241
  32.9 3.1 %collective-permute-start.10 = (bf16[256,320]{1,0:T(8,128)(2,1)S(1)}, bf16[256,320]{1,0:T(8,128)(2,1)S(1)}, u32[]{:S(2)}, u32[]{:S(2)}) collective-permute-start(bf16[256,320]{1,0:T(8,128)(2,1)S(1)} %collective-permute-done.9.refs_7_), channel_id=1, source_target_pairs={{0,4},{4,0},{8,12},{12,8},{1,5},{5,1},{9,13},{13,9},{2,6},{6,2},{1... | collective-permute-start | bytes 491528 | tf_op jit(solution)/shard_map/ppermute | solution.py:241
  42.1 8.5 %collective-permute-start.12 = (bf16[256,320]{1,0:T(8,128)(2,1)S(1)}, bf16[256,320]{1,0:T(8,128)(2,1)S(1)}, u32[]{:S(2)}, u32[]{:S(2)}) collective-permute-start(bf16[256,320]{1,0:T(8,128)(2,1)S(1)} %get-tuple-element.32.rows), channel_id=1, source_target_pairs={{0,1},{1,0},{2,3},{3,2},{4,5},{5,4},{6,7},{7,6},{8,9},{9,8},{10,11... | collective-permute-start | bytes 491528 | tf_op jit(solution)/shard_map/ppermute | solution.py:388
  45.3 12.5 %collective-permute-start.13 = (bf16[256,320]{1,0:T(8,128)(2,1)S(1)}, bf16[256,320]{1,0:T(8,128)(2,1)S(1)}, u32[]{:S(2)}, u32[]{:S(2)}) collective-permute-start(bf16[256,320]{1,0:T(8,128)(2,1)S(1)} %get-tuple-element.32.rows), channel_id=1, source_target_pairs={{0,3},{1,2},{2,1},{3,0},{4,7},{5,6},{6,5},{7,4},{8,11},{9,10},{10,... | collective-permute-start | bytes 491528 | tf_op jit(solution)/shard_map/ppermute | solution.py:388
  47.8 16.6 %collective-permute-start.11 = (bf16[256,320]{1,0:T(8,128)(2,1)S(1)}, bf16[256,320]{1,0:T(8,128)(2,1)S(1)}, u32[]{:S(2)}, u32[]{:S(2)}) collective-permute-start(bf16[256,320]{1,0:T(8,128)(2,1)S(1)} %get-tuple-element.32.rows), channel_id=1, source_target_pairs={{0,2},{1,3},{2,0},{3,1},{4,6},{5,7},{6,4},{7,5},{8,10},{9,11},{10,... | collective-permute-start | bytes 491528 | tf_op jit(solution)/shard_map/ppermute | solution.py:388

commit v4 on v3

--- a/solution.py
+++ b/solution.py
@@ -104,24 +104,23 @@
     normed[...] = layer_norm(rounded.astype(f32)).astype(bf16)
 
 
-def assemble(where, own, received, swapped, whole, first, kinds):
+def assemble(where, parts, whole):
+    own, count = parts[0], len(parts) // 2
     rows = own.shape[1]
-    start = 0 if first == 0 else 2
-    for kind in range(kinds):
-        whole[kind, pl.ds(pl.multiple_of(where[0] * rows, 16), rows), :] = own[first + kind]
-    for k in range(1, len(received) + 1):
+    for kind in range(4):
+        whole[kind, pl.ds(pl.multiple_of(where[0] * rows, 16), rows), :] = own[kind]
+    for k in range(1, count + 1):
         place = pl.ds(pl.multiple_of(where[k] * rows, 16), rows)
         for j in range(2):
-            mine = where[len(received) + 1] * 2 + j
-            whole[mine, place, :] = received[k - 1][start + j]
-            whole[2 - mine + 2 * j, place, :] = swapped[k - 1][start + j]
-
-
-def query_kernel(count, where, normed, own, *refs):
-    received, swapped = refs[:count], refs[count : 2 * count]
-    queries, epi, temp = refs[2 * count :]
-    assemble(where, own, received, swapped, epi, 0, 4)
-    assemble(where, own, received, swapped, temp, 4, 4)
+            mine = where[count + 1] * 2 + j
+            whole[mine, place, :] = parts[k][j]
+            whole[2 - mine + 2 * j, place, :] = parts[count + k][j]
+
+
+def query_kernel(where, normed, *refs):
+    parts = refs[:-2]
+    queries, epi = refs[-2:]
+    assemble(where, parts, epi)
     queries[...] = dot(normed[...], epi[0]).astype(bf16).astype(f32).T
 
 
@@ -190,7 +189,10 @@
     return (dot(high, ones) + dot(low, ones)) * (LOG2E / math.sqrt(head)), values
 
 
-def own_frame_kernel(rows, weights, queries, scores, values):
+def own_frame_kernel(where, rows, *refs):
+    parts = refs[:-4]
+    weights, queries, scores, values = refs[-4:]
+    assemble(where, parts, weights)
     queries[...] = dot(rows[...], weights[0]).astype(bf16)
     scores[...], values[...] = frame_part(queries[...].astype(f32), rows[...], weights)
 
@@ -259,16 +261,36 @@
     return value, beside, later
 
 
+def ring_gather(own, axis, size):
+    pieces = {0: own}
+    right = [(i, (i + 1) % size) for i in range(size)]
+    left = [(j, i) for i, j in right]
+    for step in range(1, size // 2 + 1):
+        pieces[step] = lax.ppermute(pieces[step - 1], axis, right)
+        if size - step > step:
+            pieces[size - step] = lax.ppermute(pieces[(size - step + 1) % size], axis, left)
+    return [pieces[k] for k in range(size)]
+
+
+def neighbours(pieces):
+    return [pieces[1], pieces[-1]] if len(pieces) > 2 else pieces[1:]
+
+
+def with_neighbours(pieces, near):
+    pieces = list(pieces)
+    if near:
+        pieces[1], pieces[-1] = near[0], near[-1]
+    return pieces
+
+
 def gather_weights(parts, frames, videos, video):
     kinds, rows, channels = parts.shape
-    halves = parts.reshape(2, 2, 2, rows, channels)
-    mine = lax.dynamic_index_in_dim(halves, video % 2, 1, keepdims=False)
-    mine = mine.reshape(4, rows, channels)
-    received = [
-        lax.ppermute(mine, "frame", partner_permutation(frames, k)) for k in range(1, frames)
-    ]
-    swapped = [lax.ppermute(part, "video", partner_permutation(videos, 1)) for part in received]
-    return received, swapped
+    mine = lax.dynamic_index_in_dim(parts.reshape(2, 2, rows, channels), video % 2, 0, keepdims=False)
+    return [parts] + ring_gather(mine, "frame", frames)[1:]
+
+
+def swap_weights(parts, videos):
+    return parts + [lax.ppermute(part, "video", partner_permutation(videos, 1)) for part in parts[1:]]
 
 
 def per_device(
@@ -292,7 +314,6 @@
     video = lax.axis_index("video")
     pixels = tokens // frames
     source = latents.reshape(tokens, channels).T
-    where = jnp.stack([partner(frame, frames, k) for k in range(frames)]).astype(jnp.int32)
 
     rows = time_proj.shape[0]
     half = rows * frames // 2
@@ -311,8 +332,19 @@
         cost_estimate=pl.CostEstimate(flops=10**10, bytes_accessed=1 << 20, transcendentals=0),
         name="time_share",
     )(time_act, time_proj)
-    parts = jnp.concatenate([epi_in, epi_out[None], temp_in, temp_out[None]], axis=0)
-    bias, source, parts = sum_over(share, source, parts, "frame", frames)
+    epi_own = jnp.concatenate([epi_in, epi_out[None]], axis=0)
+    temp_own = jnp.concatenate([temp_in, temp_out[None]], axis=0)
+    bias, source, epi_own = sum_over(share, source, epi_own, "frame", frames)
+    paired = videos % 2 == 0 and is_power(videos) and epi_own.shape[1] % 16 == 0
+    if paired:
+        places = [(frame - k) % frames for k in range(frames)] + [video % 2]
+    else:
+        places = [jnp.int32(0)] * 2
+    places = jnp.stack(places).astype(jnp.int32)
+    if paired:
+        epi_parts = gather_weights(epi_own, frames, videos, video)
+    else:
+        epi_parts = [lax.all_gather(epi_own, "frame", axis=1, tiled=True)]
 
     conv_scratch = [
         pltpu.VMEM((tokens + 2 * W, 3 * channels), bf16),
@@ -332,13 +364,6 @@
         cost_estimate=conv_cost,
         name="first_conv",
     )(source, conv_first.reshape(3, 3 * channels, channels))
-    if is_power(frames) and videos % 2 == 0 and is_power(videos) and parts.shape[1] % 16 == 0:
-        received, swapped = gather_weights(parts, frames, videos, video)
-        places = jnp.concatenate([where, (video % 2).astype(jnp.int32)[None]])
-    else:
-        parts = lax.all_gather(parts, "frame", axis=1, tiled=True)
-        received, swapped = [], []
-        places = jnp.zeros((2,), jnp.int32)
     hidden, normed = pl.pallas_call(
         second_kernel,
         out_shape=[jax.ShapeDtypeStruct((tokens, channels), bf16)] * 2,
@@ -350,7 +375,16 @@
         name="second_conv",
     )(source, inner, bias, conv_second.reshape(3, 3 * channels, channels))
 
+    if paired:
+        normed, hidden, *near = lax.optimization_barrier((normed, hidden, *neighbours(epi_parts)))
+        epi_parts = with_neighbours(epi_parts, near)
     maps = gather_maps(normed, "video", videos)
+    if paired:
+        temp_own, maps[1] = lax.optimization_barrier((temp_own, maps[1]))
+        temp_parts = gather_weights(temp_own, frames, videos, video)
+        epi_parts = swap_weights(epi_parts, videos)
+    else:
+        temp_parts = [lax.all_gather(temp_own, "frame", axis=1, tiled=True)]
     targets = lax.dynamic_index_in_dim(matchings, video, 1, keepdims=False)
     if is_power(videos):
         select = video ^ targets
@@ -358,18 +392,20 @@
         select = (video - targets) % videos
     mask = lax.dynamic_index_in_dim(tile_mask, video, 1, keepdims=False).reshape(-1)
     square = (4, channels, channels)
-    queries, epi, temp = pl.pallas_call(
-        functools.partial(query_kernel, len(received)),
+    queries, epi = pl.pallas_call(
+        query_kernel,
         out_shape=[
             jax.ShapeDtypeStruct((channels, tokens), f32),
             jax.ShapeDtypeStruct(square, bf16),
-            jax.ShapeDtypeStruct(square, bf16),
         ],
-        in_specs=[SMEM, VMEM, VMEM] + [VMEM] * (2 * len(received)),
-        out_specs=[VMEM] * 3,
+        in_specs=[SMEM, VMEM] + [VMEM] * len(epi_parts),
+        out_specs=[VMEM] * 2,
         compiler_params=params(),
         name="query",
-    )(places, normed, parts, *received, *swapped)
+    )(places, normed, *epi_parts)
+    if paired:
+        queries, *near = lax.optimization_barrier((queries, *neighbours(temp_parts)))
+        temp_parts = with_neighbours(temp_parts, near)
     second, blocks = pl.pallas_call(
         functools.partial(view_kernel, videos, tiles),
         out_shape=[jax.ShapeDtypeStruct((tokens, channels), bf16)] * 2,
@@ -383,9 +419,10 @@
         name="cross_view",
     )(select, mask, hidden, queries, epi, *maps)
 
-    arrived = {}
-    for k in reversed(range(1, frames)):
-        arrived[k] = lax.ppermute(blocks, "frame", partner_permutation(frames, k))
+    if paired:
+        blocks, *temp_parts = lax.optimization_barrier((blocks, *temp_parts))
+        temp_parts = swap_weights(temp_parts, videos)
+    arrived = ring_gather(blocks, "frame", frames)
     score_shape = jax.ShapeDtypeStruct((tokens, channels), f32)
     value_shape = jax.ShapeDtypeStruct((tokens, channels), bf16)
     frame_cost = pl.CostEstimate(
@@ -393,17 +430,17 @@
         bytes_accessed=8 * channels * channels + 8 * tokens * channels,
         transcendentals=0,
     )
-    frame_queries, *first = pl.pallas_call(
+    temp, frame_queries, *first = pl.pallas_call(
         own_frame_kernel,
-        out_shape=[value_shape, score_shape, value_shape],
-        in_specs=[VMEM] * 2,
-        out_specs=[VMEM] * 3,
+        out_shape=[jax.ShapeDtypeStruct(square, bf16), value_shape, score_shape, value_shape],
+        in_specs=[SMEM, VMEM] + [VMEM] * len(temp_parts),
+        out_specs=[VMEM] * 4,
         compiler_params=params(),
         cost_estimate=frame_cost,
         name="own_frame",
-    )(blocks, temp)
+    )(places, blocks, *temp_parts)
     scores, values = [first[0]], [first[1]]
-    order = [1] + list(range(frames - 1, 1, -1)) if frames > 1 else []
+    order = sorted(range(1, frames), key=lambda k: min(k, frames - k))
     for k in order[:-1]:
         one = pl.pallas_call(
             frame_kernel,

time: 66.6 us -> 61 us (0.916)
  waiting for transfers between devices: 29.6 us -> 21.1 us
  local copies, waits for them, and re-layouts: 1.39 us -> 3.58 us
    ppermute x9 -> x15, waiting for transfers between devices: 26.6 us -> 15.1 us  [the longest x6 12.3 us: ring_gather(): pieces[step] = lax.ppermute(pieces[step - 1], axis, right)]
    ppermute x3, waiting for transfers between devices: 0.01 us -> 2.98 us  [gather_maps(): maps[k | bit] = lax.ppermute(maps[k], axis, partner_permutation(size, bit))]
    unnamed x20 -> x24, local copies, waits for them, and re-layouts: 0.99 us -> 2.53 us
    ppermute x9 -> x15, starting transfers between devices: 10.8 us -> 12 us  [the longest x3 6.83 us: ring_gather(): lax.ppermute(pieces[(size - step + 1) % size], axis, left)]
    ppermute x3, starting transfers between devices: 2.28 us -> 1.5 us  [gather_maps(): maps[k | bit] = lax.ppermute(maps[k], axis, partner_permutation(size, bit))]
    squeeze x0 -> x2, local copies, waits for them, and re-layouts: none -> 0.67 us  [gather_weights(): lax.dynamic_index_in_dim(parts.reshape(2, 2, rows, channels), video % 2,...]
  transfers between devices with their start and end apart: 14 -> 20, of which waited for: 8 -> 12; matrix products, arithmetic and copies ran while one was open for 1% -> 2% of each run, Pallas kernels for 10% -> 22%
where the time goes in v4:
time: 61 us; the launch traced here: 60.8 us
  waiting for transfers between devices  21.1 us (35%)
  starting transfers between devices  19.6 us (32%)
  Pallas kernels  15.2 us (25%)
  local copies, waits for them, and re-layouts  3.58 us (6%)
  between operations  0.88 us (1%)
    ppermute x6, waiting for transfers between devices, ring_gather(): pieces[step] = lax.ppermute(pieces[step - 1], axis, right)  12.3 us
    ppermute x3, starting transfers between devices, ring_gather(): lax.ppermute(pieces[(size - step + 1) % size], axis, left)  6.83 us
    ppermute x2, starting transfers between devices, sum_over(): value = value + lax.ppermute(value, axis, partner_permutation(size, bit))  6.1 us
    pallas_call x1, Pallas kernels, per_device(): pl.pallas_call(functools.partial(view_kernel, videos, tiles), out_shape=[...  6.08 us
    ppermute x6, starting transfers between devices, ring_gather(): pieces[step] = lax.ppermute(pieces[step - 1], axis, right)  3.88 us
    ppermute x2, waiting for transfers between devices, sum_over(): value = value + lax.ppermute(value, axis, partner_permutation(size, bit))  3.03 us
    ppermute x3, waiting for transfers between devices, gather_maps(): maps[k | bit] = lax.ppermute(maps[k], axis, partner_permutation(size, bit))  2.98 us
    unnamed x24, local copies, waits for them, and re-layouts  2.53 us
  transfers between devices with their start and end apart: 20, of which 12 were waited for; matrix products, arithmetic and copies ran while one was open for 2% of the time, Pallas kernels for 22%

profile of v4, /device:TPU:0, one launch (start us, length us, event | category | flops | bytes accessed | tf_op | source)
XLA Modules:
  0.0 60.8 jit_solution(10372063511259220307)
XLA Ops:
  0.8 0.9 %copy-done.6 = bf16[320,320]{1,0:T(8,128)(2,1)S(1)} copy-done((bf16[320,320]{1,0:T(8,128)(2,1)S(1)}, bf16[320,320]{1,0:T(8,128)(2,1)}, u32[]{:S(2)}) %copy-start.6) | copy-done | bytes 204824
  1.8 3.1 %collective-permute-start = (f32[1,320]{1,0:T(1,128)S(1)}, f32[1,320]{1,0:T(1,128)S(1)}, u32[]{:S(2)}, u32[]{:S(2)}) collective-permute-start(f32[1,320]{1,0:T(1,128)S(1)} %time_share.1), channel_id=1, source_target_pairs={{0,1},{1,0},{2,3},{3,2},{4,5},{5,4},{6,7},{7,6},{8,9},{9,8},{10,11... | collective-permute-start | bytes 3848 | tf_op jit(solution)/shard_map/ppermute | solution.py:256
  4.9 1.6 %collective-permute-done = f32[1,320]{1,0:T(1,128)S(1)} collective-permute-done((f32[1,320]{1,0:T(1,128)S(1)}, f32[1,320]{1,0:T(1,128)S(1)}, u32[]{:S(2)}, u32[]{:S(2)}) %collective-permute-start) | collective-permute-done | bytes 1312 | tf_op jit(solution)/shard_map/ppermute | solution.py:256
  6.5 3.0 %collective-permute-start.1 = (f32[1,320]{1,0:T(1,128)S(1)}, f32[1,320]{1,0:T(1,128)S(1)}, u32[]{:S(2)}, u32[]{:S(2)}) collective-permute-start(f32[1,320]{1,0:T(1,128)S(1)} %add.75), channel_id=1, source_target_pairs={{0,2},{1,3},{2,0},{3,1},{4,6},{5,7},{6,4},{7,5},{8,10},{9,11},{10,... | collective-permute-start | bytes 3848 | tf_op jit(solution)/shard_map/ppermute | solution.py:256
  9.6 1.5 %collective-permute-done.1 = f32[1,320]{1,0:T(1,128)S(1)} collective-permute-done((f32[1,320]{1,0:T(1,128)S(1)}, f32[1,320]{1,0:T(1,128)S(1)}, u32[]{:S(2)}, u32[]{:S(2)}) %collective-permute-start.1) | collective-permute-done | bytes 1312 | tf_op jit(solution)/shard_map/ppermute | solution.py:256
  11.1 2.0 %collective-permute-start.2 = (bf16[2,80,320]{2,1,0:T(8,128)(2,1)S(1)}, bf16[2,80,320]{2,1,0:T(8,128)(2,1)S(1)}, u32[]{:S(2)}, u32[]{:S(2)}) collective-permute-start(bf16[2,80,320]{2,1,0:T(8,128)(2,1)S(1)} %dynamic-slice_bitcast_fusion.1), channel_id=1, source_target_pairs={{0,1},{1,2},{2,3},{3,0},{4,5},{5,6},{6,7},{7,4},{8,9},{9,10},{10,1... | collective-permute-start | bytes 307208 | tf_op jit(solution)/shard_map/ppermute | solution.py:269
  13.1 2.1 %collective-permute-start.3 = (bf16[2,80,320]{2,1,0:T(8,128)(2,1)S(1)}, bf16[2,80,320]{2,1,0:T(8,128)(2,1)S(1)}, u32[]{:S(2)}, u32[]{:S(2)}) collective-permute-start(bf16[2,80,320]{2,1,0:T(8,128)(2,1)S(1)} %dynamic-slice_bitcast_fusion.1), channel_id=1, source_target_pairs={{1,0},{2,1},{3,2},{0,3},{5,4},{6,5},{7,6},{4,7},{9,8},{10,9},{11,1... | collective-permute-start | bytes 307208 | tf_op jit(solution)/shard_map/ppermute | solution.py:271
  15.2 1.7 %first_conv.1.inner = f32[256,320]{1,0:T(8,128)S(1)} custom-call(bf16[320,256]{1,0:T(8,128)(2,1)S(1)} %bitcast.26, bf16[3,960,320]{2,1,0:T(8,128)(2,1)S(1)} %bitcast.22), custom_call_target="tpu_custom_call" | custom-call | flops 471859200 | bytes 2498560 | tf_op jit(solution)/shard_map/first_conv/pallas_call | solution.py:357
  16.8 1.7 %second_conv.1 = (bf16[256,320]{1,0:T(8,128)(2,1)S(1)}, bf16[256,320]{1,0:T(8,128)(2,1)S(1)}) custom-call(bf16[320,256]{1,0:T(8,128)(2,1)S(1)} %bitcast.27, f32[256,320]{1,0:T(8,128)S(1)} %first_conv.1.inner, f32[1,320]{1,0:T(1,128)S(1)} %add.76.bias, bf16[3,960,320]{2,1,0:T(8,128)(2,1)S(1)} %bitcast.23), custom_call_target="tpu_custom_call" | custom-call | flops 471859200 | bytes 2498560 | tf_op jit(solution)/shard_map/second_conv/pallas_call | solution.py:367
  19.3 1.5 %collective-permute-start.11 = (bf16[256,320]{1,0:T(8,128)(2,1)S(1)}, bf16[256,320]{1,0:T(8,128)(2,1)S(1)}, u32[]{:S(2)}, u32[]{:S(2)}) collective-permute-start(bf16[256,320]{1,0:T(8,128)(2,1)S(1)} %get-tuple-element.44.normed.refs_5_), channel_id=1, source_target_pairs={{0,8},{4,12},{8,0},{12,4},{1,9},{5,13},{9,1},{13,5},{2,10},{6,14},... | collective-permute-start | bytes 491528 | tf_op jit(solution)/shard_map/ppermute | solution.py:243
  22.5 1.1 %collective-permute-start.9 = (bf16[2,80,320]{2,1,0:T(8,128)(2,1)}, bf16[2,80,320]{2,1,0:T(8,128)(2,1)S(1)}, u32[]{:S(2)}, u32[]{:S(2)}) collective-permute-start(bf16[2,80,320]{2,1,0:T(8,128)(2,1)} %dynamic-slice_bitcast_fusion), channel_id=1, source_target_pairs={{0,1},{1,2},{2,3},{3,0},{4,5},{5,6},{6,7},{7,4},{8,9},{9,10},{10,1... | collective-permute-start | bytes 307208 | tf_op jit(solution)/shard_map/ppermute | solution.py:269
  23.6 3.0 %collective-permute-done.11.refs_7_ = bf16[256,320]{1,0:T(8,128)(2,1)S(1)} collective-permute-done((bf16[256,320]{1,0:T(8,128)(2,1)S(1)}, bf16[256,320]{1,0:T(8,128)(2,1)S(1)}, u32[]{:S(2)}, u32[]{:S(2)}) %collective-permute-start.11) | collective-permute-done | bytes 163872 | tf_op jit(solution)/shard_map/ppermute | solution.py:243
  27.1 2.0 %collective-permute-done.4.refs_2_ = bf16[2,80,320]{2,1,0:T(8,128)(2,1)S(1)} collective-permute-done((bf16[2,80,320]{2,1,0:T(8,128)(2,1)S(1)}, bf16[2,80,320]{2,1,0:T(8,128)(2,1)S(1)}, u32[]{:S(2)}, u32[]{:S(2)}) %collective-permute-start.4) | collective-permute-done | bytes 102432 | tf_op jit(solution)/shard_map/ppermute | solution.py:269
  29.1 0.9 %collective-permute-start.10 = (bf16[2,80,320]{2,1,0:T(8,128)(2,1)}, bf16[2,80,320]{2,1,0:T(8,128)(2,1)S(1)}, u32[]{:S(2)}, u32[]{:S(2)}) collective-permute-start(bf16[2,80,320]{2,1,0:T(8,128)(2,1)} %dynamic-slice_bitcast_fusion), channel_id=1, source_target_pairs={{1,0},{2,1},{3,2},{0,3},{5,4},{6,5},{7,6},{4,7},{9,8},{10,9},{11,1... | collective-permute-start | bytes 307208 | tf_op jit(solution)/shard_map/ppermute | solution.py:271
  30.0 1.1 %collective-permute-done.9.refs_1_ = bf16[2,80,320]{2,1,0:T(8,128)(2,1)S(1)} collective-permute-done((bf16[2,80,320]{2,1,0:T(8,128)(2,1)}, bf16[2,80,320]{2,1,0:T(8,128)(2,1)S(1)}, u32[]{:S(2)}, u32[]{:S(2)}) %collective-permute-start.9) | collective-permute-done | bytes 102432 | tf_op jit(solution)/shard_map/ppermute | solution.py:269
  32.3 0.9 %copy-done.5 = bf16[2,80,320]{2,1,0:T(8,128)(2,1)S(1)} copy-done((bf16[2,80,320]{2,1,0:T(8,128)(2,1)S(1)}, bf16[2,80,320]{2,1,0:T(8,128)(2,1)}, u32[]{:S(2)}) %copy-start.5) | copy-done | bytes 102424
  33.2 1.0 %query.1 = (f32[320,256]{1,0:T(8,128)S(1)}, bf16[4,320,320]{2,1,0:T(8,128)(2,1)S(1)}) custom-call(s32[5]{0:T(128)S(1)} %stack.23.where, bf16[256,320]{1,0:T(8,128)(2,1)S(1)} %get-tuple-element.44.normed.refs_5_, bf16[4,80,320]{2,1,0:T(8,128)(2,1)S(1)} %pad_maximum_fusion.refs_0_, bf16[2,80,320]{2,1,0:T(8,128)(2,1)S(1)} %collective-permute-done.2.refs_1_, ...), custom_call_target="tpu_custom_call" | custom-call | tf_op jit(solution)/shard_map/query/pallas_call | solution.py:395
  35.0 6.1 %cross_view.1 = (bf16[256,320]{1,0:T(8,128)(2,1)S(1)}, bf16[256,320]{1,0:T(8,128)(2,1)S(1)}) custom-call(s32[2]{0:T(128)S(1)} %xor_reduce_fusion.refs_0_, s32[8]{0:T(128)S(1)} %reshape.93.refs_1_, bf16[256,320]{1,0:T(8,128)(2,1)S(1)} %get-tuple-element.43.refs_2_, f32[320,256]{1,0:T(8,128)S(1)} %get-tuple-element.49.refs_3_, ...), custom_call_target="tpu_custom_call" | custom-call | tf_op jit(solution)/shard_map/cross_view/pallas_call | solution.py:409
  41.2 3.8 %collective-permute-start.19 = (bf16[256,320]{1,0:T(8,128)(2,1)S(1)}, bf16[256,320]{1,0:T(8,128)(2,1)S(1)}, u32[]{:S(2)}, u32[]{:S(2)}) collective-permute-start(bf16[256,320]{1,0:T(8,128)(2,1)S(1)} %get-tuple-element.56.rows), channel_id=1, source_target_pairs={{1,0},{2,1},{3,2},{0,3},{5,4},{6,5},{7,6},{4,7},{9,8},{10,9},{11,1... | collective-permute-start | bytes 491528 | tf_op jit(solution)/shard_map/ppermute | solution.py:271
  45.0 5.8 %collective-permute-done.17.rows = bf16[256,320]{1,0:T(8,128)(2,1)S(1)} collective-permute-done((bf16[256,320]{1,0:T(8,128)(2,1)S(1)}, bf16[256,320]{1,0:T(8,128)(2,1)S(1)}, u32[]{:S(2)}, u32[]{:S(2)}) %collective-permute-start.17) | collective-permute-done | bytes 163872 | tf_op jit(solution)/shard_map/ppermute | solution.py:269
  51.3 0.8 %collective-permute-done.14.refs_4_ = bf16[2,80,320]{2,1,0:T(8,128)(2,1)S(1)} collective-permute-done((bf16[2,80,320]{2,1,0:T(8,128)(2,1)S(1)}, bf16[2,80,320]{2,1,0:T(8,128)(2,1)S(1)}, u32[]{:S(2)}, u32[]{:S(2)}) %collective-permute-start.14) | collective-permute-done | bytes 102432 | tf_op jit(solution)/shard_map/ppermute | solution.py:293
  52.6 1.4 %own_frame.1 = (bf16[4,320,320]{2,1,0:T(8,128)(2,1)S(1)}, bf16[256,320]{1,0:T(8,128)(2,1)S(1)}, f32[256,320]{1,0:T(8,128)S(1)}, bf16[256,320]{1,0:T(8,128)(2,1)S(1)}) custom-call(s32[5]{0:T(128)S(1)} %stack.23.where, bf16[256,320]{1,0:T(8,128)(2,1)S(1)} %get-tuple-element.56.rows, bf16[4,80,320]{2,1,0:T(8,128)(2,1)S(1)} %pad_maximum_fusion.1.refs_0_, ...), custom_call_target="tpu_custom_call" | custom-call | flops 209715200 | bytes 1474560 | tf_op jit(solution)/shard_map/own_frame/pallas_call | solution.py:433
  55.3 3.5 %collective-permute-done.18.refs_2_ = bf16[256,320]{1,0:T(8,128)(2,1)S(1)} collective-permute-done((bf16[256,320]{1,0:T(8,128)(2,1)S(1)}, bf16[256,320]{1,0:T(8,128)(2,1)S(1)}, u32[]{:S(2)}, u32[]{:S(2)}) %collective-permute-start.18) | collective-permute-done | bytes 163872 | tf_op jit(solution)/shard_map/ppermute | solution.py:269
  58.8 2.0 %last.1 = bf16[320,256]{1,0:T(8,128)(2,1)} custom-call(bf16[256,320]{1,0:T(8,128)(2,1)S(1)} %get-tuple-element.52.refs_0_, bf16[256,320]{1,0:T(8,128)(2,1)S(1)} %get-tuple-element.61.queries.refs_1_, bf16[256,320]{1,0:T(8,128)(2,1)S(1)} %collective-permute-done.18.refs_2_, bf16[4,320,320]{2,1,0:T(8,128)(2,1)S(1)} %get-tuple-element.62.weights.refs_3_, ...), custom_call_target="tpu_custom_call" | custom-call | tf_op jit(solution)/shard_map/last/pallas_call | solution.py:456
  (60 shorter events, 7.7 us)
Async XLA Ops:
  0.0 31.1 %copy-start = (s32[2,4,2,2]{1,3,2,0:T(2,128)S(1)}, s32[2,4,2,2]{1,3,2,0:T(2,128)}, u32[]{:S(2)}) copy-start(s32[2,4,2,2]{1,3,2,0:T(2,128)} %param.14) | copy-start | bytes 388
  1.7 13.4 %copy-start.1 = (bf16[3,3,320,320]{3,2,1,0:T(8,128)(2,1)S(1)}, bf16[3,3,320,320]{3,2,1,0:T(8,128)(2,1)}, u32[]{:S(2)}) copy-start(bf16[3,3,320,320]{3,2,1,0:T(8,128)(2,1)} %param.15) | copy-start | bytes 5529604
  1.7 13.4 %copy-start.3 = (bf16[1,1,256,320]{2,3,1,0:T(8,128)(2,1)S(1)}, bf16[1,1,256,320]{2,3,1,0:T(8,128)(2,1)}, u32[]{:S(2)}) copy-start(bf16[1,1,256,320]{2,3,1,0:T(8,128)(2,1)} %param.11) | copy-start | bytes 491524
  1.8 4.6 %collective-permute-start = (f32[1,320]{1,0:T(1,128)S(1)}, f32[1,320]{1,0:T(1,128)S(1)}, u32[]{:S(2)}, u32[]{:S(2)}) collective-permute-start(f32[1,320]{1,0:T(1,128)S(1)} %time_share.1), channel_id=1, source_target_pairs={{0,1},{1,0},{2,3},{3,2},{4,5},{5,4},{6,7},{7,6},{8,9},{9,8},{10,11... | collective-permute-start | bytes 3848 | tf_op jit(solution)/shard_map/ppermute | solution.py:256
  6.5 4.6 %collective-permute-start.1 = (f32[1,320]{1,0:T(1,128)S(1)}, f32[1,320]{1,0:T(1,128)S(1)}, u32[]{:S(2)}, u32[]{:S(2)}) collective-permute-start(f32[1,320]{1,0:T(1,128)S(1)} %add.75), channel_id=1, source_target_pairs={{0,2},{1,3},{2,0},{3,1},{4,6},{5,7},{6,4},{7,5},{8,10},{9,11},{10,... | collective-permute-start | bytes 3848 | tf_op jit(solution)/shard_map/ppermute | solution.py:256
  11.1 7.5 %collective-permute-start.2 = (bf16[2,80,320]{2,1,0:T(8,128)(2,1)S(1)}, bf16[2,80,320]{2,1,0:T(8,128)(2,1)S(1)}, u32[]{:S(2)}, u32[]{:S(2)}) collective-permute-start(bf16[2,80,320]{2,1,0:T(8,128)(2,1)S(1)} %dynamic-slice_bitcast_fusion.1), channel_id=1, source_target_pairs={{0,1},{1,2},{2,3},{3,0},{4,5},{5,6},{6,7},{7,4},{8,9},{9,10},{10,1... | collective-permute-start | bytes 307208 | tf_op jit(solution)/shard_map/ppermute | solution.py:269
  13.1 6.2 %collective-permute-start.3 = (bf16[2,80,320]{2,1,0:T(8,128)(2,1)S(1)}, bf16[2,80,320]{2,1,0:T(8,128)(2,1)S(1)}, u32[]{:S(2)}, u32[]{:S(2)}) collective-permute-start(bf16[2,80,320]{2,1,0:T(8,128)(2,1)S(1)} %dynamic-slice_bitcast_fusion.1), channel_id=1, source_target_pairs={{1,0},{2,1},{3,2},{0,3},{5,4},{6,5},{7,6},{4,7},{9,8},{10,9},{11,1... | collective-permute-start | bytes 307208 | tf_op jit(solution)/shard_map/ppermute | solution.py:271
  16.8 14.7 %copy-start.11 = (s32[2,4]{1,0:T(2,128)S(1)}, s32[2,4]{1,0:T(2,128)}, u32[]{:S(2)}) copy-start(s32[2,4]{1,0:T(2,128)} %param.13) | copy-start | bytes 100
  19.3 2.6 %collective-permute-start.8 = (bf16[256,320]{1,0:T(8,128)(2,1)S(1)}, bf16[256,320]{1,0:T(8,128)(2,1)S(1)}, u32[]{:S(2)}, u32[]{:S(2)}) collective-permute-start(bf16[256,320]{1,0:T(8,128)(2,1)S(1)} %get-tuple-element.44.normed.refs_5_), channel_id=1, source_target_pairs={{0,4},{4,0},{8,12},{12,8},{1,5},{5,1},{9,13},{13,9},{2,6},{6,2},{1... | collective-permute-start | bytes 491528 | tf_op jit(solution)/shard_map/ppermute | solution.py:243
  19.3 7.3 %collective-permute-start.11 = (bf16[256,320]{1,0:T(8,128)(2,1)S(1)}, bf16[256,320]{1,0:T(8,128)(2,1)S(1)}, u32[]{:S(2)}, u32[]{:S(2)}) collective-permute-start(bf16[256,320]{1,0:T(8,128)(2,1)S(1)} %get-tuple-element.44.normed.refs_5_), channel_id=1, source_target_pairs={{0,8},{4,12},{8,0},{12,4},{1,9},{5,13},{9,1},{13,5},{2,10},{6,14},... | collective-permute-start | bytes 491528 | tf_op jit(solution)/shard_map/ppermute | solution.py:243
  20.8 8.2 %collective-permute-start.5 = (bf16[2,80,320]{2,1,0:T(8,128)(2,1)S(1)}, bf16[2,80,320]{2,1,0:T(8,128)(2,1)S(1)}, u32[]{:S(2)}, u32[]{:S(2)}) collective-permute-start(bf16[2,80,320]{2,1,0:T(8,128)(2,1)S(1)} %collective-permute-done.2.refs_1_), channel_id=1, source_target_pairs={{0,4},{4,0},{8,12},{12,8},{1,5},{5,1},{9,13},{13,9},{2,6},{6,2},{1... | collective-permute-start | bytes 307208 | tf_op jit(solution)/shard_map/ppermute | solution.py:293
  21.1 7.9 %collective-permute-start.4 = (bf16[2,80,320]{2,1,0:T(8,128)(2,1)S(1)}, bf16[2,80,320]{2,1,0:T(8,128)(2,1)S(1)}, u32[]{:S(2)}, u32[]{:S(2)}) collective-permute-start(bf16[2,80,320]{2,1,0:T(8,128)(2,1)S(1)} %collective-permute-done.2.refs_1_), channel_id=1, source_target_pairs={{0,1},{1,2},{2,3},{3,0},{4,5},{5,6},{6,7},{7,4},{8,9},{9,10},{10,1... | collective-permute-start | bytes 307208 | tf_op jit(solution)/shard_map/ppermute | solution.py:269
  22.5 8.5 %collective-permute-start.9 = (bf16[2,80,320]{2,1,0:T(8,128)(2,1)}, bf16[2,80,320]{2,1,0:T(8,128)(2,1)S(1)}, u32[]{:S(2)}, u32[]{:S(2)}) collective-permute-start(bf16[2,80,320]{2,1,0:T(8,128)(2,1)} %dynamic-slice_bitcast_fusion), channel_id=1, source_target_pairs={{0,1},{1,2},{2,3},{3,0},{4,5},{5,6},{6,7},{7,4},{8,9},{9,10},{10,1... | collective-permute-start | bytes 307208 | tf_op jit(solution)/shard_map/ppermute | solution.py:269
  26.6 8.4 %collective-permute-start.12 = (bf16[256,320]{1,0:T(8,128)(2,1)S(1)}, bf16[256,320]{1,0:T(8,128)(2,1)S(1)}, u32[]{:S(2)}, u32[]{:S(2)}) collective-permute-start(bf16[256,320]{1,0:T(8,128)(2,1)S(1)} %collective-permute-done.11.refs_7_), channel_id=1, source_target_pairs={{0,4},{4,0},{8,12},{12,8},{1,5},{5,1},{9,13},{13,9},{2,6},{6,2},{1... | collective-permute-start | bytes 491528 | tf_op jit(solution)/shard_map/ppermute | solution.py:243
  26.6 5.1 %collective-permute-start.7 = (bf16[2,80,320]{2,1,0:T(8,128)(2,1)S(1)}, bf16[2,80,320]{2,1,0:T(8,128)(2,1)S(1)}, u32[]{:S(2)}, u32[]{:S(2)}) collective-permute-start(bf16[2,80,320]{2,1,0:T(8,128)(2,1)S(1)} %collective-permute-done.3.refs_3_), channel_id=1, source_target_pairs={{0,4},{4,0},{8,12},{12,8},{1,5},{5,1},{9,13},{13,9},{2,6},{6,2},{1... | collective-permute-start | bytes 307208 | tf_op jit(solution)/shard_map/ppermute | solution.py:293
  29.0 2.6 %collective-permute-start.6 = (bf16[2,80,320]{2,1,0:T(8,128)(2,1)S(1)}, bf16[2,80,320]{2,1,0:T(8,128)(2,1)S(1)}, u32[]{:S(2)}, u32[]{:S(2)}) collective-permute-start(bf16[2,80,320]{2,1,0:T(8,128)(2,1)S(1)} %collective-permute-done.4.refs_2_), channel_id=1, source_target_pairs={{0,4},{4,0},{8,12},{12,8},{1,5},{5,1},{9,13},{13,9},{2,6},{6,2},{1... | collective-permute-start | bytes 307208 | tf_op jit(solution)/shard_map/ppermute | solution.py:293
  29.1 6.0 %collective-permute-start.10 = (bf16[2,80,320]{2,1,0:T(8,128)(2,1)}, bf16[2,80,320]{2,1,0:T(8,128)(2,1)S(1)}, u32[]{:S(2)}, u32[]{:S(2)}) collective-permute-start(bf16[2,80,320]{2,1,0:T(8,128)(2,1)} %dynamic-slice_bitcast_fusion), channel_id=1, source_target_pairs={{1,0},{2,1},{3,2},{0,3},{5,4},{6,5},{7,6},{4,7},{9,8},{10,9},{11,1... | collective-permute-start | bytes 307208 | tf_op jit(solution)/shard_map/ppermute | solution.py:271
  31.1 10.0 %collective-permute-start.13 = (bf16[2,80,320]{2,1,0:T(8,128)(2,1)S(1)}, bf16[2,80,320]{2,1,0:T(8,128)(2,1)S(1)}, u32[]{:S(2)}, u32[]{:S(2)}) collective-permute-start(bf16[2,80,320]{2,1,0:T(8,128)(2,1)S(1)} %collective-permute-done.9.refs_1_), channel_id=1, source_target_pairs={{0,1},{1,2},{2,3},{3,0},{4,5},{5,6},{6,7},{7,4},{8,9},{9,10},{10,1... | collective-permute-start | bytes 307208 | tf_op jit(solution)/shard_map/ppermute | solution.py:269
  41.1 9.7 %collective-permute-start.17 = (bf16[256,320]{1,0:T(8,128)(2,1)S(1)}, bf16[256,320]{1,0:T(8,128)(2,1)S(1)}, u32[]{:S(2)}, u32[]{:S(2)}) collective-permute-start(bf16[256,320]{1,0:T(8,128)(2,1)S(1)} %get-tuple-element.56.rows), channel_id=1, source_target_pairs={{0,1},{1,2},{2,3},{3,0},{4,5},{5,6},{6,7},{7,4},{8,9},{9,10},{10,1... | collective-permute-start | bytes 491528 | tf_op jit(solution)/shard_map/ppermute | solution.py:269
  41.2 13.5 %collective-permute-start.19 = (bf16[256,320]{1,0:T(8,128)(2,1)S(1)}, bf16[256,320]{1,0:T(8,128)(2,1)S(1)}, u32[]{:S(2)}, u32[]{:S(2)}) collective-permute-start(bf16[256,320]{1,0:T(8,128)(2,1)S(1)} %get-tuple-element.56.rows), channel_id=1, source_target_pairs={{1,0},{2,1},{3,2},{0,3},{5,4},{6,5},{7,6},{4,7},{9,8},{10,9},{11,1... | collective-permute-start | bytes 491528 | tf_op jit(solution)/shard_map/ppermute | solution.py:271
  50.8 8.0 %collective-permute-start.18 = (bf16[256,320]{1,0:T(8,128)(2,1)S(1)}, bf16[256,320]{1,0:T(8,128)(2,1)S(1)}, u32[]{:S(2)}, u32[]{:S(2)}) collective-permute-start(bf16[256,320]{1,0:T(8,128)(2,1)S(1)} %collective-permute-done.17.rows), channel_id=1, source_target_pairs={{0,1},{1,2},{2,3},{3,0},{4,5},{5,6},{6,7},{7,4},{8,9},{9,10},{10,1... | collective-permute-start | bytes 491528 | tf_op jit(solution)/shard_map/ppermute | solution.py:269
  50.8 1.3 %collective-permute-start.14 = (bf16[2,80,320]{2,1,0:T(8,128)(2,1)S(1)}, bf16[2,80,320]{2,1,0:T(8,128)(2,1)S(1)}, u32[]{:S(2)}, u32[]{:S(2)}) collective-permute-start(bf16[2,80,320]{2,1,0:T(8,128)(2,1)S(1)} %collective-permute-done.9.refs_1_), channel_id=1, source_target_pairs={{0,4},{4,0},{8,12},{12,8},{1,5},{5,1},{9,13},{13,9},{2,6},{6,2},{1... | collective-permute-start | bytes 307208 | tf_op jit(solution)/shard_map/ppermute | solution.py:293
  50.8 1.5 %collective-permute-start.15 = (bf16[2,80,320]{2,1,0:T(8,128)(2,1)S(1)}, bf16[2,80,320]{2,1,0:T(8,128)(2,1)S(1)}, u32[]{:S(2)}, u32[]{:S(2)}) collective-permute-start(bf16[2,80,320]{2,1,0:T(8,128)(2,1)S(1)} %collective-permute-done.13.refs_2_), channel_id=1, source_target_pairs={{0,4},{4,0},{8,12},{12,8},{1,5},{5,1},{9,13},{13,9},{2,6},{6,2},{1... | collective-permute-start | bytes 307208 | tf_op jit(solution)/shard_map/ppermute | solution.py:293
  51.3 1.3 %collective-permute-start.16 = (bf16[2,80,320]{2,1,0:T(8,128)(2,1)S(1)}, bf16[2,80,320]{2,1,0:T(8,128)(2,1)S(1)}, u32[]{:S(2)}, u32[]{:S(2)}) collective-permute-start(bf16[2,80,320]{2,1,0:T(8,128)(2,1)S(1)} %collective-permute-done.10.refs_3_), channel_id=1, source_target_pairs={{0,4},{4,0},{8,12},{12,8},{1,5},{5,1},{9,13},{13,9},{2,6},{6,2},{1... | collective-permute-start | bytes 307208 | tf_op jit(solution)/shard_map/ppermute | solution.py:293
  (8 other events, 36.6 us)

commit v5 on v4

--- a/solution.py
+++ b/solution.py
@@ -17,6 +17,7 @@
 EPSILON = 1e-05
 MASKED = -1e30
 LOG2E = 1.4426950408889634
+SHARE_ROWS = 16
 
 VMEM = pl.BlockSpec(memory_space=pltpu.VMEM)
 SMEM = pl.BlockSpec(memory_space=pltpu.SMEM)
@@ -40,15 +41,18 @@
     return (rows == cols).astype(f32).astype(bf16)
 
 
-def group_sum(row, ones):
+def terms(row):
     first = row.astype(bf16).astype(f32)
     second = (row - first).astype(bf16).astype(f32)
     third = row - first - second
-    index = lax.broadcasted_iota(jnp.int32, (16, row.shape[1]), 0)
-    stacked = jnp.where(
+    index = lax.broadcasted_iota(jnp.int32, (SHARE_ROWS, row.shape[1]), 0)
+    return jnp.where(
         index == 0, first, jnp.where(index == 1, second, jnp.where(index == 2, third, 0.0))
     )
-    return jnp.sum(dot(stacked.astype(bf16), ones), axis=0, keepdims=True)
+
+
+def group_sum(row, ones):
+    return jnp.sum(dot(terms(row).astype(bf16), ones), axis=0, keepdims=True)
 
 
 def group_norm_silu(x):
@@ -92,35 +96,61 @@
     share[...] = dot(act[...], proj[...])
 
 
+def payload_kernel(side, act, proj, three, one, payload):
+    rows, channels = one.shape
+    share = dot(act[...], proj[...])
+    payload[pl.ds(2 * rows, SHARE_ROWS), :] = terms(share).astype(bf16)
+
+    @pl.when(side[0] == 0)
+    def _():
+        payload[pl.ds(0, rows), :] = three[0]
+        payload[pl.ds(rows, rows), :] = three[1]
+
+    @pl.when(side[0] != 0)
+    def _():
+        payload[pl.ds(0, rows), :] = three[2]
+        payload[pl.ds(rows, rows), :] = one[...]
+
+
 def first_kernel(source, weight, inner, padded):
     inner[...] = convolve(group_norm_silu(source[...].astype(f32).T), weight, padded)
 
 
-def second_kernel(source, inner, bias, weight, hidden, normed, padded):
-    y = group_norm_silu(inner[...] + bias[...])
+def second_kernel(source, inner, weight, *refs):
+    shares, (hidden, normed, padded) = refs[:-3], refs[-3:]
+    bias = None
+    for share in shares:
+        rows = min(SHARE_ROWS, share.shape[0])
+        part = jnp.sum(share[pl.ds(share.shape[0] - rows, rows), :].astype(f32), axis=0, keepdims=True)
+        bias = part if bias is None else bias + part
+    y = group_norm_silu(inner[...] + bias)
     total = source[...].astype(f32).T + convolve(y, weight, padded)
     rounded = total.astype(bf16)
     hidden[...] = rounded
     normed[...] = layer_norm(rounded.astype(f32)).astype(bf16)
 
 
-def assemble(where, parts, whole):
-    own, count = parts[0], len(parts) // 2
-    rows = own.shape[1]
+def assemble(where, own, received, swapped, whole):
+    rows = own[0].shape[0]
     for kind in range(4):
         whole[kind, pl.ds(pl.multiple_of(where[0] * rows, 16), rows), :] = own[kind]
+    count = len(received)
     for k in range(1, count + 1):
         place = pl.ds(pl.multiple_of(where[k] * rows, 16), rows)
         for j in range(2):
             mine = where[count + 1] * 2 + j
-            whole[mine, place, :] = parts[k][j]
-            whole[2 - mine + 2 * j, place, :] = parts[count + k][j]
-
-
-def query_kernel(where, normed, *refs):
-    parts = refs[:-2]
-    queries, epi = refs[-2:]
-    assemble(where, parts, epi)
+            whole[mine, place, :] = received[k - 1][pl.ds(j * rows, rows), :]
+            start = ((k - 1) * 2 + j) * rows
+            whole[2 - mine + 2 * j, place, :] = swapped[pl.ds(start, rows), :]
+
+
+def own_rows(three, one):
+    return [three[0], three[1], three[2], one[...]]
+
+
+def query_kernel(where, normed, three, one, *refs):
+    parts, (queries, epi) = refs[:-2], refs[-2:]
+    assemble(where, own_rows(three, one), parts[:-1], parts[-1] if parts else None, epi)
     queries[...] = dot(normed[...], epi[0]).astype(bf16).astype(f32).T
 
 
@@ -189,10 +219,9 @@
     return (dot(high, ones) + dot(low, ones)) * (LOG2E / math.sqrt(head)), values
 
 
-def own_frame_kernel(where, rows, *refs):
-    parts = refs[:-4]
-    weights, queries, scores, values = refs[-4:]
-    assemble(where, parts, weights)
+def own_frame_kernel(where, rows, three, one, *refs):
+    parts, (weights, queries, scores, values) = refs[:-4], refs[-4:]
+    assemble(where, own_rows(three, one), parts[:-1], parts[-1] if parts else None, weights)
     queries[...] = dot(rows[...], weights[0]).astype(bf16)
     scores[...], values[...] = frame_part(queries[...].astype(f32), rows[...], weights)
 
@@ -261,7 +290,7 @@
     return value, beside, later
 
 
-def ring_gather(own, axis, size):
+def ring_gather(own, axis, size, beside=None):
     pieces = {0: own}
     right = [(i, (i + 1) % size) for i in range(size)]
     left = [(j, i) for i, j in right]
@@ -269,7 +298,10 @@
         pieces[step] = lax.ppermute(pieces[step - 1], axis, right)
         if size - step > step:
             pieces[size - step] = lax.ppermute(pieces[(size - step + 1) % size], axis, left)
-    return [pieces[k] for k in range(size)]
+        if step == 1 and beside is not None:
+            pieces[1], beside = lax.optimization_barrier((pieces[1], beside))
+    pieces = [pieces[k] for k in range(size)]
+    return pieces if beside is None else (pieces, beside)
 
 
 def neighbours(pieces):
@@ -283,14 +315,9 @@
     return pieces
 
 
-def gather_weights(parts, frames, videos, video):
-    kinds, rows, channels = parts.shape
-    mine = lax.dynamic_index_in_dim(parts.reshape(2, 2, rows, channels), video % 2, 0, keepdims=False)
-    return [parts] + ring_gather(mine, "frame", frames)[1:]
-
-
-def swap_weights(parts, videos):
-    return parts + [lax.ppermute(part, "video", partner_permutation(videos, 1)) for part in parts[1:]]
+def swap(pieces, rows, videos):
+    joined = jnp.concatenate([piece[:rows] for piece in pieces[1:]], axis=0)
+    return pieces[1:] + [lax.ppermute(joined, "video", partner_permutation(videos, 1))]
 
 
 def per_device(
@@ -323,28 +350,39 @@
     angles = timesteps.astype(f32)[:, None] * frequency[None, :]
     wave = jnp.where(index[None, :] < half, jnp.cos(angles), jnp.sin(angles))
     time_act = jax.nn.silu(wave).astype(bf16)
-    share = pl.pallas_call(
-        share_kernel,
-        out_shape=jax.ShapeDtypeStruct((1, channels), f32),
-        in_specs=[VMEM, VMEM],
-        out_specs=VMEM,
-        compiler_params=params(),
-        cost_estimate=pl.CostEstimate(flops=10**10, bytes_accessed=1 << 20, transcendentals=0),
-        name="time_share",
-    )(time_act, time_proj)
-    epi_own = jnp.concatenate([epi_in, epi_out[None]], axis=0)
-    temp_own = jnp.concatenate([temp_in, temp_out[None]], axis=0)
-    bias, source, epi_own = sum_over(share, source, epi_own, "frame", frames)
-    paired = videos % 2 == 0 and is_power(videos) and epi_own.shape[1] % 16 == 0
+    height = epi_out.shape[0]
+    paired = videos % 2 == 0 and is_power(videos) and height % 16 == 0
+    early = pl.CostEstimate(flops=10**10, bytes_accessed=1 << 20, transcendentals=0)
     if paired:
+        side = (video % 2).astype(jnp.int32).reshape(1)
+        payload = pl.pallas_call(
+            payload_kernel,
+            out_shape=jax.ShapeDtypeStruct((2 * height + SHARE_ROWS, channels), bf16),
+            in_specs=[SMEM, VMEM, VMEM, VMEM, VMEM],
+            out_specs=VMEM,
+            compiler_params=params(),
+            cost_estimate=early,
+            name="payload",
+        )(side, time_act, time_proj, epi_in, epi_out)
+        shares = [payload]
         places = [(frame - k) % frames for k in range(frames)] + [video % 2]
     else:
+        share = pl.pallas_call(
+            share_kernel,
+            out_shape=jax.ShapeDtypeStruct((1, channels), f32),
+            in_specs=[VMEM, VMEM],
+            out_specs=VMEM,
+            compiler_params=params(),
+            cost_estimate=early,
+            name="time_share",
+        )(time_act, time_proj)
+        shares = [lax.psum(share, "frame")]
         places = [jnp.int32(0)] * 2
+        epi_in = lax.all_gather(epi_in, "frame", axis=1, tiled=True)
+        epi_out = lax.all_gather(epi_out, "frame", axis=0, tiled=True)
+        temp_in = lax.all_gather(temp_in, "frame", axis=1, tiled=True)
+        temp_out = lax.all_gather(temp_out, "frame", axis=0, tiled=True)
     places = jnp.stack(places).astype(jnp.int32)
-    if paired:
-        epi_parts = gather_weights(epi_own, frames, videos, video)
-    else:
-        epi_parts = [lax.all_gather(epi_own, "frame", axis=1, tiled=True)]
 
     conv_scratch = [
         pltpu.VMEM((tokens + 2 * W, 3 * channels), bf16),
@@ -364,27 +402,33 @@
         cost_estimate=conv_cost,
         name="first_conv",
     )(source, conv_first.reshape(3, 3 * channels, channels))
+    temp_parts = []
+    if paired:
+        shares, inner = ring_gather(shares[0], "frame", frames, inner)
+        temp_own = jnp.concatenate([temp_in, temp_out[None]], axis=0)
+        temp_own = temp_own.reshape(2, 2 * height, channels)
+        mine = lax.dynamic_index_in_dim(temp_own, video % 2, 0, keepdims=False)
+        mine, *near = lax.optimization_barrier((mine, *neighbours(shares)))
+        shares = with_neighbours(shares, near)
+        temp_parts = ring_gather(mine, "frame", frames)
     hidden, normed = pl.pallas_call(
         second_kernel,
-        out_shape=[jax.ShapeDtypeStruct((tokens, channels), bf16)] * 2,
-        in_specs=[VMEM, VMEM, VMEM, VMEM],
-        out_specs=[VMEM, VMEM],
+        out_shape=[
+            jax.ShapeDtypeStruct((tokens, channels), bf16),
+            jax.ShapeDtypeStruct((tokens, channels), bf16),
+        ],
+        in_specs=[VMEM] * (3 + len(shares)),
+        out_specs=[VMEM] * 2,
         scratch_shapes=conv_scratch,
         compiler_params=params(),
         cost_estimate=conv_cost,
         name="second_conv",
-    )(source, inner, bias, conv_second.reshape(3, 3 * channels, channels))
-
+    )(source, inner, conv_second.reshape(3, 3 * channels, channels), *shares)
     if paired:
-        normed, hidden, *near = lax.optimization_barrier((normed, hidden, *neighbours(epi_parts)))
-        epi_parts = with_neighbours(epi_parts, near)
+        normed, hidden, *near = lax.optimization_barrier((normed, hidden, *neighbours(temp_parts)))
+        temp_parts = with_neighbours(temp_parts, near)
     maps = gather_maps(normed, "video", videos)
-    if paired:
-        temp_own, maps[1] = lax.optimization_barrier((temp_own, maps[1]))
-        temp_parts = gather_weights(temp_own, frames, videos, video)
-        epi_parts = swap_weights(epi_parts, videos)
-    else:
-        temp_parts = [lax.all_gather(temp_own, "frame", axis=1, tiled=True)]
+    epi_parts = swap(shares, 2 * height, videos) if paired else []
     targets = lax.dynamic_index_in_dim(matchings, video, 1, keepdims=False)
     if is_power(videos):
         select = video ^ targets
@@ -398,14 +442,11 @@
             jax.ShapeDtypeStruct((channels, tokens), f32),
             jax.ShapeDtypeStruct(square, bf16),
         ],
-        in_specs=[SMEM, VMEM] + [VMEM] * len(epi_parts),
+        in_specs=[SMEM, VMEM, VMEM, VMEM] + [VMEM] * len(epi_parts),
         out_specs=[VMEM] * 2,
         compiler_params=params(),
         name="query",
-    )(places, normed, *epi_parts)
-    if paired:
-        queries, *near = lax.optimization_barrier((queries, *neighbours(temp_parts)))
-        temp_parts = with_neighbours(temp_parts, near)
+    )(places, normed, epi_in, epi_out, *epi_parts)
     second, blocks = pl.pallas_call(
         functools.partial(view_kernel, videos, tiles),
         out_shape=[jax.ShapeDtypeStruct((tokens, channels), bf16)] * 2,
@@ -421,7 +462,7 @@
 
     if paired:
         blocks, *temp_parts = lax.optimization_barrier((blocks, *temp_parts))
-        temp_parts = swap_weights(temp_parts, videos)
+        temp_parts = swap(temp_parts, 2 * height, videos)
     arrived = ring_gather(blocks, "frame", frames)
     score_shape = jax.ShapeDtypeStruct((tokens, channels), f32)
     value_shape = jax.ShapeDtypeStruct((tokens, channels), bf16)
@@ -433,12 +474,12 @@
     temp, frame_queries, *first = pl.pallas_call(
         own_frame_kernel,
         out_shape=[jax.ShapeDtypeStruct(square, bf16), value_shape, score_shape, value_shape],
-        in_specs=[SMEM, VMEM] + [VMEM] * len(temp_parts),
+        in_specs=[SMEM, VMEM, VMEM, VMEM] + [VMEM] * len(temp_parts),
         out_specs=[VMEM] * 4,
         compiler_params=params(),
         cost_estimate=frame_cost,
         name="own_frame",
-    )(places, blocks, *temp_parts)
+    )(places, blocks, temp_in, temp_out, *temp_parts)
     scores, values = [first[0]], [first[1]]
     order = sorted(range(1, frames), key=lambda k: min(k, frames - k))
     for k in order[:-1]:

time: 61 us -> 64.2 us (1.052)
  local copies, waits for them, and re-layouts: 3.58 us -> 9.3 us
  starting transfers between devices: 19.6 us -> 15.7 us
  waiting for transfers between devices: 21.1 us -> 22.1 us
    ppermute x8 -> x2, starting transfers between devices: 7.42 us -> 0.52 us  [swap(): lax.ppermute(joined, 'video', partner_permutation(videos, 1))]
    unnamed x24 -> x40, local copies, waits for them, and re-layouts: 2.53 us -> 8.86 us
    ppermute x6, waiting for transfers between devices: 12.3 us -> 17 us  [ring_gather(): pieces[step] = lax.ppermute(pieces[step - 1], axis, right)]
    ppermute x8 -> x2, waiting for transfers between devices: 4.37 us -> 0.01 us  [swap(): lax.ppermute(joined, 'video', partner_permutation(videos, 1))]
    ppermute x6, starting transfers between devices: 3.88 us -> 5.47 us  [ring_gather(): pieces[step] = lax.ppermute(pieces[step - 1], axis, right)]
    ppermute x3, starting transfers between devices: 1.5 us -> 2.25 us  [gather_maps(): maps[k | bit] = lax.ppermute(maps[k], axis, partner_permutation(size, bit))]
    ppermute x3, waiting for transfers between devices: 2.98 us -> 3.7 us  [gather_maps(): maps[k | bit] = lax.ppermute(maps[k], axis, partner_permutation(size, bit))]
    squeeze x2 -> x1, local copies, waits for them, and re-layouts: 0.67 us -> 0.01 us  [per_device(): mine = lax.dynamic_index_in_dim(temp_own, video % 2, 0, keepdims=False)]
  transfers between devices with their start and end apart: 20 -> 14, of which waited for: 12 -> 6; matrix products, arithmetic and copies ran while one was open for 2% -> 1% of each run, Pallas kernels for 22% -> 20%
where the time goes in v5:
time: 64.2 us; the launch traced here: 63.8 us
  waiting for transfers between devices  22.1 us (34%)
  starting transfers between devices  15.7 us (24%)
  Pallas kernels  15.3 us (24%)
  local copies, waits for them, and re-layouts  9.3 us (14%)
  between operations  1.05 us (2%)
    ppermute x6, waiting for transfers between devices, ring_gather(): pieces[step] = lax.ppermute(pieces[step - 1], axis, right)  17 us
    unnamed x40, local copies, waits for them, and re-layouts  8.86 us
    ppermute x3, starting transfers between devices, ring_gather(): lax.ppermute(pieces[(size - step + 1) % size], axis, left)  7.41 us
    pallas_call x1, Pallas kernels, per_device(): pl.pallas_call(functools.partial(view_kernel, videos, tiles), out_shape=[...  6.07 us
    ppermute x6, starting transfers between devices, ring_gather(): pieces[step] = lax.ppermute(pieces[step - 1], axis, right)  5.47 us
    ppermute x3, waiting for transfers between devices, gather_maps(): maps[k | bit] = lax.ppermute(maps[k], axis, partner_permutation(size, bit))  3.7 us
    ppermute x3, starting transfers between devices, gather_maps(): maps[k | bit] = lax.ppermute(maps[k], axis, partner_permutation(size, bit))  2.25 us
    pallas_call x1, Pallas kernels, per_device(): pl.pallas_call(functools.partial(last_kernel, frames), out_shape=jax.Shap...  2.02 us
  transfers between devices with their start and end apart: 14, of which 6 were waited for; matrix products, arithmetic and copies ran while one was open for 1% of the time, Pallas kernels for 20%

profile of v5, /device:TPU:0, one launch (start us, length us, event | category | flops | bytes accessed | tf_op | source)
XLA Modules:
  0.0 63.8 jit_solution(15997276179364612165)
XLA Ops:
  0.8 0.9 %copy-done.12 = bf16[3,80,320]{2,1,0:T(8,128)(2,1)S(1)} copy-done((bf16[3,80,320]{2,1,0:T(8,128)(2,1)S(1)}, bf16[3,80,320]{2,1,0:T(8,128)(2,1)}, u32[]{:S(2)}) %copy-start.12) | copy-done | bytes 153624
  2.5 0.9 %copy-done.18 = bf16[320,320]{1,0:T(8,128)(2,1)S(1)} copy-done((bf16[320,320]{1,0:T(8,128)(2,1)S(1)}, bf16[320,320]{1,0:T(8,128)(2,1)}, u32[]{:S(2)}) %copy-start.18) | copy-done | bytes 204824
  3.7 3.1 %collective-permute-start = (bf16[176,320]{1,0:T(8,128)(2,1)S(1)}, bf16[176,320]{1,0:T(8,128)(2,1)S(1)}, u32[]{:S(2)}, u32[]{:S(2)}) collective-permute-start(bf16[176,320]{1,0:T(8,128)(2,1)S(1)} %payload.1.refs_0_), channel_id=1, source_target_pairs={{0,1},{1,2},{2,3},{3,0},{4,5},{5,6},{6,7},{7,4},{8,9},{9,10},{10,1... | collective-permute-start | bytes 337928 | tf_op jit(solution)/shard_map/ppermute | solution.py:298
  6.7 2.1 %collective-permute-start.1 = (bf16[176,320]{1,0:T(8,128)(2,1)S(1)}, bf16[176,320]{1,0:T(8,128)(2,1)S(1)}, u32[]{:S(2)}, u32[]{:S(2)}) collective-permute-start(bf16[176,320]{1,0:T(8,128)(2,1)S(1)} %payload.1.refs_0_), channel_id=1, source_target_pairs={{1,0},{2,1},{3,2},{0,3},{5,4},{6,5},{7,6},{4,7},{9,8},{10,9},{11,1... | collective-permute-start | bytes 337928 | tf_op jit(solution)/shard_map/ppermute | solution.py:300
  8.8 1.6 %copy-done.2 = bf16[3,3,320,320]{3,2,1,0:T(8,128)(2,1)S(1)} copy-done((bf16[3,3,320,320]{3,2,1,0:T(8,128)(2,1)S(1)}, bf16[3,3,320,320]{3,2,1,0:T(8,128)(2,1)}, u32[]{:S(2)}) %copy-start.2) | copy-done | bytes 1843224
  10.5 1.6 %first_conv.1.inner = f32[256,320]{1,0:T(8,128)S(1)} custom-call(bf16[320,256]{1,0:T(8,128)(2,1)S(1)} %bitcast.20, bf16[3,960,320]{2,1,0:T(8,128)(2,1)S(1)} %bitcast.19), custom_call_target="tpu_custom_call" | custom-call | flops 471859200 | bytes 2498560 | tf_op jit(solution)/shard_map/first_conv/pallas_call | solution.py:395
  12.2 1.0 %collective-permute-done.refs_1_.refs_0_ = bf16[176,320]{1,0:T(8,128)(2,1)S(1)} collective-permute-done((bf16[176,320]{1,0:T(8,128)(2,1)S(1)}, bf16[176,320]{1,0:T(8,128)(2,1)S(1)}, u32[]{:S(2)}, u32[]{:S(2)}) %collective-permute-start) | collective-permute-done | bytes 112672 | tf_op jit(solution)/shard_map/ppermute | solution.py:298
  13.2 1.5 %collective-permute-done.1.refs_3_.refs_2_ = bf16[176,320]{1,0:T(8,128)(2,1)S(1)} collective-permute-done((bf16[176,320]{1,0:T(8,128)(2,1)S(1)}, bf16[176,320]{1,0:T(8,128)(2,1)S(1)}, u32[]{:S(2)}, u32[]{:S(2)}) %collective-permute-start.1) | collective-permute-done | bytes 112672 | tf_op jit(solution)/shard_map/ppermute | solution.py:300
  14.7 1.8 %collective-permute-start.3 = (bf16[160,320]{1,0:T(8,128)(2,1)S(1)}, bf16[160,320]{1,0:T(8,128)(2,1)S(1)}, u32[]{:S(2)}, u32[]{:S(2)}) collective-permute-start(bf16[160,320]{1,0:T(8,128)(2,1)S(1)} %dynamic-slice_bitcast_fusion), channel_id=1, source_target_pairs={{0,1},{1,2},{2,3},{3,0},{4,5},{5,6},{6,7},{7,4},{8,9},{9,10},{10,1... | collective-permute-start | bytes 307208 | tf_op jit(solution)/shard_map/ppermute | solution.py:298
  16.5 2.0 %collective-permute-start.4 = (bf16[160,320]{1,0:T(8,128)(2,1)S(1)}, bf16[160,320]{1,0:T(8,128)(2,1)S(1)}, u32[]{:S(2)}, u32[]{:S(2)}) collective-permute-start(bf16[160,320]{1,0:T(8,128)(2,1)S(1)} %dynamic-slice_bitcast_fusion), channel_id=1, source_target_pairs={{1,0},{2,1},{3,2},{0,3},{5,4},{6,5},{7,6},{4,7},{9,8},{10,9},{11,1... | collective-permute-start | bytes 307208 | tf_op jit(solution)/shard_map/ppermute | solution.py:300
  18.6 3.0 %collective-permute-done.2.refs_2_.refs_1_ = bf16[176,320]{1,0:T(8,128)(2,1)S(1)} collective-permute-done((bf16[176,320]{1,0:T(8,128)(2,1)S(1)}, bf16[176,320]{1,0:T(8,128)(2,1)S(1)}, u32[]{:S(2)}, u32[]{:S(2)}) %collective-permute-start.2) | collective-permute-done | bytes 112672 | tf_op jit(solution)/shard_map/ppermute | solution.py:298
  21.5 0.9 %copy-done.5 = bf16[1,1,256,320]{2,3,1,0:T(8,128)(2,1)S(1)} copy-done((bf16[1,1,256,320]{2,3,1,0:T(8,128)(2,1)S(1)}, bf16[1,1,256,320]{2,3,1,0:T(8,128)(2,1)}, u32[]{:S(2)}) %copy-start.5) | copy-done | bytes 163864
  23.4 1.7 %second_conv.1 = (bf16[256,320]{1,0:T(8,128)(2,1)S(1)}, bf16[256,320]{1,0:T(8,128)(2,1)S(1)}) custom-call(bf16[320,256]{1,0:T(8,128)(2,1)S(1)} %bitcast.21, f32[256,320]{1,0:T(8,128)S(1)} %first_conv.1.inner, bf16[3,960,320]{2,1,0:T(8,128)(2,1)S(1)} %bitcast.18, bf16[176,320]{1,0:T(8,128)(2,1)S(1)} %copy-done.15, ...), custom_call_target="tpu_custom_call" | custom-call | flops 471859200 | bytes 2498560 | tf_op jit(solution)/shard_map/second_conv/pallas_call | solution.py:414
  25.1 1.8 %collective-permute-start.7 = (bf16[256,320]{1,0:T(8,128)(2,1)S(1)}, bf16[256,320]{1,0:T(8,128)(2,1)S(1)}, u32[]{:S(2)}, u32[]{:S(2)}) collective-permute-start(bf16[256,320]{1,0:T(8,128)(2,1)S(1)} %get-tuple-element.40.normed.refs_5_), channel_id=1, source_target_pairs={{0,8},{4,12},{8,0},{12,4},{1,9},{5,13},{9,1},{13,5},{2,10},{6,14},... | collective-permute-start | bytes 491528 | tf_op jit(solution)/shard_map/ppermute | solution.py:272
  27.6 3.7 %collective-permute-done.7.refs_7_ = bf16[256,320]{1,0:T(8,128)(2,1)S(1)} collective-permute-done((bf16[256,320]{1,0:T(8,128)(2,1)S(1)}, bf16[256,320]{1,0:T(8,128)(2,1)S(1)}, u32[]{:S(2)}, u32[]{:S(2)}) %collective-permute-start.7) | collective-permute-done | bytes 163872 | tf_op jit(solution)/shard_map/ppermute | solution.py:272
  32.0 0.9 %copy-done.13 = bf16[3,80,320]{2,1,0:T(8,128)(2,1)S(1)} copy-done((bf16[3,80,320]{2,1,0:T(8,128)(2,1)S(1)}, bf16[3,80,320]{2,1,0:T(8,128)(2,1)}, u32[]{:S(2)}) %copy-start.13) | copy-done | bytes 153624
  33.7 1.0 %query.1 = (f32[320,256]{1,0:T(8,128)S(1)}, bf16[4,320,320]{2,1,0:T(8,128)(2,1)S(1)}) custom-call(s32[5]{0:T(128)S(1)} %stack.20.where, bf16[256,320]{1,0:T(8,128)(2,1)S(1)} %get-tuple-element.40.normed.refs_5_, bf16[3,80,320]{2,1,0:T(8,128)(2,1)S(1)} %copy-done.13, bf16[80,320]{1,0:T(8,128)(2,1)S(1)} %copy-done.17, ...), custom_call_target="tpu_custom_call" | custom-call | tf_op jit(solution)/shard_map/query/pallas_call | solution.py:439
  34.8 0.9 %copy-done.11 = bf16[256,320]{1,0:T(8,128)(2,1)S(1)} copy-done((bf16[256,320]{1,0:T(8,128)(2,1)S(1)}, bf16[256,320]{1,0:T(8,128)(2,1)}, u32[]{:S(2)}) %copy-start.11) | copy-done | bytes 163864
  35.7 6.1 %cross_view.1 = (bf16[256,320]{1,0:T(8,128)(2,1)S(1)}, bf16[256,320]{1,0:T(8,128)(2,1)S(1)}) custom-call(s32[2]{0:T(128)S(1)} %xor_reduce_fusion.refs_0_, s32[8]{0:T(128)S(1)} %reshape.93.refs_1_, bf16[256,320]{1,0:T(8,128)(2,1)S(1)} %copy-done.11, f32[320,256]{1,0:T(8,128)S(1)} %get-tuple-element.41.refs_3_, ...), custom_call_target="tpu_custom_call" | custom-call | tf_op jit(solution)/shard_map/cross_view/pallas_call | solution.py:450
  42.8 3.3 %collective-permute-start.13 = (bf16[256,320]{1,0:T(8,128)(2,1)S(1)}, bf16[256,320]{1,0:T(8,128)(2,1)S(1)}, u32[]{:S(2)}, u32[]{:S(2)}) collective-permute-start(bf16[256,320]{1,0:T(8,128)(2,1)S(1)} %get-tuple-element.47.rows), channel_id=1, source_target_pairs={{1,0},{2,1},{3,2},{0,3},{5,4},{6,5},{7,6},{4,7},{9,8},{10,9},{11,1... | collective-permute-start | bytes 491528 | tf_op jit(solution)/shard_map/ppermute | solution.py:300
  46.1 5.7 %collective-permute-done.11.rows = bf16[256,320]{1,0:T(8,128)(2,1)S(1)} collective-permute-done((bf16[256,320]{1,0:T(8,128)(2,1)S(1)}, bf16[256,320]{1,0:T(8,128)(2,1)S(1)}, u32[]{:S(2)}, u32[]{:S(2)}) %collective-permute-start.11) | collective-permute-done | bytes 163872 | tf_op jit(solution)/shard_map/ppermute | solution.py:298
  51.9 1.4 %own_frame.1 = (bf16[4,320,320]{2,1,0:T(8,128)(2,1)S(1)}, bf16[256,320]{1,0:T(8,128)(2,1)S(1)}, f32[256,320]{1,0:T(8,128)S(1)}, bf16[256,320]{1,0:T(8,128)(2,1)S(1)}) custom-call(s32[5]{0:T(128)S(1)} %stack.20.where, bf16[256,320]{1,0:T(8,128)(2,1)S(1)} %get-tuple-element.47.rows, bf16[3,80,320]{2,1,0:T(8,128)(2,1)S(1)} %copy-done.3, ...), custom_call_target="tpu_custom_call" | custom-call | flops 209715200 | bytes 1474560 | tf_op jit(solution)/shard_map/own_frame/pallas_call | solution.py:474
  54.6 7.2 %collective-permute-done.12.refs_2_ = bf16[256,320]{1,0:T(8,128)(2,1)S(1)} collective-permute-done((bf16[256,320]{1,0:T(8,128)(2,1)S(1)}, bf16[256,320]{1,0:T(8,128)(2,1)S(1)}, u32[]{:S(2)}, u32[]{:S(2)}) %collective-permute-start.12) | collective-permute-done | bytes 163872 | tf_op jit(solution)/shard_map/ppermute | solution.py:298
  61.8 2.0 %last.1 = bf16[320,256]{1,0:T(8,128)(2,1)} custom-call(bf16[256,320]{1,0:T(8,128)(2,1)S(1)} %get-tuple-element.43.refs_0_, bf16[256,320]{1,0:T(8,128)(2,1)S(1)} %get-tuple-element.51.queries.refs_1_, bf16[256,320]{1,0:T(8,128)(2,1)S(1)} %collective-permute-done.12.refs_2_, bf16[4,320,320]{2,1,0:T(8,128)(2,1)S(1)} %get-tuple-element.52.weights.refs_3_, ...), custom_call_target="tpu_custom_call" | custom-call | tf_op jit(solution)/shard_map/last/pallas_call | solution.py:497
  (65 shorter events, 6.5 us)
Async XLA Ops:
  0.0 31.4 %copy-start = (s32[2,4,2,2]{1,3,2,0:T(2,128)S(1)}, s32[2,4,2,2]{1,3,2,0:T(2,128)}, u32[]{:S(2)}) copy-start(s32[2,4,2,2]{1,3,2,0:T(2,128)} %param.14) | copy-start | bytes 388
  3.5 8.6 %copy-start.3 = (bf16[3,80,320]{2,1,0:T(8,128)(2,1)S(1)}, bf16[3,80,320]{2,1,0:T(8,128)(2,1)}, u32[]{:S(2)}) copy-start(bf16[3,80,320]{2,1,0:T(8,128)(2,1)} %three.5) | copy-start | bytes 460804
  3.5 8.6 %copy-start.8 = (bf16[80,320]{1,0:T(8,128)(2,1)S(1)}, bf16[80,320]{1,0:T(8,128)(2,1)}, u32[]{:S(2)}) copy-start(bf16[80,320]{1,0:T(8,128)(2,1)} %one.5) | copy-start | bytes 153604
  3.6 9.6 %copy-start.14 = (bf16[176,320]{1,0:T(8,128)(2,1)}, bf16[176,320]{1,0:T(8,128)(2,1)S(1)}, u32[]{:S(2)}) copy-start(bf16[176,320]{1,0:T(8,128)(2,1)S(1)} %payload.1.refs_0_) | copy-start | bytes 337924
  3.7 17.9 %copy-start.1 = (bf16[3,3,320,320]{3,2,1,0:T(8,128)(2,1)S(1)}, bf16[3,3,320,320]{3,2,1,0:T(8,128)(2,1)}, u32[]{:S(2)}) copy-start(bf16[3,3,320,320]{3,2,1,0:T(8,128)(2,1)} %param.16) | copy-start | bytes 5529604
  3.7 9.5 %collective-permute-start = (bf16[176,320]{1,0:T(8,128)(2,1)S(1)}, bf16[176,320]{1,0:T(8,128)(2,1)S(1)}, u32[]{:S(2)}, u32[]{:S(2)}) collective-permute-start(bf16[176,320]{1,0:T(8,128)(2,1)S(1)} %payload.1.refs_0_), channel_id=1, source_target_pairs={{0,1},{1,2},{2,3},{3,0},{4,5},{5,6},{6,7},{7,4},{8,9},{9,10},{10,1... | collective-permute-start | bytes 337928 | tf_op jit(solution)/shard_map/ppermute | solution.py:298
  6.7 7.9 %collective-permute-start.1 = (bf16[176,320]{1,0:T(8,128)(2,1)S(1)}, bf16[176,320]{1,0:T(8,128)(2,1)S(1)}, u32[]{:S(2)}, u32[]{:S(2)}) collective-permute-start(bf16[176,320]{1,0:T(8,128)(2,1)S(1)} %payload.1.refs_0_), channel_id=1, source_target_pairs={{1,0},{2,1},{3,2},{0,3},{5,4},{6,5},{7,6},{4,7},{9,8},{10,9},{11,1... | collective-permute-start | bytes 337928 | tf_op jit(solution)/shard_map/ppermute | solution.py:300
  13.2 8.3 %collective-permute-start.2 = (bf16[176,320]{1,0:T(8,128)(2,1)S(1)}, bf16[176,320]{1,0:T(8,128)(2,1)S(1)}, u32[]{:S(2)}, u32[]{:S(2)}) collective-permute-start(bf16[176,320]{1,0:T(8,128)(2,1)S(1)} %collective-permute-done.refs_1_.refs_0_), channel_id=1, source_target_pairs={{0,1},{1,2},{2,3},{3,0},{4,5},{5,6},{6,7},{7,4},{8,9},{9,10},{10,1... | collective-permute-start | bytes 337928 | tf_op jit(solution)/shard_map/ppermute | solution.py:298
  14.7 10.4 %collective-permute-start.3 = (bf16[160,320]{1,0:T(8,128)(2,1)S(1)}, bf16[160,320]{1,0:T(8,128)(2,1)S(1)}, u32[]{:S(2)}, u32[]{:S(2)}) collective-permute-start(bf16[160,320]{1,0:T(8,128)(2,1)S(1)} %dynamic-slice_bitcast_fusion), channel_id=1, source_target_pairs={{0,1},{1,2},{2,3},{3,0},{4,5},{5,6},{6,7},{7,4},{8,9},{9,10},{10,1... | collective-permute-start | bytes 307208 | tf_op jit(solution)/shard_map/ppermute | solution.py:298
  16.5 8.6 %collective-permute-start.4 = (bf16[160,320]{1,0:T(8,128)(2,1)S(1)}, bf16[160,320]{1,0:T(8,128)(2,1)S(1)}, u32[]{:S(2)}, u32[]{:S(2)}) collective-permute-start(bf16[160,320]{1,0:T(8,128)(2,1)S(1)} %dynamic-slice_bitcast_fusion), channel_id=1, source_target_pairs={{1,0},{2,1},{3,2},{0,3},{5,4},{6,5},{7,6},{4,7},{9,8},{10,9},{11,1... | collective-permute-start | bytes 307208 | tf_op jit(solution)/shard_map/ppermute | solution.py:300
  18.6 13.2 %copy-start.19 = (s32[2,4]{1,0:T(2,128)S(1)}, s32[2,4]{1,0:T(2,128)}, u32[]{:S(2)}) copy-start(s32[2,4]{1,0:T(2,128)} %param.13) | copy-start | bytes 100
  25.1 6.2 %copy-start.10 = (bf16[256,320]{1,0:T(8,128)(2,1)}, bf16[256,320]{1,0:T(8,128)(2,1)S(1)}, u32[]{:S(2)}) copy-start(bf16[256,320]{1,0:T(8,128)(2,1)S(1)} %get-tuple-element.39.refs_2_) | copy-start | bytes 491524
  25.1 6.1 %copy-start.6 = (bf16[160,320]{1,0:T(8,128)(2,1)}, bf16[160,320]{1,0:T(8,128)(2,1)S(1)}, u32[]{:S(2)}) copy-start(bf16[160,320]{1,0:T(8,128)(2,1)S(1)} %collective-permute-done.4.refs_2_) | copy-start | bytes 307204
  25.1 6.1 %collective-permute-start.7 = (bf16[256,320]{1,0:T(8,128)(2,1)S(1)}, bf16[256,320]{1,0:T(8,128)(2,1)S(1)}, u32[]{:S(2)}, u32[]{:S(2)}) collective-permute-start(bf16[256,320]{1,0:T(8,128)(2,1)S(1)} %get-tuple-element.40.normed.refs_5_), channel_id=1, source_target_pairs={{0,8},{4,12},{8,0},{12,4},{1,9},{5,13},{9,1},{13,5},{2,10},{6,14},... | collective-permute-start | bytes 491528 | tf_op jit(solution)/shard_map/ppermute | solution.py:272
  27.0 24.9 %copy-start.9 = (bf16[80,320]{1,0:T(8,128)(2,1)S(1)}, bf16[80,320]{1,0:T(8,128)(2,1)}, u32[]{:S(2)}) copy-start(bf16[80,320]{1,0:T(8,128)(2,1)} %one.5) | copy-start | bytes 153604
  27.0 5.0 %collective-permute-start.5 = (bf16[480,320]{1,0:T(8,128)(2,1)S(1)}, bf16[480,320]{1,0:T(8,128)(2,1)S(1)}, u32[]{:S(2)}, u32[]{:S(2)}) collective-permute-start(bf16[480,320]{1,0:T(8,128)(2,1)S(1)} %pad_maximum_fusion), channel_id=1, source_target_pairs={{0,4},{4,0},{8,12},{12,8},{1,5},{5,1},{9,13},{13,9},{2,6},{6,2},{1... | collective-permute-start | bytes 921608 | tf_op jit(solution)/shard_map/ppermute | solution.py:320
  27.1 7.7 %collective-permute-start.6 = (bf16[256,320]{1,0:T(8,128)(2,1)S(1)}, bf16[256,320]{1,0:T(8,128)(2,1)S(1)}, u32[]{:S(2)}, u32[]{:S(2)}) collective-permute-start(bf16[256,320]{1,0:T(8,128)(2,1)S(1)} %get-tuple-element.40.normed.refs_5_), channel_id=1, source_target_pairs={{0,4},{4,0},{8,12},{12,8},{1,5},{5,1},{9,13},{13,9},{2,6},{6,2},{1... | collective-permute-start | bytes 491528 | tf_op jit(solution)/shard_map/ppermute | solution.py:272
  31.2 3.5 %collective-permute-start.8 = (bf16[256,320]{1,0:T(8,128)(2,1)S(1)}, bf16[256,320]{1,0:T(8,128)(2,1)S(1)}, u32[]{:S(2)}, u32[]{:S(2)}) collective-permute-start(bf16[256,320]{1,0:T(8,128)(2,1)S(1)} %collective-permute-done.7.refs_7_), channel_id=1, source_target_pairs={{0,4},{4,0},{8,12},{12,8},{1,5},{5,1},{9,13},{13,9},{2,6},{6,2},{1... | collective-permute-start | bytes 491528 | tf_op jit(solution)/shard_map/ppermute | solution.py:272
  31.3 10.5 %copy-start.7 = (bf16[160,320]{1,0:T(8,128)(2,1)S(1)}, bf16[160,320]{1,0:T(8,128)(2,1)}, u32[]{:S(2)}) copy-start(bf16[160,320]{1,0:T(8,128)(2,1)} %copy-done.6) | copy-start | bytes 307204
  31.3 10.5 %collective-permute-start.9 = (bf16[160,320]{1,0:T(8,128)(2,1)S(1)}, bf16[160,320]{1,0:T(8,128)(2,1)S(1)}, u32[]{:S(2)}, u32[]{:S(2)}) collective-permute-start(bf16[160,320]{1,0:T(8,128)(2,1)S(1)} %collective-permute-done.3.refs_0_), channel_id=1, source_target_pairs={{0,1},{1,2},{2,3},{3,0},{4,5},{5,6},{6,7},{7,4},{8,9},{9,10},{10,1... | collective-permute-start | bytes 307208 | tf_op jit(solution)/shard_map/ppermute | solution.py:298
  41.8 10.0 %collective-permute-start.10 = (bf16[480,320]{1,0:T(8,128)(2,1)S(1)}, bf16[480,320]{1,0:T(8,128)(2,1)S(1)}, u32[]{:S(2)}, u32[]{:S(2)}) collective-permute-start(bf16[480,320]{1,0:T(8,128)(2,1)S(1)} %pad_maximum_fusion.1), channel_id=1, source_target_pairs={{0,4},{4,0},{8,12},{12,8},{1,5},{5,1},{9,13},{13,9},{2,6},{6,2},{1... | collective-permute-start | bytes 921608 | tf_op jit(solution)/shard_map/ppermute | solution.py:320
  42.3 9.6 %collective-permute-start.11 = (bf16[256,320]{1,0:T(8,128)(2,1)S(1)}, bf16[256,320]{1,0:T(8,128)(2,1)S(1)}, u32[]{:S(2)}, u32[]{:S(2)}) collective-permute-start(bf16[256,320]{1,0:T(8,128)(2,1)S(1)} %get-tuple-element.47.rows), channel_id=1, source_target_pairs={{0,1},{1,2},{2,3},{3,0},{4,5},{5,6},{6,7},{7,4},{8,9},{9,10},{10,1... | collective-permute-start | bytes 491528 | tf_op jit(solution)/shard_map/ppermute | solution.py:298
  42.8 11.1 %collective-permute-start.13 = (bf16[256,320]{1,0:T(8,128)(2,1)S(1)}, bf16[256,320]{1,0:T(8,128)(2,1)S(1)}, u32[]{:S(2)}, u32[]{:S(2)}) collective-permute-start(bf16[256,320]{1,0:T(8,128)(2,1)S(1)} %get-tuple-element.47.rows), channel_id=1, source_target_pairs={{1,0},{2,1},{3,2},{0,3},{5,4},{6,5},{7,6},{4,7},{9,8},{10,9},{11,1... | collective-permute-start | bytes 491528 | tf_op jit(solution)/shard_map/ppermute | solution.py:300
  51.8 10.0 %collective-permute-start.12 = (bf16[256,320]{1,0:T(8,128)(2,1)S(1)}, bf16[256,320]{1,0:T(8,128)(2,1)S(1)}, u32[]{:S(2)}, u32[]{:S(2)}) collective-permute-start(bf16[256,320]{1,0:T(8,128)(2,1)S(1)} %collective-permute-done.11.rows), channel_id=1, source_target_pairs={{0,1},{1,2},{2,3},{3,0},{4,5},{5,6},{6,7},{7,4},{8,9},{9,10},{10,1... | collective-permute-start | bytes 491528 | tf_op jit(solution)/shard_map/ppermute | solution.py:298
  (10 other events, 14.2 us)

commit v6 on v5

--- a/solution.py
+++ b/solution.py
@@ -21,12 +21,23 @@
 
 VMEM = pl.BlockSpec(memory_space=pltpu.VMEM)
 SMEM = pl.BlockSpec(memory_space=pltpu.SMEM)
+HBM = pl.BlockSpec(memory_space=pl.ANY)
 f32 = jnp.float32
 bf16 = jnp.bfloat16
 
 
 def params():
     return pltpu.CompilerParams(vmem_limit_bytes=16 * 1024 * 1024)
+
+
+def in_hbm(x):
+    return pltpu.with_memory_space_constraint(x, pltpu.HBM)
+
+
+def fetch(source, target, sem):
+    copy = pltpu.make_async_copy(source, target, sem)
+    copy.start()
+    return copy
 
 
 def dot(a, b):
@@ -75,7 +86,7 @@
     return centred * lax.rsqrt(spread + EPSILON)
 
 
-def convolve(y, weight, padded):
+def convolve(y, weight, padded, copies):
     tokens, channels = y.shape
     column = lax.broadcasted_iota(jnp.int32, (tokens, 1), 0) & (W - 1)
     before = jnp.where(column == 0, 0.0, pltpu.roll(y, 1, 0))
@@ -87,6 +98,8 @@
     )
     total = None
     for k in range(3):
+        if copies:
+            copies[k].wait()
         part = dot(padded[pl.ds(k * W, tokens), :], weight[k])
         total = part if total is None else total + part
     return total
@@ -96,68 +109,79 @@
     share[...] = dot(act[...], proj[...])
 
 
-def payload_kernel(side, act, proj, three, one, payload):
+def payload_kernel(side, act, proj_hbm, three, one, payload, proj, sems):
     rows, channels = one.shape
-    share = dot(act[...], proj[...])
-    payload[pl.ds(2 * rows, SHARE_ROWS), :] = terms(share).astype(bf16)
+    copy = fetch(proj_hbm, proj, sems.at[0])
+    upper, lower = payload.at[pl.ds(0, rows)], payload.at[pl.ds(rows, rows)]
 
     @pl.when(side[0] == 0)
     def _():
-        payload[pl.ds(0, rows), :] = three[0]
-        payload[pl.ds(rows, rows), :] = three[1]
+        fetch(three.at[0], upper, sems.at[1])
+        fetch(three.at[1], lower, sems.at[2])
 
     @pl.when(side[0] != 0)
     def _():
-        payload[pl.ds(0, rows), :] = three[2]
-        payload[pl.ds(rows, rows), :] = one[...]
-
-
-def first_kernel(source, weight, inner, padded):
-    inner[...] = convolve(group_norm_silu(source[...].astype(f32).T), weight, padded)
-
-
-def second_kernel(source, inner, weight, *refs):
-    shares, (hidden, normed, padded) = refs[:-3], refs[-3:]
+        fetch(three.at[2], upper, sems.at[1])
+        fetch(one, lower, sems.at[2])
+
+    copy.wait()
+    payload[pl.ds(2 * rows, SHARE_ROWS), :] = terms(dot(act[...], proj[...])).astype(bf16)
+    pltpu.make_async_copy(one, upper, sems.at[1]).wait()
+    pltpu.make_async_copy(one, lower, sems.at[2]).wait()
+
+
+def first_kernel(source_hbm, weight_hbm, inner, source, weight, padded, sems):
+    copy = fetch(source_hbm, source, sems.at[0])
+    copies = [fetch(weight_hbm.at[k], weight.at[k], sems.at[1 + k]) for k in range(3)]
+    copy.wait()
+    inner[...] = convolve(group_norm_silu(source[...].astype(f32).T), weight, padded, copies)
+
+
+def second_kernel(source_hbm, inner, weight, *refs):
+    shares, (hidden, normed, source, padded, sems) = refs[:-5], refs[-5:]
+    copy = fetch(source_hbm, source, sems.at[0])
     bias = None
     for share in shares:
         rows = min(SHARE_ROWS, share.shape[0])
         part = jnp.sum(share[pl.ds(share.shape[0] - rows, rows), :].astype(f32), axis=0, keepdims=True)
         bias = part if bias is None else bias + part
     y = group_norm_silu(inner[...] + bias)
-    total = source[...].astype(f32).T + convolve(y, weight, padded)
-    rounded = total.astype(bf16)
+    total = convolve(y, weight, padded, [])
+    copy.wait()
+    rounded = (source[...].astype(f32).T + total).astype(bf16)
     hidden[...] = rounded
     normed[...] = layer_norm(rounded.astype(f32)).astype(bf16)
 
 
-def assemble(where, own, received, swapped, whole):
-    rows = own[0].shape[0]
-    for kind in range(4):
-        whole[kind, pl.ds(pl.multiple_of(where[0] * rows, 16), rows), :] = own[kind]
-    count = len(received)
+def fetch_own(where, three, one, whole, sems):
+    rows = one.shape[0]
+    place = pl.ds(pl.multiple_of(where[0] * rows, 16), rows)
+    copies = [fetch(three.at[k], whole.at[k, place], sems.at[k]) for k in range(3)]
+    return copies + [fetch(one, whole.at[3, place], sems.at[3])]
+
+
+def query_kernel(where, normed, three, one, *refs):
+    parts, (queries, epi, sems) = refs[:-3], refs[-3:]
+    copies = fetch_own(where, three, one, epi, sems)
+    rows = one.shape[0]
+    count = len(parts) - 1
     for k in range(1, count + 1):
         place = pl.ds(pl.multiple_of(where[k] * rows, 16), rows)
         for j in range(2):
             mine = where[count + 1] * 2 + j
-            whole[mine, place, :] = received[k - 1][pl.ds(j * rows, rows), :]
+            epi[mine, place, :] = parts[k - 1][pl.ds(j * rows, rows), :]
             start = ((k - 1) * 2 + j) * rows
-            whole[2 - mine + 2 * j, place, :] = swapped[pl.ds(start, rows), :]
-
-
-def own_rows(three, one):
-    return [three[0], three[1], three[2], one[...]]
-
-
-def query_kernel(where, normed, three, one, *refs):
-    parts, (queries, epi) = refs[:-2], refs[-2:]
-    assemble(where, own_rows(three, one), parts[:-1], parts[-1] if parts else None, epi)
+            epi[2 - mine + 2 * j, place, :] = parts[-1][pl.ds(start, rows), :]
+    for copy in copies:
+        copy.wait()
     queries[...] = dot(normed[...], epi[0]).astype(bf16).astype(f32).T
 
 
 def view_kernel(count, tiles, *refs):
-    select, mask, hidden, query_ref, weights = refs[:5]
+    select, mask, hidden_ref, query_ref, weights = refs[:5]
     maps = refs[5 : 5 + count]
-    second, blocks, chosen, totals = refs[5 + count :]
+    second, blocks, chosen, totals, hidden, sem = refs[5 + count :]
+    copy = fetch(hidden_ref, hidden, sem)
     tokens, channels = hidden.shape
     head = channels // HEADS
     width = tokens // tiles
@@ -202,6 +226,7 @@
             else:
                 totals[pl.ds(h * head, head), :] += part
     mixture = totals[...].T.astype(bf16)
+    copy.wait()
     result = (hidden[...].astype(f32) + dot(mixture, weights[3])).astype(bf16)
     second[...] = result
     blocks[...] = layer_norm(result.astype(f32)).astype(bf16)
@@ -220,8 +245,15 @@
 
 
 def own_frame_kernel(where, rows, three, one, *refs):
-    parts, (weights, queries, scores, values) = refs[:-4], refs[-4:]
-    assemble(where, own_rows(three, one), parts[:-1], parts[-1] if parts else None, weights)
+    parts, (weights, queries, scores, values, sems) = refs[:-5], refs[-5:]
+    copies = fetch_own(where, three, one, weights, sems)
+    height = one.shape[0]
+    for k, part in enumerate(parts):
+        place = pl.ds(pl.multiple_of(where[k + 1] * height, 16), height)
+        for kind in range(4):
+            weights[kind, place, :] = part[pl.ds(kind * height, height), :]
+    for copy in copies:
+        copy.wait()
     queries[...] = dot(rows[...], weights[0]).astype(bf16)
     scores[...], values[...] = frame_part(queries[...].astype(f32), rows[...], weights)
 
@@ -358,12 +390,16 @@
         payload = pl.pallas_call(
             payload_kernel,
             out_shape=jax.ShapeDtypeStruct((2 * height + SHARE_ROWS, channels), bf16),
-            in_specs=[SMEM, VMEM, VMEM, VMEM, VMEM],
+            in_specs=[SMEM, VMEM, HBM, HBM, HBM],
             out_specs=VMEM,
+            scratch_shapes=[
+                pltpu.VMEM(time_proj.shape, bf16),
+                pltpu.SemaphoreType.DMA((3,)),
+            ],
             compiler_params=params(),
             cost_estimate=early,
             name="payload",
-        )(side, time_act, time_proj, epi_in, epi_out)
+        )(side, time_act, in_hbm(time_proj), in_hbm(epi_in), in_hbm(epi_out))
         shares = [payload]
         places = [(frame - k) % frames for k in range(frames)] + [video % 2]
     else:
@@ -384,9 +420,8 @@
         temp_out = lax.all_gather(temp_out, "frame", axis=0, tiled=True)
     places = jnp.stack(places).astype(jnp.int32)
 
-    conv_scratch = [
-        pltpu.VMEM((tokens + 2 * W, 3 * channels), bf16),
-    ]
+    source_scratch = pltpu.VMEM((channels, tokens), bf16)
+    padded_scratch = pltpu.VMEM((tokens + 2 * W, 3 * channels), bf16)
     conv_cost = pl.CostEstimate(
         flops=2 * 9 * tokens * channels * channels,
         bytes_accessed=2 * 9 * channels * channels + 8 * tokens * channels,
@@ -395,19 +430,22 @@
     inner = pl.pallas_call(
         first_kernel,
         out_shape=jax.ShapeDtypeStruct((tokens, channels), f32),
-        in_specs=[VMEM, VMEM],
+        in_specs=[HBM, HBM],
         out_specs=VMEM,
-        scratch_shapes=conv_scratch,
+        scratch_shapes=[
+            source_scratch,
+            pltpu.VMEM((3, 3 * channels, channels), bf16),
+            padded_scratch,
+            pltpu.SemaphoreType.DMA((4,)),
+        ],
         compiler_params=params(),
         cost_estimate=conv_cost,
         name="first_conv",
-    )(source, conv_first.reshape(3, 3 * channels, channels))
+    )(in_hbm(source), in_hbm(conv_first.reshape(3, 3 * channels, channels)))
     temp_parts = []
     if paired:
         shares, inner = ring_gather(shares[0], "frame", frames, inner)
-        temp_own = jnp.concatenate([temp_in, temp_out[None]], axis=0)
-        temp_own = temp_own.reshape(2, 2 * height, channels)
-        mine = lax.dynamic_index_in_dim(temp_own, video % 2, 0, keepdims=False)
+        mine = jnp.concatenate([temp_in, temp_out[None]], axis=0).reshape(4 * height, channels)
         mine, *near = lax.optimization_barrier((mine, *neighbours(shares)))
         shares = with_neighbours(shares, near)
         temp_parts = ring_gather(mine, "frame", frames)
@@ -417,16 +455,13 @@
             jax.ShapeDtypeStruct((tokens, channels), bf16),
             jax.ShapeDtypeStruct((tokens, channels), bf16),
         ],
-        in_specs=[VMEM] * (3 + len(shares)),
+        in_specs=[HBM] + [VMEM] * (2 + len(shares)),
         out_specs=[VMEM] * 2,
-        scratch_shapes=conv_scratch,
+        scratch_shapes=[source_scratch, padded_scratch, pltpu.SemaphoreType.DMA((1,))],
         compiler_params=params(),
         cost_estimate=conv_cost,
         name="second_conv",
-    )(source, inner, conv_second.reshape(3, 3 * channels, channels), *shares)
-    if paired:
-        normed, hidden, *near = lax.optimization_barrier((normed, hidden, *neighbours(temp_parts)))
-        temp_parts = with_neighbours(temp_parts, near)
+    )(in_hbm(source), inner, conv_second.reshape(3, 3 * channels, channels), *shares)
     maps = gather_maps(normed, "video", videos)
     epi_parts = swap(shares, 2 * height, videos) if paired else []
     targets = lax.dynamic_index_in_dim(matchings, video, 1, keepdims=False)
@@ -442,19 +477,25 @@
             jax.ShapeDtypeStruct((channels, tokens), f32),
             jax.ShapeDtypeStruct(square, bf16),
         ],
-        in_specs=[SMEM, VMEM, VMEM, VMEM] + [VMEM] * len(epi_parts),
+        in_specs=[SMEM, VMEM, HBM, HBM] + [VMEM] * len(epi_parts),
         out_specs=[VMEM] * 2,
+        scratch_shapes=[pltpu.SemaphoreType.DMA((4,))],
         compiler_params=params(),
         name="query",
-    )(places, normed, epi_in, epi_out, *epi_parts)
+    )(places, normed, in_hbm(epi_in), in_hbm(epi_out), *epi_parts)
+    if paired:
+        queries, *near = lax.optimization_barrier((queries, *neighbours(temp_parts)))
+        temp_parts = with_neighbours(temp_parts, near)
     second, blocks = pl.pallas_call(
         functools.partial(view_kernel, videos, tiles),
         out_shape=[jax.ShapeDtypeStruct((tokens, channels), bf16)] * 2,
-        in_specs=[SMEM, SMEM, VMEM, VMEM, VMEM] + [VMEM] * videos,
+        in_specs=[SMEM, SMEM, HBM, VMEM, VMEM] + [VMEM] * videos,
         out_specs=[VMEM, VMEM],
         scratch_shapes=[
             pltpu.VMEM((tokens, channels), bf16),
             pltpu.VMEM((channels, tokens), f32),
+            pltpu.VMEM((tokens, channels), bf16),
+            pltpu.SemaphoreType.DMA,
         ],
         compiler_params=params(),
         name="cross_view",
@@ -462,7 +503,7 @@
 
     if paired:
         blocks, *temp_parts = lax.optimization_barrier((blocks, *temp_parts))
-        temp_parts = swap(temp_parts, 2 * height, videos)
+        temp_parts = temp_parts[1:]
     arrived = ring_gather(blocks, "frame", frames)
     score_shape = jax.ShapeDtypeStruct((tokens, channels), f32)
     value_shape = jax.ShapeDtypeStruct((tokens, channels), bf16)
@@ -474,12 +515,13 @@
     temp, frame_queries, *first = pl.pallas_call(
         own_frame_kernel,
         out_shape=[jax.ShapeDtypeStruct(square, bf16), value_shape, score_shape, value_shape],
-        in_specs=[SMEM, VMEM, VMEM, VMEM] + [VMEM] * len(temp_parts),
+        in_specs=[SMEM, VMEM, HBM, HBM] + [VMEM] * len(temp_parts),
         out_specs=[VMEM] * 4,
+        scratch_shapes=[pltpu.SemaphoreType.DMA((4,))],
         compiler_params=params(),
         cost_estimate=frame_cost,
         name="own_frame",
-    )(places, blocks, temp_in, temp_out, *temp_parts)
+    )(places, blocks, in_hbm(temp_in), in_hbm(temp_out), *temp_parts)
     scores, values = [first[0]], [first[1]]
     order = sorted(range(1, frames), key=lambda k: min(k, frames - k))
     for k in order[:-1]:

time: 64.2 us -> 63.6 us (level)
  local copies, waits for them, and re-layouts: 9.3 us -> 0.45 us
  Pallas kernels: 15.3 us -> 20.4 us
  waiting for transfers between devices: 22.1 us -> 26.5 us
  starting transfers between devices: 15.7 us -> 14.7 us
    unnamed x40 -> x10, local copies, waits for them, and re-layouts: 8.86 us -> 0.03 us
    ppermute x3, waiting for transfers between devices: 1.47 us -> 8.8 us  [ring_gather(): lax.ppermute(pieces[(size - step + 1) % size], axis, left)]
    ppermute x3, waiting for transfers between devices: 3.7 us -> 1.7 us  [gather_maps(): maps[k | bit] = lax.ppermute(maps[k], axis, partner_permutation(size, bit))]
    pallas_call x1, Pallas kernels: 1.63 us -> 2.83 us  [per_device(): pl.pallas_call(first_kernel, out_shape=jax.ShapeDtypeStruct((tokens, chan...]
    ppermute x6, waiting for transfers between devices: 17 us -> 16 us  [ring_gather(): pieces[step] = lax.ppermute(pieces[step - 1], axis, right)]
    pallas_call x1, Pallas kernels: 0.16 us -> 1.14 us  [per_device(): pl.pallas_call(payload_kernel, out_shape=jax.ShapeDtypeStruct((2 * height...]
    pallas_call x1, Pallas kernels: 0.98 us -> 1.86 us  [per_device(): pl.pallas_call(query_kernel, out_shape=[jax.ShapeDtypeStruct((channels, t...]
    pallas_call x1, Pallas kernels: 1.39 us -> 2.26 us  [per_device(): pl.pallas_call(own_frame_kernel, out_shape=[jax.ShapeDtypeStruct(square,...]
  transfers between devices with their start and end apart: 14 -> 13, of which waited for: 6 -> 7; matrix products, arithmetic and copies ran while one was open for 1% -> 1% of each run, Pallas kernels for 20% -> 27%
where the time goes in v6:
time: 63.6 us; the launch traced here: 63.3 us
  waiting for transfers between devices  26.5 us (42%)
  Pallas kernels  20.4 us (32%)
  starting transfers between devices  14.7 us (23%)
  between operations  0.86 us (1%)
    ppermute x6, waiting for transfers between devices, ring_gather(): pieces[step] = lax.ppermute(pieces[step - 1], axis, right)  16 us
    ppermute x3, waiting for transfers between devices, ring_gather(): lax.ppermute(pieces[(size - step + 1) % size], axis, left)  8.8 us
    ppermute x3, starting transfers between devices, ring_gather(): lax.ppermute(pieces[(size - step + 1) % size], axis, left)  7.11 us
    pallas_call x1, Pallas kernels, per_device(): pl.pallas_call(functools.partial(view_kernel, videos, tiles), out_shape=[...  6.46 us
    ppermute x6, starting transfers between devices, ring_gather(): pieces[step] = lax.ppermute(pieces[step - 1], axis, right)  5.73 us
    pallas_call x1, Pallas kernels, per_device(): pl.pallas_call(first_kernel, out_shape=jax.ShapeDtypeStruct((tokens, chan...  2.83 us
    pallas_call x1, Pallas kernels, per_device(): pl.pallas_call(second_kernel, out_shape=[jax.ShapeDtypeStruct((tokens, ch...  2.57 us
    pallas_call x1, Pallas kernels, per_device(): pl.pallas_call(own_frame_kernel, out_shape=[jax.ShapeDtypeStruct(square,...  2.26 us
  transfers between devices with their start and end apart: 13, of which 7 were waited for; matrix products, arithmetic and copies ran while one was open for 1% of the time, Pallas kernels for 27%

profile of v6, /device:TPU:0, one launch (start us, length us, event | category | flops | bytes accessed | tf_op | source)
XLA Modules:
  0.0 63.3 jit_solution(4433519040767531529)
XLA Ops:
  0.8 1.1 %payload.1.refs_0_ = bf16[176,320]{1,0:T(8,128)(2,1)S(1)} custom-call(s32[1]{0:T(128)} %bitcast.2.side, bf16[1,320]{1,0:T(2,128)(2,1)S(1)} %fusion.4.act, bf16[320,320]{1,0:T(8,128)(2,1)} %proj_hbm.1, bf16[3,80,320]{2,1,0:T(8,128)(2,1)} %three.4, bf16[80,320]{1,0:T(8,128)(2,1)} %one.4), custom_call_target="tpu_custom_call" | custom-call | flops 10000000000 | bytes 1048576 | tf_op jit(solution)/shard_map/payload/pallas_call | solution.py:390
  1.9 3.1 %collective-permute-start = (bf16[176,320]{1,0:T(8,128)(2,1)S(1)}, bf16[176,320]{1,0:T(8,128)(2,1)S(1)}, u32[]{:S(2)}, u32[]{:S(2)}) collective-permute-start(bf16[176,320]{1,0:T(8,128)(2,1)S(1)} %payload.1.refs_0_), channel_id=1, source_target_pairs={{0,1},{1,2},{2,3},{3,0},{4,5},{5,6},{6,7},{7,4},{8,9},{9,10},{10,1... | collective-permute-start | bytes 337928 | tf_op jit(solution)/shard_map/ppermute | solution.py:330
  5.0 2.1 %collective-permute-start.1 = (bf16[176,320]{1,0:T(8,128)(2,1)S(1)}, bf16[176,320]{1,0:T(8,128)(2,1)S(1)}, u32[]{:S(2)}, u32[]{:S(2)}) collective-permute-start(bf16[176,320]{1,0:T(8,128)(2,1)S(1)} %payload.1.refs_0_), channel_id=1, source_target_pairs={{1,0},{2,1},{3,2},{0,3},{5,4},{6,5},{7,6},{4,7},{9,8},{10,9},{11,1... | collective-permute-start | bytes 337928 | tf_op jit(solution)/shard_map/ppermute | solution.py:332
  7.1 2.8 %first_conv.1.inner = f32[256,320]{1,0:T(8,128)S(1)} custom-call(bf16[320,256]{1,0:T(8,128)(2,1)} %bitcast.18, bf16[3,960,320]{2,1,0:T(8,128)(2,1)} %bitcast.17), custom_call_target="tpu_custom_call" | custom-call | flops 471859200 | bytes 2498560 | tf_op jit(solution)/shard_map/first_conv/pallas_call | solution.py:430
  10.0 1.5 %collective-permute-done.refs_1_.refs_0_ = bf16[176,320]{1,0:T(8,128)(2,1)S(1)} collective-permute-done((bf16[176,320]{1,0:T(8,128)(2,1)S(1)}, bf16[176,320]{1,0:T(8,128)(2,1)S(1)}, u32[]{:S(2)}, u32[]{:S(2)}) %collective-permute-start) | collective-permute-done | bytes 112672 | tf_op jit(solution)/shard_map/ppermute | solution.py:330
  11.5 1.4 %collective-permute-done.1.refs_3_.refs_2_ = bf16[176,320]{1,0:T(8,128)(2,1)S(1)} collective-permute-done((bf16[176,320]{1,0:T(8,128)(2,1)S(1)}, bf16[176,320]{1,0:T(8,128)(2,1)S(1)}, u32[]{:S(2)}, u32[]{:S(2)}) %collective-permute-start.1) | collective-permute-done | bytes 112672 | tf_op jit(solution)/shard_map/ppermute | solution.py:332
  13.0 1.7 %collective-permute-start.4 = (bf16[320,320]{1,0:T(8,128)(2,1)S(1)}, bf16[320,320]{1,0:T(8,128)(2,1)S(1)}, u32[]{:S(2)}, u32[]{:S(2)}) collective-permute-start(bf16[320,320]{1,0:T(8,128)(2,1)S(1)} %bitcast.20), channel_id=1, source_target_pairs={{0,1},{1,2},{2,3},{3,0},{4,5},{5,6},{6,7},{7,4},{8,9},{9,10},{10,1... | collective-permute-start | bytes 614408 | tf_op jit(solution)/shard_map/ppermute | solution.py:330
  14.7 5.0 %collective-permute-done.2.refs_2_.refs_1_ = bf16[176,320]{1,0:T(8,128)(2,1)S(1)} collective-permute-done((bf16[176,320]{1,0:T(8,128)(2,1)S(1)}, bf16[176,320]{1,0:T(8,128)(2,1)S(1)}, u32[]{:S(2)}, u32[]{:S(2)}) %collective-permute-start.2) | collective-permute-done | bytes 112672 | tf_op jit(solution)/shard_map/ppermute | solution.py:330
  19.7 2.6 %second_conv.1 = (bf16[256,320]{1,0:T(8,128)(2,1)S(1)}, bf16[256,320]{1,0:T(8,128)(2,1)S(1)}) custom-call(bf16[320,256]{1,0:T(8,128)(2,1)} %bitcast.19, f32[256,320]{1,0:T(8,128)S(1)} %first_conv.1.inner, bf16[3,960,320]{2,1,0:T(8,128)(2,1)S(1)} %bitcast.16, bf16[176,320]{1,0:T(8,128)(2,1)S(1)} %payload.1.refs_0_, ...), custom_call_target="tpu_custom_call" | custom-call | flops 471859200 | bytes 2498560 | tf_op jit(solution)/shard_map/second_conv/pallas_call | solution.py:452
  22.3 1.8 %collective-permute-start.7 = (bf16[256,320]{1,0:T(8,128)(2,1)S(1)}, bf16[256,320]{1,0:T(8,128)(2,1)S(1)}, u32[]{:S(2)}, u32[]{:S(2)}) collective-permute-start(bf16[256,320]{1,0:T(8,128)(2,1)S(1)} %get-tuple-element.36.normed.refs_5_), channel_id=1, source_target_pairs={{0,8},{4,12},{8,0},{12,4},{1,9},{5,13},{9,1},{13,5},{2,10},{6,14},... | collective-permute-start | bytes 491528 | tf_op jit(solution)/shard_map/ppermute | solution.py:304
  24.2 1.2 %collective-permute-start.5 = (bf16[320,320]{1,0:T(8,128)(2,1)S(1)}, bf16[320,320]{1,0:T(8,128)(2,1)S(1)}, u32[]{:S(2)}, u32[]{:S(2)}) collective-permute-start(bf16[320,320]{1,0:T(8,128)(2,1)S(1)} %bitcast.21), channel_id=1, source_target_pairs={{1,0},{2,1},{3,2},{0,3},{5,4},{6,5},{7,6},{4,7},{9,8},{10,9},{11,1... | collective-permute-start | bytes 614408 | tf_op jit(solution)/shard_map/ppermute | solution.py:332
  25.5 0.9 %collective-permute-start.9 = (bf16[320,320]{1,0:T(8,128)(2,1)S(1)}, bf16[320,320]{1,0:T(8,128)(2,1)S(1)}, u32[]{:S(2)}, u32[]{:S(2)}) collective-permute-start(bf16[320,320]{1,0:T(8,128)(2,1)S(1)} %collective-permute-done.4.refs_0_), channel_id=1, source_target_pairs={{0,1},{1,2},{2,3},{3,0},{4,5},{5,6},{6,7},{7,4},{8,9},{9,10},{10,1... | collective-permute-start | bytes 614408 | tf_op jit(solution)/shard_map/ppermute | solution.py:330
  26.3 1.7 %collective-permute-done.7.refs_7_ = bf16[256,320]{1,0:T(8,128)(2,1)S(1)} collective-permute-done((bf16[256,320]{1,0:T(8,128)(2,1)S(1)}, bf16[256,320]{1,0:T(8,128)(2,1)S(1)}, u32[]{:S(2)}, u32[]{:S(2)}) %collective-permute-start.7) | collective-permute-done | bytes 163872 | tf_op jit(solution)/shard_map/ppermute | solution.py:304
  28.0 0.2 dynamic-slice_reduce_fusion
  28.6 1.9 %query.1 = (f32[320,256]{1,0:T(8,128)S(1)}, bf16[4,320,320]{2,1,0:T(8,128)(2,1)S(1)}) custom-call(s32[5]{0:T(128)S(1)} %stack.20.where, bf16[256,320]{1,0:T(8,128)(2,1)S(1)} %get-tuple-element.36.normed.refs_5_, bf16[3,80,320]{2,1,0:T(8,128)(2,1)} %three.4, bf16[80,320]{1,0:T(8,128)(2,1)} %one.4, bf16[176,320]{1,0:T(8,128)(2,1)S(1)} %collective-permute-done.refs_1_.refs_0_, ...), custom_call_target="tpu_custom_call" | custom-call | tf_op jit(solution)/shard_map/query/pallas_call | solution.py:474
  30.5 7.4 %collective-permute-done.5.refs_2_ = bf16[320,320]{1,0:T(8,128)(2,1)S(1)} collective-permute-done((bf16[320,320]{1,0:T(8,128)(2,1)S(1)}, bf16[320,320]{1,0:T(8,128)(2,1)S(1)}, u32[]{:S(2)}, u32[]{:S(2)}) %collective-permute-start.5) | collective-permute-done | bytes 204832 | tf_op jit(solution)/shard_map/ppermute | solution.py:332
  37.9 6.5 %cross_view.1 = (bf16[256,320]{1,0:T(8,128)(2,1)S(1)}, bf16[256,320]{1,0:T(8,128)(2,1)S(1)}) custom-call(s32[2]{0:T(128)S(1)} %xor_reduce_fusion.refs_0_, s32[8]{0:T(128)S(1)} %reshape.93.refs_1_, bf16[256,320]{1,0:T(8,128)(2,1)S(1)} %get-tuple-element.35.refs_2_, f32[320,256]{1,0:T(8,128)S(1)} %get-tuple-element.39.refs_3_, ...), custom_call_target="tpu_custom_call" | custom-call | tf_op jit(solution)/shard_map/cross_view/pallas_call | solution.py:489
  44.4 3.8 %collective-permute-start.12 = (bf16[256,320]{1,0:T(8,128)(2,1)S(1)}, bf16[256,320]{1,0:T(8,128)(2,1)S(1)}, u32[]{:S(2)}, u32[]{:S(2)}) collective-permute-start(bf16[256,320]{1,0:T(8,128)(2,1)S(1)} %get-tuple-element.45.rows), channel_id=1, source_target_pairs={{1,0},{2,1},{3,2},{0,3},{5,4},{6,5},{7,6},{4,7},{9,8},{10,9},{11,1... | collective-permute-start | bytes 491528 | tf_op jit(solution)/shard_map/ppermute | solution.py:332
  48.2 5.6 %collective-permute-done.10.rows = bf16[256,320]{1,0:T(8,128)(2,1)S(1)} collective-permute-done((bf16[256,320]{1,0:T(8,128)(2,1)S(1)}, bf16[256,320]{1,0:T(8,128)(2,1)S(1)}, u32[]{:S(2)}, u32[]{:S(2)}) %collective-permute-start.10) | collective-permute-done | bytes 163872 | tf_op jit(solution)/shard_map/ppermute | solution.py:330
  53.8 2.3 %own_frame.1 = (bf16[4,320,320]{2,1,0:T(8,128)(2,1)S(1)}, bf16[256,320]{1,0:T(8,128)(2,1)S(1)}, f32[256,320]{1,0:T(8,128)S(1)}, bf16[256,320]{1,0:T(8,128)(2,1)S(1)}) custom-call(s32[5]{0:T(128)S(1)} %stack.20.where, bf16[256,320]{1,0:T(8,128)(2,1)S(1)} %get-tuple-element.45.rows, bf16[3,80,320]{2,1,0:T(8,128)(2,1)} %three.5, bf16[80,320]{1,0:T(8,128)(2,1)} %one.5, ...), custom_call_target="tpu_custom_call" | custom-call | flops 209715200 | bytes 1474560 | tf_op jit(solution)/shard_map/own_frame/pallas_call | solution.py:515
  56.1 0.6 %other_frame.2 = (f32[256,320]{1,0:T(8,128)S(1)}, bf16[256,320]{1,0:T(8,128)(2,1)S(1)}) custom-call(bf16[256,320]{1,0:T(8,128)(2,1)S(1)} %get-tuple-element.49.queries.refs_1_, bf16[256,320]{1,0:T(8,128)(2,1)S(1)} %collective-permute-done.10.rows, bf16[4,320,320]{2,1,0:T(8,128)(2,1)S(1)} %get-tuple-element.50.weights.refs_3_), custom_call_target="tpu_custom_call" | custom-call | flops 209715200 | bytes 1474560 | tf_op jit(solution)/shard_map/other_frame/pallas_call | solution.py:528
  56.7 0.6 %other_frame.3 = (f32[256,320]{1,0:T(8,128)S(1)}, bf16[256,320]{1,0:T(8,128)(2,1)S(1)}) custom-call(bf16[256,320]{1,0:T(8,128)(2,1)S(1)} %get-tuple-element.49.queries.refs_1_, bf16[256,320]{1,0:T(8,128)(2,1)S(1)} %collective-permute-done.12.rows, bf16[4,320,320]{2,1,0:T(8,128)(2,1)S(1)} %get-tuple-element.50.weights.refs_3_), custom_call_target="tpu_custom_call" | custom-call | flops 209715200 | bytes 1474560 | tf_op jit(solution)/shard_map/other_frame/pallas_call | solution.py:528
  57.4 3.9 %collective-permute-done.11.refs_2_ = bf16[256,320]{1,0:T(8,128)(2,1)S(1)} collective-permute-done((bf16[256,320]{1,0:T(8,128)(2,1)S(1)}, bf16[256,320]{1,0:T(8,128)(2,1)S(1)}, u32[]{:S(2)}, u32[]{:S(2)}) %collective-permute-start.11) | collective-permute-done | bytes 163872 | tf_op jit(solution)/shard_map/ppermute | solution.py:330
  61.3 2.0 %last.1 = bf16[320,256]{1,0:T(8,128)(2,1)} custom-call(bf16[256,320]{1,0:T(8,128)(2,1)S(1)} %get-tuple-element.41.refs_0_, bf16[256,320]{1,0:T(8,128)(2,1)S(1)} %get-tuple-element.49.queries.refs_1_, bf16[256,320]{1,0:T(8,128)(2,1)S(1)} %collective-permute-done.11.refs_2_, bf16[4,320,320]{2,1,0:T(8,128)(2,1)S(1)} %get-tuple-element.50.weights.refs_3_, ...), custom_call_target="tpu_custom_call" | custom-call | tf_op jit(solution)/shard_map/last/pallas_call | solution.py:539
  (31 shorter events, 0.8 us)
Async XLA Ops:
  0.0 28.0 %copy-start = (s32[2,4,2,2]{1,3,2,0:T(2,128)S(1)}, s32[2,4,2,2]{1,3,2,0:T(2,128)}, u32[]{:S(2)}) copy-start(s32[2,4,2,2]{1,3,2,0:T(2,128)} %param.14) | copy-start | bytes 388
  1.9 9.6 %copy-start.2 = (bf16[3,80,320]{2,1,0:T(8,128)(2,1)S(1)}, bf16[3,80,320]{2,1,0:T(8,128)(2,1)}, u32[]{:S(2)}) copy-start(bf16[3,80,320]{2,1,0:T(8,128)(2,1)} %three.5) | copy-start | bytes 460804
  1.9 9.6 %copy-start.3 = (bf16[80,320]{1,0:T(8,128)(2,1)S(1)}, bf16[80,320]{1,0:T(8,128)(2,1)}, u32[]{:S(2)}) copy-start(bf16[80,320]{1,0:T(8,128)(2,1)} %one.5) | copy-start | bytes 153604
  1.9 17.8 %copy-start.1 = (bf16[3,3,320,320]{3,2,1,0:T(8,128)(2,1)S(1)}, bf16[3,3,320,320]{3,2,1,0:T(8,128)(2,1)}, u32[]{:S(2)}) copy-start(bf16[3,3,320,320]{3,2,1,0:T(8,128)(2,1)} %param.16) | copy-start | bytes 5529604
  1.9 9.5 %collective-permute-start = (bf16[176,320]{1,0:T(8,128)(2,1)S(1)}, bf16[176,320]{1,0:T(8,128)(2,1)S(1)}, u32[]{:S(2)}, u32[]{:S(2)}) collective-permute-start(bf16[176,320]{1,0:T(8,128)(2,1)S(1)} %payload.1.refs_0_), channel_id=1, source_target_pairs={{0,1},{1,2},{2,3},{3,0},{4,5},{5,6},{6,7},{7,4},{8,9},{9,10},{10,1... | collective-permute-start | bytes 337928 | tf_op jit(solution)/shard_map/ppermute | solution.py:330
  5.0 7.9 %collective-permute-start.1 = (bf16[176,320]{1,0:T(8,128)(2,1)S(1)}, bf16[176,320]{1,0:T(8,128)(2,1)S(1)}, u32[]{:S(2)}, u32[]{:S(2)}) collective-permute-start(bf16[176,320]{1,0:T(8,128)(2,1)S(1)} %payload.1.refs_0_), channel_id=1, source_target_pairs={{1,0},{2,1},{3,2},{0,3},{5,4},{6,5},{7,6},{4,7},{9,8},{10,9},{11,1... | collective-permute-start | bytes 337928 | tf_op jit(solution)/shard_map/ppermute | solution.py:332
  11.5 8.2 %collective-permute-start.2 = (bf16[176,320]{1,0:T(8,128)(2,1)S(1)}, bf16[176,320]{1,0:T(8,128)(2,1)S(1)}, u32[]{:S(2)}, u32[]{:S(2)}) collective-permute-start(bf16[176,320]{1,0:T(8,128)(2,1)S(1)} %collective-permute-done.refs_1_.refs_0_), channel_id=1, source_target_pairs={{0,1},{1,2},{2,3},{3,0},{4,5},{5,6},{6,7},{7,4},{8,9},{9,10},{10,1... | collective-permute-start | bytes 337928 | tf_op jit(solution)/shard_map/ppermute | solution.py:330
  13.0 15.4 %copy-start.4 = (s32[2,4]{1,0:T(2,128)S(1)}, s32[2,4]{1,0:T(2,128)}, u32[]{:S(2)}) copy-start(s32[2,4]{1,0:T(2,128)} %param.13) | copy-start | bytes 100
  13.0 12.4 %collective-permute-start.4 = (bf16[320,320]{1,0:T(8,128)(2,1)S(1)}, bf16[320,320]{1,0:T(8,128)(2,1)S(1)}, u32[]{:S(2)}, u32[]{:S(2)}) collective-permute-start(bf16[320,320]{1,0:T(8,128)(2,1)S(1)} %bitcast.20), channel_id=1, source_target_pairs={{0,1},{1,2},{2,3},{3,0},{4,5},{5,6},{6,7},{7,4},{8,9},{9,10},{10,1... | collective-permute-start | bytes 614408 | tf_op jit(solution)/shard_map/ppermute | solution.py:330
  22.3 5.7 %collective-permute-start.7 = (bf16[256,320]{1,0:T(8,128)(2,1)S(1)}, bf16[256,320]{1,0:T(8,128)(2,1)S(1)}, u32[]{:S(2)}, u32[]{:S(2)}) collective-permute-start(bf16[256,320]{1,0:T(8,128)(2,1)S(1)} %get-tuple-element.36.normed.refs_5_), channel_id=1, source_target_pairs={{0,8},{4,12},{8,0},{12,4},{1,9},{5,13},{9,1},{13,5},{2,10},{6,14},... | collective-permute-start | bytes 491528 | tf_op jit(solution)/shard_map/ppermute | solution.py:304
  24.2 4.4 %collective-permute-start.3 = (bf16[480,320]{1,0:T(8,128)(2,1)S(1)}, bf16[480,320]{1,0:T(8,128)(2,1)S(1)}, u32[]{:S(2)}, u32[]{:S(2)}) collective-permute-start(bf16[480,320]{1,0:T(8,128)(2,1)S(1)} %pad_maximum_fusion), channel_id=1, source_target_pairs={{0,4},{4,0},{8,12},{12,8},{1,5},{5,1},{9,13},{13,9},{2,6},{6,2},{1... | collective-permute-start | bytes 921608 | tf_op jit(solution)/shard_map/ppermute | solution.py:352
  24.2 13.6 %collective-permute-start.5 = (bf16[320,320]{1,0:T(8,128)(2,1)S(1)}, bf16[320,320]{1,0:T(8,128)(2,1)S(1)}, u32[]{:S(2)}, u32[]{:S(2)}) collective-permute-start(bf16[320,320]{1,0:T(8,128)(2,1)S(1)} %bitcast.21), channel_id=1, source_target_pairs={{1,0},{2,1},{3,2},{0,3},{5,4},{6,5},{7,6},{4,7},{9,8},{10,9},{11,1... | collective-permute-start | bytes 614408 | tf_op jit(solution)/shard_map/ppermute | solution.py:332
  25.5 18.9 %collective-permute-start.9 = (bf16[320,320]{1,0:T(8,128)(2,1)S(1)}, bf16[320,320]{1,0:T(8,128)(2,1)S(1)}, u32[]{:S(2)}, u32[]{:S(2)}) collective-permute-start(bf16[320,320]{1,0:T(8,128)(2,1)S(1)} %collective-permute-done.4.refs_0_), channel_id=1, source_target_pairs={{0,1},{1,2},{2,3},{3,0},{4,5},{5,6},{6,7},{7,4},{8,9},{9,10},{10,1... | collective-permute-start | bytes 614408 | tf_op jit(solution)/shard_map/ppermute | solution.py:330
  26.3 11.5 %collective-permute-start.6 = (bf16[256,320]{1,0:T(8,128)(2,1)S(1)}, bf16[256,320]{1,0:T(8,128)(2,1)S(1)}, u32[]{:S(2)}, u32[]{:S(2)}) collective-permute-start(bf16[256,320]{1,0:T(8,128)(2,1)S(1)} %get-tuple-element.36.normed.refs_5_), channel_id=1, source_target_pairs={{0,4},{4,0},{8,12},{12,8},{1,5},{5,1},{9,13},{13,9},{2,6},{6,2},{1... | collective-permute-start | bytes 491528 | tf_op jit(solution)/shard_map/ppermute | solution.py:304
  28.0 9.8 %collective-permute-start.8 = (bf16[256,320]{1,0:T(8,128)(2,1)S(1)}, bf16[256,320]{1,0:T(8,128)(2,1)S(1)}, u32[]{:S(2)}, u32[]{:S(2)}) collective-permute-start(bf16[256,320]{1,0:T(8,128)(2,1)S(1)} %collective-permute-done.7.refs_7_), channel_id=1, source_target_pairs={{0,4},{4,0},{8,12},{12,8},{1,5},{5,1},{9,13},{13,9},{2,6},{6,2},{1... | collective-permute-start | bytes 491528 | tf_op jit(solution)/shard_map/ppermute | solution.py:304
  44.4 9.5 %collective-permute-start.10 = (bf16[256,320]{1,0:T(8,128)(2,1)S(1)}, bf16[256,320]{1,0:T(8,128)(2,1)S(1)}, u32[]{:S(2)}, u32[]{:S(2)}) collective-permute-start(bf16[256,320]{1,0:T(8,128)(2,1)S(1)} %get-tuple-element.45.rows), channel_id=1, source_target_pairs={{0,1},{1,2},{2,3},{3,0},{4,5},{5,6},{6,7},{7,4},{8,9},{9,10},{10,1... | collective-permute-start | bytes 491528 | tf_op jit(solution)/shard_map/ppermute | solution.py:330
  44.4 12.3 %collective-permute-start.12 = (bf16[256,320]{1,0:T(8,128)(2,1)S(1)}, bf16[256,320]{1,0:T(8,128)(2,1)S(1)}, u32[]{:S(2)}, u32[]{:S(2)}) collective-permute-start(bf16[256,320]{1,0:T(8,128)(2,1)S(1)} %get-tuple-element.45.rows), channel_id=1, source_target_pairs={{1,0},{2,1},{3,2},{0,3},{5,4},{6,5},{7,6},{4,7},{9,8},{10,9},{11,1... | collective-permute-start | bytes 491528 | tf_op jit(solution)/shard_map/ppermute | solution.py:332
  53.8 7.5 %collective-permute-start.11 = (bf16[256,320]{1,0:T(8,128)(2,1)S(1)}, bf16[256,320]{1,0:T(8,128)(2,1)S(1)}, u32[]{:S(2)}, u32[]{:S(2)}) collective-permute-start(bf16[256,320]{1,0:T(8,128)(2,1)S(1)} %collective-permute-done.10.rows), channel_id=1, source_target_pairs={{0,1},{1,2},{2,3},{3,0},{4,5},{5,6},{6,7},{7,4},{8,9},{9,10},{10,1... | collective-permute-start | bytes 491528 | tf_op jit(solution)/shard_map/ppermute | solution.py:330

commit v7 on v6

--- a/solution.py
+++ b/solution.py
@@ -322,6 +322,10 @@
     return value, beside, later
 
 
+def after(x, *others):
+    return lax.optimization_barrier((x, *others))[0]
+
+
 def ring_gather(own, axis, size, beside=None):
     pieces = {0: own}
     right = [(i, (i + 1) % size) for i in range(size)]
@@ -331,20 +335,8 @@
         if size - step > step:
             pieces[size - step] = lax.ppermute(pieces[(size - step + 1) % size], axis, left)
         if step == 1 and beside is not None:
-            pieces[1], beside = lax.optimization_barrier((pieces[1], beside))
-    pieces = [pieces[k] for k in range(size)]
-    return pieces if beside is None else (pieces, beside)
-
-
-def neighbours(pieces):
-    return [pieces[1], pieces[-1]] if len(pieces) > 2 else pieces[1:]
-
-
-def with_neighbours(pieces, near):
-    pieces = list(pieces)
-    if near:
-        pieces[1], pieces[-1] = near[0], near[-1]
-    return pieces
+            pieces[1] = after(pieces[1], beside)
+    return [pieces[k] for k in range(size)]
 
 
 def swap(pieces, rows, videos):
@@ -444,11 +436,7 @@
     )(in_hbm(source), in_hbm(conv_first.reshape(3, 3 * channels, channels)))
     temp_parts = []
     if paired:
-        shares, inner = ring_gather(shares[0], "frame", frames, inner)
-        mine = jnp.concatenate([temp_in, temp_out[None]], axis=0).reshape(4 * height, channels)
-        mine, *near = lax.optimization_barrier((mine, *neighbours(shares)))
-        shares = with_neighbours(shares, near)
-        temp_parts = ring_gather(mine, "frame", frames)
+        shares = ring_gather(shares[0], "frame", frames, inner)
     hidden, normed = pl.pallas_call(
         second_kernel,
         out_shape=[
@@ -483,9 +471,6 @@
         compiler_params=params(),
         name="query",
     )(places, normed, in_hbm(epi_in), in_hbm(epi_out), *epi_parts)
-    if paired:
-        queries, *near = lax.optimization_barrier((queries, *neighbours(temp_parts)))
-        temp_parts = with_neighbours(temp_parts, near)
     second, blocks = pl.pallas_call(
         functools.partial(view_kernel, videos, tiles),
         out_shape=[jax.ShapeDtypeStruct((tokens, channels), bf16)] * 2,
@@ -502,8 +487,9 @@
     )(select, mask, hidden, queries, epi, *maps)
 
     if paired:
-        blocks, *temp_parts = lax.optimization_barrier((blocks, *temp_parts))
-        temp_parts = temp_parts[1:]
+        mine = jnp.concatenate([temp_in, temp_out[None]], axis=0).reshape(4 * height, channels)
+        temp_parts = ring_gather(after(mine, maps[videos // 2]), "frame", frames, blocks)[1:]
+        blocks = after(blocks, temp_parts[-1])
     arrived = ring_gather(blocks, "frame", frames)
     score_shape = jax.ShapeDtypeStruct((tokens, channels), f32)
     value_shape = jax.ShapeDtypeStruct((tokens, channels), bf16)

time: 63.6 us -> 62.7 us (0.986)
  starting transfers between devices: 14.7 us -> 13.4 us
    ppermute x3, waiting for transfers between devices: 8.8 us -> 2.65 us  [ring_gather(): lax.ppermute(pieces[(size - step + 1) % size], axis, left)]
    ppermute x6, waiting for transfers between devices: 16 us -> 20.5 us  [ring_gather(): pieces[step] = lax.ppermute(pieces[step - 1], axis, right)]
    ppermute x3, waiting for transfers between devices: 1.7 us -> 3.73 us  [gather_maps(): maps[k | bit] = lax.ppermute(maps[k], axis, partner_permutation(size, bit))]
    ppermute x6, starting transfers between devices: 5.73 us -> 4.33 us  [ring_gather(): pieces[step] = lax.ppermute(pieces[step - 1], axis, right)]
  transfers between devices with their start and end apart: 13 -> 13, of which waited for: 7 -> 9; matrix products, arithmetic and copies ran while one was open for 1% -> 1% of each run, Pallas kernels for 27% -> 24%
where the time goes in v7:
time: 62.7 us; the launch traced here: 62.4 us
  waiting for transfers between devices  26.9 us (43%)
  Pallas kernels  20.4 us (33%)
  starting transfers between devices  13.4 us (21%)
  between operations  0.87 us (1%)
    ppermute x6, waiting for transfers between devices, ring_gather(): pieces[step] = lax.ppermute(pieces[step - 1], axis, right)  20.5 us
    ppermute x3, starting transfers between devices, ring_gather(): lax.ppermute(pieces[(size - step + 1) % size], axis, left)  6.75 us
    pallas_call x1, Pallas kernels, per_device(): pl.pallas_call(functools.partial(view_kernel, videos, tiles), out_shape=[...  6.47 us
    ppermute x6, starting transfers between devices, ring_gather(): pieces[step] = lax.ppermute(pieces[step - 1], axis, right)  4.33 us
    ppermute x3, waiting for transfers between devices, gather_maps(): maps[k | bit] = lax.ppermute(maps[k], axis, partner_permutation(size, bit))  3.73 us
    pallas_call x1, Pallas kernels, per_device(): pl.pallas_call(first_kernel, out_shape=jax.ShapeDtypeStruct((tokens, chan...  2.83 us
    ppermute x3, waiting for transfers between devices, ring_gather(): lax.ppermute(pieces[(size - step + 1) % size], axis, left)  2.65 us
    pallas_call x1, Pallas kernels, per_device(): pl.pallas_call(second_kernel, out_shape=[jax.ShapeDtypeStruct((tokens, ch...  2.57 us
  transfers between devices with their start and end apart: 13, of which 9 were waited for; matrix products, arithmetic and copies ran while one was open for 1% of the time, Pallas kernels for 24%

profile of v7, /device:TPU:0, one launch (start us, length us, event | category | flops | bytes accessed | tf_op | source)
XLA Modules:
  0.0 62.4 jit_solution(18132833974212039640)
XLA Ops:
  0.8 1.1 %payload.1.refs_0_ = bf16[176,320]{1,0:T(8,128)(2,1)S(1)} custom-call(s32[1]{0:T(128)} %bitcast.5.side, bf16[1,320]{1,0:T(2,128)(2,1)S(1)} %fusion.4.act, bf16[320,320]{1,0:T(8,128)(2,1)} %proj_hbm.1, bf16[3,80,320]{2,1,0:T(8,128)(2,1)} %three.4, bf16[80,320]{1,0:T(8,128)(2,1)} %one.4), custom_call_target="tpu_custom_call" | custom-call | flops 10000000000 | bytes 1048576 | tf_op jit(solution)/shard_map/payload/pallas_call | solution.py:382
  1.9 3.1 %collective-permute-start = (bf16[176,320]{1,0:T(8,128)(2,1)S(1)}, bf16[176,320]{1,0:T(8,128)(2,1)S(1)}, u32[]{:S(2)}, u32[]{:S(2)}) collective-permute-start(bf16[176,320]{1,0:T(8,128)(2,1)S(1)} %payload.1.refs_0_), channel_id=1, source_target_pairs={{0,1},{1,2},{2,3},{3,0},{4,5},{5,6},{6,7},{7,4},{8,9},{9,10},{10,1... | collective-permute-start | bytes 337928 | tf_op jit(solution)/shard_map/ppermute | solution.py:334
  5.0 2.1 %collective-permute-start.2 = (bf16[176,320]{1,0:T(8,128)(2,1)S(1)}, bf16[176,320]{1,0:T(8,128)(2,1)S(1)}, u32[]{:S(2)}, u32[]{:S(2)}) collective-permute-start(bf16[176,320]{1,0:T(8,128)(2,1)S(1)} %payload.1.refs_0_), channel_id=1, source_target_pairs={{1,0},{2,1},{3,2},{0,3},{5,4},{6,5},{7,6},{4,7},{9,8},{10,9},{11,1... | collective-permute-start | bytes 337928 | tf_op jit(solution)/shard_map/ppermute | solution.py:336
  7.1 2.8 %first_conv.1.inner = f32[256,320]{1,0:T(8,128)S(1)} custom-call(bf16[320,256]{1,0:T(8,128)(2,1)} %bitcast.18, bf16[3,960,320]{2,1,0:T(8,128)(2,1)} %bitcast.17), custom_call_target="tpu_custom_call" | custom-call | flops 471859200 | bytes 2498560 | tf_op jit(solution)/shard_map/first_conv/pallas_call | solution.py:422
  9.9 1.5 %collective-permute-done.refs_1_.refs_0_ = bf16[176,320]{1,0:T(8,128)(2,1)S(1)} collective-permute-done((bf16[176,320]{1,0:T(8,128)(2,1)S(1)}, bf16[176,320]{1,0:T(8,128)(2,1)S(1)}, u32[]{:S(2)}, u32[]{:S(2)}) %collective-permute-start) | collective-permute-done | bytes 112672 | tf_op jit(solution)/shard_map/ppermute | solution.py:334
  11.5 1.4 %collective-permute-done.2.refs_3_.refs_2_ = bf16[176,320]{1,0:T(8,128)(2,1)S(1)} collective-permute-done((bf16[176,320]{1,0:T(8,128)(2,1)S(1)}, bf16[176,320]{1,0:T(8,128)(2,1)S(1)}, u32[]{:S(2)}, u32[]{:S(2)}) %collective-permute-start.2) | collective-permute-done | bytes 112672 | tf_op jit(solution)/shard_map/ppermute | solution.py:336
  13.0 5.3 %collective-permute-done.1.refs_2_.refs_1_ = bf16[176,320]{1,0:T(8,128)(2,1)S(1)} collective-permute-done((bf16[176,320]{1,0:T(8,128)(2,1)S(1)}, bf16[176,320]{1,0:T(8,128)(2,1)S(1)}, u32[]{:S(2)}, u32[]{:S(2)}) %collective-permute-start.1) | collective-permute-done | bytes 112672 | tf_op jit(solution)/shard_map/ppermute | solution.py:334
  18.3 2.6 %second_conv.1 = (bf16[256,320]{1,0:T(8,128)(2,1)S(1)}, bf16[256,320]{1,0:T(8,128)(2,1)S(1)}) custom-call(bf16[320,256]{1,0:T(8,128)(2,1)} %bitcast.19, f32[256,320]{1,0:T(8,128)S(1)} %first_conv.1.inner, bf16[3,960,320]{2,1,0:T(8,128)(2,1)S(1)} %bitcast.16, bf16[176,320]{1,0:T(8,128)(2,1)S(1)} %payload.1.refs_0_, ...), custom_call_target="tpu_custom_call" | custom-call | flops 471859200 | bytes 2498560 | tf_op jit(solution)/shard_map/second_conv/pallas_call | solution.py:440
  20.8 1.8 %collective-permute-start.5 = (bf16[256,320]{1,0:T(8,128)(2,1)S(1)}, bf16[256,320]{1,0:T(8,128)(2,1)S(1)}, u32[]{:S(2)}, u32[]{:S(2)}) collective-permute-start(bf16[256,320]{1,0:T(8,128)(2,1)S(1)} %get-tuple-element.25.normed.refs_5_), channel_id=1, source_target_pairs={{0,8},{4,12},{8,0},{12,4},{1,9},{5,13},{9,1},{13,5},{2,10},{6,14},... | collective-permute-start | bytes 491528 | tf_op jit(solution)/shard_map/ppermute | solution.py:304
  22.9 3.7 %collective-permute-done.5.refs_7_ = bf16[256,320]{1,0:T(8,128)(2,1)S(1)} collective-permute-done((bf16[256,320]{1,0:T(8,128)(2,1)S(1)}, bf16[256,320]{1,0:T(8,128)(2,1)S(1)}, u32[]{:S(2)}, u32[]{:S(2)}) %collective-permute-start.5) | collective-permute-done | bytes 163872 | tf_op jit(solution)/shard_map/ppermute | solution.py:304
  26.6 2.0 %collective-permute-start.7 = (bf16[320,320]{1,0:T(8,128)(2,1)S(1)}, bf16[320,320]{1,0:T(8,128)(2,1)S(1)}, u32[]{:S(2)}, u32[]{:S(2)}) collective-permute-start(bf16[320,320]{1,0:T(8,128)(2,1)S(1)} %bitcast.20), channel_id=1, source_target_pairs={{1,0},{2,1},{3,2},{0,3},{5,4},{6,5},{7,6},{4,7},{9,8},{10,9},{11,1... | collective-permute-start | bytes 614408 | tf_op jit(solution)/shard_map/ppermute | solution.py:336
  29.7 1.9 %query.1 = (f32[320,256]{1,0:T(8,128)S(1)}, bf16[4,320,320]{2,1,0:T(8,128)(2,1)S(1)}) custom-call(s32[5]{0:T(128)S(1)} %stack.20.where, bf16[256,320]{1,0:T(8,128)(2,1)S(1)} %get-tuple-element.25.normed.refs_5_, bf16[3,80,320]{2,1,0:T(8,128)(2,1)} %three.4, bf16[80,320]{1,0:T(8,128)(2,1)} %one.4, bf16[176,320]{1,0:T(8,128)(2,1)S(1)} %collective-permute-done.refs_1_.refs_0_, ...), custom_call_target="tpu_custom_call" | custom-call | tf_op jit(solution)/shard_map/query/pallas_call | solution.py:462
  31.6 6.5 %cross_view.1 = (bf16[256,320]{1,0:T(8,128)(2,1)S(1)}, bf16[256,320]{1,0:T(8,128)(2,1)S(1)}) custom-call(s32[2]{0:T(128)S(1)} %xor_reduce_fusion.refs_0_, s32[8]{0:T(128)S(1)} %reshape.93.refs_1_, bf16[256,320]{1,0:T(8,128)(2,1)S(1)} %get-tuple-element.24.refs_2_, f32[320,256]{1,0:T(8,128)S(1)} %get-tuple-element.26.refs_3_, ...), custom_call_target="tpu_custom_call" | custom-call | tf_op jit(solution)/shard_map/cross_view/pallas_call | solution.py:474
  38.1 0.6 collective-permute-done.8.refs_0_
  38.7 1.1 %collective-permute-start.9 = (bf16[320,320]{1,0:T(8,128)(2,1)S(1)}, bf16[320,320]{1,0:T(8,128)(2,1)S(1)}, u32[]{:S(2)}, u32[]{:S(2)}) collective-permute-start(bf16[320,320]{1,0:T(8,128)(2,1)S(1)} %collective-permute-done.8.refs_0_), channel_id=1, source_target_pairs={{0,1},{1,2},{2,3},{3,0},{4,5},{5,6},{6,7},{7,4},{8,9},{9,10},{10,1... | collective-permute-start | bytes 614408 | tf_op jit(solution)/shard_map/ppermute | solution.py:334
  39.8 2.7 %collective-permute-start.12 = (bf16[256,320]{1,0:T(8,128)(2,1)S(1)}, bf16[256,320]{1,0:T(8,128)(2,1)S(1)}, u32[]{:S(2)}, u32[]{:S(2)}) collective-permute-start(bf16[256,320]{1,0:T(8,128)(2,1)S(1)} %get-tuple-element.31.rows), channel_id=1, source_target_pairs={{1,0},{2,1},{3,2},{0,3},{5,4},{6,5},{7,6},{4,7},{9,8},{10,9},{11,1... | collective-permute-start | bytes 491528 | tf_op jit(solution)/shard_map/ppermute | solution.py:336
  42.5 5.3 %collective-permute-done.10.rows = bf16[256,320]{1,0:T(8,128)(2,1)S(1)} collective-permute-done((bf16[256,320]{1,0:T(8,128)(2,1)S(1)}, bf16[256,320]{1,0:T(8,128)(2,1)S(1)}, u32[]{:S(2)}, u32[]{:S(2)}) %collective-permute-start.10) | collective-permute-done | bytes 163872 | tf_op jit(solution)/shard_map/ppermute | solution.py:334
  47.9 5.2 %collective-permute-done.9.refs_1_ = bf16[320,320]{1,0:T(8,128)(2,1)S(1)} collective-permute-done((bf16[320,320]{1,0:T(8,128)(2,1)S(1)}, bf16[320,320]{1,0:T(8,128)(2,1)S(1)}, u32[]{:S(2)}, u32[]{:S(2)}) %collective-permute-start.9) | collective-permute-done | bytes 204832 | tf_op jit(solution)/shard_map/ppermute | solution.py:334
  53.0 2.3 %own_frame.1 = (bf16[4,320,320]{2,1,0:T(8,128)(2,1)S(1)}, bf16[256,320]{1,0:T(8,128)(2,1)S(1)}, f32[256,320]{1,0:T(8,128)S(1)}, bf16[256,320]{1,0:T(8,128)(2,1)S(1)}) custom-call(s32[5]{0:T(128)S(1)} %stack.20.where, bf16[256,320]{1,0:T(8,128)(2,1)S(1)} %get-tuple-element.31.rows, bf16[3,80,320]{2,1,0:T(8,128)(2,1)} %three.5, bf16[80,320]{1,0:T(8,128)(2,1)} %one.5, ...), custom_call_target="tpu_custom_call" | custom-call | flops 209715200 | bytes 1474560 | tf_op jit(solution)/shard_map/own_frame/pallas_call | solution.py:501
  55.3 0.6 %other_frame.2 = (f32[256,320]{1,0:T(8,128)S(1)}, bf16[256,320]{1,0:T(8,128)(2,1)S(1)}) custom-call(bf16[256,320]{1,0:T(8,128)(2,1)S(1)} %get-tuple-element.33.queries.refs_1_, bf16[256,320]{1,0:T(8,128)(2,1)S(1)} %collective-permute-done.10.rows, bf16[4,320,320]{2,1,0:T(8,128)(2,1)S(1)} %get-tuple-element.34.weights.refs_3_), custom_call_target="tpu_custom_call" | custom-call | flops 209715200 | bytes 1474560 | tf_op jit(solution)/shard_map/other_frame/pallas_call | solution.py:514
  55.9 1.2 %collective-permute-done.12.rows = bf16[256,320]{1,0:T(8,128)(2,1)S(1)} collective-permute-done((bf16[256,320]{1,0:T(8,128)(2,1)S(1)}, bf16[256,320]{1,0:T(8,128)(2,1)S(1)}, u32[]{:S(2)}, u32[]{:S(2)}) %collective-permute-start.12) | collective-permute-done | bytes 163872 | tf_op jit(solution)/shard_map/ppermute | solution.py:336
  57.1 0.6 %other_frame.3 = (f32[256,320]{1,0:T(8,128)S(1)}, bf16[256,320]{1,0:T(8,128)(2,1)S(1)}) custom-call(bf16[256,320]{1,0:T(8,128)(2,1)S(1)} %get-tuple-element.33.queries.refs_1_, bf16[256,320]{1,0:T(8,128)(2,1)S(1)} %collective-permute-done.12.rows, bf16[4,320,320]{2,1,0:T(8,128)(2,1)S(1)} %get-tuple-element.34.weights.refs_3_), custom_call_target="tpu_custom_call" | custom-call | flops 209715200 | bytes 1474560 | tf_op jit(solution)/shard_map/other_frame/pallas_call | solution.py:514
  57.8 2.6 %collective-permute-done.11.refs_2_ = bf16[256,320]{1,0:T(8,128)(2,1)S(1)} collective-permute-done((bf16[256,320]{1,0:T(8,128)(2,1)S(1)}, bf16[256,320]{1,0:T(8,128)(2,1)S(1)}, u32[]{:S(2)}, u32[]{:S(2)}) %collective-permute-start.11) | collective-permute-done | bytes 163872 | tf_op jit(solution)/shard_map/ppermute | solution.py:334
  60.4 2.0 %last.1 = bf16[320,256]{1,0:T(8,128)(2,1)} custom-call(bf16[256,320]{1,0:T(8,128)(2,1)S(1)} %get-tuple-element.28.refs_0_, bf16[256,320]{1,0:T(8,128)(2,1)S(1)} %get-tuple-element.33.queries.refs_1_, bf16[256,320]{1,0:T(8,128)(2,1)S(1)} %collective-permute-done.11.refs_2_, bf16[4,320,320]{2,1,0:T(8,128)(2,1)S(1)} %get-tuple-element.34.weights.refs_3_, ...), custom_call_target="tpu_custom_call" | custom-call | tf_op jit(solution)/shard_map/last/pallas_call | solution.py:525
  (31 shorter events, 1.5 us)
Async XLA Ops:
  0.0 29.1 %copy-start = (s32[2,4,2,2]{1,3,2,0:T(2,128)S(1)}, s32[2,4,2,2]{1,3,2,0:T(2,128)}, u32[]{:S(2)}) copy-start(s32[2,4,2,2]{1,3,2,0:T(2,128)} %param.14) | copy-start | bytes 388
  1.9 16.4 %copy-start.1 = (bf16[3,3,320,320]{3,2,1,0:T(8,128)(2,1)S(1)}, bf16[3,3,320,320]{3,2,1,0:T(8,128)(2,1)}, u32[]{:S(2)}) copy-start(bf16[3,3,320,320]{3,2,1,0:T(8,128)(2,1)} %param.16) | copy-start | bytes 5529604
  1.9 9.5 %collective-permute-start = (bf16[176,320]{1,0:T(8,128)(2,1)S(1)}, bf16[176,320]{1,0:T(8,128)(2,1)S(1)}, u32[]{:S(2)}, u32[]{:S(2)}) collective-permute-start(bf16[176,320]{1,0:T(8,128)(2,1)S(1)} %payload.1.refs_0_), channel_id=1, source_target_pairs={{0,1},{1,2},{2,3},{3,0},{4,5},{5,6},{6,7},{7,4},{8,9},{9,10},{10,1... | collective-permute-start | bytes 337928 | tf_op jit(solution)/shard_map/ppermute | solution.py:334
  5.0 7.9 %collective-permute-start.2 = (bf16[176,320]{1,0:T(8,128)(2,1)S(1)}, bf16[176,320]{1,0:T(8,128)(2,1)S(1)}, u32[]{:S(2)}, u32[]{:S(2)}) collective-permute-start(bf16[176,320]{1,0:T(8,128)(2,1)S(1)} %payload.1.refs_0_), channel_id=1, source_target_pairs={{1,0},{2,1},{3,2},{0,3},{5,4},{6,5},{7,6},{4,7},{9,8},{10,9},{11,1... | collective-permute-start | bytes 337928 | tf_op jit(solution)/shard_map/ppermute | solution.py:336
  11.5 6.8 %collective-permute-start.1 = (bf16[176,320]{1,0:T(8,128)(2,1)S(1)}, bf16[176,320]{1,0:T(8,128)(2,1)S(1)}, u32[]{:S(2)}, u32[]{:S(2)}) collective-permute-start(bf16[176,320]{1,0:T(8,128)(2,1)S(1)} %collective-permute-done.refs_1_.refs_0_), channel_id=1, source_target_pairs={{0,1},{1,2},{2,3},{3,0},{4,5},{5,6},{6,7},{7,4},{8,9},{9,10},{10,1... | collective-permute-start | bytes 337928 | tf_op jit(solution)/shard_map/ppermute | solution.py:334
  11.5 11.3 %copy-start.2 = (bf16[3,80,320]{2,1,0:T(8,128)(2,1)S(1)}, bf16[3,80,320]{2,1,0:T(8,128)(2,1)}, u32[]{:S(2)}) copy-start(bf16[3,80,320]{2,1,0:T(8,128)(2,1)} %three.5) | copy-start | bytes 460804
  11.5 11.3 %copy-start.3 = (bf16[80,320]{1,0:T(8,128)(2,1)S(1)}, bf16[80,320]{1,0:T(8,128)(2,1)}, u32[]{:S(2)}) copy-start(bf16[80,320]{1,0:T(8,128)(2,1)} %one.5) | copy-start | bytes 153604
  18.3 11.2 %copy-start.4 = (s32[2,4]{1,0:T(2,128)S(1)}, s32[2,4]{1,0:T(2,128)}, u32[]{:S(2)}) copy-start(s32[2,4]{1,0:T(2,128)} %param.13) | copy-start | bytes 100
  20.8 5.7 %collective-permute-start.5 = (bf16[256,320]{1,0:T(8,128)(2,1)S(1)}, bf16[256,320]{1,0:T(8,128)(2,1)S(1)}, u32[]{:S(2)}, u32[]{:S(2)}) collective-permute-start(bf16[256,320]{1,0:T(8,128)(2,1)S(1)} %get-tuple-element.25.normed.refs_5_), channel_id=1, source_target_pairs={{0,8},{4,12},{8,0},{12,4},{1,9},{5,13},{9,1},{13,5},{2,10},{6,14},... | collective-permute-start | bytes 491528 | tf_op jit(solution)/shard_map/ppermute | solution.py:304
  22.7 7.0 %collective-permute-start.3 = (bf16[480,320]{1,0:T(8,128)(2,1)S(1)}, bf16[480,320]{1,0:T(8,128)(2,1)S(1)}, u32[]{:S(2)}, u32[]{:S(2)}) collective-permute-start(bf16[480,320]{1,0:T(8,128)(2,1)S(1)} %pad_maximum_fusion), channel_id=1, source_target_pairs={{0,4},{4,0},{8,12},{12,8},{1,5},{5,1},{9,13},{13,9},{2,6},{6,2},{1... | collective-permute-start | bytes 921608 | tf_op jit(solution)/shard_map/ppermute | solution.py:344
  26.6 11.5 %collective-permute-start.7 = (bf16[320,320]{1,0:T(8,128)(2,1)S(1)}, bf16[320,320]{1,0:T(8,128)(2,1)S(1)}, u32[]{:S(2)}, u32[]{:S(2)}) collective-permute-start(bf16[320,320]{1,0:T(8,128)(2,1)S(1)} %bitcast.20), channel_id=1, source_target_pairs={{1,0},{2,1},{3,2},{0,3},{5,4},{6,5},{7,6},{4,7},{9,8},{10,9},{11,1... | collective-permute-start | bytes 614408 | tf_op jit(solution)/shard_map/ppermute | solution.py:336
  28.5 3.0 %collective-permute-start.4 = (bf16[256,320]{1,0:T(8,128)(2,1)S(1)}, bf16[256,320]{1,0:T(8,128)(2,1)S(1)}, u32[]{:S(2)}, u32[]{:S(2)}) collective-permute-start(bf16[256,320]{1,0:T(8,128)(2,1)S(1)} %get-tuple-element.25.normed.refs_5_), channel_id=1, source_target_pairs={{0,4},{4,0},{8,12},{12,8},{1,5},{5,1},{9,13},{13,9},{2,6},{6,2},{1... | collective-permute-start | bytes 491528 | tf_op jit(solution)/shard_map/ppermute | solution.py:304
  28.5 3.0 %collective-permute-start.6 = (bf16[256,320]{1,0:T(8,128)(2,1)S(1)}, bf16[256,320]{1,0:T(8,128)(2,1)S(1)}, u32[]{:S(2)}, u32[]{:S(2)}) collective-permute-start(bf16[256,320]{1,0:T(8,128)(2,1)S(1)} %collective-permute-done.5.refs_7_), channel_id=1, source_target_pairs={{0,4},{4,0},{8,12},{12,8},{1,5},{5,1},{9,13},{13,9},{2,6},{6,2},{1... | collective-permute-start | bytes 491528 | tf_op jit(solution)/shard_map/ppermute | solution.py:304
  29.0 9.7 %collective-permute-start.8 = (bf16[320,320]{1,0:T(8,128)(2,1)S(1)}, bf16[320,320]{1,0:T(8,128)(2,1)S(1)}, u32[]{:S(2)}, u32[]{:S(2)}) collective-permute-start(bf16[320,320]{1,0:T(8,128)(2,1)S(1)} %bitcast.21), channel_id=1, source_target_pairs={{0,1},{1,2},{2,3},{3,0},{4,5},{5,6},{6,7},{7,4},{8,9},{9,10},{10,1... | collective-permute-start | bytes 614408 | tf_op jit(solution)/shard_map/ppermute | solution.py:334
  38.1 9.8 %collective-permute-start.10 = (bf16[256,320]{1,0:T(8,128)(2,1)S(1)}, bf16[256,320]{1,0:T(8,128)(2,1)S(1)}, u32[]{:S(2)}, u32[]{:S(2)}) collective-permute-start(bf16[256,320]{1,0:T(8,128)(2,1)S(1)} %get-tuple-element.31.rows), channel_id=1, source_target_pairs={{0,1},{1,2},{2,3},{3,0},{4,5},{5,6},{6,7},{7,4},{8,9},{9,10},{10,1... | collective-permute-start | bytes 491528 | tf_op jit(solution)/shard_map/ppermute | solution.py:334
  38.7 14.3 %collective-permute-start.9 = (bf16[320,320]{1,0:T(8,128)(2,1)S(1)}, bf16[320,320]{1,0:T(8,128)(2,1)S(1)}, u32[]{:S(2)}, u32[]{:S(2)}) collective-permute-start(bf16[320,320]{1,0:T(8,128)(2,1)S(1)} %collective-permute-done.8.refs_0_), channel_id=1, source_target_pairs={{0,1},{1,2},{2,3},{3,0},{4,5},{5,6},{6,7},{7,4},{8,9},{9,10},{10,1... | collective-permute-start | bytes 614408 | tf_op jit(solution)/shard_map/ppermute | solution.py:334
  39.8 17.3 %collective-permute-start.12 = (bf16[256,320]{1,0:T(8,128)(2,1)S(1)}, bf16[256,320]{1,0:T(8,128)(2,1)S(1)}, u32[]{:S(2)}, u32[]{:S(2)}) collective-permute-start(bf16[256,320]{1,0:T(8,128)(2,1)S(1)} %get-tuple-element.31.rows), channel_id=1, source_target_pairs={{1,0},{2,1},{3,2},{0,3},{5,4},{6,5},{7,6},{4,7},{9,8},{10,9},{11,1... | collective-permute-start | bytes 491528 | tf_op jit(solution)/shard_map/ppermute | solution.py:336
  47.9 12.5 %collective-permute-start.11 = (bf16[256,320]{1,0:T(8,128)(2,1)S(1)}, bf16[256,320]{1,0:T(8,128)(2,1)S(1)}, u32[]{:S(2)}, u32[]{:S(2)}) collective-permute-start(bf16[256,320]{1,0:T(8,128)(2,1)S(1)} %collective-permute-done.10.rows), channel_id=1, source_target_pairs={{0,1},{1,2},{2,3},{3,0},{4,5},{5,6},{6,7},{7,4},{8,9},{9,10},{10,1... | collective-permute-start | bytes 491528 | tf_op jit(solution)/shard_map/ppermute | solution.py:334

commit v8 on v7

--- a/solution.py
+++ b/solution.py
@@ -105,50 +105,24 @@
     return total
 
 
-def share_kernel(act, proj, share):
+def share_kernel(act, proj_hbm, share, proj, sem):
+    fetch(proj_hbm, proj, sem).wait()
     share[...] = dot(act[...], proj[...])
 
 
-def payload_kernel(side, act, proj_hbm, three, one, payload, proj, sems):
-    rows, channels = one.shape
-    copy = fetch(proj_hbm, proj, sems.at[0])
-    upper, lower = payload.at[pl.ds(0, rows)], payload.at[pl.ds(rows, rows)]
-
-    @pl.when(side[0] == 0)
-    def _():
-        fetch(three.at[0], upper, sems.at[1])
-        fetch(three.at[1], lower, sems.at[2])
-
-    @pl.when(side[0] != 0)
-    def _():
-        fetch(three.at[2], upper, sems.at[1])
-        fetch(one, lower, sems.at[2])
-
-    copy.wait()
-    payload[pl.ds(2 * rows, SHARE_ROWS), :] = terms(dot(act[...], proj[...])).astype(bf16)
-    pltpu.make_async_copy(one, upper, sems.at[1]).wait()
-    pltpu.make_async_copy(one, lower, sems.at[2]).wait()
-
-
-def first_kernel(source_hbm, weight_hbm, inner, source, weight, padded, sems):
+def first_kernel(source_hbm, weight_hbm, inner, turned, source, weight, padded, sems):
     copy = fetch(source_hbm, source, sems.at[0])
     copies = [fetch(weight_hbm.at[k], weight.at[k], sems.at[1 + k]) for k in range(3)]
     copy.wait()
-    inner[...] = convolve(group_norm_silu(source[...].astype(f32).T), weight, padded, copies)
-
-
-def second_kernel(source_hbm, inner, weight, *refs):
-    shares, (hidden, normed, source, padded, sems) = refs[:-5], refs[-5:]
-    copy = fetch(source_hbm, source, sems.at[0])
-    bias = None
-    for share in shares:
-        rows = min(SHARE_ROWS, share.shape[0])
-        part = jnp.sum(share[pl.ds(share.shape[0] - rows, rows), :].astype(f32), axis=0, keepdims=True)
-        bias = part if bias is None else bias + part
-    y = group_norm_silu(inner[...] + bias)
+    rows = source[...].astype(f32).T
+    turned[...] = rows.astype(bf16)
+    inner[...] = convolve(group_norm_silu(rows), weight, padded, copies)
+
+
+def second_kernel(source, inner, bias, weight, hidden, normed, padded):
+    y = group_norm_silu(inner[...] + bias[...])
     total = convolve(y, weight, padded, [])
-    copy.wait()
-    rounded = (source[...].astype(f32).T + total).astype(bf16)
+    rounded = (source[...].astype(f32) + total).astype(bf16)
     hidden[...] = rounded
     normed[...] = layer_norm(rounded.astype(f32)).astype(bf16)
 
@@ -160,18 +134,19 @@
     return copies + [fetch(one, whole.at[3, place], sems.at[3])]
 
 
+def assemble(where, side, parts, whole, rows):
+    for k, part in enumerate(parts[:-1]):
+        place = pl.ds(pl.multiple_of(where[k + 1] * rows, 16), rows)
+        for j in range(2):
+            mine = side * 2 + j
+            whole[mine, place, :] = part[pl.ds(j * rows, rows), :]
+            whole[2 - mine + 2 * j, place, :] = parts[-1][pl.ds((2 * k + j) * rows, rows), :]
+
+
 def query_kernel(where, normed, three, one, *refs):
     parts, (queries, epi, sems) = refs[:-3], refs[-3:]
     copies = fetch_own(where, three, one, epi, sems)
-    rows = one.shape[0]
-    count = len(parts) - 1
-    for k in range(1, count + 1):
-        place = pl.ds(pl.multiple_of(where[k] * rows, 16), rows)
-        for j in range(2):
-            mine = where[count + 1] * 2 + j
-            epi[mine, place, :] = parts[k - 1][pl.ds(j * rows, rows), :]
-            start = ((k - 1) * 2 + j) * rows
-            epi[2 - mine + 2 * j, place, :] = parts[-1][pl.ds(start, rows), :]
+    assemble(where, where[max(1, len(parts))], parts, epi, one.shape[0])
     for copy in copies:
         copy.wait()
     queries[...] = dot(normed[...], epi[0]).astype(bf16).astype(f32).T
@@ -247,11 +222,7 @@
 def own_frame_kernel(where, rows, three, one, *refs):
     parts, (weights, queries, scores, values, sems) = refs[:-5], refs[-5:]
     copies = fetch_own(where, three, one, weights, sems)
-    height = one.shape[0]
-    for k, part in enumerate(parts):
-        place = pl.ds(pl.multiple_of(where[k + 1] * height, 16), height)
-        for kind in range(4):
-            weights[kind, place, :] = part[pl.ds(kind * height, height), :]
+    assemble(where, where[max(1, len(parts))], parts, weights, one.shape[0])
     for copy in copies:
         copy.wait()
     queries[...] = dot(rows[...], weights[0]).astype(bf16)
@@ -309,17 +280,14 @@
     return [maps[k] for k in range(size)]
 
 
-def sum_over(value, beside, later, axis, size):
+def sum_over(value, axis, size):
     if not is_power(size):
-        return lax.psum(value, axis), beside, later
+        return lax.psum(value, axis)
     bit = 1
     while bit < size:
         value = value + lax.ppermute(value, axis, partner_permutation(size, bit))
-        if bit == 1:
-            value, beside = lax.optimization_barrier((value, beside))
         bit *= 2
-    value, later = lax.optimization_barrier((value, later))
-    return value, beside, later
+    return value
 
 
 def after(x, *others):
@@ -339,8 +307,14 @@
     return [pieces[k] for k in range(size)]
 
 
-def swap(pieces, rows, videos):
-    joined = jnp.concatenate([piece[:rows] for piece in pieces[1:]], axis=0)
+def half_of(three, one, side):
+    whole = jnp.concatenate([three, one[None]], axis=0)
+    whole = whole.reshape(2, 2 * one.shape[0], one.shape[1])
+    return lax.dynamic_index_in_dim(whole, side, 0, keepdims=False)
+
+
+def swap(pieces, videos):
+    joined = jnp.concatenate(pieces[1:], axis=0)
     return pieces[1:] + [lax.ppermute(joined, "video", partner_permutation(videos, 1))]
 
 
@@ -377,40 +351,31 @@
     height = epi_out.shape[0]
     paired = videos % 2 == 0 and is_power(videos) and height % 16 == 0
     early = pl.CostEstimate(flops=10**10, bytes_accessed=1 << 20, transcendentals=0)
+    share = pl.pallas_call(
+        share_kernel,
+        out_shape=jax.ShapeDtypeStruct((1, channels), f32),
+        in_specs=[VMEM, HBM],
+        out_specs=VMEM,
+        scratch_shapes=[pltpu.VMEM(time_proj.shape, bf16), pltpu.SemaphoreType.DMA],
+        compiler_params=params(),
+        cost_estimate=early,
+        name="time_share",
+    )(time_act, in_hbm(time_proj))
+    bias = sum_over(share, "frame", frames)
     if paired:
-        side = (video % 2).astype(jnp.int32).reshape(1)
-        payload = pl.pallas_call(
-            payload_kernel,
-            out_shape=jax.ShapeDtypeStruct((2 * height + SHARE_ROWS, channels), bf16),
-            in_specs=[SMEM, VMEM, HBM, HBM, HBM],
-            out_specs=VMEM,
-            scratch_shapes=[
-                pltpu.VMEM(time_proj.shape, bf16),
-                pltpu.SemaphoreType.DMA((3,)),
-            ],
-            compiler_params=params(),
-            cost_estimate=early,
-            name="payload",
-        )(side, time_act, in_hbm(time_proj), in_hbm(epi_in), in_hbm(epi_out))
-        shares = [payload]
-        places = [(frame - k) % frames for k in range(frames)] + [video % 2]
+        steps = [frame - k for k in range(frames)]
+        places = [step % frames for step in steps] + [video % 2]
     else:
-        share = pl.pallas_call(
-            share_kernel,
-            out_shape=jax.ShapeDtypeStruct((1, channels), f32),
-            in_specs=[VMEM, VMEM],
-            out_specs=VMEM,
-            compiler_params=params(),
-            cost_estimate=early,
-            name="time_share",
-        )(time_act, time_proj)
-        shares = [lax.psum(share, "frame")]
         places = [jnp.int32(0)] * 2
         epi_in = lax.all_gather(epi_in, "frame", axis=1, tiled=True)
         epi_out = lax.all_gather(epi_out, "frame", axis=0, tiled=True)
         temp_in = lax.all_gather(temp_in, "frame", axis=1, tiled=True)
         temp_out = lax.all_gather(temp_out, "frame", axis=0, tiled=True)
     places = jnp.stack(places).astype(jnp.int32)
+    temp_places = places
+    if paired:
+        temp_places = [partner(frame, frames, k, -1) for k in range(frames)] + [video % 2]
+        temp_places = jnp.stack(temp_places).astype(jnp.int32)
 
     source_scratch = pltpu.VMEM((channels, tokens), bf16)
     padded_scratch = pltpu.VMEM((tokens + 2 * W, 3 * channels), bf16)
@@ -419,11 +384,14 @@
         bytes_accessed=2 * 9 * channels * channels + 8 * tokens * channels,
         transcendentals=tokens * channels,
     )
-    inner = pl.pallas_call(
+    inner, turned = pl.pallas_call(
         first_kernel,
-        out_shape=jax.ShapeDtypeStruct((tokens, channels), f32),
+        out_shape=[
+            jax.ShapeDtypeStruct((tokens, channels), f32),
+            jax.ShapeDtypeStruct((tokens, channels), bf16),
+        ],
         in_specs=[HBM, HBM],
-        out_specs=VMEM,
+        out_specs=[VMEM, VMEM],
         scratch_shapes=[
             source_scratch,
             pltpu.VMEM((3, 3 * channels, channels), bf16),
@@ -434,24 +402,31 @@
         cost_estimate=conv_cost,
         name="first_conv",
     )(in_hbm(source), in_hbm(conv_first.reshape(3, 3 * channels, channels)))
-    temp_parts = []
-    if paired:
-        shares = ring_gather(shares[0], "frame", frames, inner)
     hidden, normed = pl.pallas_call(
         second_kernel,
         out_shape=[
             jax.ShapeDtypeStruct((tokens, channels), bf16),
             jax.ShapeDtypeStruct((tokens, channels), bf16),
         ],
-        in_specs=[HBM] + [VMEM] * (2 + len(shares)),
+        in_specs=[VMEM] * 4,
         out_specs=[VMEM] * 2,
-        scratch_shapes=[source_scratch, padded_scratch, pltpu.SemaphoreType.DMA((1,))],
+        scratch_shapes=[padded_scratch],
         compiler_params=params(),
         cost_estimate=conv_cost,
         name="second_conv",
-    )(in_hbm(source), inner, conv_second.reshape(3, 3 * channels, channels), *shares)
+    )(turned, inner, bias, conv_second.reshape(3, 3 * channels, channels))
+    if paired:
+        mine = half_of(epi_in, epi_out, video % 2)
+        epi_parts = ring_gather(after(mine, bias), "frame", frames, normed)
+        normed = after(normed, epi_parts[-1])
     maps = gather_maps(normed, "video", videos)
-    epi_parts = swap(shares, 2 * height, videos) if paired else []
+    epi_parts = swap(epi_parts, videos) if paired else []
+    temp_parts = []
+    if paired:
+        mine = after(half_of(temp_in, temp_out, video % 2), maps[1])
+        temp_parts = [mine] + [
+            lax.ppermute(mine, "frame", partner_permutation(frames, k)) for k in range(1, frames)
+        ]
     targets = lax.dynamic_index_in_dim(matchings, video, 1, keepdims=False)
     if is_power(videos):
         select = video ^ targets
@@ -487,9 +462,9 @@
     )(select, mask, hidden, queries, epi, *maps)
 
     if paired:
-        mine = jnp.concatenate([temp_in, temp_out[None]], axis=0).reshape(4 * height, channels)
-        temp_parts = ring_gather(after(mine, maps[videos // 2]), "frame", frames, blocks)[1:]
-        blocks = after(blocks, temp_parts[-1])
+        held = [after(part, blocks) for part in temp_parts]
+        blocks = after(blocks, *temp_parts)
+        temp_parts = swap(held, videos)
     arrived = ring_gather(blocks, "frame", frames)
     score_shape = jax.ShapeDtypeStruct((tokens, channels), f32)
     value_shape = jax.ShapeDtypeStruct((tokens, channels), bf16)
@@ -507,7 +482,7 @@
         compiler_params=params(),
         cost_estimate=frame_cost,
         name="own_frame",
-    )(places, blocks, in_hbm(temp_in), in_hbm(temp_out), *temp_parts)
+    )(temp_places, blocks, in_hbm(temp_in), in_hbm(temp_out), *temp_parts)
     scores, values = [first[0]], [first[1]]
     order = sorted(range(1, frames), key=lambda k: min(k, frames - k))
     for k in order[:-1]:

time: 62.7 us -> 62.8 us (level)
  starting transfers between devices: 13.4 us -> 20.7 us
  waiting for transfers between devices: 26.9 us -> 20.4 us
  Pallas kernels: 20.4 us -> 19.5 us
    ppermute x0 -> x5, starting transfers between devices: none -> 10.6 us  [the longest x2 6.12 us: sum_over(): value = value + lax.ppermute(value, axis, partner_permutation(size, bit))]
    ppermute x6 -> x4, waiting for transfers between devices: 20.5 us -> 14.7 us  [ring_gather(): pieces[step] = lax.ppermute(pieces[step - 1], axis, right)]
    ppermute x0 -> x5, waiting for transfers between devices: none -> 4.67 us  [the longest x2 3.02 us: sum_over(): value = value + lax.ppermute(value, axis, partner_permutation(size, bit))]
    ppermute x3, waiting for transfers between devices: 3.73 us -> 0.01 us  [gather_maps(): maps[k | bit] = lax.ppermute(maps[k], axis, partner_permutation(size, bit))]
    ppermute x6 -> x4, starting transfers between devices: 4.33 us -> 2.03 us  [ring_gather(): pieces[step] = lax.ppermute(pieces[step - 1], axis, right)]
    ppermute x3 -> x2, waiting for transfers between devices: 2.65 us -> 1.07 us  [ring_gather(): lax.ppermute(pieces[(size - step + 1) % size], axis, left)]
    pallas_call x1, Pallas kernels: 2.57 us -> 1.7 us  [per_device(): pl.pallas_call(second_kernel, out_shape=[jax.ShapeDtypeStruct((tokens, ch...]
    ppermute x3 -> x2, starting transfers between devices: 6.75 us -> 5.89 us  [ring_gather(): lax.ppermute(pieces[(size - step + 1) % size], axis, left)]
  transfers between devices with their start and end apart: 13 -> 16, of which waited for: 9 -> 7; matrix products, arithmetic and copies ran while one was open for 1% -> 1% of each run, Pallas kernels for 24% -> 26%
where the time goes in v8:
time: 62.8 us; the launch traced here: 62.6 us
  starting transfers between devices  20.7 us (33%)
  waiting for transfers between devices  20.4 us (32%)
  Pallas kernels  19.5 us (31%)
  between operations  0.95 us (2%)
    ppermute x4, waiting for transfers between devices, ring_gather(): pieces[step] = lax.ppermute(pieces[step - 1], axis, right)  14.7 us
    pallas_call x1, Pallas kernels, per_device(): pl.pallas_call(functools.partial(view_kernel, videos, tiles), out_shape=[...  6.47 us
    ppermute x2, starting transfers between devices, sum_over(): value = value + lax.ppermute(value, axis, partner_permutation(size, bit))  6.12 us
    ppermute x2, starting transfers between devices, ring_gather(): lax.ppermute(pieces[(size - step + 1) % size], axis, left)  5.89 us
    ppermute x3, starting transfers between devices, per_device(): lax.ppermute(mine, 'frame', partner_permutation(frames, k))  4.45 us
    ppermute x2, waiting for transfers between devices, sum_over(): value = value + lax.ppermute(value, axis, partner_permutation(size, bit))  3.02 us
    pallas_call x1, Pallas kernels, per_device(): pl.pallas_call(first_kernel, out_shape=[jax.ShapeDtypeStruct((tokens, cha...  2.82 us
    pallas_call x1, Pallas kernels, per_device(): pl.pallas_call(own_frame_kernel, out_shape=[jax.ShapeDtypeStruct(square,...  2.27 us
  transfers between devices with their start and end apart: 16, of which 7 were waited for; matrix products, arithmetic and copies ran while one was open for 1% of the time, Pallas kernels for 26%

profile of v8, /device:TPU:0, one launch (start us, length us, event | category | flops | bytes accessed | tf_op | source)
XLA Modules:
  0.0 62.6 jit_solution(195771745734022192)
XLA Ops:
  0.8 1.1 %time_share.1 = f32[1,320]{1,0:T(1,128)S(1)} custom-call(bf16[1,320]{1,0:T(2,128)(2,1)S(1)} %fusion.4.act, bf16[320,320]{1,0:T(8,128)(2,1)} %proj_hbm.1), custom_call_target="tpu_custom_call" | custom-call | flops 10000000000 | bytes 1048576 | tf_op jit(solution)/shard_map/time_share/pallas_call | solution.py:354
  1.9 3.1 %collective-permute-start = (f32[1,320]{1,0:T(1,128)S(1)}, f32[1,320]{1,0:T(1,128)S(1)}, u32[]{:S(2)}, u32[]{:S(2)}) collective-permute-start(f32[1,320]{1,0:T(1,128)S(1)} %time_share.1), channel_id=1, source_target_pairs={{0,1},{1,0},{2,3},{3,2},{4,5},{5,4},{6,7},{7,6},{8,9},{9,8},{10,11... | collective-permute-start | bytes 3848 | tf_op jit(solution)/shard_map/ppermute | solution.py:288
  5.1 1.5 %collective-permute-done = f32[1,320]{1,0:T(1,128)S(1)} collective-permute-done((f32[1,320]{1,0:T(1,128)S(1)}, f32[1,320]{1,0:T(1,128)S(1)}, u32[]{:S(2)}, u32[]{:S(2)}) %collective-permute-start) | collective-permute-done | bytes 1312 | tf_op jit(solution)/shard_map/ppermute | solution.py:288
  6.6 3.0 %collective-permute-start.1 = (f32[1,320]{1,0:T(1,128)S(1)}, f32[1,320]{1,0:T(1,128)S(1)}, u32[]{:S(2)}, u32[]{:S(2)}) collective-permute-start(f32[1,320]{1,0:T(1,128)S(1)} %add.76), channel_id=1, source_target_pairs={{0,2},{1,3},{2,0},{3,1},{4,6},{5,7},{6,4},{7,5},{8,10},{9,11},{10,... | collective-permute-start | bytes 3848 | tf_op jit(solution)/shard_map/ppermute | solution.py:288
  9.7 1.5 %collective-permute-done.1 = f32[1,320]{1,0:T(1,128)S(1)} collective-permute-done((f32[1,320]{1,0:T(1,128)S(1)}, f32[1,320]{1,0:T(1,128)S(1)}, u32[]{:S(2)}, u32[]{:S(2)}) %collective-permute-start.1) | collective-permute-done | bytes 1312 | tf_op jit(solution)/shard_map/ppermute | solution.py:288
  11.2 1.9 %collective-permute-start.3 = (bf16[160,320]{1,0:T(8,128)(2,1)S(1)}, bf16[160,320]{1,0:T(8,128)(2,1)S(1)}, u32[]{:S(2)}, u32[]{:S(2)}) collective-permute-start(bf16[160,320]{1,0:T(8,128)(2,1)S(1)} %dynamic-slice_bitcast_fusion.1), channel_id=1, source_target_pairs={{0,1},{1,2},{2,3},{3,0},{4,5},{5,6},{6,7},{7,4},{8,9},{9,10},{10,1... | collective-permute-start | bytes 307208 | tf_op jit(solution)/shard_map/ppermute | solution.py:302
  13.1 2.8 %first_conv.1 = (f32[256,320]{1,0:T(8,128)S(1)}, bf16[256,320]{1,0:T(8,128)(2,1)S(1)}) custom-call(bf16[320,256]{1,0:T(8,128)(2,1)} %bitcast.32, bf16[3,960,320]{2,1,0:T(8,128)(2,1)} %bitcast.27), custom_call_target="tpu_custom_call" | custom-call | flops 471859200 | bytes 2498560 | tf_op jit(solution)/shard_map/first_conv/pallas_call | solution.py:387
  16.0 2.1 %collective-permute-start.2 = (bf16[160,320]{1,0:T(8,128)(2,1)S(1)}, bf16[160,320]{1,0:T(8,128)(2,1)S(1)}, u32[]{:S(2)}, u32[]{:S(2)}) collective-permute-start(bf16[160,320]{1,0:T(8,128)(2,1)S(1)} %dynamic-slice_bitcast_fusion.1), channel_id=1, source_target_pairs={{1,0},{2,1},{3,2},{0,3},{5,4},{6,5},{7,6},{4,7},{9,8},{10,9},{11,1... | collective-permute-start | bytes 307208 | tf_op jit(solution)/shard_map/ppermute | solution.py:304
  18.1 1.7 %second_conv.1 = (bf16[256,320]{1,0:T(8,128)(2,1)S(1)}, bf16[256,320]{1,0:T(8,128)(2,1)S(1)}) custom-call(bf16[256,320]{1,0:T(8,128)(2,1)S(1)} %get-tuple-element.29.source, f32[256,320]{1,0:T(8,128)S(1)} %get-tuple-element.30.inner, f32[1,320]{1,0:T(1,128)S(1)} %add.77.bias, bf16[3,960,320]{2,1,0:T(8,128)(2,1)S(1)} %bitcast.26), custom_call_target="tpu_custom_call" | custom-call | flops 471859200 | bytes 2498560 | tf_op jit(solution)/shard_map/second_conv/pallas_call | solution.py:405
  19.8 1.1 %collective-permute-done.2.refs_2_ = bf16[160,320]{1,0:T(8,128)(2,1)S(1)} collective-permute-done((bf16[160,320]{1,0:T(8,128)(2,1)S(1)}, bf16[160,320]{1,0:T(8,128)(2,1)S(1)}, u32[]{:S(2)}, u32[]{:S(2)}) %collective-permute-start.2) | collective-permute-done | bytes 102432 | tf_op jit(solution)/shard_map/ppermute | solution.py:304
  20.9 1.5 %collective-permute-start.7 = (bf16[256,320]{1,0:T(8,128)(2,1)S(1)}, bf16[256,320]{1,0:T(8,128)(2,1)S(1)}, u32[]{:S(2)}, u32[]{:S(2)}) collective-permute-start(bf16[256,320]{1,0:T(8,128)(2,1)S(1)} %get-tuple-element.34.normed.refs_5_), channel_id=1, source_target_pairs={{0,8},{4,12},{8,0},{12,4},{1,9},{5,13},{9,1},{13,5},{2,10},{6,14},... | collective-permute-start | bytes 491528 | tf_op jit(solution)/shard_map/ppermute | solution.py:275
  22.4 4.1 %collective-permute-done.4.refs_1_ = bf16[160,320]{1,0:T(8,128)(2,1)S(1)} collective-permute-done((bf16[160,320]{1,0:T(8,128)(2,1)S(1)}, bf16[160,320]{1,0:T(8,128)(2,1)S(1)}, u32[]{:S(2)}, u32[]{:S(2)}) %collective-permute-start.4) | collective-permute-done | bytes 102432 | tf_op jit(solution)/shard_map/ppermute | solution.py:302
  27.3 3.2 %collective-permute-start.11 = (bf16[160,320]{1,0:T(8,128)(2,1)S(1)}, bf16[160,320]{1,0:T(8,128)(2,1)S(1)}, u32[]{:S(2)}, u32[]{:S(2)}) collective-permute-start(bf16[160,320]{1,0:T(8,128)(2,1)S(1)} %dynamic-slice_bitcast_fusion), channel_id=1, source_target_pairs={{0,3},{1,2},{2,1},{3,0},{4,7},{5,6},{6,5},{7,4},{8,11},{9,10},{10,... | collective-permute-start | bytes 307208 | tf_op jit(solution)/shard_map/ppermute | solution.py:428
  30.5 1.2 %collective-permute-start.9 = (bf16[160,320]{1,0:T(8,128)(2,1)S(1)}, bf16[160,320]{1,0:T(8,128)(2,1)S(1)}, u32[]{:S(2)}, u32[]{:S(2)}) collective-permute-start(bf16[160,320]{1,0:T(8,128)(2,1)S(1)} %dynamic-slice_bitcast_fusion), channel_id=1, source_target_pairs={{0,1},{1,0},{2,3},{3,2},{4,5},{5,4},{6,7},{7,6},{8,9},{9,8},{10,11... | collective-permute-start | bytes 307208 | tf_op jit(solution)/shard_map/ppermute | solution.py:428
  32.3 1.9 %query.1 = (f32[320,256]{1,0:T(8,128)S(1)}, bf16[4,320,320]{2,1,0:T(8,128)(2,1)S(1)}) custom-call(s32[5]{0:T(128)S(1)} %stack.39.where, bf16[256,320]{1,0:T(8,128)(2,1)S(1)} %get-tuple-element.34.normed.refs_5_, bf16[3,80,320]{2,1,0:T(8,128)(2,1)} %three.2, bf16[80,320]{1,0:T(8,128)(2,1)} %one.2, bf16[160,320]{1,0:T(8,128)(2,1)S(1)} %collective-permute-done.3.refs_0_, ...), custom_call_target="tpu_custom_call" | custom-call | tf_op jit(solution)/shard_map/query/pallas_call | solution.py:437
  34.2 6.5 %cross_view.1 = (bf16[256,320]{1,0:T(8,128)(2,1)S(1)}, bf16[256,320]{1,0:T(8,128)(2,1)S(1)}) custom-call(s32[2]{0:T(128)S(1)} %xor_reduce_fusion.refs_0_, s32[8]{0:T(128)S(1)} %reshape.93.refs_1_, bf16[256,320]{1,0:T(8,128)(2,1)S(1)} %get-tuple-element.31.refs_2_, f32[320,256]{1,0:T(8,128)S(1)} %get-tuple-element.36.refs_3_, ...), custom_call_target="tpu_custom_call" | custom-call | tf_op jit(solution)/shard_map/cross_view/pallas_call | solution.py:449
  40.7 1.6 %collective-permute-done.10.refs_1_ = bf16[160,320]{1,0:T(8,128)(2,1)S(1)} collective-permute-done((bf16[160,320]{1,0:T(8,128)(2,1)S(1)}, bf16[160,320]{1,0:T(8,128)(2,1)S(1)}, u32[]{:S(2)}, u32[]{:S(2)}) %collective-permute-start.10) | collective-permute-done | bytes 102432 | tf_op jit(solution)/shard_map/ppermute | solution.py:428
  42.5 3.8 %collective-permute-start.15 = (bf16[256,320]{1,0:T(8,128)(2,1)S(1)}, bf16[256,320]{1,0:T(8,128)(2,1)S(1)}, u32[]{:S(2)}, u32[]{:S(2)}) collective-permute-start(bf16[256,320]{1,0:T(8,128)(2,1)S(1)} %get-tuple-element.41.rows), channel_id=1, source_target_pairs={{1,0},{2,1},{3,2},{0,3},{5,4},{6,5},{7,6},{4,7},{9,8},{10,9},{11,1... | collective-permute-start | bytes 491528 | tf_op jit(solution)/shard_map/ppermute | solution.py:304
  46.3 5.7 %collective-permute-done.13.rows = bf16[256,320]{1,0:T(8,128)(2,1)S(1)} collective-permute-done((bf16[256,320]{1,0:T(8,128)(2,1)S(1)}, bf16[256,320]{1,0:T(8,128)(2,1)S(1)}, u32[]{:S(2)}, u32[]{:S(2)}) %collective-permute-start.13) | collective-permute-done | bytes 163872 | tf_op jit(solution)/shard_map/ppermute | solution.py:302
  52.1 2.3 %own_frame.1 = (bf16[4,320,320]{2,1,0:T(8,128)(2,1)S(1)}, bf16[256,320]{1,0:T(8,128)(2,1)S(1)}, f32[256,320]{1,0:T(8,128)S(1)}, bf16[256,320]{1,0:T(8,128)(2,1)S(1)}) custom-call(s32[5]{0:T(128)S(1)} %stack.44.where, bf16[256,320]{1,0:T(8,128)(2,1)S(1)} %get-tuple-element.41.rows, bf16[3,80,320]{2,1,0:T(8,128)(2,1)} %three.3, bf16[80,320]{1,0:T(8,128)(2,1)} %one.3, ...), custom_call_target="tpu_custom_call" | custom-call | flops 209715200 | bytes 1474560 | tf_op jit(solution)/shard_map/own_frame/pallas_call | solution.py:476
  54.4 0.6 %other_frame.2 = (f32[256,320]{1,0:T(8,128)S(1)}, bf16[256,320]{1,0:T(8,128)(2,1)S(1)}) custom-call(bf16[256,320]{1,0:T(8,128)(2,1)S(1)} %get-tuple-element.45.queries.refs_1_, bf16[256,320]{1,0:T(8,128)(2,1)S(1)} %collective-permute-done.13.rows, bf16[4,320,320]{2,1,0:T(8,128)(2,1)S(1)} %get-tuple-element.46.weights.refs_3_), custom_call_target="tpu_custom_call" | custom-call | flops 209715200 | bytes 1474560 | tf_op jit(solution)/shard_map/other_frame/pallas_call | solution.py:489
  55.1 0.6 %other_frame.3 = (f32[256,320]{1,0:T(8,128)S(1)}, bf16[256,320]{1,0:T(8,128)(2,1)S(1)}) custom-call(bf16[256,320]{1,0:T(8,128)(2,1)S(1)} %get-tuple-element.45.queries.refs_1_, bf16[256,320]{1,0:T(8,128)(2,1)S(1)} %collective-permute-done.15.rows, bf16[4,320,320]{2,1,0:T(8,128)(2,1)S(1)} %get-tuple-element.46.weights.refs_3_), custom_call_target="tpu_custom_call" | custom-call | flops 209715200 | bytes 1474560 | tf_op jit(solution)/shard_map/other_frame/pallas_call | solution.py:489
  55.7 4.8 %collective-permute-done.14.refs_2_ = bf16[256,320]{1,0:T(8,128)(2,1)S(1)} collective-permute-done((bf16[256,320]{1,0:T(8,128)(2,1)S(1)}, bf16[256,320]{1,0:T(8,128)(2,1)S(1)}, u32[]{:S(2)}, u32[]{:S(2)}) %collective-permute-start.14) | collective-permute-done | bytes 163872 | tf_op jit(solution)/shard_map/ppermute | solution.py:302
  60.6 2.0 %last.1 = bf16[320,256]{1,0:T(8,128)(2,1)} custom-call(bf16[256,320]{1,0:T(8,128)(2,1)S(1)} %get-tuple-element.38.refs_0_, bf16[256,320]{1,0:T(8,128)(2,1)S(1)} %get-tuple-element.45.queries.refs_1_, bf16[256,320]{1,0:T(8,128)(2,1)S(1)} %collective-permute-done.14.refs_2_, bf16[4,320,320]{2,1,0:T(8,128)(2,1)S(1)} %get-tuple-element.46.weights.refs_3_, ...), custom_call_target="tpu_custom_call" | custom-call | tf_op jit(solution)/shard_map/last/pallas_call | solution.py:500
  (45 shorter events, 1.8 us)
Async XLA Ops:
  0.0 31.7 %copy-start = (s32[2,4,2,2]{1,3,2,0:T(2,128)S(1)}, s32[2,4,2,2]{1,3,2,0:T(2,128)}, u32[]{:S(2)}) copy-start(s32[2,4,2,2]{1,3,2,0:T(2,128)} %param.14) | copy-start | bytes 388
  0.8 4.3 %copy-start.2 = (bf16[3,80,320]{2,1,0:T(8,128)(2,1)S(1)}, bf16[3,80,320]{2,1,0:T(8,128)(2,1)}, u32[]{:S(2)}) copy-start(bf16[3,80,320]{2,1,0:T(8,128)(2,1)} %three.2) | copy-start | bytes 460804
  0.8 4.3 %copy-start.4 = (bf16[80,320]{1,0:T(8,128)(2,1)S(1)}, bf16[80,320]{1,0:T(8,128)(2,1)}, u32[]{:S(2)}) copy-start(bf16[80,320]{1,0:T(8,128)(2,1)} %one.2) | copy-start | bytes 153604
  1.9 16.1 %copy-start.1 = (bf16[3,3,320,320]{3,2,1,0:T(8,128)(2,1)S(1)}, bf16[3,3,320,320]{3,2,1,0:T(8,128)(2,1)}, u32[]{:S(2)}) copy-start(bf16[3,3,320,320]{3,2,1,0:T(8,128)(2,1)} %param.16) | copy-start | bytes 5529604
  1.9 4.6 %collective-permute-start = (f32[1,320]{1,0:T(1,128)S(1)}, f32[1,320]{1,0:T(1,128)S(1)}, u32[]{:S(2)}, u32[]{:S(2)}) collective-permute-start(f32[1,320]{1,0:T(1,128)S(1)} %time_share.1), channel_id=1, source_target_pairs={{0,1},{1,0},{2,3},{3,2},{4,5},{5,4},{6,7},{7,6},{8,9},{9,8},{10,11... | collective-permute-start | bytes 3848 | tf_op jit(solution)/shard_map/ppermute | solution.py:288
  6.6 4.6 %collective-permute-start.1 = (f32[1,320]{1,0:T(1,128)S(1)}, f32[1,320]{1,0:T(1,128)S(1)}, u32[]{:S(2)}, u32[]{:S(2)}) collective-permute-start(f32[1,320]{1,0:T(1,128)S(1)} %add.76), channel_id=1, source_target_pairs={{0,2},{1,3},{2,0},{3,1},{4,6},{5,7},{6,4},{7,5},{8,10},{9,11},{10,... | collective-permute-start | bytes 3848 | tf_op jit(solution)/shard_map/ppermute | solution.py:288
  11.2 8.6 %collective-permute-start.3 = (bf16[160,320]{1,0:T(8,128)(2,1)S(1)}, bf16[160,320]{1,0:T(8,128)(2,1)S(1)}, u32[]{:S(2)}, u32[]{:S(2)}) collective-permute-start(bf16[160,320]{1,0:T(8,128)(2,1)S(1)} %dynamic-slice_bitcast_fusion.1), channel_id=1, source_target_pairs={{0,1},{1,2},{2,3},{3,0},{4,5},{5,6},{6,7},{7,4},{8,9},{9,10},{10,1... | collective-permute-start | bytes 307208 | tf_op jit(solution)/shard_map/ppermute | solution.py:302
  15.9 10.7 %copy-start.3 = (bf16[3,80,320]{2,1,0:T(8,128)(2,1)S(1)}, bf16[3,80,320]{2,1,0:T(8,128)(2,1)}, u32[]{:S(2)}) copy-start(bf16[3,80,320]{2,1,0:T(8,128)(2,1)} %three.3) | copy-start | bytes 460804
  15.9 10.7 %copy-start.5 = (bf16[80,320]{1,0:T(8,128)(2,1)S(1)}, bf16[80,320]{1,0:T(8,128)(2,1)}, u32[]{:S(2)}) copy-start(bf16[80,320]{1,0:T(8,128)(2,1)} %one.3) | copy-start | bytes 153604
  16.0 16.2 %copy-start.6 = (s32[2,4]{1,0:T(2,128)S(1)}, s32[2,4]{1,0:T(2,128)}, u32[]{:S(2)}) copy-start(s32[2,4]{1,0:T(2,128)} %param.13) | copy-start | bytes 100
  16.0 4.9 %collective-permute-start.2 = (bf16[160,320]{1,0:T(8,128)(2,1)S(1)}, bf16[160,320]{1,0:T(8,128)(2,1)S(1)}, u32[]{:S(2)}, u32[]{:S(2)}) collective-permute-start(bf16[160,320]{1,0:T(8,128)(2,1)S(1)} %dynamic-slice_bitcast_fusion.1), channel_id=1, source_target_pairs={{1,0},{2,1},{3,2},{0,3},{5,4},{6,5},{7,6},{4,7},{9,8},{10,9},{11,1... | collective-permute-start | bytes 307208 | tf_op jit(solution)/shard_map/ppermute | solution.py:304
  19.8 6.7 %collective-permute-start.4 = (bf16[160,320]{1,0:T(8,128)(2,1)S(1)}, bf16[160,320]{1,0:T(8,128)(2,1)S(1)}, u32[]{:S(2)}, u32[]{:S(2)}) collective-permute-start(bf16[160,320]{1,0:T(8,128)(2,1)S(1)} %collective-permute-done.3.refs_0_), channel_id=1, source_target_pairs={{0,1},{1,2},{2,3},{3,0},{4,5},{5,6},{6,7},{7,4},{8,9},{9,10},{10,1... | collective-permute-start | bytes 307208 | tf_op jit(solution)/shard_map/ppermute | solution.py:302
  20.9 5.8 %collective-permute-start.7 = (bf16[256,320]{1,0:T(8,128)(2,1)S(1)}, bf16[256,320]{1,0:T(8,128)(2,1)S(1)}, u32[]{:S(2)}, u32[]{:S(2)}) collective-permute-start(bf16[256,320]{1,0:T(8,128)(2,1)S(1)} %get-tuple-element.34.normed.refs_5_), channel_id=1, source_target_pairs={{0,8},{4,12},{8,0},{12,4},{1,9},{5,13},{9,1},{13,5},{2,10},{6,14},... | collective-permute-start | bytes 491528 | tf_op jit(solution)/shard_map/ppermute | solution.py:275
  22.4 4.9 %collective-permute-start.6 = (bf16[256,320]{1,0:T(8,128)(2,1)S(1)}, bf16[256,320]{1,0:T(8,128)(2,1)S(1)}, u32[]{:S(2)}, u32[]{:S(2)}) collective-permute-start(bf16[256,320]{1,0:T(8,128)(2,1)S(1)} %get-tuple-element.34.normed.refs_5_), channel_id=1, source_target_pairs={{0,4},{4,0},{8,12},{12,8},{1,5},{5,1},{9,13},{13,9},{2,6},{6,2},{1... | collective-permute-start | bytes 491528 | tf_op jit(solution)/shard_map/ppermute | solution.py:275
  26.5 5.8 %collective-permute-start.5 = (bf16[480,320]{1,0:T(8,128)(2,1)S(1)}, bf16[480,320]{1,0:T(8,128)(2,1)S(1)}, u32[]{:S(2)}, u32[]{:S(2)}) collective-permute-start(bf16[480,320]{1,0:T(8,128)(2,1)S(1)} %pad_maximum_fusion), channel_id=1, source_target_pairs={{0,4},{4,0},{8,12},{12,8},{1,5},{5,1},{9,13},{13,9},{2,6},{6,2},{1... | collective-permute-start | bytes 921608 | tf_op jit(solution)/shard_map/ppermute | solution.py:318
  26.7 7.5 %collective-permute-start.8 = (bf16[256,320]{1,0:T(8,128)(2,1)S(1)}, bf16[256,320]{1,0:T(8,128)(2,1)S(1)}, u32[]{:S(2)}, u32[]{:S(2)}) collective-permute-start(bf16[256,320]{1,0:T(8,128)(2,1)S(1)} %collective-permute-done.7.refs_7_), channel_id=1, source_target_pairs={{0,4},{4,0},{8,12},{12,8},{1,5},{5,1},{9,13},{13,9},{2,6},{6,2},{1... | collective-permute-start | bytes 491528 | tf_op jit(solution)/shard_map/ppermute | solution.py:275
  27.3 13.4 %collective-permute-start.11 = (bf16[160,320]{1,0:T(8,128)(2,1)S(1)}, bf16[160,320]{1,0:T(8,128)(2,1)S(1)}, u32[]{:S(2)}, u32[]{:S(2)}) collective-permute-start(bf16[160,320]{1,0:T(8,128)(2,1)S(1)} %dynamic-slice_bitcast_fusion), channel_id=1, source_target_pairs={{0,3},{1,2},{2,1},{3,0},{4,7},{5,6},{6,5},{7,4},{8,11},{9,10},{10,... | collective-permute-start | bytes 307208 | tf_op jit(solution)/shard_map/ppermute | solution.py:428
  30.5 11.8 %collective-permute-start.10 = (bf16[160,320]{1,0:T(8,128)(2,1)S(1)}, bf16[160,320]{1,0:T(8,128)(2,1)S(1)}, u32[]{:S(2)}, u32[]{:S(2)}) collective-permute-start(bf16[160,320]{1,0:T(8,128)(2,1)S(1)} %dynamic-slice_bitcast_fusion), channel_id=1, source_target_pairs={{0,2},{1,3},{2,0},{3,1},{4,6},{5,7},{6,4},{7,5},{8,10},{9,11},{10,... | collective-permute-start | bytes 307208 | tf_op jit(solution)/shard_map/ppermute | solution.py:428
  30.5 11.8 %collective-permute-start.9 = (bf16[160,320]{1,0:T(8,128)(2,1)S(1)}, bf16[160,320]{1,0:T(8,128)(2,1)S(1)}, u32[]{:S(2)}, u32[]{:S(2)}) collective-permute-start(bf16[160,320]{1,0:T(8,128)(2,1)S(1)} %dynamic-slice_bitcast_fusion), channel_id=1, source_target_pairs={{0,1},{1,0},{2,3},{3,2},{4,5},{5,4},{6,7},{7,6},{8,9},{9,8},{10,11... | collective-permute-start | bytes 307208 | tf_op jit(solution)/shard_map/ppermute | solution.py:428
  42.4 9.8 %collective-permute-start.12 = (bf16[480,320]{1,0:T(8,128)(2,1)S(1)}, bf16[480,320]{1,0:T(8,128)(2,1)S(1)}, u32[]{:S(2)}, u32[]{:S(2)}) collective-permute-start(bf16[480,320]{1,0:T(8,128)(2,1)S(1)} %pad_maximum_fusion.1), channel_id=1, source_target_pairs={{0,4},{4,0},{8,12},{12,8},{1,5},{5,1},{9,13},{13,9},{2,6},{6,2},{1... | collective-permute-start | bytes 921608 | tf_op jit(solution)/shard_map/ppermute | solution.py:318
  42.5 9.6 %collective-permute-start.13 = (bf16[256,320]{1,0:T(8,128)(2,1)S(1)}, bf16[256,320]{1,0:T(8,128)(2,1)S(1)}, u32[]{:S(2)}, u32[]{:S(2)}) collective-permute-start(bf16[256,320]{1,0:T(8,128)(2,1)S(1)} %get-tuple-element.41.rows), channel_id=1, source_target_pairs={{0,1},{1,2},{2,3},{3,0},{4,5},{5,6},{6,7},{7,4},{8,9},{9,10},{10,1... | collective-permute-start | bytes 491528 | tf_op jit(solution)/shard_map/ppermute | solution.py:302
  42.5 12.6 %collective-permute-start.15 = (bf16[256,320]{1,0:T(8,128)(2,1)S(1)}, bf16[256,320]{1,0:T(8,128)(2,1)S(1)}, u32[]{:S(2)}, u32[]{:S(2)}) collective-permute-start(bf16[256,320]{1,0:T(8,128)(2,1)S(1)} %get-tuple-element.41.rows), channel_id=1, source_target_pairs={{1,0},{2,1},{3,2},{0,3},{5,4},{6,5},{7,6},{4,7},{9,8},{10,9},{11,1... | collective-permute-start | bytes 491528 | tf_op jit(solution)/shard_map/ppermute | solution.py:304
  52.1 8.5 %collective-permute-start.14 = (bf16[256,320]{1,0:T(8,128)(2,1)S(1)}, bf16[256,320]{1,0:T(8,128)(2,1)S(1)}, u32[]{:S(2)}, u32[]{:S(2)}) collective-permute-start(bf16[256,320]{1,0:T(8,128)(2,1)S(1)} %collective-permute-done.13.rows), channel_id=1, source_target_pairs={{0,1},{1,2},{2,3},{3,0},{4,5},{5,6},{6,7},{7,4},{8,9},{9,10},{10,1... | collective-permute-start | bytes 491528 | tf_op jit(solution)/shard_map/ppermute | solution.py:302

commit v9 on v8

--- a/solution.py
+++ b/solution.py
@@ -134,19 +134,20 @@
     return copies + [fetch(one, whole.at[3, place], sems.at[3])]
 
 
-def assemble(where, side, parts, whole, rows):
+def assemble(where, side, parts, whole, rows, first):
     for k, part in enumerate(parts[:-1]):
         place = pl.ds(pl.multiple_of(where[k + 1] * rows, 16), rows)
         for j in range(2):
             mine = side * 2 + j
-            whole[mine, place, :] = part[pl.ds(j * rows, rows), :]
-            whole[2 - mine + 2 * j, place, :] = parts[-1][pl.ds((2 * k + j) * rows, rows), :]
+            whole[mine, place, :] = part[pl.ds((first + j) * rows, rows), :]
+            start = (2 * k + j) * rows
+            whole[2 - mine + 2 * j, place, :] = parts[-1][pl.ds(start, rows), :]
 
 
 def query_kernel(where, normed, three, one, *refs):
     parts, (queries, epi, sems) = refs[:-3], refs[-3:]
     copies = fetch_own(where, three, one, epi, sems)
-    assemble(where, where[max(1, len(parts))], parts, epi, one.shape[0])
+    assemble(where, where[max(1, len(parts))], parts, epi, one.shape[0], 0)
     for copy in copies:
         copy.wait()
     queries[...] = dot(normed[...], epi[0]).astype(bf16).astype(f32).T
@@ -222,7 +223,7 @@
 def own_frame_kernel(where, rows, three, one, *refs):
     parts, (weights, queries, scores, values, sems) = refs[:-5], refs[-5:]
     copies = fetch_own(where, three, one, weights, sems)
-    assemble(where, where[max(1, len(parts))], parts, weights, one.shape[0])
+    assemble(where, where[max(1, len(parts))], parts, weights, one.shape[0], 2)
     for copy in copies:
         copy.wait()
     queries[...] = dot(rows[...], weights[0]).astype(bf16)
@@ -266,13 +267,14 @@
     return (me + sign * k) % size
 
 
-def gather_maps(own, axis, size):
+def gather_maps(own, axis, size, beside=None):
     maps = {0: own}
     if is_power(size):
         bit = size // 2
         while bit:
             for k in list(maps):
-                maps[k | bit] = lax.ppermute(maps[k], axis, partner_permutation(size, bit))
+                sent = maps[k] if k == 0 or beside is None else after(maps[k], beside)
+                maps[k | bit] = lax.ppermute(sent, axis, partner_permutation(size, bit))
             bit //= 2
     else:
         for k in range(1, size):
@@ -313,9 +315,9 @@
     return lax.dynamic_index_in_dim(whole, side, 0, keepdims=False)
 
 
-def swap(pieces, videos):
-    joined = jnp.concatenate(pieces[1:], axis=0)
-    return pieces[1:] + [lax.ppermute(joined, "video", partner_permutation(videos, 1))]
+def swap(pieces, first, rows, videos):
+    joined = jnp.concatenate([piece[first : first + rows] for piece in pieces], axis=0)
+    return lax.ppermute(joined, "video", partner_permutation(videos, 1))
 
 
 def per_device(
@@ -372,10 +374,6 @@
         temp_in = lax.all_gather(temp_in, "frame", axis=1, tiled=True)
         temp_out = lax.all_gather(temp_out, "frame", axis=0, tiled=True)
     places = jnp.stack(places).astype(jnp.int32)
-    temp_places = places
-    if paired:
-        temp_places = [partner(frame, frames, k, -1) for k in range(frames)] + [video % 2]
-        temp_places = jnp.stack(temp_places).astype(jnp.int32)
 
     source_scratch = pltpu.VMEM((channels, tokens), bf16)
     padded_scratch = pltpu.VMEM((tokens + 2 * W, 3 * channels), bf16)
@@ -415,18 +413,21 @@
         cost_estimate=conv_cost,
         name="second_conv",
     )(turned, inner, bias, conv_second.reshape(3, 3 * channels, channels))
+    parts = []
+    last_part = None
     if paired:
-        mine = half_of(epi_in, epi_out, video % 2)
-        epi_parts = ring_gather(after(mine, bias), "frame", frames, normed)
-        normed = after(normed, epi_parts[-1])
-    maps = gather_maps(normed, "video", videos)
-    epi_parts = swap(epi_parts, videos) if paired else []
-    temp_parts = []
+        mine = jnp.concatenate(
+            [half_of(epi_in, epi_out, video % 2), half_of(temp_in, temp_out, video % 2)], axis=0
+        )
+        parts = ring_gather(after(mine, bias), "frame", frames, normed)
+        normed = after(normed, parts[1 % frames], parts[-1])
+        last_part = parts[frames // 2]
+    maps = gather_maps(normed, "video", videos, last_part)
+    epi_parts = temp_parts = []
     if paired:
-        mine = after(half_of(temp_in, temp_out, video % 2), maps[1])
-        temp_parts = [mine] + [
-            lax.ppermute(mine, "frame", partner_permutation(frames, k)) for k in range(1, frames)
-        ]
+        parts = parts[1:]
+        epi_parts = parts + [swap(parts, 0, 2 * height, videos)]
+        temp_parts = parts + [swap(parts, 2 * height, 2 * height, videos)]
     targets = lax.dynamic_index_in_dim(matchings, video, 1, keepdims=False)
     if is_power(videos):
         select = video ^ targets
@@ -461,10 +462,6 @@
         name="cross_view",
     )(select, mask, hidden, queries, epi, *maps)
 
-    if paired:
-        held = [after(part, blocks) for part in temp_parts]
-        blocks = after(blocks, *temp_parts)
-        temp_parts = swap(held, videos)
     arrived = ring_gather(blocks, "frame", frames)
     score_shape = jax.ShapeDtypeStruct((tokens, channels), f32)
     value_shape = jax.ShapeDtypeStruct((tokens, channels), bf16)
@@ -476,13 +473,13 @@
     temp, frame_queries, *first = pl.pallas_call(
         own_frame_kernel,
         out_shape=[jax.ShapeDtypeStruct(square, bf16), value_shape, score_shape, value_shape],
-        in_specs=[SMEM, VMEM, HBM, HBM] + [VMEM] * len(temp_parts),
+        in_specs=[SMEM, VMEM, HBM, HBM] + [VMEM] * len(epi_parts),
         out_specs=[VMEM] * 4,
         scratch_shapes=[pltpu.SemaphoreType.DMA((4,))],
         compiler_params=params(),
         cost_estimate=frame_cost,
         name="own_frame",
-    )(temp_places, blocks, in_hbm(temp_in), in_hbm(temp_out), *temp_parts)
+    )(places, blocks, in_hbm(temp_in), in_hbm(temp_out), *temp_parts)
     scores, values = [first[0]], [first[1]]
     order = sorted(range(1, frames), key=lambda k: min(k, frames - k))
     for k in order[:-1]:

time: 62.8 us -> 61.2 us (0.975)
  starting transfers between devices: 20.7 us -> 17.2 us
  other arithmetic: 0.46 us -> 1.96 us
    ppermute x8 -> x5, starting transfers between devices: 6.63 us -> 2.01 us  [the longest x3 1.5 us: gather_maps(): maps[k | bit] = lax.ppermute(sent, axis, partner_permutation(size, bit))]
    ppermute x2, waiting for transfers between devices: 1.07 us -> 3.9 us  [ring_gather(): lax.ppermute(pieces[(size - step + 1) % size], axis, left)]
    ppermute x4, starting transfers between devices: 2.03 us -> 4.79 us  [ring_gather(): pieces[step] = lax.ppermute(pieces[step - 1], axis, right)]
    ppermute x2, starting transfers between devices: 5.89 us -> 4.29 us  [ring_gather(): lax.ppermute(pieces[(size - step + 1) % size], axis, left)]
    concatenate x2 -> x3, other arithmetic: 0.09 us -> 1.59 us  [the longest x2 1.56 us: swap(): jnp.concatenate([piece[first:first + rows] for piece in pieces], axis=0)]
    ppermute x8 -> x5, waiting for transfers between devices: 1.65 us -> 0.38 us  [the longest x3 0.38 us: gather_maps(): maps[k | bit] = lax.ppermute(sent, axis, partner_permutation(size, bit))]
    ppermute x4, waiting for transfers between devices: 14.7 us -> 13.6 us  [ring_gather(): pieces[step] = lax.ppermute(pieces[step - 1], axis, right)]
  transfers between devices with their start and end apart: 16 -> 13, of which waited for: 7 -> 8; matrix products, arithmetic and copies ran while one was open for 1% -> 4% of each run, Pallas kernels for 26% -> 27%
where the time goes in v9:
time: 61.2 us; the launch traced here: 61 us
  waiting for transfers between devices  20.8 us (34%)
  Pallas kernels  19.6 us (32%)
  starting transfers between devices  17.2 us (28%)
  other arithmetic  1.96 us (3%)
  between operations  0.88 us (1%)
    ppermute x4, waiting for transfers between devices, ring_gather(): pieces[step] = lax.ppermute(pieces[step - 1], axis, right)  13.6 us
    pallas_call x1, Pallas kernels, per_device(): pl.pallas_call(functools.partial(view_kernel, videos, tiles), out_shape=[...  6.45 us
    ppermute x2, starting transfers between devices, sum_over(): value = value + lax.ppermute(value, axis, partner_permutation(size, bit))  6.12 us
    ppermute x4, starting transfers between devices, ring_gather(): pieces[step] = lax.ppermute(pieces[step - 1], axis, right)  4.79 us
    ppermute x2, starting transfers between devices, ring_gather(): lax.ppermute(pieces[(size - step + 1) % size], axis, left)  4.29 us
    ppermute x2, waiting for transfers between devices, ring_gather(): lax.ppermute(pieces[(size - step + 1) % size], axis, left)  3.9 us
    ppermute x2, waiting for transfers between devices, sum_over(): value = value + lax.ppermute(value, axis, partner_permutation(size, bit))  2.91 us
    pallas_call x1, Pallas kernels, per_device(): pl.pallas_call(first_kernel, out_shape=[jax.ShapeDtypeStruct((tokens, cha...  2.82 us
  transfers between devices with their start and end apart: 13, of which 8 were waited for; matrix products, arithmetic and copies ran while one was open for 4% of the time, Pallas kernels for 27%

profile of v9, /device:TPU:0, one launch (start us, length us, event | category | flops | bytes accessed | tf_op | source)
XLA Modules:
  0.0 61.0 jit_solution(4679845172131927970)
XLA Ops:
  0.8 1.2 %time_share.1 = f32[1,320]{1,0:T(1,128)S(1)} custom-call(bf16[1,320]{1,0:T(2,128)(2,1)S(1)} %fusion.4.act, bf16[320,320]{1,0:T(8,128)(2,1)} %proj_hbm.1), custom_call_target="tpu_custom_call" | custom-call | flops 10000000000 | bytes 1048576 | tf_op jit(solution)/shard_map/time_share/pallas_call | solution.py:356
  2.0 3.1 %collective-permute-start = (f32[1,320]{1,0:T(1,128)S(1)}, f32[1,320]{1,0:T(1,128)S(1)}, u32[]{:S(2)}, u32[]{:S(2)}) collective-permute-start(f32[1,320]{1,0:T(1,128)S(1)} %time_share.1), channel_id=1, source_target_pairs={{0,1},{1,0},{2,3},{3,2},{4,5},{5,4},{6,7},{7,6},{8,9},{9,8},{10,11... | collective-permute-start | bytes 3848 | tf_op jit(solution)/shard_map/ppermute | solution.py:290
  5.3 1.4 %collective-permute-done = f32[1,320]{1,0:T(1,128)S(1)} collective-permute-done((f32[1,320]{1,0:T(1,128)S(1)}, f32[1,320]{1,0:T(1,128)S(1)}, u32[]{:S(2)}, u32[]{:S(2)}) %collective-permute-start) | collective-permute-done | bytes 1312 | tf_op jit(solution)/shard_map/ppermute | solution.py:290
  6.6 3.0 %collective-permute-start.1 = (f32[1,320]{1,0:T(1,128)S(1)}, f32[1,320]{1,0:T(1,128)S(1)}, u32[]{:S(2)}, u32[]{:S(2)}) collective-permute-start(f32[1,320]{1,0:T(1,128)S(1)} %add.75), channel_id=1, source_target_pairs={{0,2},{1,3},{2,0},{3,1},{4,6},{5,7},{6,4},{7,5},{8,10},{9,11},{10,... | collective-permute-start | bytes 3848 | tf_op jit(solution)/shard_map/ppermute | solution.py:290
  9.7 1.5 %collective-permute-done.1 = f32[1,320]{1,0:T(1,128)S(1)} collective-permute-done((f32[1,320]{1,0:T(1,128)S(1)}, f32[1,320]{1,0:T(1,128)S(1)}, u32[]{:S(2)}, u32[]{:S(2)}) %collective-permute-start.1) | collective-permute-done | bytes 1312 | tf_op jit(solution)/shard_map/ppermute | solution.py:290
  11.2 1.9 %collective-permute-start.2 = (bf16[320,320]{1,0:T(8,128)(2,1)S(1)}, bf16[320,320]{1,0:T(8,128)(2,1)S(1)}, u32[]{:S(2)}, u32[]{:S(2)}) collective-permute-start(bf16[320,320]{1,0:T(8,128)(2,1)S(1)} %pad_maximum_fusion.4), channel_id=1, source_target_pairs={{0,1},{1,2},{2,3},{3,0},{4,5},{5,6},{6,7},{7,4},{8,9},{9,10},{10,1... | collective-permute-start | bytes 614408 | tf_op jit(solution)/shard_map/ppermute | solution.py:304
  13.2 2.8 %first_conv.1 = (f32[256,320]{1,0:T(8,128)S(1)}, bf16[256,320]{1,0:T(8,128)(2,1)S(1)}) custom-call(bf16[320,256]{1,0:T(8,128)(2,1)} %bitcast.28, bf16[3,960,320]{2,1,0:T(8,128)(2,1)} %bitcast.23), custom_call_target="tpu_custom_call" | custom-call | flops 471859200 | bytes 2498560 | tf_op jit(solution)/shard_map/first_conv/pallas_call | solution.py:385
  16.0 2.1 %collective-permute-start.3 = (bf16[320,320]{1,0:T(8,128)(2,1)S(1)}, bf16[320,320]{1,0:T(8,128)(2,1)S(1)}, u32[]{:S(2)}, u32[]{:S(2)}) collective-permute-start(bf16[320,320]{1,0:T(8,128)(2,1)S(1)} %pad_maximum_fusion.4), channel_id=1, source_target_pairs={{1,0},{2,1},{3,2},{0,3},{5,4},{6,5},{7,6},{4,7},{9,8},{10,9},{11,1... | collective-permute-start | bytes 614408 | tf_op jit(solution)/shard_map/ppermute | solution.py:306
  18.1 1.7 %second_conv.1 = (bf16[256,320]{1,0:T(8,128)(2,1)S(1)}, bf16[256,320]{1,0:T(8,128)(2,1)S(1)}) custom-call(bf16[256,320]{1,0:T(8,128)(2,1)S(1)} %get-tuple-element.25.source, f32[256,320]{1,0:T(8,128)S(1)} %get-tuple-element.26.inner, f32[1,320]{1,0:T(1,128)S(1)} %add.76.bias, bf16[3,960,320]{2,1,0:T(8,128)(2,1)S(1)} %bitcast.22), custom_call_target="tpu_custom_call" | custom-call | flops 471859200 | bytes 2498560 | tf_op jit(solution)/shard_map/second_conv/pallas_call | solution.py:403
  19.8 1.0 %collective-permute-done.2.refs_0_ = bf16[320,320]{1,0:T(8,128)(2,1)S(1)} collective-permute-done((bf16[320,320]{1,0:T(8,128)(2,1)S(1)}, bf16[320,320]{1,0:T(8,128)(2,1)S(1)}, u32[]{:S(2)}, u32[]{:S(2)}) %collective-permute-start.2) | collective-permute-done | bytes 204832 | tf_op jit(solution)/shard_map/ppermute | solution.py:304
  20.8 1.2 %collective-permute-start.4 = (bf16[320,320]{1,0:T(8,128)(2,1)S(1)}, bf16[320,320]{1,0:T(8,128)(2,1)S(1)}, u32[]{:S(2)}, u32[]{:S(2)}) collective-permute-start(bf16[320,320]{1,0:T(8,128)(2,1)S(1)} %collective-permute-done.2.refs_0_), channel_id=1, source_target_pairs={{0,1},{1,2},{2,3},{3,0},{4,5},{5,6},{6,7},{7,4},{8,9},{9,10},{10,1... | collective-permute-start | bytes 614408 | tf_op jit(solution)/shard_map/ppermute | solution.py:304
  22.0 3.9 %collective-permute-done.3.refs_2_ = bf16[320,320]{1,0:T(8,128)(2,1)S(1)} collective-permute-done((bf16[320,320]{1,0:T(8,128)(2,1)S(1)}, bf16[320,320]{1,0:T(8,128)(2,1)S(1)}, u32[]{:S(2)}, u32[]{:S(2)}) %collective-permute-start.3) | collective-permute-done | bytes 204832 | tf_op jit(solution)/shard_map/ppermute | solution.py:306
  25.9 1.0 %collective-permute-start.7 = (bf16[256,320]{1,0:T(8,128)(2,1)S(1)}, bf16[256,320]{1,0:T(8,128)(2,1)S(1)}, u32[]{:S(2)}, u32[]{:S(2)}) collective-permute-start(bf16[256,320]{1,0:T(8,128)(2,1)S(1)} %get-tuple-element.31.normed.refs_5_), channel_id=1, source_target_pairs={{0,8},{4,12},{8,0},{12,4},{1,9},{5,13},{9,1},{13,5},{2,10},{6,14},... | collective-permute-start | bytes 491528 | tf_op jit(solution)/shard_map/ppermute | solution.py:277
  26.9 3.0 %collective-permute-done.4.refs_1_ = bf16[320,320]{1,0:T(8,128)(2,1)S(1)} collective-permute-done((bf16[320,320]{1,0:T(8,128)(2,1)S(1)}, bf16[320,320]{1,0:T(8,128)(2,1)S(1)}, u32[]{:S(2)}, u32[]{:S(2)}) %collective-permute-start.4) | collective-permute-done | bytes 204832 | tf_op jit(solution)/shard_map/ppermute | solution.py:304
  29.9 0.8 %pad_maximum_fusion = bf16[480,320]{1,0:T(8,128)(2,1)} fusion(bf16[160,320]{1,0:T(8,128)(2,1)S(1)} %get-tuple-element.50, bf16[160,320]{1,0:T(8,128)(2,1)S(1)} %get-tuple-element.48, bf16[160,320]{1,0:T(8,128)(2,1)S(1)} %get-tuple-element.46), kind=kLoop, calls=%fused_computation | loop fusion | flops 921600 | bytes 614400 | tf_op jit(solution)/shard_map/concatenate | solution.py:319
  31.6 0.8 %pad_maximum_fusion.1 = bf16[480,320]{1,0:T(8,128)(2,1)} fusion(bf16[160,320]{1,0:T(8,128)(2,1)S(1)} %get-tuple-element.49, bf16[160,320]{1,0:T(8,128)(2,1)S(1)} %get-tuple-element.47, bf16[160,320]{1,0:T(8,128)(2,1)S(1)} %get-tuple-element.45), kind=kLoop, calls=%fused_computation.1 | loop fusion | flops 921600 | bytes 614400 | tf_op jit(solution)/shard_map/concatenate | solution.py:319
  33.5 1.9 %query.1 = (f32[320,256]{1,0:T(8,128)S(1)}, bf16[4,320,320]{2,1,0:T(8,128)(2,1)S(1)}) custom-call(s32[5]{0:T(128)S(1)} %stack.23.where, bf16[256,320]{1,0:T(8,128)(2,1)S(1)} %get-tuple-element.31.normed.refs_5_, bf16[3,80,320]{2,1,0:T(8,128)(2,1)} %three.2, bf16[80,320]{1,0:T(8,128)(2,1)} %one.2, bf16[320,320]{1,0:T(8,128)(2,1)S(1)} %collective-permute-done.2.refs_0_, ...), custom_call_target="tpu_custom_call" | custom-call | tf_op jit(solution)/shard_map/query/pallas_call | solution.py:438
  35.3 6.5 %cross_view.1 = (bf16[256,320]{1,0:T(8,128)(2,1)S(1)}, bf16[256,320]{1,0:T(8,128)(2,1)S(1)}) custom-call(s32[2]{0:T(128)S(1)} %xor_reduce_fusion.refs_0_, s32[8]{0:T(128)S(1)} %reshape.93.refs_1_, bf16[256,320]{1,0:T(8,128)(2,1)S(1)} %get-tuple-element.27.refs_2_, f32[320,256]{1,0:T(8,128)S(1)} %get-tuple-element.32.refs_3_, ...), custom_call_target="tpu_custom_call" | custom-call | tf_op jit(solution)/shard_map/cross_view/pallas_call | solution.py:450
  41.8 1.7 %collective-permute-start.10 = (bf16[256,320]{1,0:T(8,128)(2,1)S(1)}, bf16[256,320]{1,0:T(8,128)(2,1)S(1)}, u32[]{:S(2)}, u32[]{:S(2)}) collective-permute-start(bf16[256,320]{1,0:T(8,128)(2,1)S(1)} %get-tuple-element.36.rows), channel_id=1, source_target_pairs={{0,1},{1,2},{2,3},{3,0},{4,5},{5,6},{6,7},{7,4},{8,9},{9,10},{10,1... | collective-permute-start | bytes 491528 | tf_op jit(solution)/shard_map/ppermute | solution.py:304
  43.5 2.2 %collective-permute-start.12 = (bf16[256,320]{1,0:T(8,128)(2,1)S(1)}, bf16[256,320]{1,0:T(8,128)(2,1)S(1)}, u32[]{:S(2)}, u32[]{:S(2)}) collective-permute-start(bf16[256,320]{1,0:T(8,128)(2,1)S(1)} %get-tuple-element.36.rows), channel_id=1, source_target_pairs={{1,0},{2,1},{3,2},{0,3},{5,4},{6,5},{7,6},{4,7},{9,8},{10,9},{11,1... | collective-permute-start | bytes 491528 | tf_op jit(solution)/shard_map/ppermute | solution.py:306
  45.7 5.8 %collective-permute-done.10.rows = bf16[256,320]{1,0:T(8,128)(2,1)S(1)} collective-permute-done((bf16[256,320]{1,0:T(8,128)(2,1)S(1)}, bf16[256,320]{1,0:T(8,128)(2,1)S(1)}, u32[]{:S(2)}, u32[]{:S(2)}) %collective-permute-start.10) | collective-permute-done | bytes 163872 | tf_op jit(solution)/shard_map/ppermute | solution.py:304
  51.5 2.3 %own_frame.1 = (bf16[4,320,320]{2,1,0:T(8,128)(2,1)S(1)}, bf16[256,320]{1,0:T(8,128)(2,1)S(1)}, f32[256,320]{1,0:T(8,128)S(1)}, bf16[256,320]{1,0:T(8,128)(2,1)S(1)}) custom-call(s32[5]{0:T(128)S(1)} %stack.23.where, bf16[256,320]{1,0:T(8,128)(2,1)S(1)} %get-tuple-element.36.rows, bf16[3,80,320]{2,1,0:T(8,128)(2,1)} %three.3, bf16[80,320]{1,0:T(8,128)(2,1)} %one.3, ...), custom_call_target="tpu_custom_call" | custom-call | flops 209715200 | bytes 1474560 | tf_op jit(solution)/shard_map/own_frame/pallas_call | solution.py:473
  55.1 3.9 %collective-permute-done.11.refs_2_ = bf16[256,320]{1,0:T(8,128)(2,1)S(1)} collective-permute-done((bf16[256,320]{1,0:T(8,128)(2,1)S(1)}, bf16[256,320]{1,0:T(8,128)(2,1)S(1)}, u32[]{:S(2)}, u32[]{:S(2)}) %collective-permute-start.11) | collective-permute-done | bytes 163872 | tf_op jit(solution)/shard_map/ppermute | solution.py:304
  58.9 2.0 %last.1 = bf16[320,256]{1,0:T(8,128)(2,1)} custom-call(bf16[256,320]{1,0:T(8,128)(2,1)S(1)} %get-tuple-element.35.refs_0_, bf16[256,320]{1,0:T(8,128)(2,1)S(1)} %get-tuple-element.37.queries.refs_1_, bf16[256,320]{1,0:T(8,128)(2,1)S(1)} %collective-permute-done.11.refs_2_, bf16[4,320,320]{2,1,0:T(8,128)(2,1)S(1)} %get-tuple-element.38.weights.refs_3_, ...), custom_call_target="tpu_custom_call" | custom-call | tf_op jit(solution)/shard_map/last/pallas_call | solution.py:497
  (41 shorter events, 3.6 us)
Async XLA Ops:
  0.0 32.9 %copy-start = (s32[2,4,2,2]{1,3,2,0:T(2,128)S(1)}, s32[2,4,2,2]{1,3,2,0:T(2,128)}, u32[]{:S(2)}) copy-start(s32[2,4,2,2]{1,3,2,0:T(2,128)} %param.14) | copy-start | bytes 388
  0.8 4.3 %copy-start.2 = (bf16[3,80,320]{2,1,0:T(8,128)(2,1)S(1)}, bf16[3,80,320]{2,1,0:T(8,128)(2,1)}, u32[]{:S(2)}) copy-start(bf16[3,80,320]{2,1,0:T(8,128)(2,1)} %three.2) | copy-start | bytes 460804
  0.8 4.3 %copy-start.4 = (bf16[80,320]{1,0:T(8,128)(2,1)S(1)}, bf16[80,320]{1,0:T(8,128)(2,1)}, u32[]{:S(2)}) copy-start(bf16[80,320]{1,0:T(8,128)(2,1)} %one.2) | copy-start | bytes 153604
  0.8 4.4 %copy-start.3 = (bf16[3,80,320]{2,1,0:T(8,128)(2,1)S(1)}, bf16[3,80,320]{2,1,0:T(8,128)(2,1)}, u32[]{:S(2)}) copy-start(bf16[3,80,320]{2,1,0:T(8,128)(2,1)} %three.3) | copy-start | bytes 460804
  0.8 4.4 %copy-start.5 = (bf16[80,320]{1,0:T(8,128)(2,1)S(1)}, bf16[80,320]{1,0:T(8,128)(2,1)}, u32[]{:S(2)}) copy-start(bf16[80,320]{1,0:T(8,128)(2,1)} %one.3) | copy-start | bytes 153604
  2.0 16.1 %copy-start.1 = (bf16[3,3,320,320]{3,2,1,0:T(8,128)(2,1)S(1)}, bf16[3,3,320,320]{3,2,1,0:T(8,128)(2,1)}, u32[]{:S(2)}) copy-start(bf16[3,3,320,320]{3,2,1,0:T(8,128)(2,1)} %param.16) | copy-start | bytes 5529604
  2.0 4.6 %collective-permute-start = (f32[1,320]{1,0:T(1,128)S(1)}, f32[1,320]{1,0:T(1,128)S(1)}, u32[]{:S(2)}, u32[]{:S(2)}) collective-permute-start(f32[1,320]{1,0:T(1,128)S(1)} %time_share.1), channel_id=1, source_target_pairs={{0,1},{1,0},{2,3},{3,2},{4,5},{5,4},{6,7},{7,6},{8,9},{9,8},{10,11... | collective-permute-start | bytes 3848 | tf_op jit(solution)/shard_map/ppermute | solution.py:290
  6.6 4.6 %collective-permute-start.1 = (f32[1,320]{1,0:T(1,128)S(1)}, f32[1,320]{1,0:T(1,128)S(1)}, u32[]{:S(2)}, u32[]{:S(2)}) collective-permute-start(f32[1,320]{1,0:T(1,128)S(1)} %add.75), channel_id=1, source_target_pairs={{0,2},{1,3},{2,0},{3,1},{4,6},{5,7},{6,4},{7,5},{8,10},{9,11},{10,... | collective-permute-start | bytes 3848 | tf_op jit(solution)/shard_map/ppermute | solution.py:290
  11.2 9.5 %collective-permute-start.2 = (bf16[320,320]{1,0:T(8,128)(2,1)S(1)}, bf16[320,320]{1,0:T(8,128)(2,1)S(1)}, u32[]{:S(2)}, u32[]{:S(2)}) collective-permute-start(bf16[320,320]{1,0:T(8,128)(2,1)S(1)} %pad_maximum_fusion.4), channel_id=1, source_target_pairs={{0,1},{1,2},{2,3},{3,0},{4,5},{5,6},{6,7},{7,4},{8,9},{9,10},{10,1... | collective-permute-start | bytes 614408 | tf_op jit(solution)/shard_map/ppermute | solution.py:304
  16.0 9.9 %collective-permute-start.3 = (bf16[320,320]{1,0:T(8,128)(2,1)S(1)}, bf16[320,320]{1,0:T(8,128)(2,1)S(1)}, u32[]{:S(2)}, u32[]{:S(2)}) collective-permute-start(bf16[320,320]{1,0:T(8,128)(2,1)S(1)} %pad_maximum_fusion.4), channel_id=1, source_target_pairs={{1,0},{2,1},{3,2},{0,3},{5,4},{6,5},{7,6},{4,7},{9,8},{10,9},{11,1... | collective-permute-start | bytes 614408 | tf_op jit(solution)/shard_map/ppermute | solution.py:306
  19.8 13.5 %copy-start.6 = (s32[2,4]{1,0:T(2,128)S(1)}, s32[2,4]{1,0:T(2,128)}, u32[]{:S(2)}) copy-start(s32[2,4]{1,0:T(2,128)} %param.13) | copy-start | bytes 100
  20.8 9.1 %collective-permute-start.4 = (bf16[320,320]{1,0:T(8,128)(2,1)S(1)}, bf16[320,320]{1,0:T(8,128)(2,1)S(1)}, u32[]{:S(2)}, u32[]{:S(2)}) collective-permute-start(bf16[320,320]{1,0:T(8,128)(2,1)S(1)} %collective-permute-done.2.refs_0_), channel_id=1, source_target_pairs={{0,1},{1,2},{2,3},{3,0},{4,5},{5,6},{6,7},{7,4},{8,9},{9,10},{10,1... | collective-permute-start | bytes 614408 | tf_op jit(solution)/shard_map/ppermute | solution.py:304
  25.9 5.7 %collective-permute-start.7 = (bf16[256,320]{1,0:T(8,128)(2,1)S(1)}, bf16[256,320]{1,0:T(8,128)(2,1)S(1)}, u32[]{:S(2)}, u32[]{:S(2)}) collective-permute-start(bf16[256,320]{1,0:T(8,128)(2,1)S(1)} %get-tuple-element.31.normed.refs_5_), channel_id=1, source_target_pairs={{0,8},{4,12},{8,0},{12,4},{1,9},{5,13},{9,1},{13,5},{2,10},{6,14},... | collective-permute-start | bytes 491528 | tf_op jit(solution)/shard_map/ppermute | solution.py:277
  30.7 2.8 %collective-permute-start.5 = (bf16[480,320]{1,0:T(8,128)(2,1)}, bf16[480,320]{1,0:T(8,128)(2,1)S(1)}, u32[]{:S(2)}, u32[]{:S(2)}) collective-permute-start(bf16[480,320]{1,0:T(8,128)(2,1)} %pad_maximum_fusion), channel_id=1, source_target_pairs={{0,4},{4,0},{8,12},{12,8},{1,5},{5,1},{9,13},{13,9},{2,6},{6,2},{1... | collective-permute-start | bytes 921608 | tf_op jit(solution)/shard_map/ppermute | solution.py:320
  30.7 4.6 %collective-permute-start.6 = (bf16[256,320]{1,0:T(8,128)(2,1)S(1)}, bf16[256,320]{1,0:T(8,128)(2,1)S(1)}, u32[]{:S(2)}, u32[]{:S(2)}) collective-permute-start(bf16[256,320]{1,0:T(8,128)(2,1)S(1)} %get-tuple-element.31.normed.refs_5_), channel_id=1, source_target_pairs={{0,4},{4,0},{8,12},{12,8},{1,5},{5,1},{9,13},{13,9},{2,6},{6,2},{1... | collective-permute-start | bytes 491528 | tf_op jit(solution)/shard_map/ppermute | solution.py:277
  31.6 3.8 %collective-permute-start.8 = (bf16[256,320]{1,0:T(8,128)(2,1)S(1)}, bf16[256,320]{1,0:T(8,128)(2,1)S(1)}, u32[]{:S(2)}, u32[]{:S(2)}) collective-permute-start(bf16[256,320]{1,0:T(8,128)(2,1)S(1)} %collective-permute-done.7.refs_7_), channel_id=1, source_target_pairs={{0,4},{4,0},{8,12},{12,8},{1,5},{5,1},{9,13},{13,9},{2,6},{6,2},{1... | collective-permute-start | bytes 491528 | tf_op jit(solution)/shard_map/ppermute | solution.py:277
  32.4 19.1 %collective-permute-start.9 = (bf16[480,320]{1,0:T(8,128)(2,1)}, bf16[480,320]{1,0:T(8,128)(2,1)S(1)}, u32[]{:S(2)}, u32[]{:S(2)}) collective-permute-start(bf16[480,320]{1,0:T(8,128)(2,1)} %pad_maximum_fusion.1), channel_id=1, source_target_pairs={{0,4},{4,0},{8,12},{12,8},{1,5},{5,1},{9,13},{13,9},{2,6},{6,2},{1... | collective-permute-start | bytes 921608 | tf_op jit(solution)/shard_map/ppermute | solution.py:320
  41.8 9.7 %collective-permute-start.10 = (bf16[256,320]{1,0:T(8,128)(2,1)S(1)}, bf16[256,320]{1,0:T(8,128)(2,1)S(1)}, u32[]{:S(2)}, u32[]{:S(2)}) collective-permute-start(bf16[256,320]{1,0:T(8,128)(2,1)S(1)} %get-tuple-element.36.rows), channel_id=1, source_target_pairs={{0,1},{1,2},{2,3},{3,0},{4,5},{5,6},{6,7},{7,4},{8,9},{9,10},{10,1... | collective-permute-start | bytes 491528 | tf_op jit(solution)/shard_map/ppermute | solution.py:304
  43.5 10.9 %collective-permute-start.12 = (bf16[256,320]{1,0:T(8,128)(2,1)S(1)}, bf16[256,320]{1,0:T(8,128)(2,1)S(1)}, u32[]{:S(2)}, u32[]{:S(2)}) collective-permute-start(bf16[256,320]{1,0:T(8,128)(2,1)S(1)} %get-tuple-element.36.rows), channel_id=1, source_target_pairs={{1,0},{2,1},{3,2},{0,3},{5,4},{6,5},{7,6},{4,7},{9,8},{10,9},{11,1... | collective-permute-start | bytes 491528 | tf_op jit(solution)/shard_map/ppermute | solution.py:306
  51.5 7.5 %collective-permute-start.11 = (bf16[256,320]{1,0:T(8,128)(2,1)S(1)}, bf16[256,320]{1,0:T(8,128)(2,1)S(1)}, u32[]{:S(2)}, u32[]{:S(2)}) collective-permute-start(bf16[256,320]{1,0:T(8,128)(2,1)S(1)} %collective-permute-done.10.rows), channel_id=1, source_target_pairs={{0,1},{1,2},{2,3},{3,0},{4,5},{5,6},{6,7},{7,4},{8,9},{9,10},{10,1... | collective-permute-start | bytes 491528 | tf_op jit(solution)/shard_map/ppermute | solution.py:304

commit v10 on v8

--- a/solution.py
+++ b/solution.py
@@ -266,13 +266,14 @@
     return (me + sign * k) % size
 
 
-def gather_maps(own, axis, size):
+def gather_maps(own, axis, size, beside=None):
     maps = {0: own}
     if is_power(size):
         bit = size // 2
         while bit:
             for k in list(maps):
-                maps[k | bit] = lax.ppermute(maps[k], axis, partner_permutation(size, bit))
+                sent = maps[k] if k == 0 or beside is None else after(maps[k], beside)
+                maps[k | bit] = lax.ppermute(sent, axis, partner_permutation(size, bit))
             bit //= 2
     else:
         for k in range(1, size):
@@ -280,10 +281,9 @@
     return [maps[k] for k in range(size)]
 
 
-def sum_over(value, axis, size):
+def sum_over(value, axis, size, bit=1):
     if not is_power(size):
         return lax.psum(value, axis)
-    bit = 1
     while bit < size:
         value = value + lax.ppermute(value, axis, partner_permutation(size, bit))
         bit *= 2
@@ -294,17 +294,19 @@
     return lax.optimization_barrier((x, *others))[0]
 
 
-def ring_gather(own, axis, size, beside=None):
-    pieces = {0: own}
+def ring_gather(own, axis, size, beside=None, steps=0, pieces=None):
+    pieces = dict(pieces or {0: own})
     right = [(i, (i + 1) % size) for i in range(size)]
     left = [(j, i) for i, j in right]
-    for step in range(1, size // 2 + 1):
-        pieces[step] = lax.ppermute(pieces[step - 1], axis, right)
-        if size - step > step:
+    for step in range(1, (steps or size // 2) + 1):
+        if step not in pieces:
+            sent = pieces[step - 1]
+            if beside is not None:
+                sent = after(sent, beside)
+            pieces[step] = lax.ppermute(sent, axis, right)
+        if size - step > step and size - step not in pieces:
             pieces[size - step] = lax.ppermute(pieces[(size - step + 1) % size], axis, left)
-        if step == 1 and beside is not None:
-            pieces[1] = after(pieces[1], beside)
-    return [pieces[k] for k in range(size)]
+    return pieces if steps else [pieces[k] for k in range(size)]
 
 
 def half_of(three, one, side):
@@ -361,7 +363,6 @@
         cost_estimate=early,
         name="time_share",
     )(time_act, in_hbm(time_proj))
-    bias = sum_over(share, "frame", frames)
     if paired:
         steps = [frame - k for k in range(frames)]
         places = [step % frames for step in steps] + [video % 2]
@@ -401,7 +402,18 @@
         compiler_params=params(),
         cost_estimate=conv_cost,
         name="first_conv",
-    )(in_hbm(source), in_hbm(conv_first.reshape(3, 3 * channels, channels)))
+    )(in_hbm(after(source, share)), in_hbm(conv_first.reshape(3, 3 * channels, channels)))
+    if paired:
+        mine = half_of(epi_in, epi_out, video % 2)
+        near = ring_gather(mine, "frame", frames, None, 1)
+        bias = share
+        if frames > 1 and is_power(frames):
+            bias = share + lax.ppermute(share, "frame", partner_permutation(frames, 1))
+            bias = after(bias, near[1], near[frames - 1], inner)
+        bias = sum_over(bias, "frame", frames, 2)
+        epi_parts = ring_gather(mine, "frame", frames, bias, 0, near)
+    else:
+        bias = sum_over(share, "frame", frames)
     hidden, normed = pl.pallas_call(
         second_kernel,
         out_shape=[
@@ -415,18 +427,16 @@
         cost_estimate=conv_cost,
         name="second_conv",
     )(turned, inner, bias, conv_second.reshape(3, 3 * channels, channels))
-    if paired:
-        mine = half_of(epi_in, epi_out, video % 2)
-        epi_parts = ring_gather(after(mine, bias), "frame", frames, normed)
-        normed = after(normed, epi_parts[-1])
-    maps = gather_maps(normed, "video", videos)
-    epi_parts = swap(epi_parts, videos) if paired else []
+    last_part, epi_parts = None, list(epi_parts) if paired else []
     temp_parts = []
     if paired:
-        mine = after(half_of(temp_in, temp_out, video % 2), maps[1])
+        mine = after(half_of(temp_in, temp_out, video % 2), normed)
         temp_parts = [mine] + [
             lax.ppermute(mine, "frame", partner_permutation(frames, k)) for k in range(1, frames)
         ]
+        last_part = temp_parts[1 % frames]
+        epi_parts = swap([after(part, normed) for part in epi_parts], videos)
+    maps = gather_maps(normed, "video", videos, last_part)
     targets = lax.dynamic_index_in_dim(matchings, video, 1, keepdims=False)
     if is_power(videos):
         select = video ^ targets
@@ -434,6 +444,7 @@
         select = (video - targets) % videos
     mask = lax.dynamic_index_in_dim(tile_mask, video, 1, keepdims=False).reshape(-1)
     square = (4, channels, channels)
+    small = pl.CostEstimate(flops=1, bytes_accessed=1, transcendentals=0)
     queries, epi = pl.pallas_call(
         query_kernel,
         out_shape=[
@@ -444,6 +455,7 @@
         out_specs=[VMEM] * 2,
         scratch_shapes=[pltpu.SemaphoreType.DMA((4,))],
         compiler_params=params(),
+        cost_estimate=small,
         name="query",
     )(places, normed, in_hbm(epi_in), in_hbm(epi_out), *epi_parts)
     second, blocks = pl.pallas_call(
@@ -458,6 +470,7 @@
             pltpu.SemaphoreType.DMA,
         ],
         compiler_params=params(),
+        cost_estimate=small,
         name="cross_view",
     )(select, mask, hidden, queries, epi, *maps)
 

time: 62.8 us -> 63.3 us (level)
  starting transfers between devices: 20.7 us -> 16.9 us
  waiting for transfers between devices: 20.4 us -> 23.5 us
  other arithmetic: 0.46 us -> 1.43 us
    ppermute x3, waiting for transfers between devices: 1.64 us -> 7.79 us  [per_device(): lax.ppermute(mine, 'frame', partner_permutation(frames, k))]
    ppermute x2 -> x1, starting transfers between devices: 6.12 us -> 2.64 us  [sum_over(): value = value + lax.ppermute(value, axis, partner_permutation(size, bit))]
    ppermute x2, starting transfers between devices: 5.89 us -> 8.91 us  [ring_gather(): lax.ppermute(pieces[(size - step + 1) % size], axis, left)]
    ppermute x3, starting transfers between devices: 4.45 us -> 1.82 us  [per_device(): lax.ppermute(mine, 'frame', partner_permutation(frames, k))]
    ppermute x2 -> x1, waiting for transfers between devices: 3.02 us -> 1.84 us  [sum_over(): value = value + lax.ppermute(value, axis, partner_permutation(size, bit))]
    ppermute x2, waiting for transfers between devices: 1.07 us -> 0.01 us  [ring_gather(): lax.ppermute(pieces[(size - step + 1) % size], axis, left)]
    concatenate x2, other arithmetic: 0.1 us -> 1.07 us  [half_of(): whole = jnp.concatenate([three, one[None]], axis=0)]
    ppermute x7 -> x8, waiting for transfers between devices: 14.7 us -> 13.9 us  [the longest x4 13.2 us: ring_gather(): pieces[step] = lax.ppermute(sent, axis, right)]
  transfers between devices with their start and end apart: 16 -> 16, of which waited for: 7 -> 8; matrix products, arithmetic and copies ran while one was open for 1% -> 1% of each run, Pallas kernels for 26% -> 28%
where the time goes in v10:
time: 63.3 us; the launch traced here: 63 us
  waiting for transfers between devices  23.5 us (37%)
  Pallas kernels  19.7 us (31%)
  starting transfers between devices  16.9 us (27%)
  other arithmetic  1.43 us (2%)
  between operations  0.89 us (1%)
    ppermute x4, waiting for transfers between devices, ring_gather(): pieces[step] = lax.ppermute(sent, axis, right)  13.2 us
    ppermute x2, starting transfers between devices, ring_gather(): lax.ppermute(pieces[(size - step + 1) % size], axis, left)  8.91 us
    ppermute x3, waiting for transfers between devices, per_device(): lax.ppermute(mine, 'frame', partner_permutation(frames, k))  7.79 us
    pallas_call x1, Pallas kernels, per_device(): pl.pallas_call(functools.partial(view_kernel, videos, tiles), out_shape=[...  6.47 us
    pallas_call x1, Pallas kernels, per_device(): pl.pallas_call(first_kernel, out_shape=[jax.ShapeDtypeStruct((tokens, cha...  2.97 us
    ppermute x1, starting transfers between devices, sum_over(): value = value + lax.ppermute(value, axis, partner_permutation(size, bit))  2.64 us
    pallas_call x1, Pallas kernels, per_device(): pl.pallas_call(own_frame_kernel, out_shape=[jax.ShapeDtypeStruct(square,...  2.26 us
    ppermute x3, starting transfers between devices, gather_maps(): maps[k | bit] = lax.ppermute(sent, axis, partner_permutation(size, bit))  2.11 us
  transfers between devices with their start and end apart: 16, of which 8 were waited for; matrix products, arithmetic and copies ran while one was open for 1% of the time, Pallas kernels for 28%

profile of v10, /device:TPU:0, one launch (start us, length us, event | category | flops | bytes accessed | tf_op | source)
XLA Modules:
  0.0 63.0 jit_solution(8355363414805183434)
XLA Ops:
  0.0 1.0 %pad_maximum_fusion.2 = bf16[4,80,320]{2,1,0:T(8,128)(2,1)S(1)} fusion(bf16[1,80,320]{2,1,0:T(8,128)(2,1)} %bitcast.30, bf16[3,80,320]{2,1,0:T(8,128)(2,1)} %three.2), kind=kLoop, calls=%fused_computation.2 | loop fusion | flops 102400 | bytes 409600 | tf_op jit(solution)/shard_map/concatenate | solution.py:313
  1.1 5.1 %collective-permute-start.2 = (bf16[160,320]{1,0:T(8,128)(2,1)S(1)}, bf16[160,320]{1,0:T(8,128)(2,1)S(1)}, u32[]{:S(2)}, u32[]{:S(2)}) collective-permute-start(bf16[160,320]{1,0:T(8,128)(2,1)S(1)} %dynamic-slice_bitcast_fusion.1), channel_id=1, source_target_pairs={{1,0},{2,1},{3,2},{0,3},{5,4},{6,5},{7,6},{4,7},{9,8},{10,9},{11,1... | collective-permute-start | bytes 307208 | tf_op jit(solution)/shard_map/ppermute | solution.py:308
  6.9 1.1 %time_share.1 = f32[1,320]{1,0:T(1,128)S(1)} custom-call(bf16[1,320]{1,0:T(2,128)(2,1)S(1)} %fusion.4.act, bf16[320,320]{1,0:T(8,128)(2,1)} %proj_hbm.1), custom_call_target="tpu_custom_call" | custom-call | flops 10000000000 | bytes 1048576 | tf_op jit(solution)/shard_map/time_share/pallas_call | solution.py:356
  8.2 3.0 %first_conv.1 = (f32[256,320]{1,0:T(8,128)S(1)}, bf16[256,320]{1,0:T(8,128)(2,1)S(1)}) custom-call(bf16[320,256]{1,0:T(8,128)(2,1)} %bitcast.32, bf16[3,960,320]{2,1,0:T(8,128)(2,1)} %bitcast.27), custom_call_target="tpu_custom_call" | custom-call | flops 471859200 | bytes 2498560 | tf_op jit(solution)/shard_map/first_conv/pallas_call | solution.py:388
  11.2 0.7 %collective-permute-done = f32[1,320]{1,0:T(1,128)S(1)} collective-permute-done((f32[1,320]{1,0:T(1,128)S(1)}, f32[1,320]{1,0:T(1,128)S(1)}, u32[]{:S(2)}, u32[]{:S(2)}) %collective-permute-start) | collective-permute-done | bytes 1312 | tf_op jit(solution)/shard_map/ppermute | solution.py:411
  11.8 1.0 %collective-permute-done.1.refs_0_ = bf16[160,320]{1,0:T(8,128)(2,1)S(1)} collective-permute-done((bf16[160,320]{1,0:T(8,128)(2,1)S(1)}, bf16[160,320]{1,0:T(8,128)(2,1)S(1)}, u32[]{:S(2)}, u32[]{:S(2)}) %collective-permute-start.1) | collective-permute-done | bytes 102432 | tf_op jit(solution)/shard_map/ppermute | solution.py:306
  12.8 2.6 %collective-permute-start.3 = (f32[1,320]{1,0:T(1,128)S(1)}, f32[1,320]{1,0:T(1,128)S(1)}, u32[]{:S(2)}, u32[]{:S(2)}) collective-permute-start(f32[1,320]{1,0:T(1,128)S(1)} %add.76), channel_id=1, source_target_pairs={{0,2},{1,3},{2,0},{3,1},{4,6},{5,7},{6,4},{7,5},{8,10},{9,11},{10,... | collective-permute-start | bytes 3848 | tf_op jit(solution)/shard_map/ppermute | solution.py:288
  15.5 1.8 %collective-permute-done.3 = f32[1,320]{1,0:T(1,128)S(1)} collective-permute-done((f32[1,320]{1,0:T(1,128)S(1)}, f32[1,320]{1,0:T(1,128)S(1)}, u32[]{:S(2)}, u32[]{:S(2)}) %collective-permute-start.3) | collective-permute-done | bytes 1312 | tf_op jit(solution)/shard_map/ppermute | solution.py:288
  17.3 1.2 %collective-permute-start.4 = (bf16[160,320]{1,0:T(8,128)(2,1)S(1)}, bf16[160,320]{1,0:T(8,128)(2,1)S(1)}, u32[]{:S(2)}, u32[]{:S(2)}) collective-permute-start(bf16[160,320]{1,0:T(8,128)(2,1)S(1)} %collective-permute-done.1.refs_0_), channel_id=1, source_target_pairs={{0,1},{1,2},{2,3},{3,0},{4,5},{5,6},{6,7},{7,4},{8,9},{9,10},{10,1... | collective-permute-start | bytes 307208 | tf_op jit(solution)/shard_map/ppermute | solution.py:306
  18.6 1.7 %second_conv.1 = (bf16[256,320]{1,0:T(8,128)(2,1)S(1)}, bf16[256,320]{1,0:T(8,128)(2,1)S(1)}) custom-call(bf16[256,320]{1,0:T(8,128)(2,1)S(1)} %get-tuple-element.34.source, f32[256,320]{1,0:T(8,128)S(1)} %get-tuple-element.35.inner, f32[1,320]{1,0:T(1,128)S(1)} %add.79.bias, bf16[3,960,320]{2,1,0:T(8,128)(2,1)S(1)} %bitcast.26), custom_call_target="tpu_custom_call" | custom-call | flops 471859200 | bytes 2498560 | tf_op jit(solution)/shard_map/second_conv/pallas_call | solution.py:417
  20.3 1.6 %collective-permute-start.7 = (bf16[256,320]{1,0:T(8,128)(2,1)S(1)}, bf16[256,320]{1,0:T(8,128)(2,1)S(1)}, u32[]{:S(2)}, u32[]{:S(2)}) collective-permute-start(bf16[256,320]{1,0:T(8,128)(2,1)S(1)} %get-tuple-element.38.normed.refs_5_), channel_id=1, source_target_pairs={{0,8},{4,12},{8,0},{12,4},{1,9},{5,13},{9,1},{13,5},{2,10},{6,14},... | collective-permute-start | bytes 491528 | tf_op jit(solution)/shard_map/ppermute | solution.py:276
  21.8 2.2 %collective-permute-done.4.refs_1_ = bf16[160,320]{1,0:T(8,128)(2,1)S(1)} collective-permute-done((bf16[160,320]{1,0:T(8,128)(2,1)S(1)}, bf16[160,320]{1,0:T(8,128)(2,1)S(1)}, u32[]{:S(2)}, u32[]{:S(2)}) %collective-permute-start.4) | collective-permute-done | bytes 102432 | tf_op jit(solution)/shard_map/ppermute | solution.py:306
  24.8 5.1 %collective-permute-done.8.refs_0_ = bf16[160,320]{1,0:T(8,128)(2,1)S(1)} collective-permute-done((bf16[160,320]{1,0:T(8,128)(2,1)S(1)}, bf16[160,320]{1,0:T(8,128)(2,1)S(1)}, u32[]{:S(2)}, u32[]{:S(2)}) %collective-permute-start.8) | collective-permute-done | bytes 102432 | tf_op jit(solution)/shard_map/ppermute | solution.py:435
  29.9 1.0 %collective-permute-start.11 = (bf16[160,320]{1,0:T(8,128)(2,1)S(1)}, bf16[160,320]{1,0:T(8,128)(2,1)S(1)}, u32[]{:S(2)}, u32[]{:S(2)}) collective-permute-start(bf16[160,320]{1,0:T(8,128)(2,1)S(1)} %dynamic-slice_bitcast_fusion), channel_id=1, source_target_pairs={{0,3},{1,2},{2,1},{3,0},{4,7},{5,6},{6,5},{7,4},{8,11},{9,10},{10,... | collective-permute-start | bytes 307208 | tf_op jit(solution)/shard_map/ppermute | solution.py:435
  30.9 0.8 %collective-permute-start.10 = (bf16[160,320]{1,0:T(8,128)(2,1)S(1)}, bf16[160,320]{1,0:T(8,128)(2,1)S(1)}, u32[]{:S(2)}, u32[]{:S(2)}) collective-permute-start(bf16[160,320]{1,0:T(8,128)(2,1)S(1)} %dynamic-slice_bitcast_fusion), channel_id=1, source_target_pairs={{0,2},{1,3},{2,0},{3,1},{4,6},{5,7},{6,4},{7,5},{8,10},{9,11},{10,... | collective-permute-start | bytes 307208 | tf_op jit(solution)/shard_map/ppermute | solution.py:435
  32.3 1.9 %query.1 = (f32[320,256]{1,0:T(8,128)S(1)}, bf16[4,320,320]{2,1,0:T(8,128)(2,1)S(1)}) custom-call(s32[5]{0:T(128)S(1)} %stack.39.where, bf16[256,320]{1,0:T(8,128)(2,1)S(1)} %get-tuple-element.38.normed.refs_5_, bf16[3,80,320]{2,1,0:T(8,128)(2,1)} %three.2, bf16[80,320]{1,0:T(8,128)(2,1)} %one.2, bf16[160,320]{1,0:T(8,128)(2,1)S(1)} %collective-permute-done.1.refs_0_, ...), custom_call_target="tpu_custom_call" | custom-call | flops 1 | bytes 1 | tf_op jit(solution)/shard_map/query/pallas_call | solution.py:448
  34.2 6.5 %cross_view.1 = (bf16[256,320]{1,0:T(8,128)(2,1)S(1)}, bf16[256,320]{1,0:T(8,128)(2,1)S(1)}) custom-call(s32[2]{0:T(128)S(1)} %xor_reduce_fusion.refs_0_, s32[8]{0:T(128)S(1)} %reshape.93.refs_1_, bf16[256,320]{1,0:T(8,128)(2,1)S(1)} %get-tuple-element.37.refs_2_, f32[320,256]{1,0:T(8,128)S(1)} %get-tuple-element.43.refs_3_, ...), custom_call_target="tpu_custom_call" | custom-call | flops 1 | bytes 1 | tf_op jit(solution)/shard_map/cross_view/pallas_call | solution.py:461
  40.7 2.6 %collective-permute-done.10.refs_1_ = bf16[160,320]{1,0:T(8,128)(2,1)S(1)} collective-permute-done((bf16[160,320]{1,0:T(8,128)(2,1)S(1)}, bf16[160,320]{1,0:T(8,128)(2,1)S(1)}, u32[]{:S(2)}, u32[]{:S(2)}) %collective-permute-start.10) | collective-permute-done | bytes 102432 | tf_op jit(solution)/shard_map/ppermute | solution.py:435
  43.5 3.8 %collective-permute-start.15 = (bf16[256,320]{1,0:T(8,128)(2,1)S(1)}, bf16[256,320]{1,0:T(8,128)(2,1)S(1)}, u32[]{:S(2)}, u32[]{:S(2)}) collective-permute-start(bf16[256,320]{1,0:T(8,128)(2,1)S(1)} %get-tuple-element.49.rows), channel_id=1, source_target_pairs={{1,0},{2,1},{3,2},{0,3},{5,4},{6,5},{7,6},{4,7},{9,8},{10,9},{11,1... | collective-permute-start | bytes 491528 | tf_op jit(solution)/shard_map/ppermute | solution.py:308
  47.3 5.7 %collective-permute-done.13.rows = bf16[256,320]{1,0:T(8,128)(2,1)S(1)} collective-permute-done((bf16[256,320]{1,0:T(8,128)(2,1)S(1)}, bf16[256,320]{1,0:T(8,128)(2,1)S(1)}, u32[]{:S(2)}, u32[]{:S(2)}) %collective-permute-start.13) | collective-permute-done | bytes 163872 | tf_op jit(solution)/shard_map/ppermute | solution.py:306
  53.1 2.3 %own_frame.1 = (bf16[4,320,320]{2,1,0:T(8,128)(2,1)S(1)}, bf16[256,320]{1,0:T(8,128)(2,1)S(1)}, f32[256,320]{1,0:T(8,128)S(1)}, bf16[256,320]{1,0:T(8,128)(2,1)S(1)}) custom-call(s32[5]{0:T(128)S(1)} %stack.44.where, bf16[256,320]{1,0:T(8,128)(2,1)S(1)} %get-tuple-element.49.rows, bf16[3,80,320]{2,1,0:T(8,128)(2,1)} %three.3, bf16[80,320]{1,0:T(8,128)(2,1)} %one.3, ...), custom_call_target="tpu_custom_call" | custom-call | flops 209715200 | bytes 1474560 | tf_op jit(solution)/shard_map/own_frame/pallas_call | solution.py:489
  55.4 0.6 %other_frame.2 = (f32[256,320]{1,0:T(8,128)S(1)}, bf16[256,320]{1,0:T(8,128)(2,1)S(1)}) custom-call(bf16[256,320]{1,0:T(8,128)(2,1)S(1)} %get-tuple-element.53.queries.refs_1_, bf16[256,320]{1,0:T(8,128)(2,1)S(1)} %collective-permute-done.13.rows, bf16[4,320,320]{2,1,0:T(8,128)(2,1)S(1)} %get-tuple-element.54.weights.refs_3_), custom_call_target="tpu_custom_call" | custom-call | flops 209715200 | bytes 1474560 | tf_op jit(solution)/shard_map/other_frame/pallas_call | solution.py:502
  56.7 4.3 %collective-permute-done.14.refs_2_ = bf16[256,320]{1,0:T(8,128)(2,1)S(1)} collective-permute-done((bf16[256,320]{1,0:T(8,128)(2,1)S(1)}, bf16[256,320]{1,0:T(8,128)(2,1)S(1)}, u32[]{:S(2)}, u32[]{:S(2)}) %collective-permute-start.14) | collective-permute-done | bytes 163872 | tf_op jit(solution)/shard_map/ppermute | solution.py:306
  61.0 2.0 %last.1 = bf16[320,256]{1,0:T(8,128)(2,1)} custom-call(bf16[256,320]{1,0:T(8,128)(2,1)S(1)} %get-tuple-element.47.refs_0_, bf16[256,320]{1,0:T(8,128)(2,1)S(1)} %get-tuple-element.53.queries.refs_1_, bf16[256,320]{1,0:T(8,128)(2,1)S(1)} %collective-permute-done.14.refs_2_, bf16[4,320,320]{2,1,0:T(8,128)(2,1)S(1)} %get-tuple-element.54.weights.refs_3_, ...), custom_call_target="tpu_custom_call" | custom-call | tf_op jit(solution)/shard_map/last/pallas_call | solution.py:513
  (41 shorter events, 2.5 us)
Async XLA Ops:
  0.0 31.7 %copy-start = (s32[2,4,2,2]{1,3,2,0:T(2,128)S(1)}, s32[2,4,2,2]{1,3,2,0:T(2,128)}, u32[]{:S(2)}) copy-start(s32[2,4,2,2]{1,3,2,0:T(2,128)} %param.14) | copy-start | bytes 388
  1.1 10.8 %collective-permute-start.2 = (bf16[160,320]{1,0:T(8,128)(2,1)S(1)}, bf16[160,320]{1,0:T(8,128)(2,1)S(1)}, u32[]{:S(2)}, u32[]{:S(2)}) collective-permute-start(bf16[160,320]{1,0:T(8,128)(2,1)S(1)} %dynamic-slice_bitcast_fusion.1), channel_id=1, source_target_pairs={{1,0},{2,1},{3,2},{0,3},{5,4},{6,5},{7,6},{4,7},{9,8},{10,9},{11,1... | collective-permute-start | bytes 307208 | tf_op jit(solution)/shard_map/ppermute | solution.py:308
  6.2 6.7 %collective-permute-start.1 = (bf16[160,320]{1,0:T(8,128)(2,1)S(1)}, bf16[160,320]{1,0:T(8,128)(2,1)S(1)}, u32[]{:S(2)}, u32[]{:S(2)}) collective-permute-start(bf16[160,320]{1,0:T(8,128)(2,1)S(1)} %dynamic-slice_bitcast_fusion.1), channel_id=1, source_target_pairs={{0,1},{1,2},{2,3},{3,0},{4,5},{5,6},{6,7},{7,4},{8,9},{9,10},{10,1... | collective-permute-start | bytes 307208 | tf_op jit(solution)/shard_map/ppermute | solution.py:306
  6.9 11.6 %copy-start.2 = (bf16[3,80,320]{2,1,0:T(8,128)(2,1)S(1)}, bf16[3,80,320]{2,1,0:T(8,128)(2,1)}, u32[]{:S(2)}) copy-start(bf16[3,80,320]{2,1,0:T(8,128)(2,1)} %three.3) | copy-start | bytes 460804
  8.1 10.5 %copy-start.3 = (bf16[80,320]{1,0:T(8,128)(2,1)S(1)}, bf16[80,320]{1,0:T(8,128)(2,1)}, u32[]{:S(2)}) copy-start(bf16[80,320]{1,0:T(8,128)(2,1)} %one.3) | copy-start | bytes 153604
  8.1 10.5 %copy-start.1 = (bf16[3,3,320,320]{3,2,1,0:T(8,128)(2,1)S(1)}, bf16[3,3,320,320]{3,2,1,0:T(8,128)(2,1)}, u32[]{:S(2)}) copy-start(bf16[3,3,320,320]{3,2,1,0:T(8,128)(2,1)} %param.16) | copy-start | bytes 5529604
  8.1 3.7 %collective-permute-start = (f32[1,320]{1,0:T(1,128)S(1)}, f32[1,320]{1,0:T(1,128)S(1)}, u32[]{:S(2)}, u32[]{:S(2)}) collective-permute-start(f32[1,320]{1,0:T(1,128)S(1)} %time_share.1), channel_id=1, source_target_pairs={{0,1},{1,0},{2,3},{3,2},{4,5},{5,4},{6,7},{7,6},{8,9},{9,8},{10,11... | collective-permute-start | bytes 3848 | tf_op jit(solution)/shard_map/ppermute | solution.py:411
  11.1 20.9 %copy-start.4 = (s32[2,4]{1,0:T(2,128)S(1)}, s32[2,4]{1,0:T(2,128)}, u32[]{:S(2)}) copy-start(s32[2,4]{1,0:T(2,128)} %param.13) | copy-start | bytes 100
  12.8 4.5 %collective-permute-start.3 = (f32[1,320]{1,0:T(1,128)S(1)}, f32[1,320]{1,0:T(1,128)S(1)}, u32[]{:S(2)}, u32[]{:S(2)}) collective-permute-start(f32[1,320]{1,0:T(1,128)S(1)} %add.76), channel_id=1, source_target_pairs={{0,2},{1,3},{2,0},{3,1},{4,6},{5,7},{6,4},{7,5},{8,10},{9,11},{10,... | collective-permute-start | bytes 3848 | tf_op jit(solution)/shard_map/ppermute | solution.py:288
  17.3 6.7 %collective-permute-start.4 = (bf16[160,320]{1,0:T(8,128)(2,1)S(1)}, bf16[160,320]{1,0:T(8,128)(2,1)S(1)}, u32[]{:S(2)}, u32[]{:S(2)}) collective-permute-start(bf16[160,320]{1,0:T(8,128)(2,1)S(1)} %collective-permute-done.1.refs_0_), channel_id=1, source_target_pairs={{0,1},{1,2},{2,3},{3,0},{4,5},{5,6},{6,7},{7,4},{8,9},{9,10},{10,1... | collective-permute-start | bytes 307208 | tf_op jit(solution)/shard_map/ppermute | solution.py:306
  20.3 9.7 %collective-permute-start.7 = (bf16[256,320]{1,0:T(8,128)(2,1)S(1)}, bf16[256,320]{1,0:T(8,128)(2,1)S(1)}, u32[]{:S(2)}, u32[]{:S(2)}) collective-permute-start(bf16[256,320]{1,0:T(8,128)(2,1)S(1)} %get-tuple-element.38.normed.refs_5_), channel_id=1, source_target_pairs={{0,8},{4,12},{8,0},{12,4},{1,9},{5,13},{9,1},{13,5},{2,10},{6,14},... | collective-permute-start | bytes 491528 | tf_op jit(solution)/shard_map/ppermute | solution.py:276
  24.1 8.2 %collective-permute-start.5 = (bf16[480,320]{1,0:T(8,128)(2,1)S(1)}, bf16[480,320]{1,0:T(8,128)(2,1)S(1)}, u32[]{:S(2)}, u32[]{:S(2)}) collective-permute-start(bf16[480,320]{1,0:T(8,128)(2,1)S(1)} %pad_maximum_fusion), channel_id=1, source_target_pairs={{0,4},{4,0},{8,12},{12,8},{1,5},{5,1},{9,13},{13,9},{2,6},{6,2},{1... | collective-permute-start | bytes 921608 | tf_op jit(solution)/shard_map/ppermute | solution.py:320
  24.2 5.8 %collective-permute-start.8 = (bf16[160,320]{1,0:T(8,128)(2,1)S(1)}, bf16[160,320]{1,0:T(8,128)(2,1)S(1)}, u32[]{:S(2)}, u32[]{:S(2)}) collective-permute-start(bf16[160,320]{1,0:T(8,128)(2,1)S(1)} %dynamic-slice_bitcast_fusion), channel_id=1, source_target_pairs={{0,1},{1,0},{2,3},{3,2},{4,5},{5,4},{6,7},{7,6},{8,9},{9,8},{10,11... | collective-permute-start | bytes 307208 | tf_op jit(solution)/shard_map/ppermute | solution.py:435
  24.2 9.9 %collective-permute-start.6 = (bf16[256,320]{1,0:T(8,128)(2,1)S(1)}, bf16[256,320]{1,0:T(8,128)(2,1)S(1)}, u32[]{:S(2)}, u32[]{:S(2)}) collective-permute-start(bf16[256,320]{1,0:T(8,128)(2,1)S(1)} %get-tuple-element.38.normed.refs_5_), channel_id=1, source_target_pairs={{0,4},{4,0},{8,12},{12,8},{1,5},{5,1},{9,13},{13,9},{2,6},{6,2},{1... | collective-permute-start | bytes 491528 | tf_op jit(solution)/shard_map/ppermute | solution.py:276
  29.9 4.2 %collective-permute-start.9 = (bf16[256,320]{1,0:T(8,128)(2,1)S(1)}, bf16[256,320]{1,0:T(8,128)(2,1)S(1)}, u32[]{:S(2)}, u32[]{:S(2)}) collective-permute-start(bf16[256,320]{1,0:T(8,128)(2,1)S(1)} %collective-permute-done.7.refs_7_), channel_id=1, source_target_pairs={{0,4},{4,0},{8,12},{12,8},{1,5},{5,1},{9,13},{13,9},{2,6},{6,2},{1... | collective-permute-start | bytes 491528 | tf_op jit(solution)/shard_map/ppermute | solution.py:276
  29.9 10.7 %collective-permute-start.11 = (bf16[160,320]{1,0:T(8,128)(2,1)S(1)}, bf16[160,320]{1,0:T(8,128)(2,1)S(1)}, u32[]{:S(2)}, u32[]{:S(2)}) collective-permute-start(bf16[160,320]{1,0:T(8,128)(2,1)S(1)} %dynamic-slice_bitcast_fusion), channel_id=1, source_target_pairs={{0,3},{1,2},{2,1},{3,0},{4,7},{5,6},{6,5},{7,4},{8,11},{9,10},{10,... | collective-permute-start | bytes 307208 | tf_op jit(solution)/shard_map/ppermute | solution.py:435
  30.9 12.4 %collective-permute-start.10 = (bf16[160,320]{1,0:T(8,128)(2,1)S(1)}, bf16[160,320]{1,0:T(8,128)(2,1)S(1)}, u32[]{:S(2)}, u32[]{:S(2)}) collective-permute-start(bf16[160,320]{1,0:T(8,128)(2,1)S(1)} %dynamic-slice_bitcast_fusion), channel_id=1, source_target_pairs={{0,2},{1,3},{2,0},{3,1},{4,6},{5,7},{6,4},{7,5},{8,10},{9,11},{10,... | collective-permute-start | bytes 307208 | tf_op jit(solution)/shard_map/ppermute | solution.py:435
  43.4 9.8 %collective-permute-start.12 = (bf16[480,320]{1,0:T(8,128)(2,1)S(1)}, bf16[480,320]{1,0:T(8,128)(2,1)S(1)}, u32[]{:S(2)}, u32[]{:S(2)}) collective-permute-start(bf16[480,320]{1,0:T(8,128)(2,1)S(1)} %pad_maximum_fusion.1), channel_id=1, source_target_pairs={{0,4},{4,0},{8,12},{12,8},{1,5},{5,1},{9,13},{13,9},{2,6},{6,2},{1... | collective-permute-start | bytes 921608 | tf_op jit(solution)/shard_map/ppermute | solution.py:320
  43.4 9.6 %collective-permute-start.13 = (bf16[256,320]{1,0:T(8,128)(2,1)S(1)}, bf16[256,320]{1,0:T(8,128)(2,1)S(1)}, u32[]{:S(2)}, u32[]{:S(2)}) collective-permute-start(bf16[256,320]{1,0:T(8,128)(2,1)S(1)} %get-tuple-element.49.rows), channel_id=1, source_target_pairs={{0,1},{1,2},{2,3},{3,0},{4,5},{5,6},{6,7},{7,4},{8,9},{9,10},{10,1... | collective-permute-start | bytes 491528 | tf_op jit(solution)/shard_map/ppermute | solution.py:306
  43.5 12.5 %collective-permute-start.15 = (bf16[256,320]{1,0:T(8,128)(2,1)S(1)}, bf16[256,320]{1,0:T(8,128)(2,1)S(1)}, u32[]{:S(2)}, u32[]{:S(2)}) collective-permute-start(bf16[256,320]{1,0:T(8,128)(2,1)S(1)} %get-tuple-element.49.rows), channel_id=1, source_target_pairs={{1,0},{2,1},{3,2},{0,3},{5,4},{6,5},{7,6},{4,7},{9,8},{10,9},{11,1... | collective-permute-start | bytes 491528 | tf_op jit(solution)/shard_map/ppermute | solution.py:308
  53.0 8.0 %collective-permute-start.14 = (bf16[256,320]{1,0:T(8,128)(2,1)S(1)}, bf16[256,320]{1,0:T(8,128)(2,1)S(1)}, u32[]{:S(2)}, u32[]{:S(2)}) collective-permute-start(bf16[256,320]{1,0:T(8,128)(2,1)S(1)} %collective-permute-done.13.rows), channel_id=1, source_target_pairs={{0,1},{1,2},{2,3},{3,0},{4,5},{5,6},{6,7},{7,4},{8,9},{9,10},{10,1... | collective-permute-start | bytes 491528 | tf_op jit(solution)/shard_map/ppermute | solution.py:306

commit v11 on v8

--- a/solution.py
+++ b/solution.py
@@ -372,10 +372,6 @@
         temp_in = lax.all_gather(temp_in, "frame", axis=1, tiled=True)
         temp_out = lax.all_gather(temp_out, "frame", axis=0, tiled=True)
     places = jnp.stack(places).astype(jnp.int32)
-    temp_places = places
-    if paired:
-        temp_places = [partner(frame, frames, k, -1) for k in range(frames)] + [video % 2]
-        temp_places = jnp.stack(temp_places).astype(jnp.int32)
 
     source_scratch = pltpu.VMEM((channels, tokens), bf16)
     padded_scratch = pltpu.VMEM((tokens + 2 * W, 3 * channels), bf16)
@@ -421,12 +417,6 @@
         normed = after(normed, epi_parts[-1])
     maps = gather_maps(normed, "video", videos)
     epi_parts = swap(epi_parts, videos) if paired else []
-    temp_parts = []
-    if paired:
-        mine = after(half_of(temp_in, temp_out, video % 2), maps[1])
-        temp_parts = [mine] + [
-            lax.ppermute(mine, "frame", partner_permutation(frames, k)) for k in range(1, frames)
-        ]
     targets = lax.dynamic_index_in_dim(matchings, video, 1, keepdims=False)
     if is_power(videos):
         select = video ^ targets
@@ -446,6 +436,12 @@
         compiler_params=params(),
         name="query",
     )(places, normed, in_hbm(epi_in), in_hbm(epi_out), *epi_parts)
+    temp_parts = []
+    if paired:
+        mine = after(half_of(temp_in, temp_out, video % 2), maps[1])
+        temp_parts = ring_gather(mine, "frame", frames, queries)
+    if paired:
+        queries = after(queries, temp_parts[1 % frames], temp_parts[-1])
     second, blocks = pl.pallas_call(
         functools.partial(view_kernel, videos, tiles),
         out_shape=[jax.ShapeDtypeStruct((tokens, channels), bf16)] * 2,
@@ -482,7 +478,7 @@
         compiler_params=params(),
         cost_estimate=frame_cost,
         name="own_frame",
-    )(temp_places, blocks, in_hbm(temp_in), in_hbm(temp_out), *temp_parts)
+    )(places, blocks, in_hbm(temp_in), in_hbm(temp_out), *temp_parts)
     scores, values = [first[0]], [first[1]]
     order = sorted(range(1, frames), key=lambda k: min(k, frames - k))
     for k in order[:-1]:

time: 62.8 us -> 62 us (0.987)
  starting transfers between devices: 20.7 us -> 20 us
    ppermute x3 -> x0, starting transfers between devices: 4.45 us -> none  [per_device(): lax.ppermute(mine, 'frame', partner_permutation(frames, k))]
    ppermute x4 -> x6, starting transfers between devices: 2.03 us -> 4.53 us  [ring_gather(): pieces[step] = lax.ppermute(pieces[step - 1], axis, right)]
    ppermute x3 -> x0, waiting for transfers between devices: 1.64 us -> none  [per_device(): lax.ppermute(mine, 'frame', partner_permutation(frames, k))]
    ppermute x2 -> x3, starting transfers between devices: 5.89 us -> 7.2 us  [ring_gather(): lax.ppermute(pieces[(size - step + 1) % size], axis, left)]
    ppermute x4 -> x6, waiting for transfers between devices: 14.7 us -> 15.6 us  [ring_gather(): pieces[step] = lax.ppermute(pieces[step - 1], axis, right)]
    ppermute x2 -> x3, waiting for transfers between devices: 1.07 us -> 1.69 us  [ring_gather(): lax.ppermute(pieces[(size - step + 1) % size], axis, left)]
  transfers between devices with their start and end apart: 16 -> 16, of which waited for: 7 -> 9; matrix products, arithmetic and copies ran while one was open for 1% -> 1% of each run, Pallas kernels for 26% -> 27%
where the time goes in v11:
time: 62 us; the launch traced here: 61.7 us
  waiting for transfers between devices  20.3 us (33%)
  starting transfers between devices  20 us (32%)
  Pallas kernels  19.5 us (31%)
  between operations  0.93 us (2%)
    ppermute x6, waiting for transfers between devices, ring_gather(): pieces[step] = lax.ppermute(pieces[step - 1], axis, right)  15.6 us
    ppermute x3, starting transfers between devices, ring_gather(): lax.ppermute(pieces[(size - step + 1) % size], axis, left)  7.2 us
    pallas_call x1, Pallas kernels, per_device(): pl.pallas_call(functools.partial(view_kernel, videos, tiles), out_shape=[...  6.45 us
    ppermute x2, starting transfers between devices, sum_over(): value = value + lax.ppermute(value, axis, partner_permutation(size, bit))  6.12 us
    ppermute x6, starting transfers between devices, ring_gather(): pieces[step] = lax.ppermute(pieces[step - 1], axis, right)  4.53 us
    ppermute x2, waiting for transfers between devices, sum_over(): value = value + lax.ppermute(value, axis, partner_permutation(size, bit))  3.03 us
    pallas_call x1, Pallas kernels, per_device(): pl.pallas_call(first_kernel, out_shape=[jax.ShapeDtypeStruct((tokens, cha...  2.82 us
    pallas_call x1, Pallas kernels, per_device(): pl.pallas_call(own_frame_kernel, out_shape=[jax.ShapeDtypeStruct(square,...  2.26 us
  transfers between devices with their start and end apart: 16, of which 9 were waited for; matrix products, arithmetic and copies ran while one was open for 1% of the time, Pallas kernels for 27%

profile of v11, /device:TPU:0, one launch (start us, length us, event | category | flops | bytes accessed | tf_op | source)
XLA Modules:
  0.0 61.7 jit_solution(13794218471379781884)
XLA Ops:
  0.8 1.1 %time_share.1 = f32[1,320]{1,0:T(1,128)S(1)} custom-call(bf16[1,320]{1,0:T(2,128)(2,1)S(1)} %fusion.4.act, bf16[320,320]{1,0:T(8,128)(2,1)} %proj_hbm.1), custom_call_target="tpu_custom_call" | custom-call | flops 10000000000 | bytes 1048576 | tf_op jit(solution)/shard_map/time_share/pallas_call | solution.py:354
  1.9 3.1 %collective-permute-start = (f32[1,320]{1,0:T(1,128)S(1)}, f32[1,320]{1,0:T(1,128)S(1)}, u32[]{:S(2)}, u32[]{:S(2)}) collective-permute-start(f32[1,320]{1,0:T(1,128)S(1)} %time_share.1), channel_id=1, source_target_pairs={{0,1},{1,0},{2,3},{3,2},{4,5},{5,4},{6,7},{7,6},{8,9},{9,8},{10,11... | collective-permute-start | bytes 3848 | tf_op jit(solution)/shard_map/ppermute | solution.py:288
  5.1 1.5 %collective-permute-done = f32[1,320]{1,0:T(1,128)S(1)} collective-permute-done((f32[1,320]{1,0:T(1,128)S(1)}, f32[1,320]{1,0:T(1,128)S(1)}, u32[]{:S(2)}, u32[]{:S(2)}) %collective-permute-start) | collective-permute-done | bytes 1312 | tf_op jit(solution)/shard_map/ppermute | solution.py:288
  6.6 3.0 %collective-permute-start.1 = (f32[1,320]{1,0:T(1,128)S(1)}, f32[1,320]{1,0:T(1,128)S(1)}, u32[]{:S(2)}, u32[]{:S(2)}) collective-permute-start(f32[1,320]{1,0:T(1,128)S(1)} %add.75), channel_id=1, source_target_pairs={{0,2},{1,3},{2,0},{3,1},{4,6},{5,7},{6,4},{7,5},{8,10},{9,11},{10,... | collective-permute-start | bytes 3848 | tf_op jit(solution)/shard_map/ppermute | solution.py:288
  9.7 1.5 %collective-permute-done.1 = f32[1,320]{1,0:T(1,128)S(1)} collective-permute-done((f32[1,320]{1,0:T(1,128)S(1)}, f32[1,320]{1,0:T(1,128)S(1)}, u32[]{:S(2)}, u32[]{:S(2)}) %collective-permute-start.1) | collective-permute-done | bytes 1312 | tf_op jit(solution)/shard_map/ppermute | solution.py:288
  11.2 1.9 %collective-permute-start.3 = (bf16[160,320]{1,0:T(8,128)(2,1)S(1)}, bf16[160,320]{1,0:T(8,128)(2,1)S(1)}, u32[]{:S(2)}, u32[]{:S(2)}) collective-permute-start(bf16[160,320]{1,0:T(8,128)(2,1)S(1)} %dynamic-slice_bitcast_fusion.1), channel_id=1, source_target_pairs={{0,1},{1,2},{2,3},{3,0},{4,5},{5,6},{6,7},{7,4},{8,9},{9,10},{10,1... | collective-permute-start | bytes 307208 | tf_op jit(solution)/shard_map/ppermute | solution.py:302
  13.1 2.8 %first_conv.1 = (f32[256,320]{1,0:T(8,128)S(1)}, bf16[256,320]{1,0:T(8,128)(2,1)S(1)}) custom-call(bf16[320,256]{1,0:T(8,128)(2,1)} %bitcast.28, bf16[3,960,320]{2,1,0:T(8,128)(2,1)} %bitcast.23), custom_call_target="tpu_custom_call" | custom-call | flops 471859200 | bytes 2498560 | tf_op jit(solution)/shard_map/first_conv/pallas_call | solution.py:383
  16.0 2.1 %collective-permute-start.2 = (bf16[160,320]{1,0:T(8,128)(2,1)S(1)}, bf16[160,320]{1,0:T(8,128)(2,1)S(1)}, u32[]{:S(2)}, u32[]{:S(2)}) collective-permute-start(bf16[160,320]{1,0:T(8,128)(2,1)S(1)} %dynamic-slice_bitcast_fusion.1), channel_id=1, source_target_pairs={{1,0},{2,1},{3,2},{0,3},{5,4},{6,5},{7,6},{4,7},{9,8},{10,9},{11,1... | collective-permute-start | bytes 307208 | tf_op jit(solution)/shard_map/ppermute | solution.py:304
  18.0 1.7 %second_conv.1 = (bf16[256,320]{1,0:T(8,128)(2,1)S(1)}, bf16[256,320]{1,0:T(8,128)(2,1)S(1)}) custom-call(bf16[256,320]{1,0:T(8,128)(2,1)S(1)} %get-tuple-element.31.source, f32[256,320]{1,0:T(8,128)S(1)} %get-tuple-element.32.inner, f32[1,320]{1,0:T(1,128)S(1)} %add.76.bias, bf16[3,960,320]{2,1,0:T(8,128)(2,1)S(1)} %bitcast.22), custom_call_target="tpu_custom_call" | custom-call | flops 471859200 | bytes 2498560 | tf_op jit(solution)/shard_map/second_conv/pallas_call | solution.py:401
  19.8 1.1 %collective-permute-done.2.refs_2_ = bf16[160,320]{1,0:T(8,128)(2,1)S(1)} collective-permute-done((bf16[160,320]{1,0:T(8,128)(2,1)S(1)}, bf16[160,320]{1,0:T(8,128)(2,1)S(1)}, u32[]{:S(2)}, u32[]{:S(2)}) %collective-permute-start.2) | collective-permute-done | bytes 102432 | tf_op jit(solution)/shard_map/ppermute | solution.py:304
  20.9 1.5 %collective-permute-start.9 = (bf16[256,320]{1,0:T(8,128)(2,1)S(1)}, bf16[256,320]{1,0:T(8,128)(2,1)S(1)}, u32[]{:S(2)}, u32[]{:S(2)}) collective-permute-start(bf16[256,320]{1,0:T(8,128)(2,1)S(1)} %get-tuple-element.36.normed.refs_5_), channel_id=1, source_target_pairs={{0,8},{4,12},{8,0},{12,4},{1,9},{5,13},{9,1},{13,5},{2,10},{6,14},... | collective-permute-start | bytes 491528 | tf_op jit(solution)/shard_map/ppermute | solution.py:275
  22.4 4.1 %collective-permute-done.4.refs_1_ = bf16[160,320]{1,0:T(8,128)(2,1)S(1)} collective-permute-done((bf16[160,320]{1,0:T(8,128)(2,1)S(1)}, bf16[160,320]{1,0:T(8,128)(2,1)S(1)}, u32[]{:S(2)}, u32[]{:S(2)}) %collective-permute-start.4) | collective-permute-done | bytes 102432 | tf_op jit(solution)/shard_map/ppermute | solution.py:302
  27.4 3.5 %collective-permute-start.8 = (bf16[160,320]{1,0:T(8,128)(2,1)S(1)}, bf16[160,320]{1,0:T(8,128)(2,1)S(1)}, u32[]{:S(2)}, u32[]{:S(2)}) collective-permute-start(bf16[160,320]{1,0:T(8,128)(2,1)S(1)} %dynamic-slice_bitcast_fusion), channel_id=1, source_target_pairs={{1,0},{2,1},{3,2},{0,3},{5,4},{6,5},{7,6},{4,7},{9,8},{10,9},{11,1... | collective-permute-start | bytes 307208 | tf_op jit(solution)/shard_map/ppermute | solution.py:304
  30.9 1.9 %query.1 = (f32[320,256]{1,0:T(8,128)S(1)}, bf16[4,320,320]{2,1,0:T(8,128)(2,1)S(1)}) custom-call(s32[5]{0:T(128)S(1)} %stack.23.where, bf16[256,320]{1,0:T(8,128)(2,1)S(1)} %get-tuple-element.36.normed.refs_5_, bf16[3,80,320]{2,1,0:T(8,128)(2,1)} %three.2, bf16[80,320]{1,0:T(8,128)(2,1)} %one.2, bf16[160,320]{1,0:T(8,128)(2,1)S(1)} %collective-permute-done.3.refs_0_, ...), custom_call_target="tpu_custom_call" | custom-call | tf_op jit(solution)/shard_map/query/pallas_call | solution.py:427
  32.8 2.0 %collective-permute-done.7.refs_0_ = bf16[160,320]{1,0:T(8,128)(2,1)S(1)} collective-permute-done((bf16[160,320]{1,0:T(8,128)(2,1)S(1)}, bf16[160,320]{1,0:T(8,128)(2,1)S(1)}, u32[]{:S(2)}, u32[]{:S(2)}) %collective-permute-start.7) | collective-permute-done | bytes 102432 | tf_op jit(solution)/shard_map/ppermute | solution.py:302
  35.3 6.5 %cross_view.1 = (bf16[256,320]{1,0:T(8,128)(2,1)S(1)}, bf16[256,320]{1,0:T(8,128)(2,1)S(1)}) custom-call(s32[2]{0:T(128)S(1)} %xor_reduce_fusion.refs_0_, s32[8]{0:T(128)S(1)} %reshape.93.refs_1_, bf16[256,320]{1,0:T(8,128)(2,1)S(1)} %get-tuple-element.33.refs_2_, f32[320,256]{1,0:T(8,128)S(1)} %get-tuple-element.41.refs_3_, ...), custom_call_target="tpu_custom_call" | custom-call | tf_op jit(solution)/shard_map/cross_view/pallas_call | solution.py:445
  41.9 2.2 %collective-permute-start.13 = (bf16[256,320]{1,0:T(8,128)(2,1)S(1)}, bf16[256,320]{1,0:T(8,128)(2,1)S(1)}, u32[]{:S(2)}, u32[]{:S(2)}) collective-permute-start(bf16[256,320]{1,0:T(8,128)(2,1)S(1)} %get-tuple-element.45.rows), channel_id=1, source_target_pairs={{0,1},{1,2},{2,3},{3,0},{4,5},{5,6},{6,7},{7,4},{8,9},{9,10},{10,1... | collective-permute-start | bytes 491528 | tf_op jit(solution)/shard_map/ppermute | solution.py:302
  44.2 1.7 %collective-permute-start.15 = (bf16[256,320]{1,0:T(8,128)(2,1)S(1)}, bf16[256,320]{1,0:T(8,128)(2,1)S(1)}, u32[]{:S(2)}, u32[]{:S(2)}) collective-permute-start(bf16[256,320]{1,0:T(8,128)(2,1)S(1)} %get-tuple-element.45.rows), channel_id=1, source_target_pairs={{1,0},{2,1},{3,2},{0,3},{5,4},{6,5},{7,6},{4,7},{9,8},{10,9},{11,1... | collective-permute-start | bytes 491528 | tf_op jit(solution)/shard_map/ppermute | solution.py:304
  45.8 5.8 %collective-permute-done.13.rows = bf16[256,320]{1,0:T(8,128)(2,1)S(1)} collective-permute-done((bf16[256,320]{1,0:T(8,128)(2,1)S(1)}, bf16[256,320]{1,0:T(8,128)(2,1)S(1)}, u32[]{:S(2)}, u32[]{:S(2)}) %collective-permute-start.13) | collective-permute-done | bytes 163872 | tf_op jit(solution)/shard_map/ppermute | solution.py:302
  51.9 2.3 %own_frame.1 = (bf16[4,320,320]{2,1,0:T(8,128)(2,1)S(1)}, bf16[256,320]{1,0:T(8,128)(2,1)S(1)}, f32[256,320]{1,0:T(8,128)S(1)}, bf16[256,320]{1,0:T(8,128)(2,1)S(1)}) custom-call(s32[5]{0:T(128)S(1)} %stack.23.where, bf16[256,320]{1,0:T(8,128)(2,1)S(1)} %get-tuple-element.45.rows, bf16[3,80,320]{2,1,0:T(8,128)(2,1)} %three.3, bf16[80,320]{1,0:T(8,128)(2,1)} %one.3, ...), custom_call_target="tpu_custom_call" | custom-call | flops 209715200 | bytes 1474560 | tf_op jit(solution)/shard_map/own_frame/pallas_call | solution.py:472
  54.2 0.6 %other_frame.2 = (f32[256,320]{1,0:T(8,128)S(1)}, bf16[256,320]{1,0:T(8,128)(2,1)S(1)}) custom-call(bf16[256,320]{1,0:T(8,128)(2,1)S(1)} %get-tuple-element.49.queries.refs_1_, bf16[256,320]{1,0:T(8,128)(2,1)S(1)} %collective-permute-done.13.rows, bf16[4,320,320]{2,1,0:T(8,128)(2,1)S(1)} %get-tuple-element.50.weights.refs_3_), custom_call_target="tpu_custom_call" | custom-call | flops 209715200 | bytes 1474560 | tf_op jit(solution)/shard_map/other_frame/pallas_call | solution.py:485
  55.3 0.6 %other_frame.3 = (f32[256,320]{1,0:T(8,128)S(1)}, bf16[256,320]{1,0:T(8,128)(2,1)S(1)}) custom-call(bf16[256,320]{1,0:T(8,128)(2,1)S(1)} %get-tuple-element.49.queries.refs_1_, bf16[256,320]{1,0:T(8,128)(2,1)S(1)} %collective-permute-done.15.rows, bf16[4,320,320]{2,1,0:T(8,128)(2,1)S(1)} %get-tuple-element.50.weights.refs_3_), custom_call_target="tpu_custom_call" | custom-call | flops 209715200 | bytes 1474560 | tf_op jit(solution)/shard_map/other_frame/pallas_call | solution.py:485
  56.0 3.7 %collective-permute-done.14.refs_2_ = bf16[256,320]{1,0:T(8,128)(2,1)S(1)} collective-permute-done((bf16[256,320]{1,0:T(8,128)(2,1)S(1)}, bf16[256,320]{1,0:T(8,128)(2,1)S(1)}, u32[]{:S(2)}, u32[]{:S(2)}) %collective-permute-start.14) | collective-permute-done | bytes 163872 | tf_op jit(solution)/shard_map/ppermute | solution.py:302
  59.7 2.0 %last.1 = bf16[320,256]{1,0:T(8,128)(2,1)} custom-call(bf16[256,320]{1,0:T(8,128)(2,1)S(1)} %get-tuple-element.43.refs_0_, bf16[256,320]{1,0:T(8,128)(2,1)S(1)} %get-tuple-element.49.queries.refs_1_, bf16[256,320]{1,0:T(8,128)(2,1)S(1)} %collective-permute-done.14.refs_2_, bf16[4,320,320]{2,1,0:T(8,128)(2,1)S(1)} %get-tuple-element.50.weights.refs_3_, ...), custom_call_target="tpu_custom_call" | custom-call | tf_op jit(solution)/shard_map/last/pallas_call | solution.py:496
  (44 shorter events, 2.6 us)
Async XLA Ops:
  0.0 34.8 %copy-start = (s32[2,4,2,2]{1,3,2,0:T(2,128)S(1)}, s32[2,4,2,2]{1,3,2,0:T(2,128)}, u32[]{:S(2)}) copy-start(s32[2,4,2,2]{1,3,2,0:T(2,128)} %param.14) | copy-start | bytes 388
  0.8 4.3 %copy-start.2 = (bf16[3,80,320]{2,1,0:T(8,128)(2,1)S(1)}, bf16[3,80,320]{2,1,0:T(8,128)(2,1)}, u32[]{:S(2)}) copy-start(bf16[3,80,320]{2,1,0:T(8,128)(2,1)} %three.2) | copy-start | bytes 460804
  0.8 4.3 %copy-start.4 = (bf16[80,320]{1,0:T(8,128)(2,1)S(1)}, bf16[80,320]{1,0:T(8,128)(2,1)}, u32[]{:S(2)}) copy-start(bf16[80,320]{1,0:T(8,128)(2,1)} %one.2) | copy-start | bytes 153604
  1.9 16.1 %copy-start.1 = (bf16[3,3,320,320]{3,2,1,0:T(8,128)(2,1)S(1)}, bf16[3,3,320,320]{3,2,1,0:T(8,128)(2,1)}, u32[]{:S(2)}) copy-start(bf16[3,3,320,320]{3,2,1,0:T(8,128)(2,1)} %param.16) | copy-start | bytes 5529604
  1.9 4.6 %collective-permute-start = (f32[1,320]{1,0:T(1,128)S(1)}, f32[1,320]{1,0:T(1,128)S(1)}, u32[]{:S(2)}, u32[]{:S(2)}) collective-permute-start(f32[1,320]{1,0:T(1,128)S(1)} %time_share.1), channel_id=1, source_target_pairs={{0,1},{1,0},{2,3},{3,2},{4,5},{5,4},{6,7},{7,6},{8,9},{9,8},{10,11... | collective-permute-start | bytes 3848 | tf_op jit(solution)/shard_map/ppermute | solution.py:288
  6.6 4.6 %collective-permute-start.1 = (f32[1,320]{1,0:T(1,128)S(1)}, f32[1,320]{1,0:T(1,128)S(1)}, u32[]{:S(2)}, u32[]{:S(2)}) collective-permute-start(f32[1,320]{1,0:T(1,128)S(1)} %add.75), channel_id=1, source_target_pairs={{0,2},{1,3},{2,0},{3,1},{4,6},{5,7},{6,4},{7,5},{8,10},{9,11},{10,... | collective-permute-start | bytes 3848 | tf_op jit(solution)/shard_map/ppermute | solution.py:288
  11.2 8.6 %collective-permute-start.3 = (bf16[160,320]{1,0:T(8,128)(2,1)S(1)}, bf16[160,320]{1,0:T(8,128)(2,1)S(1)}, u32[]{:S(2)}, u32[]{:S(2)}) collective-permute-start(bf16[160,320]{1,0:T(8,128)(2,1)S(1)} %dynamic-slice_bitcast_fusion.1), channel_id=1, source_target_pairs={{0,1},{1,2},{2,3},{3,0},{4,5},{5,6},{6,7},{7,4},{8,9},{9,10},{10,1... | collective-permute-start | bytes 307208 | tf_op jit(solution)/shard_map/ppermute | solution.py:302
  15.9 10.7 %copy-start.3 = (bf16[3,80,320]{2,1,0:T(8,128)(2,1)S(1)}, bf16[3,80,320]{2,1,0:T(8,128)(2,1)}, u32[]{:S(2)}) copy-start(bf16[3,80,320]{2,1,0:T(8,128)(2,1)} %three.3) | copy-start | bytes 460804
  15.9 10.7 %copy-start.5 = (bf16[80,320]{1,0:T(8,128)(2,1)S(1)}, bf16[80,320]{1,0:T(8,128)(2,1)}, u32[]{:S(2)}) copy-start(bf16[80,320]{1,0:T(8,128)(2,1)} %one.3) | copy-start | bytes 153604
  16.0 4.9 %collective-permute-start.2 = (bf16[160,320]{1,0:T(8,128)(2,1)S(1)}, bf16[160,320]{1,0:T(8,128)(2,1)S(1)}, u32[]{:S(2)}, u32[]{:S(2)}) collective-permute-start(bf16[160,320]{1,0:T(8,128)(2,1)S(1)} %dynamic-slice_bitcast_fusion.1), channel_id=1, source_target_pairs={{1,0},{2,1},{3,2},{0,3},{5,4},{6,5},{7,6},{4,7},{9,8},{10,9},{11,1... | collective-permute-start | bytes 307208 | tf_op jit(solution)/shard_map/ppermute | solution.py:304
  18.0 17.0 %copy-start.6 = (s32[2,4]{1,0:T(2,128)S(1)}, s32[2,4]{1,0:T(2,128)}, u32[]{:S(2)}) copy-start(s32[2,4]{1,0:T(2,128)} %param.13) | copy-start | bytes 100
  19.8 6.7 %collective-permute-start.4 = (bf16[160,320]{1,0:T(8,128)(2,1)S(1)}, bf16[160,320]{1,0:T(8,128)(2,1)S(1)}, u32[]{:S(2)}, u32[]{:S(2)}) collective-permute-start(bf16[160,320]{1,0:T(8,128)(2,1)S(1)} %collective-permute-done.3.refs_0_), channel_id=1, source_target_pairs={{0,1},{1,2},{2,3},{3,0},{4,5},{5,6},{6,7},{7,4},{8,9},{9,10},{10,1... | collective-permute-start | bytes 307208 | tf_op jit(solution)/shard_map/ppermute | solution.py:302
  20.9 5.9 %collective-permute-start.9 = (bf16[256,320]{1,0:T(8,128)(2,1)S(1)}, bf16[256,320]{1,0:T(8,128)(2,1)S(1)}, u32[]{:S(2)}, u32[]{:S(2)}) collective-permute-start(bf16[256,320]{1,0:T(8,128)(2,1)S(1)} %get-tuple-element.36.normed.refs_5_), channel_id=1, source_target_pairs={{0,8},{4,12},{8,0},{12,4},{1,9},{5,13},{9,1},{13,5},{2,10},{6,14},... | collective-permute-start | bytes 491528 | tf_op jit(solution)/shard_map/ppermute | solution.py:275
  22.4 4.3 %collective-permute-start.6 = (bf16[256,320]{1,0:T(8,128)(2,1)S(1)}, bf16[256,320]{1,0:T(8,128)(2,1)S(1)}, u32[]{:S(2)}, u32[]{:S(2)}) collective-permute-start(bf16[256,320]{1,0:T(8,128)(2,1)S(1)} %get-tuple-element.36.normed.refs_5_), channel_id=1, source_target_pairs={{0,4},{4,0},{8,12},{12,8},{1,5},{5,1},{9,13},{13,9},{2,6},{6,2},{1... | collective-permute-start | bytes 491528 | tf_op jit(solution)/shard_map/ppermute | solution.py:275
  26.5 4.4 %collective-permute-start.5 = (bf16[480,320]{1,0:T(8,128)(2,1)S(1)}, bf16[480,320]{1,0:T(8,128)(2,1)S(1)}, u32[]{:S(2)}, u32[]{:S(2)}) collective-permute-start(bf16[480,320]{1,0:T(8,128)(2,1)S(1)} %pad_maximum_fusion), channel_id=1, source_target_pairs={{0,4},{4,0},{8,12},{12,8},{1,5},{5,1},{9,13},{13,9},{2,6},{6,2},{1... | collective-permute-start | bytes 921608 | tf_op jit(solution)/shard_map/ppermute | solution.py:318
  26.7 8.0 %collective-permute-start.7 = (bf16[160,320]{1,0:T(8,128)(2,1)S(1)}, bf16[160,320]{1,0:T(8,128)(2,1)S(1)}, u32[]{:S(2)}, u32[]{:S(2)}) collective-permute-start(bf16[160,320]{1,0:T(8,128)(2,1)S(1)} %dynamic-slice_bitcast_fusion), channel_id=1, source_target_pairs={{0,1},{1,2},{2,3},{3,0},{4,5},{5,6},{6,7},{7,4},{8,9},{9,10},{10,1... | collective-permute-start | bytes 307208 | tf_op jit(solution)/shard_map/ppermute | solution.py:302
  26.8 8.5 %collective-permute-start.10 = (bf16[256,320]{1,0:T(8,128)(2,1)S(1)}, bf16[256,320]{1,0:T(8,128)(2,1)S(1)}, u32[]{:S(2)}, u32[]{:S(2)}) collective-permute-start(bf16[256,320]{1,0:T(8,128)(2,1)S(1)} %collective-permute-done.9.refs_7_), channel_id=1, source_target_pairs={{0,4},{4,0},{8,12},{12,8},{1,5},{5,1},{9,13},{13,9},{2,6},{6,2},{1... | collective-permute-start | bytes 491528 | tf_op jit(solution)/shard_map/ppermute | solution.py:275
  27.4 8.0 %collective-permute-start.8 = (bf16[160,320]{1,0:T(8,128)(2,1)S(1)}, bf16[160,320]{1,0:T(8,128)(2,1)S(1)}, u32[]{:S(2)}, u32[]{:S(2)}) collective-permute-start(bf16[160,320]{1,0:T(8,128)(2,1)S(1)} %dynamic-slice_bitcast_fusion), channel_id=1, source_target_pairs={{1,0},{2,1},{3,2},{0,3},{5,4},{6,5},{7,6},{4,7},{9,8},{10,9},{11,1... | collective-permute-start | bytes 307208 | tf_op jit(solution)/shard_map/ppermute | solution.py:304
  34.7 7.1 %collective-permute-start.11 = (bf16[160,320]{1,0:T(8,128)(2,1)S(1)}, bf16[160,320]{1,0:T(8,128)(2,1)S(1)}, u32[]{:S(2)}, u32[]{:S(2)}) collective-permute-start(bf16[160,320]{1,0:T(8,128)(2,1)S(1)} %collective-permute-done.7.refs_0_), channel_id=1, source_target_pairs={{0,1},{1,2},{2,3},{3,0},{4,5},{5,6},{6,7},{7,4},{8,9},{9,10},{10,1... | collective-permute-start | bytes 307208 | tf_op jit(solution)/shard_map/ppermute | solution.py:302
  41.9 10.0 %collective-permute-start.12 = (bf16[480,320]{1,0:T(8,128)(2,1)S(1)}, bf16[480,320]{1,0:T(8,128)(2,1)S(1)}, u32[]{:S(2)}, u32[]{:S(2)}) collective-permute-start(bf16[480,320]{1,0:T(8,128)(2,1)S(1)} %pad_maximum_fusion.1), channel_id=1, source_target_pairs={{0,4},{4,0},{8,12},{12,8},{1,5},{5,1},{9,13},{13,9},{2,6},{6,2},{1... | collective-permute-start | bytes 921608 | tf_op jit(solution)/shard_map/ppermute | solution.py:318
  41.9 9.7 %collective-permute-start.13 = (bf16[256,320]{1,0:T(8,128)(2,1)S(1)}, bf16[256,320]{1,0:T(8,128)(2,1)S(1)}, u32[]{:S(2)}, u32[]{:S(2)}) collective-permute-start(bf16[256,320]{1,0:T(8,128)(2,1)S(1)} %get-tuple-element.45.rows), channel_id=1, source_target_pairs={{0,1},{1,2},{2,3},{3,0},{4,5},{5,6},{6,7},{7,4},{8,9},{9,10},{10,1... | collective-permute-start | bytes 491528 | tf_op jit(solution)/shard_map/ppermute | solution.py:302
  44.2 11.2 %collective-permute-start.15 = (bf16[256,320]{1,0:T(8,128)(2,1)S(1)}, bf16[256,320]{1,0:T(8,128)(2,1)S(1)}, u32[]{:S(2)}, u32[]{:S(2)}) collective-permute-start(bf16[256,320]{1,0:T(8,128)(2,1)S(1)} %get-tuple-element.45.rows), channel_id=1, source_target_pairs={{1,0},{2,1},{3,2},{0,3},{5,4},{6,5},{7,6},{4,7},{9,8},{10,9},{11,1... | collective-permute-start | bytes 491528 | tf_op jit(solution)/shard_map/ppermute | solution.py:304
  51.6 8.1 %collective-permute-start.14 = (bf16[256,320]{1,0:T(8,128)(2,1)S(1)}, bf16[256,320]{1,0:T(8,128)(2,1)S(1)}, u32[]{:S(2)}, u32[]{:S(2)}) collective-permute-start(bf16[256,320]{1,0:T(8,128)(2,1)S(1)} %collective-permute-done.13.rows), channel_id=1, source_target_pairs={{0,1},{1,2},{2,3},{3,0},{4,5},{5,6},{6,7},{7,4},{8,9},{9,10},{10,1... | collective-permute-start | bytes 491528 | tf_op jit(solution)/shard_map/ppermute | solution.py:302

commit v12 on v4

--- a/solution.py
+++ b/solution.py
@@ -146,31 +146,37 @@
 
             @pl.when(select[matching] == j)
             def _():
-                chosen[...] = maps[j][...]
-
-        other = chosen[...]
-        keys = dot(other, weights[1]).astype(bf16)
-        values = dot(other, weights[2]).T
-        shifts = []
-        for j in range(tiles):
-            row = jnp.zeros((1, tokens), f32)
-            for i in range(tiles):
-                bit = mask[(matching * tiles + i) * tiles + j]
-                row = jnp.where(lane_tile == i, jnp.where(bit > 0, 0.0, MASKED), row)
-            shifts.append(row)
-        for h in range(HEADS):
-            low, high, wanted = windows[h]
-            scores = dot(keys[:, low:high], wanted) * scale
+                chosen[pl.ds(matching * tokens, tokens), :] = maps[j][...]
+
+    keys = dot(chosen[...], weights[1]).astype(bf16)
+    values = dot(chosen[...], weights[2]).T
+    shifts = []
+    for block in range(2 * tiles):
+        matching, j = divmod(block, tiles)
+        row = jnp.zeros((1, tokens), f32)
+        for i in range(tiles):
+            bit = mask[(matching * tiles + i) * tiles + j]
+            row = jnp.where(lane_tile == i, jnp.where(bit > 0, 0.0, MASKED), row)
+        shifts.append(row)
+    for h in range(HEADS):
+        low, high, wanted = windows[h]
+        both = dot(keys[:, low:high], wanted)
+        total = None
+        for matching in range(2):
+            first = matching * tiles
             scores = jnp.concatenate(
-                [scores[j * width : (j + 1) * width] + shifts[j] for j in range(tiles)], axis=0
+                [
+                    both[k * width : (k + 1) * width] * scale + shifts[k]
+                    for k in range(first, first + tiles)
+                ],
+                axis=0,
             )
             powers = jnp.exp2(scores - jnp.max(scores, axis=0, keepdims=True))
             norm = 1.0 / jnp.sum(powers, axis=0, keepdims=True)
-            part = dot(values[h * head : (h + 1) * head].astype(bf16), powers.astype(bf16)) * norm
-            if matching == 0:
-                totals[pl.ds(h * head, head), :] = part
-            else:
-                totals[pl.ds(h * head, head), :] += part
+            rows = values[h * head : (h + 1) * head, matching * tokens : (matching + 1) * tokens]
+            part = dot(rows.astype(bf16), powers.astype(bf16)) * norm
+            total = part if total is None else total + part
+        totals[pl.ds(h * head, head), :] = total
     mixture = totals[...].T.astype(bf16)
     result = (hidden[...].astype(f32) + dot(mixture, weights[3])).astype(bf16)
     second[...] = result
@@ -183,10 +189,8 @@
     ones = block_diagonal(channels, head)
     keys = dot(rows, weights[1]).astype(bf16).astype(f32)
     values = dot(rows, weights[2]).astype(bf16)
-    products = queries * keys
-    high = products.astype(bf16)
-    low = (products - high.astype(f32)).astype(bf16)
-    return (dot(high, ones) + dot(low, ones)) * (LOG2E / math.sqrt(head)), values
+    products = (queries * keys).astype(bf16)
+    return dot(products, ones) * (LOG2E / math.sqrt(head)), values
 
 
 def own_frame_kernel(where, rows, *refs):
@@ -412,7 +416,7 @@
         in_specs=[SMEM, SMEM, VMEM, VMEM, VMEM] + [VMEM] * videos,
         out_specs=[VMEM, VMEM],
         scratch_shapes=[
-            pltpu.VMEM((tokens, channels), bf16),
+            pltpu.VMEM((2 * tokens, channels), bf16),
             pltpu.VMEM((channels, tokens), f32),
         ],
         compiler_params=params(),

time: 61 us -> 59 us (0.967)
  Pallas kernels: 15.2 us -> 12.8 us
    pallas_call x1, Pallas kernels: 6.08 us -> 4.23 us  [per_device(): pl.pallas_call(functools.partial(view_kernel, videos, tiles), out_shape=[...]
  transfers between devices with their start and end apart: 20 -> 20, of which waited for: 12 -> 12; matrix products, arithmetic and copies ran while one was open for 2% -> 2% of each run, Pallas kernels for 22% -> 18%
where the time goes in v12:
time: 59 us; the launch traced here: 58.8 us
  waiting for transfers between devices  21.5 us (36%)
  starting transfers between devices  19.6 us (33%)
  Pallas kernels  12.8 us (22%)
  local copies, waits for them, and re-layouts  3.58 us (6%)
  between operations  0.88 us (1%)
    ppermute x6, waiting for transfers between devices, ring_gather(): pieces[step] = lax.ppermute(pieces[step - 1], axis, right)  12.6 us
    ppermute x3, starting transfers between devices, ring_gather(): lax.ppermute(pieces[(size - step + 1) % size], axis, left)  6.83 us
    ppermute x2, starting transfers between devices, sum_over(): value = value + lax.ppermute(value, axis, partner_permutation(size, bit))  6.1 us
    pallas_call x1, Pallas kernels, per_device(): pl.pallas_call(functools.partial(view_kernel, videos, tiles), out_shape=[...  4.23 us
    ppermute x6, starting transfers between devices, ring_gather(): pieces[step] = lax.ppermute(pieces[step - 1], axis, right)  3.88 us
    ppermute x2, waiting for transfers between devices, sum_over(): value = value + lax.ppermute(value, axis, partner_permutation(size, bit))  3.03 us
    ppermute x3, waiting for transfers between devices, gather_maps(): maps[k | bit] = lax.ppermute(maps[k], axis, partner_permutation(size, bit))  2.98 us
    unnamed x24, local copies, waits for them, and re-layouts  2.53 us
  transfers between devices with their start and end apart: 20, of which 12 were waited for; matrix products, arithmetic and copies ran while one was open for 2% of the time, Pallas kernels for 18%

profile of v12, /device:TPU:0, one launch (start us, length us, event | category | flops | bytes accessed | tf_op | source)
XLA Modules:
  0.0 58.8 jit_solution(18141323832087697217)
XLA Ops:
  0.8 0.9 %copy-done.6 = bf16[320,320]{1,0:T(8,128)(2,1)S(1)} copy-done((bf16[320,320]{1,0:T(8,128)(2,1)S(1)}, bf16[320,320]{1,0:T(8,128)(2,1)}, u32[]{:S(2)}) %copy-start.6) | copy-done | bytes 204824
  1.8 3.1 %collective-permute-start = (f32[1,320]{1,0:T(1,128)S(1)}, f32[1,320]{1,0:T(1,128)S(1)}, u32[]{:S(2)}, u32[]{:S(2)}) collective-permute-start(f32[1,320]{1,0:T(1,128)S(1)} %time_share.1), channel_id=1, source_target_pairs={{0,1},{1,0},{2,3},{3,2},{4,5},{5,4},{6,7},{7,6},{8,9},{9,8},{10,11... | collective-permute-start | bytes 3848 | tf_op jit(solution)/shard_map/ppermute | solution.py:260
  4.9 1.6 %collective-permute-done = f32[1,320]{1,0:T(1,128)S(1)} collective-permute-done((f32[1,320]{1,0:T(1,128)S(1)}, f32[1,320]{1,0:T(1,128)S(1)}, u32[]{:S(2)}, u32[]{:S(2)}) %collective-permute-start) | collective-permute-done | bytes 1312 | tf_op jit(solution)/shard_map/ppermute | solution.py:260
  6.5 3.0 %collective-permute-start.1 = (f32[1,320]{1,0:T(1,128)S(1)}, f32[1,320]{1,0:T(1,128)S(1)}, u32[]{:S(2)}, u32[]{:S(2)}) collective-permute-start(f32[1,320]{1,0:T(1,128)S(1)} %add.75), channel_id=1, source_target_pairs={{0,2},{1,3},{2,0},{3,1},{4,6},{5,7},{6,4},{7,5},{8,10},{9,11},{10,... | collective-permute-start | bytes 3848 | tf_op jit(solution)/shard_map/ppermute | solution.py:260
  9.6 1.5 %collective-permute-done.1 = f32[1,320]{1,0:T(1,128)S(1)} collective-permute-done((f32[1,320]{1,0:T(1,128)S(1)}, f32[1,320]{1,0:T(1,128)S(1)}, u32[]{:S(2)}, u32[]{:S(2)}) %collective-permute-start.1) | collective-permute-done | bytes 1312 | tf_op jit(solution)/shard_map/ppermute | solution.py:260
  11.1 2.0 %collective-permute-start.2 = (bf16[2,80,320]{2,1,0:T(8,128)(2,1)S(1)}, bf16[2,80,320]{2,1,0:T(8,128)(2,1)S(1)}, u32[]{:S(2)}, u32[]{:S(2)}) collective-permute-start(bf16[2,80,320]{2,1,0:T(8,128)(2,1)S(1)} %dynamic-slice_bitcast_fusion.1), channel_id=1, source_target_pairs={{0,1},{1,2},{2,3},{3,0},{4,5},{5,6},{6,7},{7,4},{8,9},{9,10},{10,1... | collective-permute-start | bytes 307208 | tf_op jit(solution)/shard_map/ppermute | solution.py:273
  13.1 2.1 %collective-permute-start.3 = (bf16[2,80,320]{2,1,0:T(8,128)(2,1)S(1)}, bf16[2,80,320]{2,1,0:T(8,128)(2,1)S(1)}, u32[]{:S(2)}, u32[]{:S(2)}) collective-permute-start(bf16[2,80,320]{2,1,0:T(8,128)(2,1)S(1)} %dynamic-slice_bitcast_fusion.1), channel_id=1, source_target_pairs={{1,0},{2,1},{3,2},{0,3},{5,4},{6,5},{7,6},{4,7},{9,8},{10,9},{11,1... | collective-permute-start | bytes 307208 | tf_op jit(solution)/shard_map/ppermute | solution.py:275
  15.2 1.6 %first_conv.1.inner = f32[256,320]{1,0:T(8,128)S(1)} custom-call(bf16[320,256]{1,0:T(8,128)(2,1)S(1)} %bitcast.26, bf16[3,960,320]{2,1,0:T(8,128)(2,1)S(1)} %bitcast.22), custom_call_target="tpu_custom_call" | custom-call | flops 471859200 | bytes 2498560 | tf_op jit(solution)/shard_map/first_conv/pallas_call | solution.py:361
  16.8 1.7 %second_conv.1 = (bf16[256,320]{1,0:T(8,128)(2,1)S(1)}, bf16[256,320]{1,0:T(8,128)(2,1)S(1)}) custom-call(bf16[320,256]{1,0:T(8,128)(2,1)S(1)} %bitcast.27, f32[256,320]{1,0:T(8,128)S(1)} %first_conv.1.inner, f32[1,320]{1,0:T(1,128)S(1)} %add.76.bias, bf16[3,960,320]{2,1,0:T(8,128)(2,1)S(1)} %bitcast.23), custom_call_target="tpu_custom_call" | custom-call | flops 471859200 | bytes 2498560 | tf_op jit(solution)/shard_map/second_conv/pallas_call | solution.py:371
  19.3 1.5 %collective-permute-start.11 = (bf16[256,320]{1,0:T(8,128)(2,1)S(1)}, bf16[256,320]{1,0:T(8,128)(2,1)S(1)}, u32[]{:S(2)}, u32[]{:S(2)}) collective-permute-start(bf16[256,320]{1,0:T(8,128)(2,1)S(1)} %get-tuple-element.44.normed.refs_5_), channel_id=1, source_target_pairs={{0,8},{4,12},{8,0},{12,4},{1,9},{5,13},{9,1},{13,5},{2,10},{6,14},... | collective-permute-start | bytes 491528 | tf_op jit(solution)/shard_map/ppermute | solution.py:247
  22.5 1.1 %collective-permute-start.9 = (bf16[2,80,320]{2,1,0:T(8,128)(2,1)}, bf16[2,80,320]{2,1,0:T(8,128)(2,1)S(1)}, u32[]{:S(2)}, u32[]{:S(2)}) collective-permute-start(bf16[2,80,320]{2,1,0:T(8,128)(2,1)} %dynamic-slice_bitcast_fusion), channel_id=1, source_target_pairs={{0,1},{1,2},{2,3},{3,0},{4,5},{5,6},{6,7},{7,4},{8,9},{9,10},{10,1... | collective-permute-start | bytes 307208 | tf_op jit(solution)/shard_map/ppermute | solution.py:273
  23.6 3.0 %collective-permute-done.11.refs_7_ = bf16[256,320]{1,0:T(8,128)(2,1)S(1)} collective-permute-done((bf16[256,320]{1,0:T(8,128)(2,1)S(1)}, bf16[256,320]{1,0:T(8,128)(2,1)S(1)}, u32[]{:S(2)}, u32[]{:S(2)}) %collective-permute-start.11) | collective-permute-done | bytes 163872 | tf_op jit(solution)/shard_map/ppermute | solution.py:247
  27.1 2.0 %collective-permute-done.4.refs_2_ = bf16[2,80,320]{2,1,0:T(8,128)(2,1)S(1)} collective-permute-done((bf16[2,80,320]{2,1,0:T(8,128)(2,1)S(1)}, bf16[2,80,320]{2,1,0:T(8,128)(2,1)S(1)}, u32[]{:S(2)}, u32[]{:S(2)}) %collective-permute-start.4) | collective-permute-done | bytes 102432 | tf_op jit(solution)/shard_map/ppermute | solution.py:273
  29.1 0.9 %collective-permute-start.10 = (bf16[2,80,320]{2,1,0:T(8,128)(2,1)}, bf16[2,80,320]{2,1,0:T(8,128)(2,1)S(1)}, u32[]{:S(2)}, u32[]{:S(2)}) collective-permute-start(bf16[2,80,320]{2,1,0:T(8,128)(2,1)} %dynamic-slice_bitcast_fusion), channel_id=1, source_target_pairs={{1,0},{2,1},{3,2},{0,3},{5,4},{6,5},{7,6},{4,7},{9,8},{10,9},{11,1... | collective-permute-start | bytes 307208 | tf_op jit(solution)/shard_map/ppermute | solution.py:275
  30.0 1.1 %collective-permute-done.9.refs_1_ = bf16[2,80,320]{2,1,0:T(8,128)(2,1)S(1)} collective-permute-done((bf16[2,80,320]{2,1,0:T(8,128)(2,1)}, bf16[2,80,320]{2,1,0:T(8,128)(2,1)S(1)}, u32[]{:S(2)}, u32[]{:S(2)}) %collective-permute-start.9) | collective-permute-done | bytes 102432 | tf_op jit(solution)/shard_map/ppermute | solution.py:273
  32.3 0.9 %copy-done.5 = bf16[2,80,320]{2,1,0:T(8,128)(2,1)S(1)} copy-done((bf16[2,80,320]{2,1,0:T(8,128)(2,1)S(1)}, bf16[2,80,320]{2,1,0:T(8,128)(2,1)}, u32[]{:S(2)}) %copy-start.5) | copy-done | bytes 102424
  33.2 1.0 %query.1 = (f32[320,256]{1,0:T(8,128)S(1)}, bf16[4,320,320]{2,1,0:T(8,128)(2,1)S(1)}) custom-call(s32[5]{0:T(128)S(1)} %stack.23.where, bf16[256,320]{1,0:T(8,128)(2,1)S(1)} %get-tuple-element.44.normed.refs_5_, bf16[4,80,320]{2,1,0:T(8,128)(2,1)S(1)} %pad_maximum_fusion.refs_0_, bf16[2,80,320]{2,1,0:T(8,128)(2,1)S(1)} %collective-permute-done.2.refs_1_, ...), custom_call_target="tpu_custom_call" | custom-call | tf_op jit(solution)/shard_map/query/pallas_call | solution.py:399
  35.0 4.2 %cross_view.1 = (bf16[256,320]{1,0:T(8,128)(2,1)S(1)}, bf16[256,320]{1,0:T(8,128)(2,1)S(1)}) custom-call(s32[2]{0:T(128)S(1)} %xor_reduce_fusion.refs_0_, s32[8]{0:T(128)S(1)} %reshape.93.refs_1_, bf16[256,320]{1,0:T(8,128)(2,1)S(1)} %get-tuple-element.43.refs_2_, f32[320,256]{1,0:T(8,128)S(1)} %get-tuple-element.49.refs_3_, ...), custom_call_target="tpu_custom_call" | custom-call | tf_op jit(solution)/shard_map/cross_view/pallas_call | solution.py:413
  39.3 3.8 %collective-permute-start.19 = (bf16[256,320]{1,0:T(8,128)(2,1)S(1)}, bf16[256,320]{1,0:T(8,128)(2,1)S(1)}, u32[]{:S(2)}, u32[]{:S(2)}) collective-permute-start(bf16[256,320]{1,0:T(8,128)(2,1)S(1)} %get-tuple-element.56.rows), channel_id=1, source_target_pairs={{1,0},{2,1},{3,2},{0,3},{5,4},{6,5},{7,6},{4,7},{9,8},{10,9},{11,1... | collective-permute-start | bytes 491528 | tf_op jit(solution)/shard_map/ppermute | solution.py:275
  43.1 5.8 %collective-permute-done.17.rows = bf16[256,320]{1,0:T(8,128)(2,1)S(1)} collective-permute-done((bf16[256,320]{1,0:T(8,128)(2,1)S(1)}, bf16[256,320]{1,0:T(8,128)(2,1)S(1)}, u32[]{:S(2)}, u32[]{:S(2)}) %collective-permute-start.17) | collective-permute-done | bytes 163872 | tf_op jit(solution)/shard_map/ppermute | solution.py:273
  49.4 0.8 %collective-permute-done.14.refs_4_ = bf16[2,80,320]{2,1,0:T(8,128)(2,1)S(1)} collective-permute-done((bf16[2,80,320]{2,1,0:T(8,128)(2,1)S(1)}, bf16[2,80,320]{2,1,0:T(8,128)(2,1)S(1)}, u32[]{:S(2)}, u32[]{:S(2)}) %collective-permute-start.14) | collective-permute-done | bytes 102432 | tf_op jit(solution)/shard_map/ppermute | solution.py:297
  50.8 1.3 %own_frame.1 = (bf16[4,320,320]{2,1,0:T(8,128)(2,1)S(1)}, bf16[256,320]{1,0:T(8,128)(2,1)S(1)}, f32[256,320]{1,0:T(8,128)S(1)}, bf16[256,320]{1,0:T(8,128)(2,1)S(1)}) custom-call(s32[5]{0:T(128)S(1)} %stack.23.where, bf16[256,320]{1,0:T(8,128)(2,1)S(1)} %get-tuple-element.56.rows, bf16[4,80,320]{2,1,0:T(8,128)(2,1)S(1)} %pad_maximum_fusion.1.refs_0_, ...), custom_call_target="tpu_custom_call" | custom-call | flops 209715200 | bytes 1474560 | tf_op jit(solution)/shard_map/own_frame/pallas_call | solution.py:437
  53.1 3.8 %collective-permute-done.18.refs_2_ = bf16[256,320]{1,0:T(8,128)(2,1)S(1)} collective-permute-done((bf16[256,320]{1,0:T(8,128)(2,1)S(1)}, bf16[256,320]{1,0:T(8,128)(2,1)S(1)}, u32[]{:S(2)}, u32[]{:S(2)}) %collective-permute-start.18) | collective-permute-done | bytes 163872 | tf_op jit(solution)/shard_map/ppermute | solution.py:273
  56.9 1.8 %last.1 = bf16[320,256]{1,0:T(8,128)(2,1)} custom-call(bf16[256,320]{1,0:T(8,128)(2,1)S(1)} %get-tuple-element.52.refs_0_, bf16[256,320]{1,0:T(8,128)(2,1)S(1)} %get-tuple-element.61.queries.refs_1_, bf16[256,320]{1,0:T(8,128)(2,1)S(1)} %collective-permute-done.18.refs_2_, bf16[4,320,320]{2,1,0:T(8,128)(2,1)S(1)} %get-tuple-element.62.weights.refs_3_, ...), custom_call_target="tpu_custom_call" | custom-call | tf_op jit(solution)/shard_map/last/pallas_call | solution.py:460
  (60 shorter events, 7.5 us)
Async XLA Ops:
  0.0 31.1 %copy-start = (s32[2,4,2,2]{1,3,2,0:T(2,128)S(1)}, s32[2,4,2,2]{1,3,2,0:T(2,128)}, u32[]{:S(2)}) copy-start(s32[2,4,2,2]{1,3,2,0:T(2,128)} %param.14) | copy-start | bytes 388
  1.7 13.4 %copy-start.1 = (bf16[3,3,320,320]{3,2,1,0:T(8,128)(2,1)S(1)}, bf16[3,3,320,320]{3,2,1,0:T(8,128)(2,1)}, u32[]{:S(2)}) copy-start(bf16[3,3,320,320]{3,2,1,0:T(8,128)(2,1)} %param.15) | copy-start | bytes 5529604
  1.7 13.4 %copy-start.3 = (bf16[1,1,256,320]{2,3,1,0:T(8,128)(2,1)S(1)}, bf16[1,1,256,320]{2,3,1,0:T(8,128)(2,1)}, u32[]{:S(2)}) copy-start(bf16[1,1,256,320]{2,3,1,0:T(8,128)(2,1)} %param.11) | copy-start | bytes 491524
  1.8 4.6 %collective-permute-start = (f32[1,320]{1,0:T(1,128)S(1)}, f32[1,320]{1,0:T(1,128)S(1)}, u32[]{:S(2)}, u32[]{:S(2)}) collective-permute-start(f32[1,320]{1,0:T(1,128)S(1)} %time_share.1), channel_id=1, source_target_pairs={{0,1},{1,0},{2,3},{3,2},{4,5},{5,4},{6,7},{7,6},{8,9},{9,8},{10,11... | collective-permute-start | bytes 3848 | tf_op jit(solution)/shard_map/ppermute | solution.py:260
  6.5 4.6 %collective-permute-start.1 = (f32[1,320]{1,0:T(1,128)S(1)}, f32[1,320]{1,0:T(1,128)S(1)}, u32[]{:S(2)}, u32[]{:S(2)}) collective-permute-start(f32[1,320]{1,0:T(1,128)S(1)} %add.75), channel_id=1, source_target_pairs={{0,2},{1,3},{2,0},{3,1},{4,6},{5,7},{6,4},{7,5},{8,10},{9,11},{10,... | collective-permute-start | bytes 3848 | tf_op jit(solution)/shard_map/ppermute | solution.py:260
  11.1 7.5 %collective-permute-start.2 = (bf16[2,80,320]{2,1,0:T(8,128)(2,1)S(1)}, bf16[2,80,320]{2,1,0:T(8,128)(2,1)S(1)}, u32[]{:S(2)}, u32[]{:S(2)}) collective-permute-start(bf16[2,80,320]{2,1,0:T(8,128)(2,1)S(1)} %dynamic-slice_bitcast_fusion.1), channel_id=1, source_target_pairs={{0,1},{1,2},{2,3},{3,0},{4,5},{5,6},{6,7},{7,4},{8,9},{9,10},{10,1... | collective-permute-start | bytes 307208 | tf_op jit(solution)/shard_map/ppermute | solution.py:273
  13.1 6.2 %collective-permute-start.3 = (bf16[2,80,320]{2,1,0:T(8,128)(2,1)S(1)}, bf16[2,80,320]{2,1,0:T(8,128)(2,1)S(1)}, u32[]{:S(2)}, u32[]{:S(2)}) collective-permute-start(bf16[2,80,320]{2,1,0:T(8,128)(2,1)S(1)} %dynamic-slice_bitcast_fusion.1), channel_id=1, source_target_pairs={{1,0},{2,1},{3,2},{0,3},{5,4},{6,5},{7,6},{4,7},{9,8},{10,9},{11,1... | collective-permute-start | bytes 307208 | tf_op jit(solution)/shard_map/ppermute | solution.py:275
  16.8 14.7 %copy-start.11 = (s32[2,4]{1,0:T(2,128)S(1)}, s32[2,4]{1,0:T(2,128)}, u32[]{:S(2)}) copy-start(s32[2,4]{1,0:T(2,128)} %param.13) | copy-start | bytes 100
  19.3 2.6 %collective-permute-start.8 = (bf16[256,320]{1,0:T(8,128)(2,1)S(1)}, bf16[256,320]{1,0:T(8,128)(2,1)S(1)}, u32[]{:S(2)}, u32[]{:S(2)}) collective-permute-start(bf16[256,320]{1,0:T(8,128)(2,1)S(1)} %get-tuple-element.44.normed.refs_5_), channel_id=1, source_target_pairs={{0,4},{4,0},{8,12},{12,8},{1,5},{5,1},{9,13},{13,9},{2,6},{6,2},{1... | collective-permute-start | bytes 491528 | tf_op jit(solution)/shard_map/ppermute | solution.py:247
  19.3 7.3 %collective-permute-start.11 = (bf16[256,320]{1,0:T(8,128)(2,1)S(1)}, bf16[256,320]{1,0:T(8,128)(2,1)S(1)}, u32[]{:S(2)}, u32[]{:S(2)}) collective-permute-start(bf16[256,320]{1,0:T(8,128)(2,1)S(1)} %get-tuple-element.44.normed.refs_5_), channel_id=1, source_target_pairs={{0,8},{4,12},{8,0},{12,4},{1,9},{5,13},{9,1},{13,5},{2,10},{6,14},... | collective-permute-start | bytes 491528 | tf_op jit(solution)/shard_map/ppermute | solution.py:247
  20.8 8.2 %collective-permute-start.5 = (bf16[2,80,320]{2,1,0:T(8,128)(2,1)S(1)}, bf16[2,80,320]{2,1,0:T(8,128)(2,1)S(1)}, u32[]{:S(2)}, u32[]{:S(2)}) collective-permute-start(bf16[2,80,320]{2,1,0:T(8,128)(2,1)S(1)} %collective-permute-done.2.refs_1_), channel_id=1, source_target_pairs={{0,4},{4,0},{8,12},{12,8},{1,5},{5,1},{9,13},{13,9},{2,6},{6,2},{1... | collective-permute-start | bytes 307208 | tf_op jit(solution)/shard_map/ppermute | solution.py:297
  21.1 7.9 %collective-permute-start.4 = (bf16[2,80,320]{2,1,0:T(8,128)(2,1)S(1)}, bf16[2,80,320]{2,1,0:T(8,128)(2,1)S(1)}, u32[]{:S(2)}, u32[]{:S(2)}) collective-permute-start(bf16[2,80,320]{2,1,0:T(8,128)(2,1)S(1)} %collective-permute-done.2.refs_1_), channel_id=1, source_target_pairs={{0,1},{1,2},{2,3},{3,0},{4,5},{5,6},{6,7},{7,4},{8,9},{9,10},{10,1... | collective-permute-start | bytes 307208 | tf_op jit(solution)/shard_map/ppermute | solution.py:273
  22.5 8.5 %collective-permute-start.9 = (bf16[2,80,320]{2,1,0:T(8,128)(2,1)}, bf16[2,80,320]{2,1,0:T(8,128)(2,1)S(1)}, u32[]{:S(2)}, u32[]{:S(2)}) collective-permute-start(bf16[2,80,320]{2,1,0:T(8,128)(2,1)} %dynamic-slice_bitcast_fusion), channel_id=1, source_target_pairs={{0,1},{1,2},{2,3},{3,0},{4,5},{5,6},{6,7},{7,4},{8,9},{9,10},{10,1... | collective-permute-start | bytes 307208 | tf_op jit(solution)/shard_map/ppermute | solution.py:273
  26.6 8.4 %collective-permute-start.12 = (bf16[256,320]{1,0:T(8,128)(2,1)S(1)}, bf16[256,320]{1,0:T(8,128)(2,1)S(1)}, u32[]{:S(2)}, u32[]{:S(2)}) collective-permute-start(bf16[256,320]{1,0:T(8,128)(2,1)S(1)} %collective-permute-done.11.refs_7_), channel_id=1, source_target_pairs={{0,4},{4,0},{8,12},{12,8},{1,5},{5,1},{9,13},{13,9},{2,6},{6,2},{1... | collective-permute-start | bytes 491528 | tf_op jit(solution)/shard_map/ppermute | solution.py:247
  26.6 5.1 %collective-permute-start.7 = (bf16[2,80,320]{2,1,0:T(8,128)(2,1)S(1)}, bf16[2,80,320]{2,1,0:T(8,128)(2,1)S(1)}, u32[]{:S(2)}, u32[]{:S(2)}) collective-permute-start(bf16[2,80,320]{2,1,0:T(8,128)(2,1)S(1)} %collective-permute-done.3.refs_3_), channel_id=1, source_target_pairs={{0,4},{4,0},{8,12},{12,8},{1,5},{5,1},{9,13},{13,9},{2,6},{6,2},{1... | collective-permute-start | bytes 307208 | tf_op jit(solution)/shard_map/ppermute | solution.py:297
  29.0 2.6 %collective-permute-start.6 = (bf16[2,80,320]{2,1,0:T(8,128)(2,1)S(1)}, bf16[2,80,320]{2,1,0:T(8,128)(2,1)S(1)}, u32[]{:S(2)}, u32[]{:S(2)}) collective-permute-start(bf16[2,80,320]{2,1,0:T(8,128)(2,1)S(1)} %collective-permute-done.4.refs_2_), channel_id=1, source_target_pairs={{0,4},{4,0},{8,12},{12,8},{1,5},{5,1},{9,13},{13,9},{2,6},{6,2},{1... | collective-permute-start | bytes 307208 | tf_op jit(solution)/shard_map/ppermute | solution.py:297
  29.1 6.0 %collective-permute-start.10 = (bf16[2,80,320]{2,1,0:T(8,128)(2,1)}, bf16[2,80,320]{2,1,0:T(8,128)(2,1)S(1)}, u32[]{:S(2)}, u32[]{:S(2)}) collective-permute-start(bf16[2,80,320]{2,1,0:T(8,128)(2,1)} %dynamic-slice_bitcast_fusion), channel_id=1, source_target_pairs={{1,0},{2,1},{3,2},{0,3},{5,4},{6,5},{7,6},{4,7},{9,8},{10,9},{11,1... | collective-permute-start | bytes 307208 | tf_op jit(solution)/shard_map/ppermute | solution.py:275
  31.1 8.2 %collective-permute-start.13 = (bf16[2,80,320]{2,1,0:T(8,128)(2,1)S(1)}, bf16[2,80,320]{2,1,0:T(8,128)(2,1)S(1)}, u32[]{:S(2)}, u32[]{:S(2)}) collective-permute-start(bf16[2,80,320]{2,1,0:T(8,128)(2,1)S(1)} %collective-permute-done.9.refs_1_), channel_id=1, source_target_pairs={{0,1},{1,2},{2,3},{3,0},{4,5},{5,6},{6,7},{7,4},{8,9},{9,10},{10,1... | collective-permute-start | bytes 307208 | tf_op jit(solution)/shard_map/ppermute | solution.py:273
  39.3 9.7 %collective-permute-start.17 = (bf16[256,320]{1,0:T(8,128)(2,1)S(1)}, bf16[256,320]{1,0:T(8,128)(2,1)S(1)}, u32[]{:S(2)}, u32[]{:S(2)}) collective-permute-start(bf16[256,320]{1,0:T(8,128)(2,1)S(1)} %get-tuple-element.56.rows), channel_id=1, source_target_pairs={{0,1},{1,2},{2,3},{3,0},{4,5},{5,6},{6,7},{7,4},{8,9},{9,10},{10,1... | collective-permute-start | bytes 491528 | tf_op jit(solution)/shard_map/ppermute | solution.py:273
  39.3 13.3 %collective-permute-start.19 = (bf16[256,320]{1,0:T(8,128)(2,1)S(1)}, bf16[256,320]{1,0:T(8,128)(2,1)S(1)}, u32[]{:S(2)}, u32[]{:S(2)}) collective-permute-start(bf16[256,320]{1,0:T(8,128)(2,1)S(1)} %get-tuple-element.56.rows), channel_id=1, source_target_pairs={{1,0},{2,1},{3,2},{0,3},{5,4},{6,5},{7,6},{4,7},{9,8},{10,9},{11,1... | collective-permute-start | bytes 491528 | tf_op jit(solution)/shard_map/ppermute | solution.py:275
  48.9 8.0 %collective-permute-start.18 = (bf16[256,320]{1,0:T(8,128)(2,1)S(1)}, bf16[256,320]{1,0:T(8,128)(2,1)S(1)}, u32[]{:S(2)}, u32[]{:S(2)}) collective-permute-start(bf16[256,320]{1,0:T(8,128)(2,1)S(1)} %collective-permute-done.17.rows), channel_id=1, source_target_pairs={{0,1},{1,2},{2,3},{3,0},{4,5},{5,6},{6,7},{7,4},{8,9},{9,10},{10,1... | collective-permute-start | bytes 491528 | tf_op jit(solution)/shard_map/ppermute | solution.py:273
  48.9 1.3 %collective-permute-start.14 = (bf16[2,80,320]{2,1,0:T(8,128)(2,1)S(1)}, bf16[2,80,320]{2,1,0:T(8,128)(2,1)S(1)}, u32[]{:S(2)}, u32[]{:S(2)}) collective-permute-start(bf16[2,80,320]{2,1,0:T(8,128)(2,1)S(1)} %collective-permute-done.9.refs_1_), channel_id=1, source_target_pairs={{0,4},{4,0},{8,12},{12,8},{1,5},{5,1},{9,13},{13,9},{2,6},{6,2},{1... | collective-permute-start | bytes 307208 | tf_op jit(solution)/shard_map/ppermute | solution.py:297
  48.9 1.5 %collective-permute-start.15 = (bf16[2,80,320]{2,1,0:T(8,128)(2,1)S(1)}, bf16[2,80,320]{2,1,0:T(8,128)(2,1)S(1)}, u32[]{:S(2)}, u32[]{:S(2)}) collective-permute-start(bf16[2,80,320]{2,1,0:T(8,128)(2,1)S(1)} %collective-permute-done.13.refs_2_), channel_id=1, source_target_pairs={{0,4},{4,0},{8,12},{12,8},{1,5},{5,1},{9,13},{13,9},{2,6},{6,2},{1... | collective-permute-start | bytes 307208 | tf_op jit(solution)/shard_map/ppermute | solution.py:297
  49.4 1.3 %collective-permute-start.16 = (bf16[2,80,320]{2,1,0:T(8,128)(2,1)S(1)}, bf16[2,80,320]{2,1,0:T(8,128)(2,1)S(1)}, u32[]{:S(2)}, u32[]{:S(2)}) collective-permute-start(bf16[2,80,320]{2,1,0:T(8,128)(2,1)S(1)} %collective-permute-done.10.refs_3_), channel_id=1, source_target_pairs={{0,4},{4,0},{8,12},{12,8},{1,5},{5,1},{9,13},{13,9},{2,6},{6,2},{1... | collective-permute-start | bytes 307208 | tf_op jit(solution)/shard_map/ppermute | solution.py:297
  (8 other events, 36.5 us)

commit v13 on v9

--- a/solution.py
+++ b/solution.py
@@ -135,19 +135,20 @@
 
 
 def assemble(where, side, parts, whole, rows, first):
-    for k, part in enumerate(parts[:-1]):
+    count = len(parts) // 2
+    for k in range(count):
         place = pl.ds(pl.multiple_of(where[k + 1] * rows, 16), rows)
         for j in range(2):
+            block = pl.ds((first + j) * rows, rows)
             mine = side * 2 + j
-            whole[mine, place, :] = part[pl.ds((first + j) * rows, rows), :]
-            start = (2 * k + j) * rows
-            whole[2 - mine + 2 * j, place, :] = parts[-1][pl.ds(start, rows), :]
+            whole[mine, place, :] = parts[k][block, :]
+            whole[2 - mine + 2 * j, place, :] = parts[count + k][block, :]
 
 
 def query_kernel(where, normed, three, one, *refs):
     parts, (queries, epi, sems) = refs[:-3], refs[-3:]
     copies = fetch_own(where, three, one, epi, sems)
-    assemble(where, where[max(1, len(parts))], parts, epi, one.shape[0], 0)
+    assemble(where, where[len(parts) // 2 + 1], parts, epi, one.shape[0], 0)
     for copy in copies:
         copy.wait()
     queries[...] = dot(normed[...], epi[0]).astype(bf16).astype(f32).T
@@ -176,31 +177,37 @@
 
             @pl.when(select[matching] == j)
             def _():
-                chosen[...] = maps[j][...]
-
-        other = chosen[...]
-        keys = dot(other, weights[1]).astype(bf16)
-        values = dot(other, weights[2]).T
-        shifts = []
-        for j in range(tiles):
-            row = jnp.zeros((1, tokens), f32)
-            for i in range(tiles):
-                bit = mask[(matching * tiles + i) * tiles + j]
-                row = jnp.where(lane_tile == i, jnp.where(bit > 0, 0.0, MASKED), row)
-            shifts.append(row)
-        for h in range(HEADS):
-            low, high, wanted = windows[h]
-            scores = dot(keys[:, low:high], wanted) * scale
+                chosen[pl.ds(matching * tokens, tokens), :] = maps[j][...]
+
+    keys = dot(chosen[...], weights[1]).astype(bf16)
+    values = dot(chosen[...], weights[2]).T
+    shifts = []
+    for block in range(2 * tiles):
+        matching, j = divmod(block, tiles)
+        row = jnp.zeros((1, tokens), f32)
+        for i in range(tiles):
+            bit = mask[(matching * tiles + i) * tiles + j]
+            row = jnp.where(lane_tile == i, jnp.where(bit > 0, 0.0, MASKED), row)
+        shifts.append(row)
+    for h in range(HEADS):
+        low, high, wanted = windows[h]
+        both = dot(keys[:, low:high], wanted)
+        total = None
+        for matching in range(2):
+            first = matching * tiles
             scores = jnp.concatenate(
-                [scores[j * width : (j + 1) * width] + shifts[j] for j in range(tiles)], axis=0
+                [
+                    both[k * width : (k + 1) * width] * scale + shifts[k]
+                    for k in range(first, first + tiles)
+                ],
+                axis=0,
             )
             powers = jnp.exp2(scores - jnp.max(scores, axis=0, keepdims=True))
             norm = 1.0 / jnp.sum(powers, axis=0, keepdims=True)
-            part = dot(values[h * head : (h + 1) * head].astype(bf16), powers.astype(bf16)) * norm
-            if matching == 0:
-                totals[pl.ds(h * head, head), :] = part
-            else:
-                totals[pl.ds(h * head, head), :] += part
+            rows = values[h * head : (h + 1) * head, matching * tokens : (matching + 1) * tokens]
+            part = dot(rows.astype(bf16), powers.astype(bf16)) * norm
+            total = part if total is None else total + part
+        totals[pl.ds(h * head, head), :] = total
     mixture = totals[...].T.astype(bf16)
     copy.wait()
     result = (hidden[...].astype(f32) + dot(mixture, weights[3])).astype(bf16)
@@ -214,16 +221,14 @@
     ones = block_diagonal(channels, head)
     keys = dot(rows, weights[1]).astype(bf16).astype(f32)
     values = dot(rows, weights[2]).astype(bf16)
-    products = queries * keys
-    high = products.astype(bf16)
-    low = (products - high.astype(f32)).astype(bf16)
-    return (dot(high, ones) + dot(low, ones)) * (LOG2E / math.sqrt(head)), values
+    products = (queries * keys).astype(bf16)
+    return dot(products, ones) * (LOG2E / math.sqrt(head)), values
 
 
 def own_frame_kernel(where, rows, three, one, *refs):
     parts, (weights, queries, scores, values, sems) = refs[:-5], refs[-5:]
     copies = fetch_own(where, three, one, weights, sems)
-    assemble(where, where[max(1, len(parts))], parts, weights, one.shape[0], 2)
+    assemble(where, where[len(parts) // 2 + 1], parts, weights, one.shape[0], 2)
     for copy in copies:
         copy.wait()
     queries[...] = dot(rows[...], weights[0]).astype(bf16)
@@ -315,9 +320,8 @@
     return lax.dynamic_index_in_dim(whole, side, 0, keepdims=False)
 
 
-def swap(pieces, first, rows, videos):
-    joined = jnp.concatenate([piece[first : first + rows] for piece in pieces], axis=0)
-    return lax.ppermute(joined, "video", partner_permutation(videos, 1))
+def swap(pieces, videos):
+    return [lax.ppermute(piece, "video", partner_permutation(videos, 1)) for piece in pieces]
 
 
 def per_device(
@@ -426,8 +430,7 @@
     epi_parts = temp_parts = []
     if paired:
         parts = parts[1:]
-        epi_parts = parts + [swap(parts, 0, 2 * height, videos)]
-        temp_parts = parts + [swap(parts, 2 * height, 2 * height, videos)]
+        epi_parts = temp_parts = parts + swap(parts, videos)
     targets = lax.dynamic_index_in_dim(matchings, video, 1, keepdims=False)
     if is_power(videos):
         select = video ^ targets
@@ -453,7 +456,7 @@
         in_specs=[SMEM, SMEM, HBM, VMEM, VMEM] + [VMEM] * videos,
         out_specs=[VMEM, VMEM],
         scratch_shapes=[
-            pltpu.VMEM((tokens, channels), bf16),
+            pltpu.VMEM((2 * tokens, channels), bf16),
             pltpu.VMEM((channels, tokens), f32),
             pltpu.VMEM((tokens, channels), bf16),
             pltpu.SemaphoreType.DMA,

time: 61.2 us -> 58.1 us (0.949)
  Pallas kernels: 19.6 us -> 17.2 us
  other arithmetic: 1.96 us -> 0.4 us
  waiting for transfers between devices: 20.8 us -> 22 us
    pallas_call x1, Pallas kernels: 6.45 us -> 4.6 us  [per_device(): pl.pallas_call(functools.partial(view_kernel, videos, tiles), out_shape=[...]
    concatenate x2 -> x0, other arithmetic: 1.56 us -> none  [swap(): jnp.concatenate([piece[first:first + rows] for piece in pieces], axis=0)]
    ppermute x4, starting transfers between devices: 4.79 us -> 4.03 us  [ring_gather(): pieces[step] = lax.ppermute(pieces[step - 1], axis, right)]
    ppermute x3, waiting for transfers between devices: 0.38 us -> 1.05 us  [gather_maps(): maps[k | bit] = lax.ppermute(sent, axis, partner_permutation(size, bit))]
  transfers between devices with their start and end apart: 13 -> 14, of which waited for: 8 -> 9; matrix products, arithmetic and copies ran while one was open for 4% -> 1% of each run, Pallas kernels for 27% -> 17%
where the time goes in v13:
time: 58.1 us; the launch traced here: 57.8 us
  waiting for transfers between devices  22 us (38%)
  Pallas kernels  17.2 us (30%)
  starting transfers between devices  16.8 us (29%)
  between operations  0.88 us (2%)
    ppermute x4, waiting for transfers between devices, ring_gather(): pieces[step] = lax.ppermute(pieces[step - 1], axis, right)  13.9 us
    ppermute x2, starting transfers between devices, sum_over(): value = value + lax.ppermute(value, axis, partner_permutation(size, bit))  6.12 us
    pallas_call x1, Pallas kernels, per_device(): pl.pallas_call(functools.partial(view_kernel, videos, tiles), out_shape=[...  4.6 us
    ppermute x2, waiting for transfers between devices, ring_gather(): lax.ppermute(pieces[(size - step + 1) % size], axis, left)  4.22 us
    ppermute x2, starting transfers between devices, ring_gather(): lax.ppermute(pieces[(size - step + 1) % size], axis, left)  4.17 us
    ppermute x4, starting transfers between devices, ring_gather(): pieces[step] = lax.ppermute(pieces[step - 1], axis, right)  4.03 us
    ppermute x2, waiting for transfers between devices, sum_over(): value = value + lax.ppermute(value, axis, partner_permutation(size, bit))  2.91 us
    pallas_call x1, Pallas kernels, per_device(): pl.pallas_call(first_kernel, out_shape=[jax.ShapeDtypeStruct((tokens, cha...  2.84 us
  transfers between devices with their start and end apart: 14, of which 9 were waited for; matrix products, arithmetic and copies ran while one was open for 1% of the time, Pallas kernels for 17%

profile of v13, /device:TPU:0, one launch (start us, length us, event | category | flops | bytes accessed | tf_op | source)
XLA Modules:
  0.0 57.8 jit_solution(17673347553406730703)
XLA Ops:
  0.8 1.2 %time_share.1 = f32[1,320]{1,0:T(1,128)S(1)} custom-call(bf16[1,320]{1,0:T(2,128)(2,1)S(1)} %fusion.4.act, bf16[320,320]{1,0:T(8,128)(2,1)} %proj_hbm.1), custom_call_target="tpu_custom_call" | custom-call | flops 10000000000 | bytes 1048576 | tf_op jit(solution)/shard_map/time_share/pallas_call | solution.py:360
  2.0 3.1 %collective-permute-start = (f32[1,320]{1,0:T(1,128)S(1)}, f32[1,320]{1,0:T(1,128)S(1)}, u32[]{:S(2)}, u32[]{:S(2)}) collective-permute-start(f32[1,320]{1,0:T(1,128)S(1)} %time_share.1), channel_id=1, source_target_pairs={{0,1},{1,0},{2,3},{3,2},{4,5},{5,4},{6,7},{7,6},{8,9},{9,8},{10,11... | collective-permute-start | bytes 3848 | tf_op jit(solution)/shard_map/ppermute | solution.py:295
  5.3 1.4 %collective-permute-done = f32[1,320]{1,0:T(1,128)S(1)} collective-permute-done((f32[1,320]{1,0:T(1,128)S(1)}, f32[1,320]{1,0:T(1,128)S(1)}, u32[]{:S(2)}, u32[]{:S(2)}) %collective-permute-start) | collective-permute-done | bytes 1312 | tf_op jit(solution)/shard_map/ppermute | solution.py:295
  6.6 3.0 %collective-permute-start.1 = (f32[1,320]{1,0:T(1,128)S(1)}, f32[1,320]{1,0:T(1,128)S(1)}, u32[]{:S(2)}, u32[]{:S(2)}) collective-permute-start(f32[1,320]{1,0:T(1,128)S(1)} %add.75), channel_id=1, source_target_pairs={{0,2},{1,3},{2,0},{3,1},{4,6},{5,7},{6,4},{7,5},{8,10},{9,11},{10,... | collective-permute-start | bytes 3848 | tf_op jit(solution)/shard_map/ppermute | solution.py:295
  9.7 1.5 %collective-permute-done.1 = f32[1,320]{1,0:T(1,128)S(1)} collective-permute-done((f32[1,320]{1,0:T(1,128)S(1)}, f32[1,320]{1,0:T(1,128)S(1)}, u32[]{:S(2)}, u32[]{:S(2)}) %collective-permute-start.1) | collective-permute-done | bytes 1312 | tf_op jit(solution)/shard_map/ppermute | solution.py:295
  11.2 1.9 %collective-permute-start.2 = (bf16[320,320]{1,0:T(8,128)(2,1)S(1)}, bf16[320,320]{1,0:T(8,128)(2,1)S(1)}, u32[]{:S(2)}, u32[]{:S(2)}) collective-permute-start(bf16[320,320]{1,0:T(8,128)(2,1)S(1)} %pad_maximum_fusion.2), channel_id=1, source_target_pairs={{0,1},{1,2},{2,3},{3,0},{4,5},{5,6},{6,7},{7,4},{8,9},{9,10},{10,1... | collective-permute-start | bytes 614408 | tf_op jit(solution)/shard_map/ppermute | solution.py:309
  13.2 2.0 %collective-permute-start.3 = (bf16[320,320]{1,0:T(8,128)(2,1)S(1)}, bf16[320,320]{1,0:T(8,128)(2,1)S(1)}, u32[]{:S(2)}, u32[]{:S(2)}) collective-permute-start(bf16[320,320]{1,0:T(8,128)(2,1)S(1)} %pad_maximum_fusion.2), channel_id=1, source_target_pairs={{1,0},{2,1},{3,2},{0,3},{5,4},{6,5},{7,6},{4,7},{9,8},{10,9},{11,1... | collective-permute-start | bytes 614408 | tf_op jit(solution)/shard_map/ppermute | solution.py:311
  15.2 2.8 %first_conv.1 = (f32[256,320]{1,0:T(8,128)S(1)}, bf16[256,320]{1,0:T(8,128)(2,1)S(1)}) custom-call(bf16[320,256]{1,0:T(8,128)(2,1)} %bitcast.28, bf16[3,960,320]{2,1,0:T(8,128)(2,1)} %bitcast.23), custom_call_target="tpu_custom_call" | custom-call | flops 471859200 | bytes 2498560 | tf_op jit(solution)/shard_map/first_conv/pallas_call | solution.py:389
  18.0 1.7 %second_conv.1 = (bf16[256,320]{1,0:T(8,128)(2,1)S(1)}, bf16[256,320]{1,0:T(8,128)(2,1)S(1)}) custom-call(bf16[256,320]{1,0:T(8,128)(2,1)S(1)} %get-tuple-element.25.source, f32[256,320]{1,0:T(8,128)S(1)} %get-tuple-element.26.inner, f32[1,320]{1,0:T(1,128)S(1)} %add.76.bias, bf16[3,960,320]{2,1,0:T(8,128)(2,1)S(1)} %bitcast.22), custom_call_target="tpu_custom_call" | custom-call | flops 471859200 | bytes 2498560 | tf_op jit(solution)/shard_map/second_conv/pallas_call | solution.py:407
  19.7 1.9 %collective-permute-done.2.refs_0_ = bf16[320,320]{1,0:T(8,128)(2,1)S(1)} collective-permute-done((bf16[320,320]{1,0:T(8,128)(2,1)S(1)}, bf16[320,320]{1,0:T(8,128)(2,1)S(1)}, u32[]{:S(2)}, u32[]{:S(2)}) %collective-permute-start.2) | collective-permute-done | bytes 204832 | tf_op jit(solution)/shard_map/ppermute | solution.py:309
  22.0 3.5 %collective-permute-done.3.refs_2_ = bf16[320,320]{1,0:T(8,128)(2,1)S(1)} collective-permute-done((bf16[320,320]{1,0:T(8,128)(2,1)S(1)}, bf16[320,320]{1,0:T(8,128)(2,1)S(1)}, u32[]{:S(2)}, u32[]{:S(2)}) %collective-permute-start.3) | collective-permute-done | bytes 204832 | tf_op jit(solution)/shard_map/ppermute | solution.py:311
  25.5 1.5 %collective-permute-start.9 = (bf16[256,320]{1,0:T(8,128)(2,1)S(1)}, bf16[256,320]{1,0:T(8,128)(2,1)S(1)}, u32[]{:S(2)}, u32[]{:S(2)}) collective-permute-start(bf16[256,320]{1,0:T(8,128)(2,1)S(1)} %get-tuple-element.31.normed.refs_5_), channel_id=1, source_target_pairs={{0,8},{4,12},{8,0},{12,4},{1,9},{5,13},{9,1},{13,5},{2,10},{6,14},... | collective-permute-start | bytes 491528 | tf_op jit(solution)/shard_map/ppermute | solution.py:282
  27.5 2.1 %collective-permute-done.4.refs_1_ = bf16[320,320]{1,0:T(8,128)(2,1)S(1)} collective-permute-done((bf16[320,320]{1,0:T(8,128)(2,1)S(1)}, bf16[320,320]{1,0:T(8,128)(2,1)S(1)}, u32[]{:S(2)}, u32[]{:S(2)}) %collective-permute-start.4) | collective-permute-done | bytes 204832 | tf_op jit(solution)/shard_map/ppermute | solution.py:309
  30.2 1.0 %collective-permute-done.9.refs_7_ = bf16[256,320]{1,0:T(8,128)(2,1)S(1)} collective-permute-done((bf16[256,320]{1,0:T(8,128)(2,1)S(1)}, bf16[256,320]{1,0:T(8,128)(2,1)S(1)}, u32[]{:S(2)}, u32[]{:S(2)}) %collective-permute-start.9) | collective-permute-done | bytes 163872 | tf_op jit(solution)/shard_map/ppermute | solution.py:282
  31.8 1.9 %query.1 = (f32[320,256]{1,0:T(8,128)S(1)}, bf16[4,320,320]{2,1,0:T(8,128)(2,1)S(1)}) custom-call(s32[5]{0:T(128)S(1)} %stack.23.where, bf16[256,320]{1,0:T(8,128)(2,1)S(1)} %get-tuple-element.31.normed.refs_5_, bf16[3,80,320]{2,1,0:T(8,128)(2,1)} %three.2, bf16[80,320]{1,0:T(8,128)(2,1)} %one.2, bf16[320,320]{1,0:T(8,128)(2,1)S(1)} %collective-permute-done.2.refs_0_, ...), custom_call_target="tpu_custom_call" | custom-call | tf_op jit(solution)/shard_map/query/pallas_call | solution.py:441
  33.7 4.6 %cross_view.1 = (bf16[256,320]{1,0:T(8,128)(2,1)S(1)}, bf16[256,320]{1,0:T(8,128)(2,1)S(1)}) custom-call(s32[2]{0:T(128)S(1)} %xor_reduce_fusion.refs_0_, s32[8]{0:T(128)S(1)} %reshape.93.refs_1_, bf16[256,320]{1,0:T(8,128)(2,1)S(1)} %get-tuple-element.27.refs_2_, f32[320,256]{1,0:T(8,128)S(1)} %get-tuple-element.32.refs_3_, ...), custom_call_target="tpu_custom_call" | custom-call | tf_op jit(solution)/shard_map/cross_view/pallas_call | solution.py:453
  38.3 1.7 %collective-permute-start.11 = (bf16[256,320]{1,0:T(8,128)(2,1)S(1)}, bf16[256,320]{1,0:T(8,128)(2,1)S(1)}, u32[]{:S(2)}, u32[]{:S(2)}) collective-permute-start(bf16[256,320]{1,0:T(8,128)(2,1)S(1)} %get-tuple-element.36.rows), channel_id=1, source_target_pairs={{0,1},{1,2},{2,3},{3,0},{4,5},{5,6},{6,7},{7,4},{8,9},{9,10},{10,1... | collective-permute-start | bytes 491528 | tf_op jit(solution)/shard_map/ppermute | solution.py:309
  40.1 2.1 %collective-permute-start.13 = (bf16[256,320]{1,0:T(8,128)(2,1)S(1)}, bf16[256,320]{1,0:T(8,128)(2,1)S(1)}, u32[]{:S(2)}, u32[]{:S(2)}) collective-permute-start(bf16[256,320]{1,0:T(8,128)(2,1)S(1)} %get-tuple-element.36.rows), channel_id=1, source_target_pairs={{1,0},{2,1},{3,2},{0,3},{5,4},{6,5},{7,6},{4,7},{9,8},{10,9},{11,1... | collective-permute-start | bytes 491528 | tf_op jit(solution)/shard_map/ppermute | solution.py:311
  42.2 5.7 %collective-permute-done.11.rows = bf16[256,320]{1,0:T(8,128)(2,1)S(1)} collective-permute-done((bf16[256,320]{1,0:T(8,128)(2,1)S(1)}, bf16[256,320]{1,0:T(8,128)(2,1)S(1)}, u32[]{:S(2)}, u32[]{:S(2)}) %collective-permute-start.11) | collective-permute-done | bytes 163872 | tf_op jit(solution)/shard_map/ppermute | solution.py:309
  47.9 2.1 %own_frame.1 = (bf16[4,320,320]{2,1,0:T(8,128)(2,1)S(1)}, bf16[256,320]{1,0:T(8,128)(2,1)S(1)}, f32[256,320]{1,0:T(8,128)S(1)}, bf16[256,320]{1,0:T(8,128)(2,1)S(1)}) custom-call(s32[5]{0:T(128)S(1)} %stack.23.where, bf16[256,320]{1,0:T(8,128)(2,1)S(1)} %get-tuple-element.36.rows, bf16[3,80,320]{2,1,0:T(8,128)(2,1)} %three.3, bf16[80,320]{1,0:T(8,128)(2,1)} %one.3, ...), custom_call_target="tpu_custom_call" | custom-call | flops 209715200 | bytes 1474560 | tf_op jit(solution)/shard_map/own_frame/pallas_call | solution.py:476
  50.1 0.5 other_frame.2
  50.6 0.7 %collective-permute-done.13.rows = bf16[256,320]{1,0:T(8,128)(2,1)S(1)} collective-permute-done((bf16[256,320]{1,0:T(8,128)(2,1)S(1)}, bf16[256,320]{1,0:T(8,128)(2,1)S(1)}, u32[]{:S(2)}, u32[]{:S(2)}) %collective-permute-start.13) | collective-permute-done | bytes 163872 | tf_op jit(solution)/shard_map/ppermute | solution.py:311
  51.8 4.1 %collective-permute-done.12.refs_2_ = bf16[256,320]{1,0:T(8,128)(2,1)S(1)} collective-permute-done((bf16[256,320]{1,0:T(8,128)(2,1)S(1)}, bf16[256,320]{1,0:T(8,128)(2,1)S(1)}, u32[]{:S(2)}, u32[]{:S(2)}) %collective-permute-start.12) | collective-permute-done | bytes 163872 | tf_op jit(solution)/shard_map/ppermute | solution.py:309
  56.0 1.8 %last.1 = bf16[320,256]{1,0:T(8,128)(2,1)} custom-call(bf16[256,320]{1,0:T(8,128)(2,1)S(1)} %get-tuple-element.35.refs_0_, bf16[256,320]{1,0:T(8,128)(2,1)S(1)} %get-tuple-element.37.queries.refs_1_, bf16[256,320]{1,0:T(8,128)(2,1)S(1)} %collective-permute-done.12.refs_2_, bf16[4,320,320]{2,1,0:T(8,128)(2,1)S(1)} %get-tuple-element.38.weights.refs_3_, ...), custom_call_target="tpu_custom_call" | custom-call | tf_op jit(solution)/shard_map/last/pallas_call | solution.py:500
  (38 shorter events, 2.8 us)
Async XLA Ops:
  0.0 31.2 %copy-start = (s32[2,4,2,2]{1,3,2,0:T(2,128)S(1)}, s32[2,4,2,2]{1,3,2,0:T(2,128)}, u32[]{:S(2)}) copy-start(s32[2,4,2,2]{1,3,2,0:T(2,128)} %param.14) | copy-start | bytes 388
  0.8 4.3 %copy-start.2 = (bf16[3,80,320]{2,1,0:T(8,128)(2,1)S(1)}, bf16[3,80,320]{2,1,0:T(8,128)(2,1)}, u32[]{:S(2)}) copy-start(bf16[3,80,320]{2,1,0:T(8,128)(2,1)} %three.2) | copy-start | bytes 460804
  0.8 4.3 %copy-start.4 = (bf16[80,320]{1,0:T(8,128)(2,1)S(1)}, bf16[80,320]{1,0:T(8,128)(2,1)}, u32[]{:S(2)}) copy-start(bf16[80,320]{1,0:T(8,128)(2,1)} %one.2) | copy-start | bytes 153604
  0.8 4.4 %copy-start.3 = (bf16[3,80,320]{2,1,0:T(8,128)(2,1)S(1)}, bf16[3,80,320]{2,1,0:T(8,128)(2,1)}, u32[]{:S(2)}) copy-start(bf16[3,80,320]{2,1,0:T(8,128)(2,1)} %three.3) | copy-start | bytes 460804
  0.8 4.4 %copy-start.5 = (bf16[80,320]{1,0:T(8,128)(2,1)S(1)}, bf16[80,320]{1,0:T(8,128)(2,1)}, u32[]{:S(2)}) copy-start(bf16[80,320]{1,0:T(8,128)(2,1)} %one.3) | copy-start | bytes 153604
  2.0 16.0 %copy-start.1 = (bf16[3,3,320,320]{3,2,1,0:T(8,128)(2,1)S(1)}, bf16[3,3,320,320]{3,2,1,0:T(8,128)(2,1)}, u32[]{:S(2)}) copy-start(bf16[3,3,320,320]{3,2,1,0:T(8,128)(2,1)} %param.16) | copy-start | bytes 5529604
  2.0 4.6 %collective-permute-start = (f32[1,320]{1,0:T(1,128)S(1)}, f32[1,320]{1,0:T(1,128)S(1)}, u32[]{:S(2)}, u32[]{:S(2)}) collective-permute-start(f32[1,320]{1,0:T(1,128)S(1)} %time_share.1), channel_id=1, source_target_pairs={{0,1},{1,0},{2,3},{3,2},{4,5},{5,4},{6,7},{7,6},{8,9},{9,8},{10,11... | collective-permute-start | bytes 3848 | tf_op jit(solution)/shard_map/ppermute | solution.py:295
  6.6 4.6 %collective-permute-start.1 = (f32[1,320]{1,0:T(1,128)S(1)}, f32[1,320]{1,0:T(1,128)S(1)}, u32[]{:S(2)}, u32[]{:S(2)}) collective-permute-start(f32[1,320]{1,0:T(1,128)S(1)} %add.75), channel_id=1, source_target_pairs={{0,2},{1,3},{2,0},{3,1},{4,6},{5,7},{6,4},{7,5},{8,10},{9,11},{10,... | collective-permute-start | bytes 3848 | tf_op jit(solution)/shard_map/ppermute | solution.py:295
  11.2 10.4 %collective-permute-start.2 = (bf16[320,320]{1,0:T(8,128)(2,1)S(1)}, bf16[320,320]{1,0:T(8,128)(2,1)S(1)}, u32[]{:S(2)}, u32[]{:S(2)}) collective-permute-start(bf16[320,320]{1,0:T(8,128)(2,1)S(1)} %pad_maximum_fusion.2), channel_id=1, source_target_pairs={{0,1},{1,2},{2,3},{3,0},{4,5},{5,6},{6,7},{7,4},{8,9},{9,10},{10,1... | collective-permute-start | bytes 614408 | tf_op jit(solution)/shard_map/ppermute | solution.py:309
  13.2 12.4 %collective-permute-start.3 = (bf16[320,320]{1,0:T(8,128)(2,1)S(1)}, bf16[320,320]{1,0:T(8,128)(2,1)S(1)}, u32[]{:S(2)}, u32[]{:S(2)}) collective-permute-start(bf16[320,320]{1,0:T(8,128)(2,1)S(1)} %pad_maximum_fusion.2), channel_id=1, source_target_pairs={{1,0},{2,1},{3,2},{0,3},{5,4},{6,5},{7,6},{4,7},{9,8},{10,9},{11,1... | collective-permute-start | bytes 614408 | tf_op jit(solution)/shard_map/ppermute | solution.py:311
  15.2 16.4 %copy-start.6 = (s32[2,4]{1,0:T(2,128)S(1)}, s32[2,4]{1,0:T(2,128)}, u32[]{:S(2)}) copy-start(s32[2,4]{1,0:T(2,128)} %param.13) | copy-start | bytes 100
  21.7 8.0 %collective-permute-start.4 = (bf16[320,320]{1,0:T(8,128)(2,1)S(1)}, bf16[320,320]{1,0:T(8,128)(2,1)S(1)}, u32[]{:S(2)}, u32[]{:S(2)}) collective-permute-start(bf16[320,320]{1,0:T(8,128)(2,1)S(1)} %collective-permute-done.2.refs_0_), channel_id=1, source_target_pairs={{0,1},{1,2},{2,3},{3,0},{4,5},{5,6},{6,7},{7,4},{8,9},{9,10},{10,1... | collective-permute-start | bytes 614408 | tf_op jit(solution)/shard_map/ppermute | solution.py:309
  25.5 5.7 %collective-permute-start.9 = (bf16[256,320]{1,0:T(8,128)(2,1)S(1)}, bf16[256,320]{1,0:T(8,128)(2,1)S(1)}, u32[]{:S(2)}, u32[]{:S(2)}) collective-permute-start(bf16[256,320]{1,0:T(8,128)(2,1)S(1)} %get-tuple-element.31.normed.refs_5_), channel_id=1, source_target_pairs={{0,8},{4,12},{8,0},{12,4},{1,9},{5,13},{9,1},{13,5},{2,10},{6,14},... | collective-permute-start | bytes 491528 | tf_op jit(solution)/shard_map/ppermute | solution.py:282
  27.0 4.8 %collective-permute-start.5 = (bf16[320,320]{1,0:T(8,128)(2,1)S(1)}, bf16[320,320]{1,0:T(8,128)(2,1)S(1)}, u32[]{:S(2)}, u32[]{:S(2)}) collective-permute-start(bf16[320,320]{1,0:T(8,128)(2,1)S(1)} %collective-permute-done.2.refs_0_), channel_id=1, source_target_pairs={{0,4},{4,0},{8,12},{12,8},{1,5},{5,1},{9,13},{13,9},{2,6},{6,2},{1... | collective-permute-start | bytes 614408 | tf_op jit(solution)/shard_map/ppermute | solution.py:324
  27.0 4.8 %collective-permute-start.7 = (bf16[320,320]{1,0:T(8,128)(2,1)S(1)}, bf16[320,320]{1,0:T(8,128)(2,1)S(1)}, u32[]{:S(2)}, u32[]{:S(2)}) collective-permute-start(bf16[320,320]{1,0:T(8,128)(2,1)S(1)} %collective-permute-done.3.refs_2_), channel_id=1, source_target_pairs={{0,4},{4,0},{8,12},{12,8},{1,5},{5,1},{9,13},{13,9},{2,6},{6,2},{1... | collective-permute-start | bytes 614408 | tf_op jit(solution)/shard_map/ppermute | solution.py:324
  29.7 2.2 %collective-permute-start.6 = (bf16[320,320]{1,0:T(8,128)(2,1)S(1)}, bf16[320,320]{1,0:T(8,128)(2,1)S(1)}, u32[]{:S(2)}, u32[]{:S(2)}) collective-permute-start(bf16[320,320]{1,0:T(8,128)(2,1)S(1)} %collective-permute-done.4.refs_1_), channel_id=1, source_target_pairs={{0,4},{4,0},{8,12},{12,8},{1,5},{5,1},{9,13},{13,9},{2,6},{6,2},{1... | collective-permute-start | bytes 614408 | tf_op jit(solution)/shard_map/ppermute | solution.py:324
  29.7 4.0 %collective-permute-start.8 = (bf16[256,320]{1,0:T(8,128)(2,1)S(1)}, bf16[256,320]{1,0:T(8,128)(2,1)S(1)}, u32[]{:S(2)}, u32[]{:S(2)}) collective-permute-start(bf16[256,320]{1,0:T(8,128)(2,1)S(1)} %get-tuple-element.31.normed.refs_5_), channel_id=1, source_target_pairs={{0,4},{4,0},{8,12},{12,8},{1,5},{5,1},{9,13},{13,9},{2,6},{6,2},{1... | collective-permute-start | bytes 491528 | tf_op jit(solution)/shard_map/ppermute | solution.py:282
  31.2 2.5 %collective-permute-start.10 = (bf16[256,320]{1,0:T(8,128)(2,1)S(1)}, bf16[256,320]{1,0:T(8,128)(2,1)S(1)}, u32[]{:S(2)}, u32[]{:S(2)}) collective-permute-start(bf16[256,320]{1,0:T(8,128)(2,1)S(1)} %collective-permute-done.9.refs_7_), channel_id=1, source_target_pairs={{0,4},{4,0},{8,12},{12,8},{1,5},{5,1},{9,13},{13,9},{2,6},{6,2},{1... | collective-permute-start | bytes 491528 | tf_op jit(solution)/shard_map/ppermute | solution.py:282
  38.3 9.6 %collective-permute-start.11 = (bf16[256,320]{1,0:T(8,128)(2,1)S(1)}, bf16[256,320]{1,0:T(8,128)(2,1)S(1)}, u32[]{:S(2)}, u32[]{:S(2)}) collective-permute-start(bf16[256,320]{1,0:T(8,128)(2,1)S(1)} %get-tuple-element.36.rows), channel_id=1, source_target_pairs={{0,1},{1,2},{2,3},{3,0},{4,5},{5,6},{6,7},{7,4},{8,9},{9,10},{10,1... | collective-permute-start | bytes 491528 | tf_op jit(solution)/shard_map/ppermute | solution.py:309
  40.1 11.3 %collective-permute-start.13 = (bf16[256,320]{1,0:T(8,128)(2,1)S(1)}, bf16[256,320]{1,0:T(8,128)(2,1)S(1)}, u32[]{:S(2)}, u32[]{:S(2)}) collective-permute-start(bf16[256,320]{1,0:T(8,128)(2,1)S(1)} %get-tuple-element.36.rows), channel_id=1, source_target_pairs={{1,0},{2,1},{3,2},{0,3},{5,4},{6,5},{7,6},{4,7},{9,8},{10,9},{11,1... | collective-permute-start | bytes 491528 | tf_op jit(solution)/shard_map/ppermute | solution.py:311
  47.9 8.0 %collective-permute-start.12 = (bf16[256,320]{1,0:T(8,128)(2,1)S(1)}, bf16[256,320]{1,0:T(8,128)(2,1)S(1)}, u32[]{:S(2)}, u32[]{:S(2)}) collective-permute-start(bf16[256,320]{1,0:T(8,128)(2,1)S(1)} %collective-permute-done.11.rows), channel_id=1, source_target_pairs={{0,1},{1,2},{2,3},{3,0},{4,5},{5,6},{6,7},{7,4},{8,9},{9,10},{10,1... | collective-permute-start | bytes 491528 | tf_op jit(solution)/shard_map/ppermute | solution.py:309

commit v14 on v13

--- a/solution.py
+++ b/solution.py
@@ -424,7 +424,7 @@
             [half_of(epi_in, epi_out, video % 2), half_of(temp_in, temp_out, video % 2)], axis=0
         )
         parts = ring_gather(after(mine, bias), "frame", frames, normed)
-        normed = after(normed, parts[1 % frames], parts[-1])
+        normed = after(normed, parts[1 % frames])
         last_part = parts[frames // 2]
     maps = gather_maps(normed, "video", videos, last_part)
     epi_parts = temp_parts = []

time: 58.1 us -> 57.3 us (0.986)
  waiting for transfers between devices: 22 us -> 21.1 us
    ppermute x2, starting transfers between devices: 4.17 us -> 5.86 us  [ring_gather(): lax.ppermute(pieces[(size - step + 1) % size], axis, left)]
    ppermute x2, waiting for transfers between devices: 4.22 us -> 2.7 us  [ring_gather(): lax.ppermute(pieces[(size - step + 1) % size], axis, left)]
    ppermute x4, waiting for transfers between devices: 13.9 us -> 15.1 us  [ring_gather(): pieces[step] = lax.ppermute(pieces[step - 1], axis, right)]
    ppermute x3, waiting for transfers between devices: 1.05 us -> 0.01 us  [gather_maps(): maps[k | bit] = lax.ppermute(sent, axis, partner_permutation(size, bit))]
    ppermute x4, starting transfers between devices: 4.03 us -> 3.22 us  [ring_gather(): pieces[step] = lax.ppermute(pieces[step - 1], axis, right)]
  transfers between devices with their start and end apart: 14 -> 14, of which waited for: 9 -> 8; matrix products, arithmetic and copies ran while one was open for 1% -> 1% of each run, Pallas kernels for 17% -> 17%
where the time goes in v14:
time: 57.3 us; the launch traced here: 57 us
  waiting for transfers between devices  21.1 us (37%)
  Pallas kernels  17.2 us (30%)
  starting transfers between devices  17 us (30%)
  between operations  0.87 us (2%)
    ppermute x4, waiting for transfers between devices, ring_gather(): pieces[step] = lax.ppermute(pieces[step - 1], axis, right)  15.1 us
    ppermute x2, starting transfers between devices, sum_over(): value = value + lax.ppermute(value, axis, partner_permutation(size, bit))  6.12 us
    ppermute x2, starting transfers between devices, ring_gather(): lax.ppermute(pieces[(size - step + 1) % size], axis, left)  5.86 us
    pallas_call x1, Pallas kernels, per_device(): pl.pallas_call(functools.partial(view_kernel, videos, tiles), out_shape=[...  4.6 us
    ppermute x4, starting transfers between devices, ring_gather(): pieces[step] = lax.ppermute(pieces[step - 1], axis, right)  3.22 us
    ppermute x2, waiting for transfers between devices, sum_over(): value = value + lax.ppermute(value, axis, partner_permutation(size, bit))  2.91 us
    pallas_call x1, Pallas kernels, per_device(): pl.pallas_call(first_kernel, out_shape=[jax.ShapeDtypeStruct((tokens, cha...  2.83 us
    ppermute x2, waiting for transfers between devices, ring_gather(): lax.ppermute(pieces[(size - step + 1) % size], axis, left)  2.7 us
  transfers between devices with their start and end apart: 14, of which 8 were waited for; matrix products, arithmetic and copies ran while one was open for 1% of the time, Pallas kernels for 17%

profile of v14, /device:TPU:0, one launch (start us, length us, event | category | flops | bytes accessed | tf_op | source)
XLA Modules:
  0.0 57.0 jit_solution(9551955980856713536)
XLA Ops:
  0.8 1.2 %time_share.1 = f32[1,320]{1,0:T(1,128)S(1)} custom-call(bf16[1,320]{1,0:T(2,128)(2,1)S(1)} %fusion.4.act, bf16[320,320]{1,0:T(8,128)(2,1)} %proj_hbm.1), custom_call_target="tpu_custom_call" | custom-call | flops 10000000000 | bytes 1048576 | tf_op jit(solution)/shard_map/time_share/pallas_call | solution.py:360
  2.0 3.1 %collective-permute-start = (f32[1,320]{1,0:T(1,128)S(1)}, f32[1,320]{1,0:T(1,128)S(1)}, u32[]{:S(2)}, u32[]{:S(2)}) collective-permute-start(f32[1,320]{1,0:T(1,128)S(1)} %time_share.1), channel_id=1, source_target_pairs={{0,1},{1,0},{2,3},{3,2},{4,5},{5,4},{6,7},{7,6},{8,9},{9,8},{10,11... | collective-permute-start | bytes 3848 | tf_op jit(solution)/shard_map/ppermute | solution.py:295
  5.3 1.4 %collective-permute-done = f32[1,320]{1,0:T(1,128)S(1)} collective-permute-done((f32[1,320]{1,0:T(1,128)S(1)}, f32[1,320]{1,0:T(1,128)S(1)}, u32[]{:S(2)}, u32[]{:S(2)}) %collective-permute-start) | collective-permute-done | bytes 1312 | tf_op jit(solution)/shard_map/ppermute | solution.py:295
  6.6 3.0 %collective-permute-start.1 = (f32[1,320]{1,0:T(1,128)S(1)}, f32[1,320]{1,0:T(1,128)S(1)}, u32[]{:S(2)}, u32[]{:S(2)}) collective-permute-start(f32[1,320]{1,0:T(1,128)S(1)} %add.75), channel_id=1, source_target_pairs={{0,2},{1,3},{2,0},{3,1},{4,6},{5,7},{6,4},{7,5},{8,10},{9,11},{10,... | collective-permute-start | bytes 3848 | tf_op jit(solution)/shard_map/ppermute | solution.py:295
  9.7 1.5 %collective-permute-done.1 = f32[1,320]{1,0:T(1,128)S(1)} collective-permute-done((f32[1,320]{1,0:T(1,128)S(1)}, f32[1,320]{1,0:T(1,128)S(1)}, u32[]{:S(2)}, u32[]{:S(2)}) %collective-permute-start.1) | collective-permute-done | bytes 1312 | tf_op jit(solution)/shard_map/ppermute | solution.py:295
  11.2 1.9 %collective-permute-start.2 = (bf16[320,320]{1,0:T(8,128)(2,1)S(1)}, bf16[320,320]{1,0:T(8,128)(2,1)S(1)}, u32[]{:S(2)}, u32[]{:S(2)}) collective-permute-start(bf16[320,320]{1,0:T(8,128)(2,1)S(1)} %pad_maximum_fusion.2), channel_id=1, source_target_pairs={{0,1},{1,2},{2,3},{3,0},{4,5},{5,6},{6,7},{7,4},{8,9},{9,10},{10,1... | collective-permute-start | bytes 614408 | tf_op jit(solution)/shard_map/ppermute | solution.py:309
  13.2 2.8 %first_conv.1 = (f32[256,320]{1,0:T(8,128)S(1)}, bf16[256,320]{1,0:T(8,128)(2,1)S(1)}) custom-call(bf16[320,256]{1,0:T(8,128)(2,1)} %bitcast.28, bf16[3,960,320]{2,1,0:T(8,128)(2,1)} %bitcast.23), custom_call_target="tpu_custom_call" | custom-call | flops 471859200 | bytes 2498560 | tf_op jit(solution)/shard_map/first_conv/pallas_call | solution.py:389
  16.0 2.1 %collective-permute-start.4 = (bf16[320,320]{1,0:T(8,128)(2,1)S(1)}, bf16[320,320]{1,0:T(8,128)(2,1)S(1)}, u32[]{:S(2)}, u32[]{:S(2)}) collective-permute-start(bf16[320,320]{1,0:T(8,128)(2,1)S(1)} %pad_maximum_fusion.2), channel_id=1, source_target_pairs={{1,0},{2,1},{3,2},{0,3},{5,4},{6,5},{7,6},{4,7},{9,8},{10,9},{11,1... | collective-permute-start | bytes 614408 | tf_op jit(solution)/shard_map/ppermute | solution.py:311
  18.1 1.7 %second_conv.1 = (bf16[256,320]{1,0:T(8,128)(2,1)S(1)}, bf16[256,320]{1,0:T(8,128)(2,1)S(1)}) custom-call(bf16[256,320]{1,0:T(8,128)(2,1)S(1)} %get-tuple-element.25.source, f32[256,320]{1,0:T(8,128)S(1)} %get-tuple-element.26.inner, f32[1,320]{1,0:T(1,128)S(1)} %add.76.bias, bf16[3,960,320]{2,1,0:T(8,128)(2,1)S(1)} %bitcast.22), custom_call_target="tpu_custom_call" | custom-call | flops 471859200 | bytes 2498560 | tf_op jit(solution)/shard_map/second_conv/pallas_call | solution.py:407
  19.8 1.0 %collective-permute-done.2.refs_0_ = bf16[320,320]{1,0:T(8,128)(2,1)S(1)} collective-permute-done((bf16[320,320]{1,0:T(8,128)(2,1)S(1)}, bf16[320,320]{1,0:T(8,128)(2,1)S(1)}, u32[]{:S(2)}, u32[]{:S(2)}) %collective-permute-start.2) | collective-permute-done | bytes 204832 | tf_op jit(solution)/shard_map/ppermute | solution.py:309
  20.8 1.2 %collective-permute-start.3 = (bf16[320,320]{1,0:T(8,128)(2,1)S(1)}, bf16[320,320]{1,0:T(8,128)(2,1)S(1)}, u32[]{:S(2)}, u32[]{:S(2)}) collective-permute-start(bf16[320,320]{1,0:T(8,128)(2,1)S(1)} %collective-permute-done.2.refs_0_), channel_id=1, source_target_pairs={{0,1},{1,2},{2,3},{3,0},{4,5},{5,6},{6,7},{7,4},{8,9},{9,10},{10,1... | collective-permute-start | bytes 614408 | tf_op jit(solution)/shard_map/ppermute | solution.py:309
  22.0 1.3 %collective-permute-start.9 = (bf16[256,320]{1,0:T(8,128)(2,1)S(1)}, bf16[256,320]{1,0:T(8,128)(2,1)S(1)}, u32[]{:S(2)}, u32[]{:S(2)}) collective-permute-start(bf16[256,320]{1,0:T(8,128)(2,1)S(1)} %get-tuple-element.31.normed.refs_5_), channel_id=1, source_target_pairs={{0,8},{4,12},{8,0},{12,4},{1,9},{5,13},{9,1},{13,5},{2,10},{6,14},... | collective-permute-start | bytes 491528 | tf_op jit(solution)/shard_map/ppermute | solution.py:282
  23.2 2.7 %collective-permute-done.4.refs_2_ = bf16[320,320]{1,0:T(8,128)(2,1)S(1)} collective-permute-done((bf16[320,320]{1,0:T(8,128)(2,1)S(1)}, bf16[320,320]{1,0:T(8,128)(2,1)S(1)}, u32[]{:S(2)}, u32[]{:S(2)}) %collective-permute-start.4) | collective-permute-done | bytes 204832 | tf_op jit(solution)/shard_map/ppermute | solution.py:311
  25.9 4.0 %collective-permute-done.3.refs_1_ = bf16[320,320]{1,0:T(8,128)(2,1)S(1)} collective-permute-done((bf16[320,320]{1,0:T(8,128)(2,1)S(1)}, bf16[320,320]{1,0:T(8,128)(2,1)S(1)}, u32[]{:S(2)}, u32[]{:S(2)}) %collective-permute-start.3) | collective-permute-done | bytes 204832 | tf_op jit(solution)/shard_map/ppermute | solution.py:309
  29.9 0.5 collective-permute-start.8
  31.4 1.9 %query.1 = (f32[320,256]{1,0:T(8,128)S(1)}, bf16[4,320,320]{2,1,0:T(8,128)(2,1)S(1)}) custom-call(s32[5]{0:T(128)S(1)} %stack.23.where, bf16[256,320]{1,0:T(8,128)(2,1)S(1)} %get-tuple-element.31.normed.refs_5_, bf16[3,80,320]{2,1,0:T(8,128)(2,1)} %three.2, bf16[80,320]{1,0:T(8,128)(2,1)} %one.2, bf16[320,320]{1,0:T(8,128)(2,1)S(1)} %collective-permute-done.2.refs_0_, ...), custom_call_target="tpu_custom_call" | custom-call | tf_op jit(solution)/shard_map/query/pallas_call | solution.py:441
  33.3 4.6 %cross_view.1 = (bf16[256,320]{1,0:T(8,128)(2,1)S(1)}, bf16[256,320]{1,0:T(8,128)(2,1)S(1)}) custom-call(s32[2]{0:T(128)S(1)} %xor_reduce_fusion.refs_0_, s32[8]{0:T(128)S(1)} %reshape.93.refs_1_, bf16[256,320]{1,0:T(8,128)(2,1)S(1)} %get-tuple-element.27.refs_2_, f32[320,256]{1,0:T(8,128)S(1)} %get-tuple-element.32.refs_3_, ...), custom_call_target="tpu_custom_call" | custom-call | tf_op jit(solution)/shard_map/cross_view/pallas_call | solution.py:453
  38.0 3.8 %collective-permute-start.13 = (bf16[256,320]{1,0:T(8,128)(2,1)S(1)}, bf16[256,320]{1,0:T(8,128)(2,1)S(1)}, u32[]{:S(2)}, u32[]{:S(2)}) collective-permute-start(bf16[256,320]{1,0:T(8,128)(2,1)S(1)} %get-tuple-element.36.rows), channel_id=1, source_target_pairs={{1,0},{2,1},{3,2},{0,3},{5,4},{6,5},{7,6},{4,7},{9,8},{10,9},{11,1... | collective-permute-start | bytes 491528 | tf_op jit(solution)/shard_map/ppermute | solution.py:311
  41.8 5.8 %collective-permute-done.11.rows = bf16[256,320]{1,0:T(8,128)(2,1)S(1)} collective-permute-done((bf16[256,320]{1,0:T(8,128)(2,1)S(1)}, bf16[256,320]{1,0:T(8,128)(2,1)S(1)}, u32[]{:S(2)}, u32[]{:S(2)}) %collective-permute-start.11) | collective-permute-done | bytes 163872 | tf_op jit(solution)/shard_map/ppermute | solution.py:309
  47.5 2.1 %own_frame.1 = (bf16[4,320,320]{2,1,0:T(8,128)(2,1)S(1)}, bf16[256,320]{1,0:T(8,128)(2,1)S(1)}, f32[256,320]{1,0:T(8,128)S(1)}, bf16[256,320]{1,0:T(8,128)(2,1)S(1)}) custom-call(s32[5]{0:T(128)S(1)} %stack.23.where, bf16[256,320]{1,0:T(8,128)(2,1)S(1)} %get-tuple-element.36.rows, bf16[3,80,320]{2,1,0:T(8,128)(2,1)} %three.3, bf16[80,320]{1,0:T(8,128)(2,1)} %one.3, ...), custom_call_target="tpu_custom_call" | custom-call | flops 209715200 | bytes 1474560 | tf_op jit(solution)/shard_map/own_frame/pallas_call | solution.py:476
  49.7 0.5 other_frame.2
  50.2 0.5 other_frame.3
  50.8 4.4 %collective-permute-done.12.refs_2_ = bf16[256,320]{1,0:T(8,128)(2,1)S(1)} collective-permute-done((bf16[256,320]{1,0:T(8,128)(2,1)S(1)}, bf16[256,320]{1,0:T(8,128)(2,1)S(1)}, u32[]{:S(2)}, u32[]{:S(2)}) %collective-permute-start.12) | collective-permute-done | bytes 163872 | tf_op jit(solution)/shard_map/ppermute | solution.py:309
  55.2 1.8 %last.1 = bf16[320,256]{1,0:T(8,128)(2,1)} custom-call(bf16[256,320]{1,0:T(8,128)(2,1)S(1)} %get-tuple-element.35.refs_0_, bf16[256,320]{1,0:T(8,128)(2,1)S(1)} %get-tuple-element.37.queries.refs_1_, bf16[256,320]{1,0:T(8,128)(2,1)S(1)} %collective-permute-done.12.refs_2_, bf16[4,320,320]{2,1,0:T(8,128)(2,1)S(1)} %get-tuple-element.38.weights.refs_3_, ...), custom_call_target="tpu_custom_call" | custom-call | tf_op jit(solution)/shard_map/last/pallas_call | solution.py:500
  (38 shorter events, 1.4 us)
Async XLA Ops:
  0.0 30.4 %copy-start = (s32[2,4,2,2]{1,3,2,0:T(2,128)S(1)}, s32[2,4,2,2]{1,3,2,0:T(2,128)}, u32[]{:S(2)}) copy-start(s32[2,4,2,2]{1,3,2,0:T(2,128)} %param.14) | copy-start | bytes 388
  0.8 4.3 %copy-start.2 = (bf16[3,80,320]{2,1,0:T(8,128)(2,1)S(1)}, bf16[3,80,320]{2,1,0:T(8,128)(2,1)}, u32[]{:S(2)}) copy-start(bf16[3,80,320]{2,1,0:T(8,128)(2,1)} %three.2) | copy-start | bytes 460804
  0.8 4.3 %copy-start.4 = (bf16[80,320]{1,0:T(8,128)(2,1)S(1)}, bf16[80,320]{1,0:T(8,128)(2,1)}, u32[]{:S(2)}) copy-start(bf16[80,320]{1,0:T(8,128)(2,1)} %one.2) | copy-start | bytes 153604
  0.8 4.4 %copy-start.3 = (bf16[3,80,320]{2,1,0:T(8,128)(2,1)S(1)}, bf16[3,80,320]{2,1,0:T(8,128)(2,1)}, u32[]{:S(2)}) copy-start(bf16[3,80,320]{2,1,0:T(8,128)(2,1)} %three.3) | copy-start | bytes 460804
  0.8 4.4 %copy-start.5 = (bf16[80,320]{1,0:T(8,128)(2,1)S(1)}, bf16[80,320]{1,0:T(8,128)(2,1)}, u32[]{:S(2)}) copy-start(bf16[80,320]{1,0:T(8,128)(2,1)} %one.3) | copy-start | bytes 153604
  2.0 16.1 %copy-start.1 = (bf16[3,3,320,320]{3,2,1,0:T(8,128)(2,1)S(1)}, bf16[3,3,320,320]{3,2,1,0:T(8,128)(2,1)}, u32[]{:S(2)}) copy-start(bf16[3,3,320,320]{3,2,1,0:T(8,128)(2,1)} %param.16) | copy-start | bytes 5529604
  2.0 4.6 %collective-permute-start = (f32[1,320]{1,0:T(1,128)S(1)}, f32[1,320]{1,0:T(1,128)S(1)}, u32[]{:S(2)}, u32[]{:S(2)}) collective-permute-start(f32[1,320]{1,0:T(1,128)S(1)} %time_share.1), channel_id=1, source_target_pairs={{0,1},{1,0},{2,3},{3,2},{4,5},{5,4},{6,7},{7,6},{8,9},{9,8},{10,11... | collective-permute-start | bytes 3848 | tf_op jit(solution)/shard_map/ppermute | solution.py:295
  6.6 4.6 %collective-permute-start.1 = (f32[1,320]{1,0:T(1,128)S(1)}, f32[1,320]{1,0:T(1,128)S(1)}, u32[]{:S(2)}, u32[]{:S(2)}) collective-permute-start(f32[1,320]{1,0:T(1,128)S(1)} %add.75), channel_id=1, source_target_pairs={{0,2},{1,3},{2,0},{3,1},{4,6},{5,7},{6,4},{7,5},{8,10},{9,11},{10,... | collective-permute-start | bytes 3848 | tf_op jit(solution)/shard_map/ppermute | solution.py:295
  11.2 9.5 %collective-permute-start.2 = (bf16[320,320]{1,0:T(8,128)(2,1)S(1)}, bf16[320,320]{1,0:T(8,128)(2,1)S(1)}, u32[]{:S(2)}, u32[]{:S(2)}) collective-permute-start(bf16[320,320]{1,0:T(8,128)(2,1)S(1)} %pad_maximum_fusion.2), channel_id=1, source_target_pairs={{0,1},{1,2},{2,3},{3,0},{4,5},{5,6},{6,7},{7,4},{8,9},{9,10},{10,1... | collective-permute-start | bytes 614408 | tf_op jit(solution)/shard_map/ppermute | solution.py:309
  13.2 17.6 %copy-start.6 = (s32[2,4]{1,0:T(2,128)S(1)}, s32[2,4]{1,0:T(2,128)}, u32[]{:S(2)}) copy-start(s32[2,4]{1,0:T(2,128)} %param.13) | copy-start | bytes 100
  16.0 9.9 %collective-permute-start.4 = (bf16[320,320]{1,0:T(8,128)(2,1)S(1)}, bf16[320,320]{1,0:T(8,128)(2,1)S(1)}, u32[]{:S(2)}, u32[]{:S(2)}) collective-permute-start(bf16[320,320]{1,0:T(8,128)(2,1)S(1)} %pad_maximum_fusion.2), channel_id=1, source_target_pairs={{1,0},{2,1},{3,2},{0,3},{5,4},{6,5},{7,6},{4,7},{9,8},{10,9},{11,1... | collective-permute-start | bytes 614408 | tf_op jit(solution)/shard_map/ppermute | solution.py:311
  20.8 9.1 %collective-permute-start.3 = (bf16[320,320]{1,0:T(8,128)(2,1)S(1)}, bf16[320,320]{1,0:T(8,128)(2,1)S(1)}, u32[]{:S(2)}, u32[]{:S(2)}) collective-permute-start(bf16[320,320]{1,0:T(8,128)(2,1)S(1)} %collective-permute-done.2.refs_0_), channel_id=1, source_target_pairs={{0,1},{1,2},{2,3},{3,0},{4,5},{5,6},{6,7},{7,4},{8,9},{9,10},{10,1... | collective-permute-start | bytes 614408 | tf_op jit(solution)/shard_map/ppermute | solution.py:309
  22.0 8.4 %collective-permute-start.9 = (bf16[256,320]{1,0:T(8,128)(2,1)S(1)}, bf16[256,320]{1,0:T(8,128)(2,1)S(1)}, u32[]{:S(2)}, u32[]{:S(2)}) collective-permute-start(bf16[256,320]{1,0:T(8,128)(2,1)S(1)} %get-tuple-element.31.normed.refs_5_), channel_id=1, source_target_pairs={{0,8},{4,12},{8,0},{12,4},{1,9},{5,13},{9,1},{13,5},{2,10},{6,14},... | collective-permute-start | bytes 491528 | tf_op jit(solution)/shard_map/ppermute | solution.py:282
  23.2 7.8 %collective-permute-start.5 = (bf16[320,320]{1,0:T(8,128)(2,1)S(1)}, bf16[320,320]{1,0:T(8,128)(2,1)S(1)}, u32[]{:S(2)}, u32[]{:S(2)}) collective-permute-start(bf16[320,320]{1,0:T(8,128)(2,1)S(1)} %collective-permute-done.2.refs_0_), channel_id=1, source_target_pairs={{0,4},{4,0},{8,12},{12,8},{1,5},{5,1},{9,13},{13,9},{2,6},{6,2},{1... | collective-permute-start | bytes 614408 | tf_op jit(solution)/shard_map/ppermute | solution.py:324
  25.9 5.1 %collective-permute-start.7 = (bf16[320,320]{1,0:T(8,128)(2,1)S(1)}, bf16[320,320]{1,0:T(8,128)(2,1)S(1)}, u32[]{:S(2)}, u32[]{:S(2)}) collective-permute-start(bf16[320,320]{1,0:T(8,128)(2,1)S(1)} %collective-permute-done.4.refs_2_), channel_id=1, source_target_pairs={{0,4},{4,0},{8,12},{12,8},{1,5},{5,1},{9,13},{13,9},{2,6},{6,2},{1... | collective-permute-start | bytes 614408 | tf_op jit(solution)/shard_map/ppermute | solution.py:324
  29.9 1.5 %collective-permute-start.6 = (bf16[320,320]{1,0:T(8,128)(2,1)S(1)}, bf16[320,320]{1,0:T(8,128)(2,1)S(1)}, u32[]{:S(2)}, u32[]{:S(2)}) collective-permute-start(bf16[320,320]{1,0:T(8,128)(2,1)S(1)} %collective-permute-done.3.refs_1_), channel_id=1, source_target_pairs={{0,4},{4,0},{8,12},{12,8},{1,5},{5,1},{9,13},{13,9},{2,6},{6,2},{1... | collective-permute-start | bytes 614408 | tf_op jit(solution)/shard_map/ppermute | solution.py:324
  29.9 3.4 %collective-permute-start.8 = (bf16[256,320]{1,0:T(8,128)(2,1)S(1)}, bf16[256,320]{1,0:T(8,128)(2,1)S(1)}, u32[]{:S(2)}, u32[]{:S(2)}) collective-permute-start(bf16[256,320]{1,0:T(8,128)(2,1)S(1)} %get-tuple-element.31.normed.refs_5_), channel_id=1, source_target_pairs={{0,4},{4,0},{8,12},{12,8},{1,5},{5,1},{9,13},{13,9},{2,6},{6,2},{1... | collective-permute-start | bytes 491528 | tf_op jit(solution)/shard_map/ppermute | solution.py:282
  30.4 2.9 %collective-permute-start.10 = (bf16[256,320]{1,0:T(8,128)(2,1)S(1)}, bf16[256,320]{1,0:T(8,128)(2,1)S(1)}, u32[]{:S(2)}, u32[]{:S(2)}) collective-permute-start(bf16[256,320]{1,0:T(8,128)(2,1)S(1)} %collective-permute-done.9.refs_7_), channel_id=1, source_target_pairs={{0,4},{4,0},{8,12},{12,8},{1,5},{5,1},{9,13},{13,9},{2,6},{6,2},{1... | collective-permute-start | bytes 491528 | tf_op jit(solution)/shard_map/ppermute | solution.py:282
  37.9 9.6 %collective-permute-start.11 = (bf16[256,320]{1,0:T(8,128)(2,1)S(1)}, bf16[256,320]{1,0:T(8,128)(2,1)S(1)}, u32[]{:S(2)}, u32[]{:S(2)}) collective-permute-start(bf16[256,320]{1,0:T(8,128)(2,1)S(1)} %get-tuple-element.36.rows), channel_id=1, source_target_pairs={{0,1},{1,2},{2,3},{3,0},{4,5},{5,6},{6,7},{7,4},{8,9},{9,10},{10,1... | collective-permute-start | bytes 491528 | tf_op jit(solution)/shard_map/ppermute | solution.py:309
  38.0 12.2 %collective-permute-start.13 = (bf16[256,320]{1,0:T(8,128)(2,1)S(1)}, bf16[256,320]{1,0:T(8,128)(2,1)S(1)}, u32[]{:S(2)}, u32[]{:S(2)}) collective-permute-start(bf16[256,320]{1,0:T(8,128)(2,1)S(1)} %get-tuple-element.36.rows), channel_id=1, source_target_pairs={{1,0},{2,1},{3,2},{0,3},{5,4},{6,5},{7,6},{4,7},{9,8},{10,9},{11,1... | collective-permute-start | bytes 491528 | tf_op jit(solution)/shard_map/ppermute | solution.py:311
  47.5 7.6 %collective-permute-start.12 = (bf16[256,320]{1,0:T(8,128)(2,1)S(1)}, bf16[256,320]{1,0:T(8,128)(2,1)S(1)}, u32[]{:S(2)}, u32[]{:S(2)}) collective-permute-start(bf16[256,320]{1,0:T(8,128)(2,1)S(1)} %collective-permute-done.11.rows), channel_id=1, source_target_pairs={{0,1},{1,2},{2,3},{3,0},{4,5},{5,6},{6,7},{7,4},{8,9},{9,10},{10,1... | collective-permute-start | bytes 491528 | tf_op jit(solution)/shard_map/ppermute | solution.py:309
